TPU v7x, 32 devices: a whole 2x2x4 slice. The times are simulated.
32 devices in a mesh: groups: 2 (over y), seq: 4 (over z), expert: 4 (over x, core), tensor: 1.
Axes of the slice: x: 2, y: 2, z: 4, core: 2. Of those that a mesh axis runs over, the one named last changes fastest.
Arguments:
- text_tokens: bfloat16 [1024, 2560], P(('groups', 'seq', 'expert'), 'tensor'), parts along dimension 0, may hold values from -6 to 6
- panels: bfloat16 [512, 8, 2560], P(('groups', 'seq', 'expert'), None, 'tensor'), parts along dimension 0, may hold values from -6 to 6
- panel_target: int32 [512], P(('groups', 'seq', 'expert')), parts along dimension 0, may hold values from 0 to 255, as said below
- expert_ids: int32 [5120, 6], P(('groups', 'seq', 'expert')), parts along dimension 0, may hold values from 0 to 15, all different within a row; in each aligned block of 160 rows (0 to 159, 160 to 319, ...) at most 120 rows name the same one
- gate_weights: float32 [5120, 6], P(('groups', 'seq', 'expert')), parts along dimension 0, may hold values from 0.05 to 0.5
- gate_up_weight: bfloat16 [16, 2, 1408, 2560], P(('seq', 'expert'), None, 'tensor'), may hold values from -0.125 to 0.125
- down_weight: bfloat16 [16, 1408, 2560], P(('seq', 'expert'), 'tensor'), may hold values from -0.15625 to 0.15625
Outputs:
- mixed_out: bfloat16 [5120, 2560], P(('groups', 'seq', 'expert'), 'tensor'), parts along dimension 0
There are 2 independent parts, one for each index of `groups`. A program takes and returns all parts, laid end to end along the dimension named above; an argument that names none is the same for every part. Nothing has to cross between parts.
Inputs may be any that keep to these rules, and one draw needn't show every extreme that they name: `panel_target`: every value appears once. A panel held by owner index d targets an owner with the same index along expert (d % 4 equal). One owner sends at most 6 of its panels to one owner, and exactly 6 to some owner. `expert_ids`: the 6 experts of a token differ. Among the 160 tokens of one owner (aligned blocks of rows), no expert is named more than 120 times.
All inputs are finite; a program needn't handle non-finite values.
Results may differ from a plain program's by a relative error of at most 0.0057.
Values may be sent and summed in bfloat16 or wider, within the bound.
No kernel may reach another device: no remote copies, remote signals or barrier semaphores. Data moves between devices by JAX's collectives and lax.ppermute only.
A program may use at most 128 MiB of HBM per device.

v0:
```python
import jax
import jax.numpy as jnp
from jax import lax
from jax.sharding import PartitionSpec as P


def shards(
    text_tokens, panels, panel_target, expert_ids, gate_weights, gate_up_weight, down_weight
):
    seq_count = lax.axis_size("seq")
    expert_count = lax.axis_size("expert")
    owner_count = seq_count * expert_count
    pan_count = panels.shape[0]
    cap_panel = max(2, (3 * pan_count + 2 * seq_count - 1) // (2 * seq_count))
    slot_range = jnp.arange(pan_count, dtype=jnp.int32)
    owner_dev = panel_target // pan_count
    dest_seq = owner_dev // expert_count
    dest_slot = panel_target % pan_count
    onehot = (dest_seq[:, None] == jnp.arange(seq_count, dtype=jnp.int32)[None, :]).astype(
        jnp.int32
    )
    earlier = jnp.cumsum(onehot, axis=0) - onehot
    placing = dest_seq * cap_panel + jnp.sum(earlier * onehot, axis=1)
    outgoing = (
        jnp.zeros((seq_count * cap_panel,) + panels.shape[1:], panels.dtype).at[placing].set(panels)
    )
    labels = jnp.full((seq_count * cap_panel,), -1, jnp.int32).at[placing].set(dest_slot)
    arrived, arrived_labels = (
        lax.all_to_all(outgoing, "seq", split_axis=0, concat_axis=0, tiled=True),
        lax.all_to_all(labels, "seq", split_axis=0, concat_axis=0, tiled=True),
    )
    matches = (arrived_labels[None, :] == slot_range[:, None]).astype(jnp.bfloat16)
    image_rows = jnp.einsum(
        "qn,nrd->qrd", matches, arrived, preferred_element_type=jnp.float32
    ).astype(jnp.bfloat16)
    half_rows = jnp.concatenate([text_tokens, image_rows.reshape(-1, image_rows.shape[-1])], axis=0)
    tokens = lax.all_gather(half_rows, "tensor", axis=1, tiled=True)
    feature_width = tokens.shape[1]
    tok_count, top_count = expert_ids.shape
    experts_all = owner_count * gate_up_weight.shape[0]
    capacity = min(tok_count, (2 * tok_count * top_count // experts_all + 7) // 8 * 8)
    flat_ids = expert_ids.reshape(-1)
    onehot_ids = (flat_ids[:, None] == jnp.arange(experts_all, dtype=jnp.int32)[None, :]).astype(
        jnp.int32
    )
    before = jnp.cumsum(onehot_ids, axis=0) - onehot_ids
    placing_ids = flat_ids * capacity + jnp.sum(before * onehot_ids, axis=1)
    source_rows = jnp.arange(tok_count * top_count, dtype=jnp.int32) // top_count
    outgoing_rows = (
        jnp.zeros((experts_all * capacity, feature_width), tokens.dtype)
        .at[placing_ids]
        .set(tokens[source_rows])
    )
    load_counts = jnp.sum(onehot_ids, axis=0).reshape(experts_all, 1)
    outgoing_rows = outgoing_rows.reshape(experts_all, capacity, feature_width)
    pair_weight = gate_up_weight[0]
    out_weight = down_weight[0]
    arrived_rows, arrived_loads = (
        lax.all_to_all(outgoing_rows, ("seq", "expert"), split_axis=0, concat_axis=0, tiled=True),
        lax.all_to_all(load_counts, ("seq", "expert"), split_axis=0, concat_axis=0, tiled=True),
    )
    arrived_rows = arrived_rows.reshape(-1, feature_width)
    slot_total = arrived_rows.shape[0]
    slot_index = jnp.arange(capacity, dtype=jnp.int32)
    is_live = (slot_index[None, :] < arrived_loads).reshape(-1)
    live_int = is_live.astype(jnp.int32)
    compact_at = jnp.cumsum(live_int) - live_int
    live_total = jnp.sum(live_int)
    compact_src = (
        jnp.zeros((slot_total,), jnp.int32)
        .at[jnp.where(is_live, compact_at, slot_total)]
        .set(jnp.arange(slot_total, dtype=jnp.int32), mode="drop")
    )

    def expert_block(block_no, partial_out):
        chosen = lax.dynamic_slice_in_dim(compact_src, block_no * 128, 128)
        block_rows = arrived_rows[chosen]
        gate_up = jnp.einsum(
            "rd,gfd->grf", block_rows, pair_weight, preferred_element_type=jnp.float32
        )
        hidden = (jax.nn.silu(gate_up[0]) * gate_up[1]).astype(jnp.bfloat16)
        result = jnp.dot(hidden, out_weight, preferred_element_type=jnp.float32)
        return lax.dynamic_update_slice_in_dim(partial_out, result, block_no * 128, 0)

    block_total = (live_total + 127) // 128
    padded_total = (slot_total + 127) // 128 * 128
    partial_out = lax.fori_loop(
        0, block_total, expert_block, jnp.zeros((padded_total, feature_width), jnp.float32)
    )
    summed = lax.psum_scatter(partial_out, "tensor", scatter_dimension=1, tiled=True).astype(
        jnp.bfloat16
    )
    out_width = summed.shape[1]
    returned = jnp.where(
        is_live[:, None], summed[jnp.where(is_live, compact_at, 0)], jnp.zeros((), jnp.bfloat16)
    )
    came_back = lax.all_to_all(
        returned.reshape(experts_all, capacity, out_width),
        ("seq", "expert"),
        split_axis=0,
        concat_axis=0,
        tiled=True,
    )
    half_width = came_back.shape[2]
    picked = came_back.reshape(-1, half_width)[placing_ids].reshape(
        tok_count, top_count, half_width
    )
    mixed_out = jnp.sum(gate_weights[:, :, None] * picked.astype(jnp.float32), axis=1)
    return mixed_out.astype(jnp.bfloat16)


def solution(mesh):
    placed = (
        P(("groups", "seq", "expert"), "tensor"),
        P(("groups", "seq", "expert"), None, "tensor"),
        P(("groups", "seq", "expert")),
        P(("groups", "seq", "expert"), None),
        P(("groups", "seq", "expert"), None),
        P(("seq", "expert"), None, "tensor", None),
        P(("seq", "expert"), "tensor", None),
    )
    return jax.shard_map(
        shards,
        mesh=mesh,
        in_specs=placed,
        out_specs=P(("groups", "seq", "expert"), "tensor"),
        check_vma=False,
    )
```

profile of v0, /device:TPU:11, one launch (start us, length us, event | category | flops | bytes accessed | tf_op | source)
XLA Modules:
  0.0 912.4 jit_solution(13532973829083209814)
XLA Ops:
  24.8 10.7 %all-to-all-done.2 = bf16[24,8,2560]{2,1,0:T(8,128)(2,1)S(1)} async-done(((bf16[24,8,2560]{2,1,0:T(8,128)(2,1)}), bf16[24,8,2560]{2,1,0:T(8,128)(2,1)S(1)}, u32[]{:S(2)}, u32[]{:S(2)}) %all-to-all-start.2) | async-done | bytes 983072 | tf_op jit(solution)/shard_map/all_to_all | solution.py:29
  35.5 9.0 all-to-all-start
  46.6 30.5 %scatter_custom_fusion.3 = bf16[1920,2560]{1,0:T(8,128)(2,1)} fusion(s32[960]{0:T(1024)S(1)} %bitcast.79, bf16[160,2560]{1,0:T(8,128)(2,1)S(1)} %pad_maximum_fusion, s32[1024]{0:T(1024)S(1)} %pad_clamp_fusion.3, bf16[]{:T(256)} %constant.99.clone.1), kind=kCustom, calls=%fused_computation.21 | custom fusion | bytes 9830402 | tf_op jit(solution)/shard_map/scatter | solution.py:52
  77.1 6.0 all-to-all-start.3
  85.7 10.0 %scatter_custom_fusion = s32[1920]{0:T(1024)S(1)} fusion(s32[1920]{0:T(1024)S(1)} %get-tuple-element.45, s32[1920]{0:T(1024)S(1)} %iota.25, s32[]{:T(128)} %constant.92.clone.1), kind=kCustom, calls=%fused_computation.61 | custom fusion | bytes 7684 | tf_op jit(solution)/shard_map/scatter | solution.py:72
  95.7 200.6 %all-to-all-done.3 = bf16[16,120,2560]{2,1,0:T(8,128)(2,1)} async-done(((bf16[16,120,2560]{2,1,0:T(8,128)(2,1)}), bf16[16,120,2560]{2,1,0:T(8,128)(2,1)}, u32[]{:S(2)}, u32[]{:S(2)}) %all-to-all-start.3) | async-done | bytes 9830432 | tf_op jit(solution)/shard_map/all_to_all | solution.py:59
  300.8 151.7 %while.10 = (s32[]{:T(128)}, bf16[1920,2560]{1,0:T(8,128)(2,1)}, s32[]{:T(128)}, s32[1920]{0:T(1024)S(1)}, bf16[1920,2560]{1,0:T(8,128)(2,1)}, /*index=5*/bf16[2...) while((s32[]{:T(128)}, bf16[1920,2560]{1,0:T(8,128)(2,1)}, ...), condition=%wide.region_14.15_spmd, body=%wide.region_13.14_spmd.sunk | while | flops 2769323520 | bytes 27793572 | solution.py:87
  300.8 6.7 gather_fusion
  307.5 9.7 %convolution_bitcast_fusion.2 = f32[2,128,1408]{2,1,0:T(8,128)S(1)} fusion(bf16[2,1408,2560]{2,1,0:T(8,128)(2,1)} %get-tuple-element.137, bf16[128,2560]{1,0:T(8,128)(2,1)S(1)} %gather_fusion), kind=kOutput, calls=%fused_computation.9.clone.1 | convolution fusion | flops 1845493760 | bytes 16515072 | tf_op jit(solution)/shard_map/while/body/rd,gfd->grf/dot_general | solution.py:78
  322.5 6.7 gather_fusion
  329.2 9.7 %convolution_bitcast_fusion.2 = f32[2,128,1408]{2,1,0:T(8,128)S(1)} fusion(bf16[2,1408,2560]{2,1,0:T(8,128)(2,1)} %get-tuple-element.137, bf16[128,2560]{1,0:T(8,128)(2,1)S(1)} %gather_fusion), kind=kOutput, calls=%fused_computation.9.clone.1 | convolution fusion | flops 1845493760 | bytes 16515072 | tf_op jit(solution)/shard_map/while/body/rd,gfd->grf/dot_general | solution.py:78
  338.9 5.2 convolution_dynamic-update-slice_fusion.2
  344.2 6.7 gather_fusion
  350.8 9.7 %convolution_bitcast_fusion.2 = f32[2,128,1408]{2,1,0:T(8,128)S(1)} fusion(bf16[2,1408,2560]{2,1,0:T(8,128)(2,1)} %get-tuple-element.137, bf16[128,2560]{1,0:T(8,128)(2,1)S(1)} %gather_fusion), kind=kOutput, calls=%fused_computation.9.clone.1 | convolution fusion | flops 1845493760 | bytes 16515072 | tf_op jit(solution)/shard_map/while/body/rd,gfd->grf/dot_general | solution.py:78
  365.8 6.7 gather_fusion
  372.5 9.7 %convolution_bitcast_fusion.2 = f32[2,128,1408]{2,1,0:T(8,128)S(1)} fusion(bf16[2,1408,2560]{2,1,0:T(8,128)(2,1)} %get-tuple-element.137, bf16[128,2560]{1,0:T(8,128)(2,1)S(1)} %gather_fusion), kind=kOutput, calls=%fused_computation.9.clone.1 | convolution fusion | flops 1845493760 | bytes 16515072 | tf_op jit(solution)/shard_map/while/body/rd,gfd->grf/dot_general | solution.py:78
  387.4 6.7 gather_fusion
  394.1 9.7 %convolution_bitcast_fusion.2 = f32[2,128,1408]{2,1,0:T(8,128)S(1)} fusion(bf16[2,1408,2560]{2,1,0:T(8,128)(2,1)} %get-tuple-element.137, bf16[128,2560]{1,0:T(8,128)(2,1)S(1)} %gather_fusion), kind=kOutput, calls=%fused_computation.9.clone.1 | convolution fusion | flops 1845493760 | bytes 16515072 | tf_op jit(solution)/shard_map/while/body/rd,gfd->grf/dot_general | solution.py:78
  403.8 5.2 convolution_dynamic-update-slice_fusion.2
  409.1 6.7 gather_fusion
  415.8 9.7 %convolution_bitcast_fusion.2 = f32[2,128,1408]{2,1,0:T(8,128)S(1)} fusion(bf16[2,1408,2560]{2,1,0:T(8,128)(2,1)} %get-tuple-element.137, bf16[128,2560]{1,0:T(8,128)(2,1)S(1)} %gather_fusion), kind=kOutput, calls=%fused_computation.9.clone.1 | convolution fusion | flops 1845493760 | bytes 16515072 | tf_op jit(solution)/shard_map/while/body/rd,gfd->grf/dot_general | solution.py:78
  425.5 5.2 convolution_dynamic-update-slice_fusion.2
  430.8 6.7 gather_fusion
  437.5 9.7 %convolution_bitcast_fusion.2 = f32[2,128,1408]{2,1,0:T(8,128)S(1)} fusion(bf16[2,1408,2560]{2,1,0:T(8,128)(2,1)} %get-tuple-element.137, bf16[128,2560]{1,0:T(8,128)(2,1)S(1)} %gather_fusion), kind=kOutput, calls=%fused_computation.9.clone.1 | convolution fusion | flops 1845493760 | bytes 16515072 | tf_op jit(solution)/shard_map/while/body/rd,gfd->grf/dot_general | solution.py:78
  447.2 5.2 convolution_dynamic-update-slice_fusion.2
  452.5 24.5 %gather_fusion.1 = bf16[1920,2560]{1,0:T(8,128)(2,1)} fusion(bf16[1920,2560]{1,0:T(8,128)(2,1)} %get-tuple-element.43, s32[2048]{0:T(1024)S(1)} %pad_clamp_fusion.1), kind=kCustom, calls=%fused_computation.2 | custom fusion | bytes 19668480 | tf_op jit(solution)/shard_map/gather | solution.py:95
  477.0 8.3 broadcast_select_fusion
  485.3 178.2 %all-to-all-start.4 = ((bf16[16,120,2560]{2,1,0:T(8,128)(2,1)}), bf16[16,120,2560]{2,1,0:T(8,128)(2,1)}, u32[]{:S(2)}, u32[]{:S(2)}) async-start(bf16[16,120,2560]{2,1,0:T(8,128)(2,1)} %broadcast_select_fusion), calls=%async_computation.4 | async-start | bytes 19660800 | tf_op jit(solution)/shard_map/all_to_all | solution.py:97
  663.6 213.1 %all-to-all-done.4 = bf16[16,120,2560]{2,1,0:T(8,128)(2,1)} async-done(((bf16[16,120,2560]{2,1,0:T(8,128)(2,1)}), bf16[16,120,2560]{2,1,0:T(8,128)(2,1)}, u32[]{:S(2)}, u32[]{:S(2)}) %all-to-all-start.4) | async-done | bytes 9830432 | tf_op jit(solution)/shard_map/all_to_all | solution.py:97
  876.7 15.4 %gather_fusion.2 = bf16[960,2560]{1,0:T(8,128)(2,1)} fusion(bf16[1920,2560]{1,0:T(8,128)(2,1)} %bitcast.18, s32[1024]{0:T(1024)S(1)} %pad_clamp_fusion.2), kind=kCustom, calls=%fused_computation.3 | custom fusion | bytes 9834240 | tf_op jit(solution)/shard_map/gather | solution.py:105
  892.1 9.4 %reshape.235 = f32[160,6,2560]{2,1,0:T(8,128)} reshape(bf16[960,2560]{1,0:T(8,128)(2,1)} %gather_fusion.2) | data formatting | bytes 14745600 | tf_op jit(solution)/shard_map/convert_element_type | solution.py:108
  901.5 10.8 %multiply_reduce_fusion = bf16[160,2560]{1,0:T(8,128)(2,1)} fusion(f32[160,6,2560]{2,1,0:T(8,128)} %reshape.235, f32[160,6]{1,0:T(8,128)S(1)} %copy.28), kind=kLoop, calls=%fused_computation.19 | loop fusion | flops 4505600 | bytes 10653440 | tf_op jit(solution)/shard_map/reduce_sum | solution.py:108
  (75 shorter events, 49.4 us)
Async XLA Ops:
  2.3 8.8 all-to-all-start.1
  11.1 24.4 %all-to-all-start.2 = ((bf16[24,8,2560]{2,1,0:T(8,128)(2,1)}), bf16[24,8,2560]{2,1,0:T(8,128)(2,1)S(1)}, u32[]{:S(2)}, u32[]{:S(2)}) async-start(bf16[24,8,2560]{2,1,0:T(8,128)(2,1)} %scatter_fusion), calls=%async_computation.2 | async-start | bytes 1966080 | tf_op jit(solution)/shard_map/all_to_all | solution.py:29
  35.5 41.6 %all-to-all-start = ((s32[16,1,1]{2,1,0:T(1,128)}), s32[16,1,1]{2,1,0:T(1,128)S(1)}, u32[]{:S(2)}, u32[]{:S(2)}) async-start(s32[16,1,1]{2,1,0:T(1,128)} %copy.30), calls=%async_computation | async-start | bytes 16384 | tf_op jit(solution)/shard_map/all_to_all | solution.py:60
  77.1 219.3 %all-to-all-start.3 = ((bf16[16,120,2560]{2,1,0:T(8,128)(2,1)}), bf16[16,120,2560]{2,1,0:T(8,128)(2,1)}, u32[]{:S(2)}, u32[]{:S(2)}) async-start(bf16[16,120,2560]{2,1,0:T(8,128)(2,1)} %bitcast.71), calls=%async_computation.3 | async-start | bytes 19660800 | tf_op jit(solution)/shard_map/all_to_all | solution.py:59
  485.3 178.2 %copy-start = (f32[160,6]{0,1:T(8,128)S(1)}, f32[160,6]{0,1:T(8,128)}, u32[]{:S(2)}) copy-start(f32[160,6]{0,1:T(8,128)} %param.13) | copy-start | bytes 11524
  485.3 391.4 %all-to-all-start.4 = ((bf16[16,120,2560]{2,1,0:T(8,128)(2,1)}), bf16[16,120,2560]{2,1,0:T(8,128)(2,1)}, u32[]{:S(2)}, u32[]{:S(2)}) async-start(bf16[16,120,2560]{2,1,0:T(8,128)(2,1)} %broadcast_select_fusion), calls=%async_computation.4 | async-start | bytes 19660800 | tf_op jit(solution)/shard_map/all_to_all | solution.py:97
where the time goes:
time: 918 us; the launch traced here: 912 us
  waiting for transfers between devices  424 us (46%)
  starting transfers between devices  202 us (22%)
  local copies, waits for them, and re-layouts  150 us (16%)
  matrix products  105 us (11%)
  other arithmetic  29.5 us (3%)
    all_to_all x1, waiting for transfers between devices, shards(): lax.all_to_all(returned.reshape(experts_all, capacity, out_width), ('seq'...  213 us
    all_to_all x1, waiting for transfers between devices, shards(): lax.all_to_all(outgoing_rows, ('seq', 'expert'), split_axis=0, concat_axi...  201 us
    all_to_all x1, starting transfers between devices, shards(): lax.all_to_all(returned.reshape(experts_all, capacity, out_width), ('seq'...  178 us
    dot_general x7, matrix products, expert_block(): jnp.einsum('rd,gfd->grf', block_rows, pair_weight, preferred_element_type...  67.8 us
    gather x7, local copies, waits for them, and re-layouts, expert_block(): block_rows = arrived_rows[chosen]  46.8 us
    dot_general x7, matrix products, expert_block(): result = jnp.dot(hidden, out_weight, preferred_element_type=jnp.float32)  36.3 us
    scatter x1, local copies, waits for them, and re-layouts, shards(): outgoing_rows = jnp.zeros((experts_all * capacity, feature_width), tokens...  30.5 us
    gather x1, local copies, waits for them, and re-layouts, shards(): summed[jnp.where(is_live, compact_at, 0)]  24.5 us
  transfers between devices with their start and end apart: 5, of which 3 were waited for; matrix products, arithmetic and copies ran while one was open for 6% of the time, Pallas kernels for 0%

commit v1 on v0

--- a/solution.py
+++ b/solution.py
@@ -1,10 +1,17 @@
+import functools
+
 import jax
 import jax.numpy as jnp
+import numpy as np
 from jax import lax
+from jax.experimental import pallas as pl
+from jax.experimental.pallas import tpu as pltpu
 from jax.sharding import PartitionSpec as P
 
-
-def shards(
+AXES = ("seq", "expert")
+
+
+def slot_shards(
     text_tokens, panels, panel_target, expert_ids, gate_weights, gate_up_weight, down_weight
 ):
     seq_count = lax.axis_size("seq")
@@ -38,7 +45,7 @@
     feature_width = tokens.shape[1]
     tok_count, top_count = expert_ids.shape
     experts_all = owner_count * gate_up_weight.shape[0]
-    capacity = min(tok_count, (2 * tok_count * top_count // experts_all + 7) // 8 * 8)
+    capacity = slot_capacity(tok_count, top_count, experts_all)
     flat_ids = expert_ids.reshape(-1)
     onehot_ids = (flat_ids[:, None] == jnp.arange(experts_all, dtype=jnp.int32)[None, :]).astype(
         jnp.int32
@@ -56,8 +63,8 @@
     pair_weight = gate_up_weight[0]
     out_weight = down_weight[0]
     arrived_rows, arrived_loads = (
-        lax.all_to_all(outgoing_rows, ("seq", "expert"), split_axis=0, concat_axis=0, tiled=True),
-        lax.all_to_all(load_counts, ("seq", "expert"), split_axis=0, concat_axis=0, tiled=True),
+        lax.all_to_all(outgoing_rows, AXES, split_axis=0, concat_axis=0, tiled=True),
+        lax.all_to_all(load_counts, AXES, split_axis=0, concat_axis=0, tiled=True),
     )
     arrived_rows = arrived_rows.reshape(-1, feature_width)
     slot_total = arrived_rows.shape[0]
@@ -96,7 +103,7 @@
     )
     came_back = lax.all_to_all(
         returned.reshape(experts_all, capacity, out_width),
-        ("seq", "expert"),
+        AXES,
         split_axis=0,
         concat_axis=0,
         tiled=True,
@@ -107,6 +114,254 @@
     )
     mixed_out = jnp.sum(gate_weights[:, :, None] * picked.astype(jnp.float32), axis=1)
     return mixed_out.astype(jnp.bfloat16)
+
+
+def slot_capacity(tok_count, top_count, experts_all):
+    return min(tok_count, (2 * tok_count * top_count // experts_all + 7) // 8 * 8)
+
+
+class Ring:
+    def __init__(self, seq_count, expert_count):
+        self.seq, self.expert = seq_count, expert_count
+        self.chips = 2 * seq_count
+        self.half = seq_count
+        self.devices = seq_count * expert_count
+        self.slots = [(0, 0), (0, 1), (self.half, 0), (self.half, 1)]
+        for s in range(1, self.half):
+            self.slots += [(s, 0), (-s, 0), (s, 1), (-s, 1)]
+        slot_of = {(r % self.chips, k): i for i, (r, k) in enumerate(self.slots)}
+        self.owner_of = np.zeros((self.devices, len(self.slots)), np.int32)
+        self.sources_of = np.zeros((self.devices, len(self.slots), seq_count), np.int32)
+        for d in range(self.devices):
+            p, c = self.place(d)
+            for i, (r, k) in enumerate(self.slots):
+                q = (p + r) % self.chips
+                self.owner_of[d, i] = self.device(q, c ^ k)
+                x = q // seq_count
+                for z in range(seq_count):
+                    pos = z if x == 0 else self.chips - 1 - z
+                    self.sources_of[d, i, z] = slot_of[((pos - p) % self.chips, k)]
+
+    def place(self, d):
+        z, e = divmod(d, self.expert)
+        x, c = divmod(e, 2)
+        return (z if x == 0 else self.chips - 1 - z), c
+
+    def device(self, pos, c):
+        x, z = (0, pos) if pos < self.seq else (1, self.chips - 1 - pos)
+        return z * self.expert + x * 2 + c
+
+    def step(self, by):
+        pairs = []
+        for d in range(self.devices):
+            p, c = self.place(d)
+            pairs.append((d, self.device((p + by) % self.chips, c)))
+        return pairs
+
+    def swap(self):
+        return [(d, d ^ 1) for d in range(self.devices)]
+
+
+def hidden_kernel(count, rows, *refs):
+    x_refs = refs[:count]
+    w_ref = refs[count]
+    out_ref, x_all = refs[-2:]
+
+    @pl.when(pl.program_id(0) == 0)
+    def _():
+        for i in range(count):
+            x_all[i * rows : (i + 1) * rows, :] = x_refs[i][...]
+
+    width = w_ref.shape[2]
+    weight = w_ref[0].reshape(2 * width, w_ref.shape[3])
+    both = lax.dot_general(
+        x_all[...], weight, (((1,), (1,)), ((), ())), preferred_element_type=jnp.float32
+    )
+    gate, up = both[:, :width], both[:, width:]
+    out_ref[...] = (gate / (1.0 + jnp.exp(-gate)) * up).astype(out_ref.dtype)
+
+
+def hidden_call(blocks, gate_up_weight, hidden, first_slot, slot_count):
+    rows, wide = blocks[0].shape
+    _, _, ff, _ = gate_up_weight.shape
+    count = len(blocks)
+    chunk = 128
+    place = first_slot // count
+    whole = pl.BlockSpec((rows, wide), lambda i: (0, 0))
+    in_specs = [whole] * count + [pl.BlockSpec((1, 2, chunk, wide), lambda i: (0, 0, i, 0))]
+    args = list(blocks) + [gate_up_weight]
+    aliases = {}
+    if hidden is not None:
+        in_specs.append(pl.BlockSpec(memory_space=pl.ANY))
+        args.append(hidden)
+        aliases = {len(args) - 1: 0}
+    return pl.pallas_call(
+        functools.partial(hidden_kernel, count, rows),
+        grid=(ff // chunk,),
+        in_specs=in_specs,
+        out_specs=pl.BlockSpec((count * rows, chunk), lambda i: (place, i)),
+        out_shape=jax.ShapeDtypeStruct((slot_count * rows, ff), jnp.bfloat16),
+        scratch_shapes=[pltpu.VMEM((count * rows, wide), jnp.bfloat16)],
+        input_output_aliases=aliases,
+        compiler_params=pltpu.CompilerParams(vmem_limit_bytes=32 * 1024 * 1024),
+        cost_estimate=pl.CostEstimate(
+            flops=4 * count * rows * wide * ff,
+            bytes_accessed=4 * ff * wide + 2 * count * rows * (wide + ff),
+            transcendentals=count * rows * ff,
+        ),
+    )(*args)
+
+
+def down_kernel(
+    slots, first_slot, rows, text_rows, sources_ref, hidden_ref, order_ref, scale_ref, w_ref,
+    own_ref, other_ref, picked,
+):
+    image_rows = rows - text_rows
+    seq_count = order_ref.shape[2] // image_rows
+
+    @pl.when(pl.program_id(0) == 0)
+    def _():
+        for j in range(slots):
+            at = (first_slot + j) * rows
+            picked[j * rows : j * rows + text_rows, :] = hidden_ref[at : at + text_rows, :]
+            wanted = lax.broadcasted_iota(jnp.int32, (image_rows, order_ref.shape[2]), 0)
+            match = jnp.where(order_ref[j] == wanted, 1.0, 0.0).astype(jnp.bfloat16)
+            total = jnp.zeros((image_rows, hidden_ref.shape[1]), jnp.float32)
+            for z in range(seq_count):
+                source = sources_ref[(first_slot + j) * seq_count + z]
+                start = pl.multiple_of(source * rows + text_rows, 16)
+                total += jnp.dot(
+                    match[:, z * image_rows : (z + 1) * image_rows],
+                    hidden_ref[pl.ds(start, image_rows), :],
+                    preferred_element_type=jnp.float32,
+                )
+            picked[j * rows + text_rows : (j + 1) * rows, :] = total.astype(jnp.bfloat16)
+
+    result = jnp.dot(picked[...], w_ref[0], preferred_element_type=jnp.float32)
+    scaled = (result.astype(jnp.bfloat16).astype(jnp.float32) * scale_ref[...]).astype(jnp.bfloat16)
+    half = slots * rows // 2
+    own_ref[...] = scaled[:half]
+    other_ref[...] = scaled[half:]
+
+
+def down_call(hidden, order, scale, sources, down_weight, first_slot, slots, rows, text_rows):
+    _, ff, wide = down_weight.shape
+    chunk = 512
+    half = slots * rows // 2
+    slot_total = order.shape[0]
+    grid_spec = pltpu.PrefetchScalarGridSpec(
+        num_scalar_prefetch=1,
+        grid=(wide // chunk,),
+        in_specs=[
+            pl.BlockSpec(hidden.shape, lambda i, s: (0, 0), pipeline_mode=pl.Buffered(1)),
+            pl.BlockSpec((slots, 1, order.shape[2]), lambda i, s: (first_slot // slots, 0, 0)),
+            pl.BlockSpec((slots * rows, 1), lambda i, s: (first_slot // slots, 0)),
+            pl.BlockSpec((1, ff, chunk), lambda i, s: (0, 0, i)),
+        ],
+        out_specs=[pl.BlockSpec((half, chunk), lambda i, s: (0, i))] * 2,
+        scratch_shapes=[pltpu.VMEM((slots * rows, ff), jnp.bfloat16)],
+    )
+    del slot_total
+    return pl.pallas_call(
+        functools.partial(down_kernel, slots, first_slot, rows, text_rows),
+        grid_spec=grid_spec,
+        out_shape=[jax.ShapeDtypeStruct((half, wide), jnp.bfloat16)] * 2,
+        compiler_params=pltpu.CompilerParams(vmem_limit_bytes=40 * 1024 * 1024),
+        cost_estimate=pl.CostEstimate(
+            flops=2 * slots * rows * wide * ff,
+            bytes_accessed=2 * ff * wide + 2 * hidden.size + 2 * slots * rows * wide,
+            transcendentals=0,
+        ),
+    )(sources, hidden, order, scale, down_weight)
+
+
+def add_up(*parts):
+    total = parts[0].astype(jnp.float32)
+    for part in parts[1:]:
+        total = total + part.astype(jnp.float32)
+    return total.astype(jnp.bfloat16)
+
+
+def ring_shards(
+    text_tokens, panels, panel_target, expert_ids, gate_weights, gate_up_weight, down_weight
+):
+    seq_count, expert_count = lax.axis_size("seq"), lax.axis_size("expert")
+    ring = Ring(seq_count, expert_count)
+    pan_count, panel_rows, wide = panels.shape
+    text_rows = text_tokens.shape[0]
+    tok_count, top_count = expert_ids.shape
+    image_rows = pan_count * panel_rows
+    slot_count = len(ring.slots)
+    me = lax.axis_index(AXES)
+
+    def onward(array):
+        return lax.ppermute(array, AXES, ring.step(1))
+
+    def back(array):
+        return lax.ppermute(array, AXES, ring.step(-1))
+
+    def across(array):
+        return lax.ppermute(array, AXES, ring.swap())
+
+    own = jnp.concatenate([text_tokens, panels.reshape(image_rows, wide)], axis=0)
+    before, after = onward(own), back(own)
+    other = across(own)
+
+    table = jnp.concatenate(
+        [
+            expert_ids.astype(jnp.float32).reshape(-1),
+            gate_weights.reshape(-1),
+            panel_target.astype(jnp.float32),
+        ]
+    )
+    tables = lax.all_gather(table, AXES)
+    pairs = tok_count * top_count
+    all_ids = tables[:, :pairs].reshape(-1, tok_count, top_count)
+    all_gates = tables[:, pairs : 2 * pairs].reshape(-1, tok_count, top_count)
+    weights = jnp.sum(jnp.where(all_ids == me.astype(jnp.float32), all_gates, 0.0), axis=-1)
+    target = tables[:, 2 * pairs :].astype(jnp.int32)
+    target_seq = target // pan_count // expert_count
+    first_row = target_seq * image_rows + target % pan_count * panel_rows
+    target_row = first_row[:, :, None] + jnp.arange(panel_rows, dtype=jnp.int32)
+    by_column = target_row.reshape(seq_count, expert_count, image_rows).transpose(1, 0, 2)
+    by_column = by_column.reshape(expert_count, seq_count * image_rows)
+    owners = jnp.asarray(ring.owner_of)[me]
+    sources = jnp.asarray(ring.sources_of.reshape(ring.devices, -1))[me]
+    order = by_column[owners % expert_count] - (owners // expert_count * image_rows)[:, None]
+    order = order[:, None, :]
+    scale = weights[owners].reshape(slot_count * tok_count, 1)
+
+    hidden = hidden_call([own, other], gate_up_weight, None, 0, slot_count)
+    for s in range(1, ring.half):
+        here = [after, before]
+        there = [across(after), across(before)]
+        if s + 1 < ring.half:
+            before, after = onward(before), back(after)
+        else:
+            cut = tok_count // 2
+            far_before, far_after = onward(before[:cut]), back(after[cut:])
+        hidden = hidden_call(here + there, gate_up_weight, hidden, 4 * s, slot_count)
+    far = jnp.concatenate([far_before, far_after], axis=0)
+    hidden = hidden_call([far, across(far)], gate_up_weight, hidden, 2, slot_count)
+
+    def outputs(first_slot, slots):
+        mine, others = down_call(
+            hidden, order, scale, sources, down_weight, first_slot, slots, tok_count, text_rows
+        )
+        return mine, across(others)
+
+    mine, swapped = outputs(2, 2)
+    cut = tok_count // 2
+    ahead = onward(add_up(mine[:cut], swapped[:cut]))
+    behind = back(add_up(mine[cut:], swapped[cut:]))
+    ahead = jnp.pad(ahead, ((0, tok_count - cut), (0, 0)))
+    behind = jnp.pad(behind, ((cut, 0), (0, 0)))
+    for s in range(ring.half - 1, 0, -1):
+        mine, swapped = outputs(4 * s, 4)
+        ahead = onward(add_up(ahead, mine[:tok_count], swapped[:tok_count]))
+        behind = back(add_up(behind, mine[tok_count:], swapped[tok_count:]))
+    mine, swapped = outputs(0, 2)
+    return add_up(mine, swapped, ahead, behind)
 
 
 def solution(mesh):
@@ -119,10 +374,22 @@
         P(("seq", "expert"), None, "tensor", None),
         P(("seq", "expert"), "tensor", None),
     )
-    return jax.shard_map(
-        shards,
-        mesh=mesh,
-        in_specs=placed,
-        out_specs=P(("groups", "seq", "expert"), "tensor"),
-        check_vma=False,
-    )
+
+    def chosen(*args):
+        seq_count, expert_count = mesh.shape["seq"], mesh.shape["expert"]
+        owners = seq_count * expert_count
+        tok_count, top_count = args[3].shape[0] // (mesh.shape["groups"] * owners), args[3].shape[1]
+        experts_all = args[5].shape[0]
+        slot_rows = experts_all * slot_capacity(tok_count, top_count, experts_all)
+        dense = owners * tok_count <= 2 * slot_rows
+        ring = dense and mesh.shape["tensor"] == 1 and expert_count == 4 and experts_all == owners
+        body = ring_shards if ring else slot_shards
+        return jax.shard_map(
+            body,
+            mesh=mesh,
+            in_specs=placed,
+            out_specs=P(("groups", "seq", "expert"), "tensor"),
+            check_vma=False,
+        )(*args)
+
+    return chosen

time: 918 us -> 301 us (0.33)
  the two profiles are of different devices: /device:TPU:11 before, /device:TPU:0 now
where the time goes in v1:
time: 301 us; the launch traced here: 299 us
  waiting for transfers between devices  134 us (45%)
  Pallas kernels  115 us (38%)
  starting transfers between devices  22.7 us (8%)
  between operations  14.4 us (5%)
  local copies, waits for them, and re-layouts  6.9 us (2%)
  other arithmetic  6.14 us (2%)
    unnamed x2, waiting for transfers between devices  86.6 us
    pallas_call x5, Pallas kernels, hidden_call(): pl.pallas_call(functools.partial(hidden_kernel, count, rows), grid=(ff //...  69.9 us
    pallas_call x5, Pallas kernels, down_call(): pl.pallas_call(functools.partial(down_kernel, slots, first_slot, rows, te...  45.4 us
    ppermute x8, waiting for transfers between devices, onward(): return lax.ppermute(array, AXES, ring.step(1))  42.3 us
    ppermute x8, starting transfers between devices, onward(): return lax.ppermute(array, AXES, ring.step(1))  12.1 us
    ppermute x8, starting transfers between devices, back(): return lax.ppermute(array, AXES, ring.step(-1))  7.27 us
  transfers between devices with their start and end apart: 30, of which 11 were waited for; matrix products, arithmetic and copies ran while one was open for 3% of the time, Pallas kernels for 32%

profile of v1, /device:TPU:0, one launch (start us, length us, event | category | flops | bytes accessed | tf_op | source)
XLA Modules:
  0.0 299.2 jit_solution(2404685466899337460)
XLA Ops:
  6.6 1.2 pad_maximum_fusion.refs_0_
  8.3 2.6 collective-permute-start.4
  16.1 86.5 %all-reduce.5.cloned.1.call-done = f32[30976]{0:T(1024)} async-done(((f32[30976]{0:T(1024)}), f32[30976]{0:T(1024)}) %all-reduce.5.cloned.1.call-update) | async-done | bytes 123920
  102.7 1.0 reshape.183
  105.2 1.1 reshape.189.scale_ref
  106.3 0.9 collective-permute-start.13
  107.9 3.7 %collective-permute-start.1 = (bf16[160,2560]{1,0:T(8,128)(2,1)}, bf16[160,2560]{1,0:T(8,128)(2,1)}, u32[]{:S(2)}, u32[]{:S(2)}) collective-permute-start(bf16[160,2560]{1,0:T(8,128)(2,1)} %collective-permute-done.refs_1_), channel_id=1, source_target_pairs={{0,4},{1,5},{2,0},{3,1},{4,8},{5,9},{6,2},{7,3},{8,12},{9,13},{10,... | collective-permute-start | bytes 2457608 | tf_op jit(solution)/shard_map/ppermute | solution.py:298
  112.2 12.1 %shard_map.91.refs_5_ = bf16[2560,1408]{1,0:T(8,128)(2,1)S(1)} custom-call(bf16[160,2560]{1,0:T(8,128)(2,1)S(1)} %pad_maximum_fusion.refs_0_, bf16[160,2560]{1,0:T(8,128)(2,1)S(1)} %collective-permute-done.15.refs_1_, bf16[1,2,1408,2560]{3,2,1,0:T(8,128)(2,1)} %refs_2_.3), custom_call_target="tpu_custom_call" | custom-call | flops 4613734400 | bytes 16957440 | tf_op jit(solution)/shard_map/pallas_call | solution.py:198
  124.4 6.5 %collective-permute-done.1.refs_1_ = bf16[160,2560]{1,0:T(8,128)(2,1)} collective-permute-done((bf16[160,2560]{1,0:T(8,128)(2,1)}, bf16[160,2560]{1,0:T(8,128)(2,1)}, u32[]{:S(2)}, u32[]{:S(2)}) %collective-permute-start.1) | collective-permute-done | bytes 819232 | tf_op jit(solution)/shard_map/ppermute | solution.py:298
  130.9 1.3 collective-permute-start.2
  132.4 0.8 collective-permute-start.6
  133.2 15.7 %shard_map.92.refs_5_ = bf16[2560,1408]{1,0:T(8,128)(2,1)S(1)} custom-call(bf16[160,2560]{1,0:T(8,128)(2,1)} %collective-permute-done.4.refs_0_, bf16[160,2560]{1,0:T(8,128)(2,1)} %collective-permute-done.refs_1_, bf16[160,2560]{1,0:T(8,128)(2,1)} %collective-permute-done.13.refs_2_, ...), custom_call_target="tpu_custom_call", output_to_operand_aliasing={{}: (5, {})} | custom-call | flops 9227468800 | bytes 19496960 | tf_op jit(solution)/shard_map/pallas_call | solution.py:198
  148.9 2.9 collective-permute-done.2.refs_1_
  151.8 1.3 collective-permute-start.3
  154.5 15.2 %shard_map.93.refs_5_ = bf16[2560,1408]{1,0:T(8,128)(2,1)S(1)} custom-call(bf16[160,2560]{1,0:T(8,128)(2,1)} %collective-permute-done.5.refs_0_, bf16[160,2560]{1,0:T(8,128)(2,1)} %collective-permute-done.1.refs_1_, bf16[160,2560]{1,0:T(8,128)(2,1)S(1)} %collective-permute-done.11.refs_2_, ...), custom_call_target="tpu_custom_call", output_to_operand_aliasing={{}: (5, {})} | custom-call | flops 9227468800 | bytes 19496960 | tf_op jit(solution)/shard_map/pallas_call | solution.py:198
  169.9 14.7 %shard_map.94.refs_3_ = bf16[2560,1408]{1,0:T(8,128)(2,1)S(1)} custom-call(bf16[160,2560]{1,0:T(8,128)(2,1)S(1)} %collective-permute-done.6.refs_0_, bf16[160,2560]{1,0:T(8,128)(2,1)S(1)} %collective-permute-done.2.refs_1_, bf16[160,2560]{1,0:T(8,128)(2,1)S(1)} %collective-permute-done.9.refs_2_, ...), custom_call_target="tpu_custom_call", output_to_operand_aliasing={{}: (5, {})} | custom-call | flops 9227468800 | bytes 19496960 | tf_op jit(solution)/shard_map/pallas_call | solution.py:198
  184.6 12.1 %shard_map.95.hidden_ref = bf16[2560,1408]{1,0:T(8,128)(2,1)S(1)} custom-call(bf16[160,2560]{1,0:T(8,128)(2,1)S(1)} %constant_dynamic-update-slice_fusion.refs_0_, bf16[160,2560]{1,0:T(8,128)(2,1)S(1)} %collective-permute-done.8.refs_1_, bf16[1,2,1408,2560]{3,2,1,0:T(8,128)(2,1)} %refs_2_.3, ...), custom_call_target="tpu_custom_call", output_to_operand_aliasing={{}: (3, {})} | custom-call | flops 4613734400 | bytes 16957440 | tf_op jit(solution)/shard_map/pallas_call | solution.py:198
  196.8 7.7 %shard_map.97 = (bf16[160,2560]{1,0:T(8,128)(2,1)S(1)}, bf16[160,2560]{1,0:T(8,128)(2,1)S(1)}) custom-call(s32[64]{0:T(128)S(1)} %dynamic-slice_bitcast_fusion.sources_ref, bf16[2560,1408]{1,0:T(8,128)(2,1)S(1)} %shard_map.95.hidden_ref, s32[16,1,512]{2,1,0:T(1,128)S(1)} %reshape_subtract_fusion.order_ref, f32[2560,1]{1,0:T(8,128)S(1)} %reshape.189.scale_ref, ...), custom_call_target="tpu_custom_call" | custom-call | flops 2306867200 | bytes 16056320 | tf_op jit(solution)/shard_map/pallas_call | solution.py:265
  205.0 10.0 %shard_map.98 = (bf16[320,2560]{1,0:T(8,128)(2,1)S(1)}, bf16[320,2560]{1,0:T(8,128)(2,1)S(1)}) custom-call(s32[64]{0:T(128)S(1)} %dynamic-slice_bitcast_fusion.sources_ref, bf16[2560,1408]{1,0:T(8,128)(2,1)S(1)} %shard_map.95.hidden_ref, s32[16,1,512]{2,1,0:T(1,128)S(1)} %reshape_subtract_fusion.order_ref, f32[2560,1]{1,0:T(8,128)S(1)} %reshape.189.scale_ref, ...), custom_call_target="tpu_custom_call" | custom-call | flops 4613734400 | bytes 17694720 | tf_op jit(solution)/shard_map/pallas_call | solution.py:265
  215.4 1.4 collective-permute-start.18
  217.4 10.0 %shard_map.99 = (bf16[320,2560]{1,0:T(8,128)(2,1)S(1)}, bf16[320,2560]{1,0:T(8,128)(2,1)S(1)}) custom-call(s32[64]{0:T(128)S(1)} %dynamic-slice_bitcast_fusion.sources_ref, bf16[2560,1408]{1,0:T(8,128)(2,1)S(1)} %shard_map.95.hidden_ref, s32[16,1,512]{2,1,0:T(1,128)S(1)} %reshape_subtract_fusion.order_ref, f32[2560,1]{1,0:T(8,128)S(1)} %reshape.189.scale_ref, ...), custom_call_target="tpu_custom_call" | custom-call | flops 4613734400 | bytes 17694720 | tf_op jit(solution)/shard_map/pallas_call | solution.py:265
  228.9 1.8 collective-permute-start.20
  231.0 10.0 %shard_map.100 = (bf16[320,2560]{1,0:T(8,128)(2,1)S(1)}, bf16[320,2560]{1,0:T(8,128)(2,1)S(1)}) custom-call(s32[64]{0:T(128)S(1)} %dynamic-slice_bitcast_fusion.sources_ref, bf16[2560,1408]{1,0:T(8,128)(2,1)S(1)} %shard_map.95.hidden_ref, s32[16,1,512]{2,1,0:T(1,128)S(1)} %reshape_subtract_fusion.order_ref, f32[2560,1]{1,0:T(8,128)S(1)} %reshape.189.scale_ref, ...), custom_call_target="tpu_custom_call" | custom-call | flops 4613734400 | bytes 17694720 | tf_op jit(solution)/shard_map/pallas_call | solution.py:265
  241.1 7.6 %collective-permute-done.20 = bf16[160,2560]{1,0:T(8,128)(2,1)S(1)} collective-permute-done((bf16[160,2560]{1,0:T(8,128)(2,1)S(1)}, bf16[160,2560]{1,0:T(8,128)(2,1)S(1)}, u32[]{:S(2)}, u32[]{:S(2)}) %collective-permute-start.20) | collective-permute-done | bytes 819232 | tf_op jit(solution)/shard_map/ppermute | solution.py:298
  248.7 1.2 collective-permute-done.26
  250.5 1.8 collective-permute-start.22
  252.6 7.7 %shard_map.96 = (bf16[160,2560]{1,0:T(8,128)(2,1)S(1)}, bf16[160,2560]{1,0:T(8,128)(2,1)S(1)}) custom-call(s32[64]{0:T(128)S(1)} %dynamic-slice_bitcast_fusion.sources_ref, bf16[2560,1408]{1,0:T(8,128)(2,1)S(1)} %shard_map.95.hidden_ref, s32[16,1,512]{2,1,0:T(1,128)S(1)} %reshape_subtract_fusion.order_ref, f32[2560,1]{1,0:T(8,128)S(1)} %reshape.189.scale_ref, ...), custom_call_target="tpu_custom_call" | custom-call | flops 2306867200 | bytes 16056320 | tf_op jit(solution)/shard_map/pallas_call | solution.py:265
  260.4 8.9 %collective-permute-done.22 = bf16[160,2560]{1,0:T(8,128)(2,1)S(1)} collective-permute-done((bf16[160,2560]{1,0:T(8,128)(2,1)S(1)}, bf16[160,2560]{1,0:T(8,128)(2,1)S(1)}, u32[]{:S(2)}, u32[]{:S(2)}) %collective-permute-start.22) | collective-permute-done | bytes 819232 | tf_op jit(solution)/shard_map/ppermute | solution.py:298
  269.3 2.2 collective-permute-done.27
  272.8 1.4 collective-permute-start.28
  274.2 16.3 %collective-permute-done.24 = bf16[160,2560]{1,0:T(8,128)(2,1)S(1)} collective-permute-done((bf16[160,2560]{1,0:T(8,128)(2,1)S(1)}, bf16[160,2560]{1,0:T(8,128)(2,1)S(1)}, u32[]{:S(2)}, u32[]{:S(2)}) %collective-permute-start.24) | collective-permute-done | bytes 819232 | tf_op jit(solution)/shard_map/ppermute | solution.py:298
  291.1 1.3 add_convert_fusion
  (89 shorter events, 15.7 us)
Async XLA Ops:
  6.5 5.0 %copy-start.4 = (u32[32]{0:T(128)S(1)}, u32[32]{0:T(128)}, u32[]{:S(2)}) copy-start(u32[32]{0:T(128)} %constant.95) | copy-start | bytes 388
  6.5 5.0 %copy-start.3 = (s32[16]{0:T(128)S(1)}, s32[16]{0:T(128)}, u32[]{:S(2)}) copy-start(s32[16]{0:T(128)} %param.11) | copy-start | bytes 196
  6.5 96.1 %all-reduce.5.cloned.1.call-start = ((), (), s32[]{:S(2)}) async-start(), calls=%async_computation | async-start | bytes 253952
  7.8 104.4 %collective-permute-start.15 = (bf16[160,2560]{1,0:T(8,128)(2,1)S(1)}, bf16[160,2560]{1,0:T(8,128)(2,1)S(1)}, u32[]{:S(2)}, u32[]{:S(2)}) collective-permute-start(bf16[160,2560]{1,0:T(8,128)(2,1)S(1)} %pad_maximum_fusion.refs_0_), channel_id=1, source_target_pairs={{0,1},{1,0},{2,3},{3,2},{4,5},{5,4},{6,7},{7,6},{8,9},{9,8},{10,11... | collective-permute-start | bytes 2457608 | tf_op jit(solution)/shard_map/ppermute | solution.py:304
  8.3 98.0 %collective-permute-start.4 = (bf16[160,2560]{1,0:T(8,128)(2,1)S(1)}, bf16[160,2560]{1,0:T(8,128)(2,1)}, u32[]{:S(2)}, u32[]{:S(2)}) collective-permute-start(bf16[160,2560]{1,0:T(8,128)(2,1)S(1)} %pad_maximum_fusion.refs_0_), channel_id=1, source_target_pairs={{0,2},{1,3},{2,6},{3,7},{4,0},{5,1},{6,10},{7,11},{8,4},{9,5},{10,... | collective-permute-start | bytes 2457608 | tf_op jit(solution)/shard_map/ppermute | solution.py:301
  10.8 97.0 %collective-permute-start = (bf16[160,2560]{1,0:T(8,128)(2,1)S(1)}, bf16[160,2560]{1,0:T(8,128)(2,1)}, u32[]{:S(2)}, u32[]{:S(2)}) collective-permute-start(bf16[160,2560]{1,0:T(8,128)(2,1)S(1)} %pad_maximum_fusion.refs_0_), channel_id=1, source_target_pairs={{0,4},{1,5},{2,0},{3,1},{4,8},{5,9},{6,2},{7,3},{8,12},{9,13},{10,... | collective-permute-start | bytes 2457608 | tf_op jit(solution)/shard_map/ppermute | solution.py:298
  106.3 26.0 %collective-permute-start.13 = (bf16[160,2560]{1,0:T(8,128)(2,1)}, bf16[160,2560]{1,0:T(8,128)(2,1)}, u32[]{:S(2)}, u32[]{:S(2)}) collective-permute-start(bf16[160,2560]{1,0:T(8,128)(2,1)} %collective-permute-done.4.refs_0_), channel_id=1, source_target_pairs={{0,1},{1,0},{2,3},{3,2},{4,5},{5,4},{6,7},{7,6},{8,9},{9,8},{10,11... | collective-permute-start | bytes 2457608 | tf_op jit(solution)/shard_map/ppermute | solution.py:304
  107.3 24.9 %collective-permute-start.5 = (bf16[160,2560]{1,0:T(8,128)(2,1)}, bf16[160,2560]{1,0:T(8,128)(2,1)}, u32[]{:S(2)}, u32[]{:S(2)}) collective-permute-start(bf16[160,2560]{1,0:T(8,128)(2,1)} %collective-permute-done.4.refs_0_), channel_id=1, source_target_pairs={{0,2},{1,3},{2,6},{3,7},{4,0},{5,1},{6,10},{7,11},{8,4},{9,5},{10,... | collective-permute-start | bytes 2457608 | tf_op jit(solution)/shard_map/ppermute | solution.py:301
  107.9 25.3 %collective-permute-start.14 = (bf16[160,2560]{1,0:T(8,128)(2,1)}, bf16[160,2560]{1,0:T(8,128)(2,1)}, u32[]{:S(2)}, u32[]{:S(2)}) collective-permute-start(bf16[160,2560]{1,0:T(8,128)(2,1)} %collective-permute-done.refs_1_), channel_id=1, source_target_pairs={{0,1},{1,0},{2,3},{3,2},{4,5},{5,4},{6,7},{7,6},{8,9},{9,8},{10,11... | collective-permute-start | bytes 2457608 | tf_op jit(solution)/shard_map/ppermute | solution.py:304
  107.9 23.0 %collective-permute-start.1 = (bf16[160,2560]{1,0:T(8,128)(2,1)}, bf16[160,2560]{1,0:T(8,128)(2,1)}, u32[]{:S(2)}, u32[]{:S(2)}) collective-permute-start(bf16[160,2560]{1,0:T(8,128)(2,1)} %collective-permute-done.refs_1_), channel_id=1, source_target_pairs={{0,4},{1,5},{2,0},{3,1},{4,8},{5,9},{6,2},{7,3},{8,12},{9,13},{10,... | collective-permute-start | bytes 2457608 | tf_op jit(solution)/shard_map/ppermute | solution.py:298
  130.9 23.6 %collective-permute-start.12 = (bf16[160,2560]{1,0:T(8,128)(2,1)}, bf16[160,2560]{1,0:T(8,128)(2,1)S(1)}, u32[]{:S(2)}, u32[]{:S(2)}) collective-permute-start(bf16[160,2560]{1,0:T(8,128)(2,1)} %collective-permute-done.1.refs_1_), channel_id=1, source_target_pairs={{0,1},{1,0},{2,3},{3,2},{4,5},{5,4},{6,7},{7,6},{8,9},{9,8},{10,11... | collective-permute-start | bytes 2457608 | tf_op jit(solution)/shard_map/ppermute | solution.py:304
  130.9 20.9 %collective-permute-start.2 = (bf16[160,2560]{1,0:T(8,128)(2,1)}, bf16[160,2560]{1,0:T(8,128)(2,1)S(1)}, u32[]{:S(2)}, u32[]{:S(2)}) collective-permute-start(bf16[160,2560]{1,0:T(8,128)(2,1)} %collective-permute-done.1.refs_1_), channel_id=1, source_target_pairs={{0,4},{1,5},{2,0},{3,1},{4,8},{5,9},{6,2},{7,3},{8,12},{9,13},{10,... | collective-permute-start | bytes 2457608 | tf_op jit(solution)/shard_map/ppermute | solution.py:298
  132.2 21.8 %collective-permute-start.11 = (bf16[160,2560]{1,0:T(8,128)(2,1)}, bf16[160,2560]{1,0:T(8,128)(2,1)S(1)}, u32[]{:S(2)}, u32[]{:S(2)}) collective-permute-start(bf16[160,2560]{1,0:T(8,128)(2,1)} %collective-permute-done.5.refs_0_), channel_id=1, source_target_pairs={{0,1},{1,0},{2,3},{3,2},{4,5},{5,4},{6,7},{7,6},{8,9},{9,8},{10,11... | collective-permute-start | bytes 2457608 | tf_op jit(solution)/shard_map/ppermute | solution.py:304
  132.4 20.8 %collective-permute-start.6 = (bf16[160,2560]{1,0:T(8,128)(2,1)}, bf16[160,2560]{1,0:T(8,128)(2,1)S(1)}, u32[]{:S(2)}, u32[]{:S(2)}) collective-permute-start(bf16[160,2560]{1,0:T(8,128)(2,1)} %collective-permute-done.5.refs_0_), channel_id=1, source_target_pairs={{0,2},{1,3},{2,6},{3,7},{4,0},{5,1},{6,10},{7,11},{8,4},{9,5},{10,... | collective-permute-start | bytes 2457608 | tf_op jit(solution)/shard_map/ppermute | solution.py:301
  151.8 17.9 %collective-permute-start.3 = (bf16[80,2560]{1,0:T(8,128)(2,1)S(1)}, bf16[80,2560]{1,0:T(8,128)(2,1)S(1)}, u32[]{:S(2)}, u32[]{:S(2)}) collective-permute-start(bf16[80,2560]{1,0:T(8,128)(2,1)S(1)} %slice.88), channel_id=1, source_target_pairs={{0,4},{1,5},{2,0},{3,1},{4,8},{5,9},{6,2},{7,3},{8,12},{9,13},{10,... | collective-permute-start | bytes 1228808 | tf_op jit(solution)/shard_map/ppermute | solution.py:298
  153.3 16.5 %collective-permute-start.7 = (bf16[80,2560]{1,0:T(8,128)(2,1)S(1)}, bf16[80,2560]{1,0:T(8,128)(2,1)S(1)}, u32[]{:S(2)}, u32[]{:S(2)}) collective-permute-start(bf16[80,2560]{1,0:T(8,128)(2,1)S(1)} %slice.89), channel_id=1, source_target_pairs={{0,2},{1,3},{2,6},{3,7},{4,0},{5,1},{6,10},{7,11},{8,4},{9,5},{10,... | collective-permute-start | bytes 1228808 | tf_op jit(solution)/shard_map/ppermute | solution.py:301
  154.0 15.9 %collective-permute-start.10 = (bf16[160,2560]{1,0:T(8,128)(2,1)S(1)}, bf16[160,2560]{1,0:T(8,128)(2,1)S(1)}, u32[]{:S(2)}, u32[]{:S(2)}) collective-permute-start(bf16[160,2560]{1,0:T(8,128)(2,1)S(1)} %collective-permute-done.2.refs_1_), channel_id=1, source_target_pairs={{0,1},{1,0},{2,3},{3,2},{4,5},{5,4},{6,7},{7,6},{8,9},{9,8},{10,11... | collective-permute-start | bytes 2457608 | tf_op jit(solution)/shard_map/ppermute | solution.py:304
  154.0 15.9 %collective-permute-start.9 = (bf16[160,2560]{1,0:T(8,128)(2,1)S(1)}, bf16[160,2560]{1,0:T(8,128)(2,1)S(1)}, u32[]{:S(2)}, u32[]{:S(2)}) collective-permute-start(bf16[160,2560]{1,0:T(8,128)(2,1)S(1)} %collective-permute-done.6.refs_0_), channel_id=1, source_target_pairs={{0,1},{1,0},{2,3},{3,2},{4,5},{5,4},{6,7},{7,6},{8,9},{9,8},{10,11... | collective-permute-start | bytes 2457608 | tf_op jit(solution)/shard_map/ppermute | solution.py:304
  169.8 14.8 %collective-permute-start.8 = (bf16[160,2560]{1,0:T(8,128)(2,1)S(1)}, bf16[160,2560]{1,0:T(8,128)(2,1)S(1)}, u32[]{:S(2)}, u32[]{:S(2)}) collective-permute-start(bf16[160,2560]{1,0:T(8,128)(2,1)S(1)} %constant_dynamic-update-slice_fusion.refs_0_), channel_id=1, source_target_pairs={{0,1},{1,0},{2,3},{3,2},{4,5},{5,4},{6,7},{7,6},{8,9},{9,8},{10,11... | collective-permute-start | bytes 2457608 | tf_op jit(solution)/shard_map/ppermute | solution.py:304
  204.5 10.7 %collective-permute-start.17 = (bf16[160,2560]{1,0:T(8,128)(2,1)S(1)}, bf16[160,2560]{1,0:T(8,128)(2,1)S(1)}, u32[]{:S(2)}, u32[]{:S(2)}) collective-permute-start(bf16[160,2560]{1,0:T(8,128)(2,1)S(1)} %get-tuple-element.18), channel_id=1, source_target_pairs={{0,1},{1,0},{2,3},{3,2},{4,5},{5,4},{6,7},{7,6},{8,9},{9,8},{10,11... | collective-permute-start | bytes 2457608 | tf_op jit(solution)/shard_map/ppermute | solution.py:304
  215.0 13.4 %collective-permute-start.19 = (bf16[320,2560]{1,0:T(8,128)(2,1)S(1)}, bf16[320,2560]{1,0:T(8,128)(2,1)S(1)}, u32[]{:S(2)}, u32[]{:S(2)}) collective-permute-start(bf16[320,2560]{1,0:T(8,128)(2,1)S(1)} %get-tuple-element.20), channel_id=1, source_target_pairs={{0,1},{1,0},{2,3},{3,2},{4,5},{5,4},{6,7},{7,6},{8,9},{9,8},{10,11... | collective-permute-start | bytes 4915208 | tf_op jit(solution)/shard_map/ppermute | solution.py:304
  215.4 12.3 %collective-permute-start.18 = (bf16[80,2560]{1,0:T(8,128)(2,1)S(1)}, bf16[80,2560]{1,0:T(8,128)(2,1)S(1)}, u32[]{:S(2)}, u32[]{:S(2)}) collective-permute-start(bf16[80,2560]{1,0:T(8,128)(2,1)S(1)} %get-tuple-element.31), channel_id=1, source_target_pairs={{0,4},{1,5},{2,0},{3,1},{4,8},{5,9},{6,2},{7,3},{8,12},{9,13},{10,... | collective-permute-start | bytes 1228808 | tf_op jit(solution)/shard_map/ppermute | solution.py:298
  216.8 11.6 %collective-permute-start.25 = (bf16[80,2560]{1,0:T(8,128)(2,1)S(1)}, bf16[80,2560]{1,0:T(8,128)(2,1)S(1)}, u32[]{:S(2)}, u32[]{:S(2)}) collective-permute-start(bf16[80,2560]{1,0:T(8,128)(2,1)S(1)} %get-tuple-element.32), channel_id=1, source_target_pairs={{0,2},{1,3},{2,6},{3,7},{4,0},{5,1},{6,10},{7,11},{8,4},{9,5},{10,... | collective-permute-start | bytes 1228808 | tf_op jit(solution)/shard_map/ppermute | solution.py:301
  227.5 13.6 %collective-permute-start.21 = (bf16[320,2560]{1,0:T(8,128)(2,1)S(1)}, bf16[320,2560]{1,0:T(8,128)(2,1)S(1)}, u32[]{:S(2)}, u32[]{:S(2)}) collective-permute-start(bf16[320,2560]{1,0:T(8,128)(2,1)S(1)} %get-tuple-element.22), channel_id=1, source_target_pairs={{0,1},{1,0},{2,3},{3,2},{4,5},{5,4},{6,7},{7,6},{8,9},{9,8},{10,11... | collective-permute-start | bytes 4915208 | tf_op jit(solution)/shard_map/ppermute | solution.py:304
  228.9 19.8 %collective-permute-start.20 = (bf16[160,2560]{1,0:T(8,128)(2,1)S(1)}, bf16[160,2560]{1,0:T(8,128)(2,1)S(1)}, u32[]{:S(2)}, u32[]{:S(2)}) collective-permute-start(bf16[160,2560]{1,0:T(8,128)(2,1)S(1)} %get-tuple-element.29), channel_id=1, source_target_pairs={{0,4},{1,5},{2,0},{3,1},{4,8},{5,9},{6,2},{7,3},{8,12},{9,13},{10,... | collective-permute-start | bytes 2457608 | tf_op jit(solution)/shard_map/ppermute | solution.py:298
  230.7 19.2 %collective-permute-start.26 = (bf16[160,2560]{1,0:T(8,128)(2,1)S(1)}, bf16[160,2560]{1,0:T(8,128)(2,1)S(1)}, u32[]{:S(2)}, u32[]{:S(2)}) collective-permute-start(bf16[160,2560]{1,0:T(8,128)(2,1)S(1)} %get-tuple-element.30), channel_id=1, source_target_pairs={{0,2},{1,3},{2,6},{3,7},{4,0},{5,1},{6,10},{7,11},{8,4},{9,5},{10,... | collective-permute-start | bytes 2457608 | tf_op jit(solution)/shard_map/ppermute | solution.py:301
  241.0 19.4 %collective-permute-start.23 = (bf16[320,2560]{1,0:T(8,128)(2,1)S(1)}, bf16[320,2560]{1,0:T(8,128)(2,1)S(1)}, u32[]{:S(2)}, u32[]{:S(2)}) collective-permute-start(bf16[320,2560]{1,0:T(8,128)(2,1)S(1)} %get-tuple-element.24), channel_id=1, source_target_pairs={{0,1},{1,0},{2,3},{3,2},{4,5},{5,4},{6,7},{7,6},{8,9},{9,8},{10,11... | collective-permute-start | bytes 4915208 | tf_op jit(solution)/shard_map/ppermute | solution.py:304
  250.5 18.8 %collective-permute-start.22 = (bf16[160,2560]{1,0:T(8,128)(2,1)S(1)}, bf16[160,2560]{1,0:T(8,128)(2,1)S(1)}, u32[]{:S(2)}, u32[]{:S(2)}) collective-permute-start(bf16[160,2560]{1,0:T(8,128)(2,1)S(1)} %get-tuple-element.27), channel_id=1, source_target_pairs={{0,4},{1,5},{2,0},{3,1},{4,8},{5,9},{6,2},{7,3},{8,12},{9,13},{10,... | collective-permute-start | bytes 2457608 | tf_op jit(solution)/shard_map/ppermute | solution.py:298
  252.3 19.2 %collective-permute-start.27 = (bf16[160,2560]{1,0:T(8,128)(2,1)S(1)}, bf16[160,2560]{1,0:T(8,128)(2,1)S(1)}, u32[]{:S(2)}, u32[]{:S(2)}) collective-permute-start(bf16[160,2560]{1,0:T(8,128)(2,1)S(1)} %get-tuple-element.28), channel_id=1, source_target_pairs={{0,2},{1,3},{2,6},{3,7},{4,0},{5,1},{6,10},{7,11},{8,4},{9,5},{10,... | collective-permute-start | bytes 2457608 | tf_op jit(solution)/shard_map/ppermute | solution.py:301
  260.3 13.9 %collective-permute-start.16 = (bf16[160,2560]{1,0:T(8,128)(2,1)S(1)}, bf16[160,2560]{1,0:T(8,128)(2,1)S(1)}, u32[]{:S(2)}, u32[]{:S(2)}) collective-permute-start(bf16[160,2560]{1,0:T(8,128)(2,1)S(1)} %get-tuple-element.16), channel_id=1, source_target_pairs={{0,1},{1,0},{2,3},{3,2},{4,5},{5,4},{6,7},{7,6},{8,9},{9,8},{10,11... | collective-permute-start | bytes 2457608 | tf_op jit(solution)/shard_map/ppermute | solution.py:304
  272.1 18.4 %collective-permute-start.24 = (bf16[160,2560]{1,0:T(8,128)(2,1)S(1)}, bf16[160,2560]{1,0:T(8,128)(2,1)S(1)}, u32[]{:S(2)}, u32[]{:S(2)}) collective-permute-start(bf16[160,2560]{1,0:T(8,128)(2,1)S(1)} %get-tuple-element.25), channel_id=1, source_target_pairs={{0,4},{1,5},{2,0},{3,1},{4,8},{5,9},{6,2},{7,3},{8,12},{9,13},{10,... | collective-permute-start | bytes 2457608 | tf_op jit(solution)/shard_map/ppermute | solution.py:298
  272.8 18.3 %collective-permute-start.28 = (bf16[160,2560]{1,0:T(8,128)(2,1)S(1)}, bf16[160,2560]{1,0:T(8,128)(2,1)S(1)}, u32[]{:S(2)}, u32[]{:S(2)}) collective-permute-start(bf16[160,2560]{1,0:T(8,128)(2,1)S(1)} %get-tuple-element.26), channel_id=1, source_target_pairs={{0,2},{1,3},{2,6},{3,7},{4,0},{5,1},{6,10},{7,11},{8,4},{9,5},{10,... | collective-permute-start | bytes 2457608 | tf_op jit(solution)/shard_map/ppermute | solution.py:301
  (3 other events, 9.9 us)
Sparse Core Ops, SparseCore 0:
  14.0 88.5 all-reduce.4

commit v2 on v1

--- a/solution.py
+++ b/solution.py
@@ -185,7 +185,7 @@
     rows, wide = blocks[0].shape
     _, _, ff, _ = gate_up_weight.shape
     count = len(blocks)
-    chunk = 128
+    chunk = 256
     place = first_slot // count
     whole = pl.BlockSpec((rows, wide), lambda i: (0, 0))
     in_specs = [whole] * count + [pl.BlockSpec((1, 2, chunk, wide), lambda i: (0, 0, i, 0))]
@@ -197,7 +197,7 @@
         aliases = {len(args) - 1: 0}
     return pl.pallas_call(
         functools.partial(hidden_kernel, count, rows),
-        grid=(ff // chunk,),
+        grid=(pl.cdiv(ff, chunk),),
         in_specs=in_specs,
         out_specs=pl.BlockSpec((count * rows, chunk), lambda i: (place, i)),
         out_shape=jax.ShapeDtypeStruct((slot_count * rows, ff), jnp.bfloat16),
@@ -248,7 +248,6 @@
     _, ff, wide = down_weight.shape
     chunk = 512
     half = slots * rows // 2
-    slot_total = order.shape[0]
     grid_spec = pltpu.PrefetchScalarGridSpec(
         num_scalar_prefetch=1,
         grid=(wide // chunk,),
@@ -261,7 +260,6 @@
         out_specs=[pl.BlockSpec((half, chunk), lambda i, s: (0, i))] * 2,
         scratch_shapes=[pltpu.VMEM((slots * rows, ff), jnp.bfloat16)],
     )
-    del slot_total
     return pl.pallas_call(
         functools.partial(down_kernel, slots, first_slot, rows, text_rows),
         grid_spec=grid_spec,
@@ -289,7 +287,7 @@
     ring = Ring(seq_count, expert_count)
     pan_count, panel_rows, wide = panels.shape
     text_rows = text_tokens.shape[0]
-    tok_count, top_count = expert_ids.shape
+    tok_count = expert_ids.shape[0]
     image_rows = pan_count * panel_rows
     slot_count = len(ring.slots)
     me = lax.axis_index(AXES)
@@ -307,19 +305,14 @@
     before, after = onward(own), back(own)
     other = across(own)
 
-    table = jnp.concatenate(
-        [
-            expert_ids.astype(jnp.float32).reshape(-1),
-            gate_weights.reshape(-1),
-            panel_target.astype(jnp.float32),
-        ]
-    )
-    tables = lax.all_gather(table, AXES)
-    pairs = tok_count * top_count
-    all_ids = tables[:, :pairs].reshape(-1, tok_count, top_count)
-    all_gates = tables[:, pairs : 2 * pairs].reshape(-1, tok_count, top_count)
-    weights = jnp.sum(jnp.where(all_ids == me.astype(jnp.float32), all_gates, 0.0), axis=-1)
-    target = tables[:, 2 * pairs :].astype(jnp.int32)
+    experts = jnp.arange(ring.devices, dtype=jnp.int32)[:, None, None]
+    routed = jnp.where(expert_ids[None] == experts, gate_weights[None], 0.0).sum(axis=-1)
+    targets = jnp.broadcast_to(panel_target.astype(jnp.float32), (ring.devices, pan_count))
+    tables = lax.all_to_all(
+        jnp.concatenate([routed, targets], axis=1), AXES, split_axis=0, concat_axis=0, tiled=True
+    )
+    weights = tables[:, :tok_count]
+    target = tables[:, tok_count:].astype(jnp.int32)
     target_seq = target // pan_count // expert_count
     first_row = target_seq * image_rows + target % pan_count * panel_rows
     target_row = first_row[:, :, None] + jnp.arange(panel_rows, dtype=jnp.int32)
@@ -350,16 +343,20 @@
         )
         return mine, across(others)
 
+    cut = tok_count // 2
     mine, swapped = outputs(2, 2)
-    cut = tok_count // 2
-    ahead = onward(add_up(mine[:cut], swapped[:cut]))
-    behind = back(add_up(mine[cut:], swapped[cut:]))
-    ahead = jnp.pad(ahead, ((0, tok_count - cut), (0, 0)))
-    behind = jnp.pad(behind, ((cut, 0), (0, 0)))
-    for s in range(ring.half - 1, 0, -1):
-        mine, swapped = outputs(4 * s, 4)
-        ahead = onward(add_up(ahead, mine[:tok_count], swapped[:tok_count]))
-        behind = back(add_up(behind, mine[tok_count:], swapped[tok_count:]))
+    leaving = add_up(mine[:cut], swapped[:cut]), add_up(mine[cut:], swapped[cut:])
+    for s in range(ring.half - 1, -1, -1):
+        ahead, behind = onward(leaving[0]), back(leaving[1])
+        if s == ring.half - 1:
+            ahead = jnp.pad(ahead, ((0, tok_count - cut), (0, 0)))
+            behind = jnp.pad(behind, ((cut, 0), (0, 0)))
+        if s:
+            mine, swapped = outputs(4 * s, 4)
+            leaving = (
+                add_up(ahead, mine[:tok_count], swapped[:tok_count]),
+                add_up(behind, mine[tok_count:], swapped[tok_count:]),
+            )
     mine, swapped = outputs(0, 2)
     return add_up(mine, swapped, ahead, behind)
 

time: 301 us -> 209 us (0.69)
  waiting for transfers between devices: 134 us -> 63.2 us
  between operations: 14.4 us -> 0.32 us
  Pallas kernels: 115 us -> 108 us
  starting transfers between devices: 22.7 us -> 26.2 us
    unnamed x2 -> x0, waiting for transfers between devices: 86.6 us -> none
    all_to_all x0 -> x1, waiting for transfers between devices: none -> 14.2 us  [ring_shards(): lax.all_to_all(jnp.concatenate([routed, targets], axis=1), AXES, split_ax...]
    pallas_call x5, Pallas kernels: 69.9 us -> 62.4 us  [hidden_call(): pl.pallas_call(functools.partial(hidden_kernel, count, rows), grid=(pl.cd...]
    all_to_all x0 -> x1, starting transfers between devices: none -> 6.27 us  [ring_shards(): lax.all_to_all(jnp.concatenate([routed, targets], axis=1), AXES, split_ax...]
    ppermute x8, waiting for transfers between devices: 42.3 us -> 46.3 us  [onward(): return lax.ppermute(array, AXES, ring.step(1))]
    ppermute x8, starting transfers between devices: 12.1 us -> 8.21 us  [onward(): return lax.ppermute(array, AXES, ring.step(1))]
  transfers between devices with their start and end apart: 30 -> 30, of which waited for: 11 -> 10; matrix products, arithmetic and copies ran while one was open for 3% -> 4% of each run, Pallas kernels for 32% -> 44%
where the time goes in v2:
time: 209 us; the launch traced here: 208 us
  Pallas kernels  108 us (52%)
  waiting for transfers between devices  63.2 us (30%)
  starting transfers between devices  26.2 us (13%)
  other arithmetic  6.03 us (3%)
  local copies, waits for them, and re-layouts  4.11 us (2%)
    pallas_call x5, Pallas kernels, hidden_call(): pl.pallas_call(functools.partial(hidden_kernel, count, rows), grid=(pl.cd...  62.4 us
    ppermute x8, waiting for transfers between devices, onward(): return lax.ppermute(array, AXES, ring.step(1))  46.3 us
    pallas_call x5, Pallas kernels, down_call(): pl.pallas_call(functools.partial(down_kernel, slots, first_slot, rows, te...  45.5 us
    all_to_all x1, waiting for transfers between devices, ring_shards(): lax.all_to_all(jnp.concatenate([routed, targets], axis=1), AXES, split_ax...  14.2 us
    ppermute x8, starting transfers between devices, back(): return lax.ppermute(array, AXES, ring.step(-1))  9.32 us
    ppermute x8, starting transfers between devices, onward(): return lax.ppermute(array, AXES, ring.step(1))  8.21 us
    all_to_all x1, starting transfers between devices, ring_shards(): lax.all_to_all(jnp.concatenate([routed, targets], axis=1), AXES, split_ax...  6.27 us
  transfers between devices with their start and end apart: 30, of which 10 were waited for; matrix products, arithmetic and copies ran while one was open for 4% of the time, Pallas kernels for 44%

profile of v2, /device:TPU:0, one launch (start us, length us, event | category | flops | bytes accessed | tf_op | source)
XLA Modules:
  0.0 207.7 jit_solution(3186344486522297729)
XLA Ops:
  0.0 1.2 pad_maximum_fusion.refs_0_
  1.7 2.6 %collective-permute-start.4 = (bf16[160,2560]{1,0:T(8,128)(2,1)S(1)}, bf16[160,2560]{1,0:T(8,128)(2,1)}, u32[]{:S(2)}, u32[]{:S(2)}) collective-permute-start(bf16[160,2560]{1,0:T(8,128)(2,1)S(1)} %pad_maximum_fusion.refs_0_), channel_id=1, source_target_pairs={{0,2},{1,3},{2,6},{3,7},{4,0},{5,1},{6,10},{7,11},{8,4},{9,5},{10,... | collective-permute-start | bytes 2457608 | tf_op jit(solution)/shard_map/ppermute | solution.py:299
  5.2 6.3 %all-to-all-start = ((f32[16,1,176]{2,1,0:T(1,128)}), f32[16,1,176]{2,1,0:T(1,128)S(1)}, u32[]{:S(2)}, u32[]{:S(2)}) async-start(f32[16,1,176]{2,1,0:T(1,128)} %copy.30), calls=%async_computation | async-start | bytes 32768 | tf_op jit(solution)/shard_map/all_to_all | solution.py:311
  11.5 0.7 fusion.8
  13.7 14.2 %all-to-all-done = f32[16,1,176]{2,1,0:T(1,128)S(1)} async-done(((f32[16,1,176]{2,1,0:T(1,128)}), f32[16,1,176]{2,1,0:T(1,128)S(1)}, u32[]{:S(2)}, u32[]{:S(2)}) %all-to-all-start) | async-done | bytes 11296 | tf_op jit(solution)/shard_map/all_to_all | solution.py:311
  28.8 1.1 reshape.173.scale_ref
  30.7 1.6 collective-permute-start.1
  33.0 9.8 %shard_map.91.refs_5_ = bf16[2560,1408]{1,0:T(8,128)(2,1)S(1)} custom-call(bf16[160,2560]{1,0:T(8,128)(2,1)S(1)} %pad_maximum_fusion.refs_0_, bf16[160,2560]{1,0:T(8,128)(2,1)S(1)} %collective-permute-done.15.refs_1_, bf16[1,2,1408,2560]{3,2,1,0:T(8,128)(2,1)} %refs_2_.3), custom_call_target="tpu_custom_call" | custom-call | flops 4613734400 | bytes 16957440 | tf_op jit(solution)/shard_map/pallas_call | solution.py:198
  42.8 8.8 %collective-permute-done.1.refs_1_ = bf16[160,2560]{1,0:T(8,128)(2,1)} collective-permute-done((bf16[160,2560]{1,0:T(8,128)(2,1)}, bf16[160,2560]{1,0:T(8,128)(2,1)}, u32[]{:S(2)}, u32[]{:S(2)}) %collective-permute-start.1) | collective-permute-done | bytes 819232 | tf_op jit(solution)/shard_map/ppermute | solution.py:296
  51.6 1.5 collective-permute-start.2
  53.9 14.7 %shard_map.92.refs_5_ = bf16[2560,1408]{1,0:T(8,128)(2,1)S(1)} custom-call(bf16[160,2560]{1,0:T(8,128)(2,1)} %collective-permute-done.4.refs_0_, bf16[160,2560]{1,0:T(8,128)(2,1)} %collective-permute-done.refs_1_, bf16[160,2560]{1,0:T(8,128)(2,1)} %collective-permute-done.13.refs_2_, ...), custom_call_target="tpu_custom_call", output_to_operand_aliasing={{}: (5, {})} | custom-call | flops 9227468800 | bytes 19496960 | tf_op jit(solution)/shard_map/pallas_call | solution.py:198
  68.6 3.8 %collective-permute-done.2.refs_1_ = bf16[160,2560]{1,0:T(8,128)(2,1)S(1)} collective-permute-done((bf16[160,2560]{1,0:T(8,128)(2,1)}, bf16[160,2560]{1,0:T(8,128)(2,1)S(1)}, u32[]{:S(2)}, u32[]{:S(2)}) %collective-permute-start.2) | collective-permute-done | bytes 819232 | tf_op jit(solution)/shard_map/ppermute | solution.py:296
  72.5 1.5 collective-permute-start.3
  74.1 0.8 collective-permute-start.7
  75.4 14.2 %shard_map.93.refs_5_ = bf16[2560,1408]{1,0:T(8,128)(2,1)S(1)} custom-call(bf16[160,2560]{1,0:T(8,128)(2,1)} %collective-permute-done.5.refs_0_, bf16[160,2560]{1,0:T(8,128)(2,1)} %collective-permute-done.1.refs_1_, bf16[160,2560]{1,0:T(8,128)(2,1)S(1)} %collective-permute-done.11.refs_2_, ...), custom_call_target="tpu_custom_call", output_to_operand_aliasing={{}: (5, {})} | custom-call | flops 9227468800 | bytes 19496960 | tf_op jit(solution)/shard_map/pallas_call | solution.py:198
  89.8 13.8 %shard_map.94.refs_3_ = bf16[2560,1408]{1,0:T(8,128)(2,1)S(1)} custom-call(bf16[160,2560]{1,0:T(8,128)(2,1)S(1)} %collective-permute-done.6.refs_0_, bf16[160,2560]{1,0:T(8,128)(2,1)S(1)} %collective-permute-done.2.refs_1_, bf16[160,2560]{1,0:T(8,128)(2,1)S(1)} %collective-permute-done.9.refs_2_, ...), custom_call_target="tpu_custom_call", output_to_operand_aliasing={{}: (5, {})} | custom-call | flops 9227468800 | bytes 19496960 | tf_op jit(solution)/shard_map/pallas_call | solution.py:198
  103.6 9.8 %shard_map.95.hidden_ref = bf16[2560,1408]{1,0:T(8,128)(2,1)S(1)} custom-call(bf16[160,2560]{1,0:T(8,128)(2,1)S(1)} %constant_dynamic-update-slice_fusion.refs_0_, bf16[160,2560]{1,0:T(8,128)(2,1)S(1)} %collective-permute-done.8.refs_1_, bf16[1,2,1408,2560]{3,2,1,0:T(8,128)(2,1)} %refs_2_.3, ...), custom_call_target="tpu_custom_call", output_to_operand_aliasing={{}: (3, {})} | custom-call | flops 4613734400 | bytes 16957440 | tf_op jit(solution)/shard_map/pallas_call | solution.py:198
  113.5 7.7 %shard_map.97 = (bf16[160,2560]{1,0:T(8,128)(2,1)S(1)}, bf16[160,2560]{1,0:T(8,128)(2,1)S(1)}) custom-call(s32[64]{0:T(128)S(1)} %dynamic-slice_bitcast_fusion.sources_ref, bf16[2560,1408]{1,0:T(8,128)(2,1)S(1)} %shard_map.95.hidden_ref, s32[16,1,512]{2,1,0:T(1,128)S(1)} %reshape_subtract_fusion.order_ref, f32[2560,1]{1,0:T(8,128)S(1)} %reshape.173.scale_ref, ...), custom_call_target="tpu_custom_call" | custom-call | flops 2306867200 | bytes 16056320 | tf_op jit(solution)/shard_map/pallas_call | solution.py:263
  121.7 10.0 %shard_map.98 = (bf16[320,2560]{1,0:T(8,128)(2,1)S(1)}, bf16[320,2560]{1,0:T(8,128)(2,1)S(1)}) custom-call(s32[64]{0:T(128)S(1)} %dynamic-slice_bitcast_fusion.sources_ref, bf16[2560,1408]{1,0:T(8,128)(2,1)S(1)} %shard_map.95.hidden_ref, s32[16,1,512]{2,1,0:T(1,128)S(1)} %reshape_subtract_fusion.order_ref, f32[2560,1]{1,0:T(8,128)S(1)} %reshape.173.scale_ref, ...), custom_call_target="tpu_custom_call" | custom-call | flops 4613734400 | bytes 17694720 | tf_op jit(solution)/shard_map/pallas_call | solution.py:263
  132.0 1.5 collective-permute-start.18
  134.1 10.0 %shard_map.99 = (bf16[320,2560]{1,0:T(8,128)(2,1)S(1)}, bf16[320,2560]{1,0:T(8,128)(2,1)S(1)}) custom-call(s32[64]{0:T(128)S(1)} %dynamic-slice_bitcast_fusion.sources_ref, bf16[2560,1408]{1,0:T(8,128)(2,1)S(1)} %shard_map.95.hidden_ref, s32[16,1,512]{2,1,0:T(1,128)S(1)} %reshape_subtract_fusion.order_ref, f32[2560,1]{1,0:T(8,128)S(1)} %reshape.173.scale_ref, ...), custom_call_target="tpu_custom_call" | custom-call | flops 4613734400 | bytes 17694720 | tf_op jit(solution)/shard_map/pallas_call | solution.py:263
  144.2 0.9 collective-permute-done.25
  146.3 1.4 collective-permute-start.26
  147.7 10.0 %shard_map.100 = (bf16[320,2560]{1,0:T(8,128)(2,1)S(1)}, bf16[320,2560]{1,0:T(8,128)(2,1)S(1)}) custom-call(s32[64]{0:T(128)S(1)} %dynamic-slice_bitcast_fusion.sources_ref, bf16[2560,1408]{1,0:T(8,128)(2,1)S(1)} %shard_map.95.hidden_ref, s32[16,1,512]{2,1,0:T(1,128)S(1)} %reshape_subtract_fusion.order_ref, f32[2560,1]{1,0:T(8,128)S(1)} %reshape.173.scale_ref, ...), custom_call_target="tpu_custom_call" | custom-call | flops 4613734400 | bytes 17694720 | tf_op jit(solution)/shard_map/pallas_call | solution.py:263
  157.8 7.6 %collective-permute-done.20 = bf16[160,2560]{1,0:T(8,128)(2,1)S(1)} collective-permute-done((bf16[160,2560]{1,0:T(8,128)(2,1)S(1)}, bf16[160,2560]{1,0:T(8,128)(2,1)S(1)}, u32[]{:S(2)}, u32[]{:S(2)}) %collective-permute-start.20) | collective-permute-done | bytes 819232 | tf_op jit(solution)/shard_map/ppermute | solution.py:296
  165.4 1.2 collective-permute-done.26
  167.8 1.5 collective-permute-start.27
  169.3 7.7 %shard_map.96 = (bf16[160,2560]{1,0:T(8,128)(2,1)S(1)}, bf16[160,2560]{1,0:T(8,128)(2,1)S(1)}) custom-call(s32[64]{0:T(128)S(1)} %dynamic-slice_bitcast_fusion.sources_ref, bf16[2560,1408]{1,0:T(8,128)(2,1)S(1)} %shard_map.95.hidden_ref, s32[16,1,512]{2,1,0:T(1,128)S(1)} %reshape_subtract_fusion.order_ref, f32[2560,1]{1,0:T(8,128)S(1)} %reshape.173.scale_ref, ...), custom_call_target="tpu_custom_call" | custom-call | flops 2306867200 | bytes 16056320 | tf_op jit(solution)/shard_map/pallas_call | solution.py:263
  177.1 9.7 %collective-permute-done.22 = bf16[160,2560]{1,0:T(8,128)(2,1)S(1)} collective-permute-done((bf16[160,2560]{1,0:T(8,128)(2,1)S(1)}, bf16[160,2560]{1,0:T(8,128)(2,1)S(1)}, u32[]{:S(2)}, u32[]{:S(2)}) %collective-permute-start.22) | collective-permute-done | bytes 819232 | tf_op jit(solution)/shard_map/ppermute | solution.py:296
  188.3 1.5 collective-permute-start.28
  189.8 16.3 %collective-permute-done.24 = bf16[160,2560]{1,0:T(8,128)(2,1)S(1)} collective-permute-done((bf16[160,2560]{1,0:T(8,128)(2,1)S(1)}, bf16[160,2560]{1,0:T(8,128)(2,1)S(1)}, u32[]{:S(2)}, u32[]{:S(2)}) %collective-permute-start.24) | collective-permute-done | bytes 819232 | tf_op jit(solution)/shard_map/ppermute | solution.py:296
  206.4 1.3 add_convert_fusion
  (75 shorter events, 12.5 us)
Async XLA Ops:
  0.0 4.5 %copy-start.1 = (s32[160,6]{0,1:T(8,128)S(1)}, s32[160,6]{0,1:T(8,128)}, u32[]{:S(2)}) copy-start(s32[160,6]{0,1:T(8,128)} %param.12) | copy-start | bytes 11524
  0.0 4.5 %copy-start = (f32[160,6]{0,1:T(8,128)S(1)}, f32[160,6]{0,1:T(8,128)}, u32[]{:S(2)}) copy-start(f32[160,6]{0,1:T(8,128)} %param.13) | copy-start | bytes 11524
  1.2 31.7 %collective-permute-start.15 = (bf16[160,2560]{1,0:T(8,128)(2,1)S(1)}, bf16[160,2560]{1,0:T(8,128)(2,1)S(1)}, u32[]{:S(2)}, u32[]{:S(2)}) collective-permute-start(bf16[160,2560]{1,0:T(8,128)(2,1)S(1)} %pad_maximum_fusion.refs_0_), channel_id=1, source_target_pairs={{0,1},{1,0},{2,3},{3,2},{4,5},{5,4},{6,7},{7,6},{8,9},{9,8},{10,11... | collective-permute-start | bytes 2457608 | tf_op jit(solution)/shard_map/ppermute | solution.py:302
  1.7 28.2 %collective-permute-start.4 = (bf16[160,2560]{1,0:T(8,128)(2,1)S(1)}, bf16[160,2560]{1,0:T(8,128)(2,1)}, u32[]{:S(2)}, u32[]{:S(2)}) collective-permute-start(bf16[160,2560]{1,0:T(8,128)(2,1)S(1)} %pad_maximum_fusion.refs_0_), channel_id=1, source_target_pairs={{0,2},{1,3},{2,6},{3,7},{4,0},{5,1},{6,10},{7,11},{8,4},{9,5},{10,... | collective-permute-start | bytes 2457608 | tf_op jit(solution)/shard_map/ppermute | solution.py:299
  4.3 26.3 %collective-permute-start = (bf16[160,2560]{1,0:T(8,128)(2,1)S(1)}, bf16[160,2560]{1,0:T(8,128)(2,1)}, u32[]{:S(2)}, u32[]{:S(2)}) collective-permute-start(bf16[160,2560]{1,0:T(8,128)(2,1)S(1)} %pad_maximum_fusion.refs_0_), channel_id=1, source_target_pairs={{0,4},{1,5},{2,0},{3,1},{4,8},{5,9},{6,2},{7,3},{8,12},{9,13},{10,... | collective-permute-start | bytes 2457608 | tf_op jit(solution)/shard_map/ppermute | solution.py:296
  5.2 22.7 %all-to-all-start = ((f32[16,1,176]{2,1,0:T(1,128)}), f32[16,1,176]{2,1,0:T(1,128)S(1)}, u32[]{:S(2)}, u32[]{:S(2)}) async-start(f32[16,1,176]{2,1,0:T(1,128)} %copy.30), calls=%async_computation | async-start | bytes 32768 | tf_op jit(solution)/shard_map/all_to_all | solution.py:311
  30.0 23.4 %collective-permute-start.13 = (bf16[160,2560]{1,0:T(8,128)(2,1)}, bf16[160,2560]{1,0:T(8,128)(2,1)}, u32[]{:S(2)}, u32[]{:S(2)}) collective-permute-start(bf16[160,2560]{1,0:T(8,128)(2,1)} %collective-permute-done.4.refs_0_), channel_id=1, source_target_pairs={{0,1},{1,0},{2,3},{3,2},{4,5},{5,4},{6,7},{7,6},{8,9},{9,8},{10,11... | collective-permute-start | bytes 2457608 | tf_op jit(solution)/shard_map/ppermute | solution.py:302
  30.0 23.1 %collective-permute-start.5 = (bf16[160,2560]{1,0:T(8,128)(2,1)}, bf16[160,2560]{1,0:T(8,128)(2,1)}, u32[]{:S(2)}, u32[]{:S(2)}) collective-permute-start(bf16[160,2560]{1,0:T(8,128)(2,1)} %collective-permute-done.4.refs_0_), channel_id=1, source_target_pairs={{0,2},{1,3},{2,6},{3,7},{4,0},{5,1},{6,10},{7,11},{8,4},{9,5},{10,... | collective-permute-start | bytes 2457608 | tf_op jit(solution)/shard_map/ppermute | solution.py:299
  30.6 23.3 %collective-permute-start.14 = (bf16[160,2560]{1,0:T(8,128)(2,1)}, bf16[160,2560]{1,0:T(8,128)(2,1)}, u32[]{:S(2)}, u32[]{:S(2)}) collective-permute-start(bf16[160,2560]{1,0:T(8,128)(2,1)} %collective-permute-done.refs_1_), channel_id=1, source_target_pairs={{0,1},{1,0},{2,3},{3,2},{4,5},{5,4},{6,7},{7,6},{8,9},{9,8},{10,11... | collective-permute-start | bytes 2457608 | tf_op jit(solution)/shard_map/ppermute | solution.py:302
  30.7 20.9 %collective-permute-start.1 = (bf16[160,2560]{1,0:T(8,128)(2,1)}, bf16[160,2560]{1,0:T(8,128)(2,1)}, u32[]{:S(2)}, u32[]{:S(2)}) collective-permute-start(bf16[160,2560]{1,0:T(8,128)(2,1)} %collective-permute-done.refs_1_), channel_id=1, source_target_pairs={{0,4},{1,5},{2,0},{3,1},{4,8},{5,9},{6,2},{7,3},{8,12},{9,13},{10,... | collective-permute-start | bytes 2457608 | tf_op jit(solution)/shard_map/ppermute | solution.py:296
  51.6 23.8 %collective-permute-start.12 = (bf16[160,2560]{1,0:T(8,128)(2,1)}, bf16[160,2560]{1,0:T(8,128)(2,1)S(1)}, u32[]{:S(2)}, u32[]{:S(2)}) collective-permute-start(bf16[160,2560]{1,0:T(8,128)(2,1)} %collective-permute-done.1.refs_1_), channel_id=1, source_target_pairs={{0,1},{1,0},{2,3},{3,2},{4,5},{5,4},{6,7},{7,6},{8,9},{9,8},{10,11... | collective-permute-start | bytes 2457608 | tf_op jit(solution)/shard_map/ppermute | solution.py:302
  51.6 20.9 %collective-permute-start.2 = (bf16[160,2560]{1,0:T(8,128)(2,1)}, bf16[160,2560]{1,0:T(8,128)(2,1)S(1)}, u32[]{:S(2)}, u32[]{:S(2)}) collective-permute-start(bf16[160,2560]{1,0:T(8,128)(2,1)} %collective-permute-done.1.refs_1_), channel_id=1, source_target_pairs={{0,4},{1,5},{2,0},{3,1},{4,8},{5,9},{6,2},{7,3},{8,12},{9,13},{10,... | collective-permute-start | bytes 2457608 | tf_op jit(solution)/shard_map/ppermute | solution.py:296
  53.1 21.8 %collective-permute-start.11 = (bf16[160,2560]{1,0:T(8,128)(2,1)}, bf16[160,2560]{1,0:T(8,128)(2,1)S(1)}, u32[]{:S(2)}, u32[]{:S(2)}) collective-permute-start(bf16[160,2560]{1,0:T(8,128)(2,1)} %collective-permute-done.5.refs_0_), channel_id=1, source_target_pairs={{0,1},{1,0},{2,3},{3,2},{4,5},{5,4},{6,7},{7,6},{8,9},{9,8},{10,11... | collective-permute-start | bytes 2457608 | tf_op jit(solution)/shard_map/ppermute | solution.py:302
  53.3 20.7 %collective-permute-start.6 = (bf16[160,2560]{1,0:T(8,128)(2,1)}, bf16[160,2560]{1,0:T(8,128)(2,1)S(1)}, u32[]{:S(2)}, u32[]{:S(2)}) collective-permute-start(bf16[160,2560]{1,0:T(8,128)(2,1)} %collective-permute-done.5.refs_0_), channel_id=1, source_target_pairs={{0,2},{1,3},{2,6},{3,7},{4,0},{5,1},{6,10},{7,11},{8,4},{9,5},{10,... | collective-permute-start | bytes 2457608 | tf_op jit(solution)/shard_map/ppermute | solution.py:299
  72.5 17.1 %collective-permute-start.3 = (bf16[80,2560]{1,0:T(8,128)(2,1)S(1)}, bf16[80,2560]{1,0:T(8,128)(2,1)S(1)}, u32[]{:S(2)}, u32[]{:S(2)}) collective-permute-start(bf16[80,2560]{1,0:T(8,128)(2,1)S(1)} %slice.84), channel_id=1, source_target_pairs={{0,4},{1,5},{2,0},{3,1},{4,8},{5,9},{6,2},{7,3},{8,12},{9,13},{10,... | collective-permute-start | bytes 1228808 | tf_op jit(solution)/shard_map/ppermute | solution.py:296
  74.1 15.6 %collective-permute-start.7 = (bf16[80,2560]{1,0:T(8,128)(2,1)S(1)}, bf16[80,2560]{1,0:T(8,128)(2,1)S(1)}, u32[]{:S(2)}, u32[]{:S(2)}) collective-permute-start(bf16[80,2560]{1,0:T(8,128)(2,1)S(1)} %slice.85), channel_id=1, source_target_pairs={{0,2},{1,3},{2,6},{3,7},{4,0},{5,1},{6,10},{7,11},{8,4},{9,5},{10,... | collective-permute-start | bytes 1228808 | tf_op jit(solution)/shard_map/ppermute | solution.py:299
  74.9 15.0 %collective-permute-start.10 = (bf16[160,2560]{1,0:T(8,128)(2,1)S(1)}, bf16[160,2560]{1,0:T(8,128)(2,1)S(1)}, u32[]{:S(2)}, u32[]{:S(2)}) collective-permute-start(bf16[160,2560]{1,0:T(8,128)(2,1)S(1)} %collective-permute-done.2.refs_1_), channel_id=1, source_target_pairs={{0,1},{1,0},{2,3},{3,2},{4,5},{5,4},{6,7},{7,6},{8,9},{9,8},{10,11... | collective-permute-start | bytes 2457608 | tf_op jit(solution)/shard_map/ppermute | solution.py:302
  74.9 15.0 %collective-permute-start.9 = (bf16[160,2560]{1,0:T(8,128)(2,1)S(1)}, bf16[160,2560]{1,0:T(8,128)(2,1)S(1)}, u32[]{:S(2)}, u32[]{:S(2)}) collective-permute-start(bf16[160,2560]{1,0:T(8,128)(2,1)S(1)} %collective-permute-done.6.refs_0_), channel_id=1, source_target_pairs={{0,1},{1,0},{2,3},{3,2},{4,5},{5,4},{6,7},{7,6},{8,9},{9,8},{10,11... | collective-permute-start | bytes 2457608 | tf_op jit(solution)/shard_map/ppermute | solution.py:302
  89.7 13.9 %collective-permute-start.8 = (bf16[160,2560]{1,0:T(8,128)(2,1)S(1)}, bf16[160,2560]{1,0:T(8,128)(2,1)S(1)}, u32[]{:S(2)}, u32[]{:S(2)}) collective-permute-start(bf16[160,2560]{1,0:T(8,128)(2,1)S(1)} %constant_dynamic-update-slice_fusion.refs_0_), channel_id=1, source_target_pairs={{0,1},{1,0},{2,3},{3,2},{4,5},{5,4},{6,7},{7,6},{8,9},{9,8},{10,11... | collective-permute-start | bytes 2457608 | tf_op jit(solution)/shard_map/ppermute | solution.py:302
  121.2 10.7 %collective-permute-start.17 = (bf16[160,2560]{1,0:T(8,128)(2,1)S(1)}, bf16[160,2560]{1,0:T(8,128)(2,1)S(1)}, u32[]{:S(2)}, u32[]{:S(2)}) collective-permute-start(bf16[160,2560]{1,0:T(8,128)(2,1)S(1)} %get-tuple-element.18), channel_id=1, source_target_pairs={{0,1},{1,0},{2,3},{3,2},{4,5},{5,4},{6,7},{7,6},{8,9},{9,8},{10,11... | collective-permute-start | bytes 2457608 | tf_op jit(solution)/shard_map/ppermute | solution.py:302
  131.7 13.4 %collective-permute-start.19 = (bf16[320,2560]{1,0:T(8,128)(2,1)S(1)}, bf16[320,2560]{1,0:T(8,128)(2,1)S(1)}, u32[]{:S(2)}, u32[]{:S(2)}) collective-permute-start(bf16[320,2560]{1,0:T(8,128)(2,1)S(1)} %get-tuple-element.20), channel_id=1, source_target_pairs={{0,1},{1,0},{2,3},{3,2},{4,5},{5,4},{6,7},{7,6},{8,9},{9,8},{10,11... | collective-permute-start | bytes 4915208 | tf_op jit(solution)/shard_map/ppermute | solution.py:302
  132.0 12.2 %collective-permute-start.18 = (bf16[80,2560]{1,0:T(8,128)(2,1)S(1)}, bf16[80,2560]{1,0:T(8,128)(2,1)S(1)}, u32[]{:S(2)}, u32[]{:S(2)}) collective-permute-start(bf16[80,2560]{1,0:T(8,128)(2,1)S(1)} %get-tuple-element.31), channel_id=1, source_target_pairs={{0,4},{1,5},{2,0},{3,1},{4,8},{5,9},{6,2},{7,3},{8,12},{9,13},{10,... | collective-permute-start | bytes 1228808 | tf_op jit(solution)/shard_map/ppermute | solution.py:296
  133.6 11.5 %collective-permute-start.25 = (bf16[80,2560]{1,0:T(8,128)(2,1)S(1)}, bf16[80,2560]{1,0:T(8,128)(2,1)S(1)}, u32[]{:S(2)}, u32[]{:S(2)}) collective-permute-start(bf16[80,2560]{1,0:T(8,128)(2,1)S(1)} %get-tuple-element.32), channel_id=1, source_target_pairs={{0,2},{1,3},{2,6},{3,7},{4,0},{5,1},{6,10},{7,11},{8,4},{9,5},{10,... | collective-permute-start | bytes 1228808 | tf_op jit(solution)/shard_map/ppermute | solution.py:299
  144.1 13.7 %collective-permute-start.21 = (bf16[320,2560]{1,0:T(8,128)(2,1)S(1)}, bf16[320,2560]{1,0:T(8,128)(2,1)S(1)}, u32[]{:S(2)}, u32[]{:S(2)}) collective-permute-start(bf16[320,2560]{1,0:T(8,128)(2,1)S(1)} %get-tuple-element.22), channel_id=1, source_target_pairs={{0,1},{1,0},{2,3},{3,2},{4,5},{5,4},{6,7},{7,6},{8,9},{9,8},{10,11... | collective-permute-start | bytes 4915208 | tf_op jit(solution)/shard_map/ppermute | solution.py:302
  145.6 19.8 %collective-permute-start.20 = (bf16[160,2560]{1,0:T(8,128)(2,1)S(1)}, bf16[160,2560]{1,0:T(8,128)(2,1)S(1)}, u32[]{:S(2)}, u32[]{:S(2)}) collective-permute-start(bf16[160,2560]{1,0:T(8,128)(2,1)S(1)} %get-tuple-element.29), channel_id=1, source_target_pairs={{0,4},{1,5},{2,0},{3,1},{4,8},{5,9},{6,2},{7,3},{8,12},{9,13},{10,... | collective-permute-start | bytes 2457608 | tf_op jit(solution)/shard_map/ppermute | solution.py:296
  146.3 20.3 %collective-permute-start.26 = (bf16[160,2560]{1,0:T(8,128)(2,1)S(1)}, bf16[160,2560]{1,0:T(8,128)(2,1)S(1)}, u32[]{:S(2)}, u32[]{:S(2)}) collective-permute-start(bf16[160,2560]{1,0:T(8,128)(2,1)S(1)} %get-tuple-element.30), channel_id=1, source_target_pairs={{0,2},{1,3},{2,6},{3,7},{4,0},{5,1},{6,10},{7,11},{8,4},{9,5},{10,... | collective-permute-start | bytes 2457608 | tf_op jit(solution)/shard_map/ppermute | solution.py:299
  157.7 19.4 %collective-permute-start.23 = (bf16[320,2560]{1,0:T(8,128)(2,1)S(1)}, bf16[320,2560]{1,0:T(8,128)(2,1)S(1)}, u32[]{:S(2)}, u32[]{:S(2)}) collective-permute-start(bf16[320,2560]{1,0:T(8,128)(2,1)S(1)} %get-tuple-element.24), channel_id=1, source_target_pairs={{0,1},{1,0},{2,3},{3,2},{4,5},{5,4},{6,7},{7,6},{8,9},{9,8},{10,11... | collective-permute-start | bytes 4915208 | tf_op jit(solution)/shard_map/ppermute | solution.py:302
  167.2 19.6 %collective-permute-start.22 = (bf16[160,2560]{1,0:T(8,128)(2,1)S(1)}, bf16[160,2560]{1,0:T(8,128)(2,1)S(1)}, u32[]{:S(2)}, u32[]{:S(2)}) collective-permute-start(bf16[160,2560]{1,0:T(8,128)(2,1)S(1)} %get-tuple-element.27), channel_id=1, source_target_pairs={{0,4},{1,5},{2,0},{3,1},{4,8},{5,9},{6,2},{7,3},{8,12},{9,13},{10,... | collective-permute-start | bytes 2457608 | tf_op jit(solution)/shard_map/ppermute | solution.py:296
  167.8 19.3 %collective-permute-start.27 = (bf16[160,2560]{1,0:T(8,128)(2,1)S(1)}, bf16[160,2560]{1,0:T(8,128)(2,1)S(1)}, u32[]{:S(2)}, u32[]{:S(2)}) collective-permute-start(bf16[160,2560]{1,0:T(8,128)(2,1)S(1)} %get-tuple-element.28), channel_id=1, source_target_pairs={{0,2},{1,3},{2,6},{3,7},{4,0},{5,1},{6,10},{7,11},{8,4},{9,5},{10,... | collective-permute-start | bytes 2457608 | tf_op jit(solution)/shard_map/ppermute | solution.py:299
  177.0 12.8 %collective-permute-start.16 = (bf16[160,2560]{1,0:T(8,128)(2,1)S(1)}, bf16[160,2560]{1,0:T(8,128)(2,1)S(1)}, u32[]{:S(2)}, u32[]{:S(2)}) collective-permute-start(bf16[160,2560]{1,0:T(8,128)(2,1)S(1)} %get-tuple-element.16), channel_id=1, source_target_pairs={{0,1},{1,0},{2,3},{3,2},{4,5},{5,4},{6,7},{7,6},{8,9},{9,8},{10,11... | collective-permute-start | bytes 2457608 | tf_op jit(solution)/shard_map/ppermute | solution.py:302
  187.7 18.4 %collective-permute-start.24 = (bf16[160,2560]{1,0:T(8,128)(2,1)S(1)}, bf16[160,2560]{1,0:T(8,128)(2,1)S(1)}, u32[]{:S(2)}, u32[]{:S(2)}) collective-permute-start(bf16[160,2560]{1,0:T(8,128)(2,1)S(1)} %get-tuple-element.25), channel_id=1, source_target_pairs={{0,4},{1,5},{2,0},{3,1},{4,8},{5,9},{6,2},{7,3},{8,12},{9,13},{10,... | collective-permute-start | bytes 2457608 | tf_op jit(solution)/shard_map/ppermute | solution.py:296
  188.3 18.1 %collective-permute-start.28 = (bf16[160,2560]{1,0:T(8,128)(2,1)S(1)}, bf16[160,2560]{1,0:T(8,128)(2,1)S(1)}, u32[]{:S(2)}, u32[]{:S(2)}) collective-permute-start(bf16[160,2560]{1,0:T(8,128)(2,1)S(1)} %get-tuple-element.26), channel_id=1, source_target_pairs={{0,2},{1,3},{2,6},{3,7},{4,0},{5,1},{6,10},{7,11},{8,4},{9,5},{10,... | collective-permute-start | bytes 2457608 | tf_op jit(solution)/shard_map/ppermute | solution.py:299
  (1 other events, 4.5 us)

commit v3 on v2

--- a/solution.py
+++ b/solution.py
@@ -162,46 +162,84 @@
         return [(d, d ^ 1) for d in range(self.devices)]
 
 
-def hidden_kernel(count, rows, *refs):
+def hidden_kernel(count, rows, first_row, chunk, *refs):
     x_refs = refs[:count]
     w_ref = refs[count]
-    out_ref, x_all = refs[-2:]
-
-    @pl.when(pl.program_id(0) == 0)
-    def _():
-        for i in range(count):
-            x_all[i * rows : (i + 1) * rows, :] = x_refs[i][...]
-
-    width = w_ref.shape[2]
-    weight = w_ref[0].reshape(2 * width, w_ref.shape[3])
-    both = lax.dot_general(
-        x_all[...], weight, (((1,), (1,)), ((), ())), preferred_element_type=jnp.float32
-    )
-    gate, up = both[:, :width], both[:, width:]
-    out_ref[...] = (gate / (1.0 + jnp.exp(-gate)) * up).astype(out_ref.dtype)
-
-
-def hidden_call(blocks, gate_up_weight, hidden, first_slot, slot_count):
+    out_ref, x_all, w_all, h_all, x_sems, w_sems, h_sems = refs[-7:]
+    ff = w_ref.shape[2]
+    whole, rest = divmod(ff, chunk)
+    total = count * rows
+
+    def row_copy(i):
+        return pltpu.make_async_copy(
+            x_refs[i], x_all.at[i * rows : (i + 1) * rows], x_sems.at[i]
+        )
+
+    def weight_copy(i, width):
+        part = pl.ds(pl.multiple_of(i * chunk, chunk), width)
+        return pltpu.make_async_copy(w_ref.at[0, :, part], w_all.at[:, part], w_sems.at[i])
+
+    def out_copy(i, width):
+        part = pl.ds(pl.multiple_of(i * chunk, chunk), width)
+        return pltpu.make_async_copy(
+            h_all.at[i, :, :width],
+            out_ref.at[first_row : first_row + total, part],
+            h_sems.at[i],
+        )
+
+    widths = [chunk] * whole + [rest] * (rest > 0)
+    for i in range(count):
+        row_copy(i).start()
+    for i, width in enumerate(widths):
+        weight_copy(i, width).start()
+    for i in range(count):
+        row_copy(i).wait()
+
+    def step(i, width):
+        weight_copy(i, width).wait()
+        part = pl.ds(pl.multiple_of(i * chunk, chunk), width)
+        weight = w_all[:, part, :].reshape(2 * width, w_ref.shape[3])
+        both = lax.dot_general(
+            x_all[...], weight, (((1,), (1,)), ((), ())), preferred_element_type=jnp.float32
+        )
+        gate, up = both[:, :width], both[:, width:]
+        h_all[i, :, :width] = (gate / (1.0 + jnp.exp(-gate)) * up).astype(h_all.dtype)
+        out_copy(i, width).start()
+
+    @pl.loop(0, whole)
+    def _(i):
+        step(i, chunk)
+
+    if rest:
+        step(whole, rest)
+    for i, width in enumerate(widths):
+        out_copy(i, width).wait()
+
+
+def hidden_call(blocks, gate_up_weight, hidden, first_row, all_rows):
     rows, wide = blocks[0].shape
     _, _, ff, _ = gate_up_weight.shape
     count = len(blocks)
     chunk = 256
-    place = first_slot // count
-    whole = pl.BlockSpec((rows, wide), lambda i: (0, 0))
-    in_specs = [whole] * count + [pl.BlockSpec((1, 2, chunk, wide), lambda i: (0, 0, i, 0))]
+    chunks = pl.cdiv(ff, chunk)
     args = list(blocks) + [gate_up_weight]
     aliases = {}
     if hidden is not None:
-        in_specs.append(pl.BlockSpec(memory_space=pl.ANY))
         args.append(hidden)
         aliases = {len(args) - 1: 0}
     return pl.pallas_call(
-        functools.partial(hidden_kernel, count, rows),
-        grid=(pl.cdiv(ff, chunk),),
-        in_specs=in_specs,
-        out_specs=pl.BlockSpec((count * rows, chunk), lambda i: (place, i)),
-        out_shape=jax.ShapeDtypeStruct((slot_count * rows, ff), jnp.bfloat16),
-        scratch_shapes=[pltpu.VMEM((count * rows, wide), jnp.bfloat16)],
+        functools.partial(hidden_kernel, count, rows, first_row, chunk),
+        in_specs=[pl.BlockSpec(memory_space=pl.ANY)] * len(args),
+        out_specs=pl.BlockSpec(memory_space=pl.ANY),
+        out_shape=jax.ShapeDtypeStruct((all_rows, ff), jnp.bfloat16),
+        scratch_shapes=[
+            pltpu.VMEM((count * rows, wide), jnp.bfloat16),
+            pltpu.VMEM((2, ff, wide), jnp.bfloat16),
+            pltpu.VMEM((chunks, count * rows, chunk), jnp.bfloat16),
+            pltpu.SemaphoreType.DMA((count,)),
+            pltpu.SemaphoreType.DMA((chunks,)),
+            pltpu.SemaphoreType.DMA((chunks,)),
+        ],
         input_output_aliases=aliases,
         compiler_params=pltpu.CompilerParams(vmem_limit_bytes=32 * 1024 * 1024),
         cost_estimate=pl.CostEstimate(
@@ -213,61 +251,106 @@
 
 
 def down_kernel(
-    slots, first_slot, rows, text_rows, sources_ref, hidden_ref, order_ref, scale_ref, w_ref,
-    own_ref, other_ref, picked,
+    slots, first_slot, rows, text_rows, seq_count, sources_ref, hidden_ref, order_ref, scale_ref,
+    w_ref, own_ref, other_ref, column, picked, w_all, y_all, text_sems, image_sems, w_sems, y_sems,
 ):
     image_rows = rows - text_rows
-    seq_count = order_ref.shape[2] // image_rows
-
-    @pl.when(pl.program_id(0) == 0)
-    def _():
-        for j in range(slots):
-            at = (first_slot + j) * rows
-            picked[j * rows : j * rows + text_rows, :] = hidden_ref[at : at + text_rows, :]
-            wanted = lax.broadcasted_iota(jnp.int32, (image_rows, order_ref.shape[2]), 0)
-            match = jnp.where(order_ref[j] == wanted, 1.0, 0.0).astype(jnp.bfloat16)
-            total = jnp.zeros((image_rows, hidden_ref.shape[1]), jnp.float32)
-            for z in range(seq_count):
-                source = sources_ref[(first_slot + j) * seq_count + z]
-                start = pl.multiple_of(source * rows + text_rows, 16)
-                total += jnp.dot(
-                    match[:, z * image_rows : (z + 1) * image_rows],
-                    hidden_ref[pl.ds(start, image_rows), :],
-                    preferred_element_type=jnp.float32,
-                )
-            picked[j * rows + text_rows : (j + 1) * rows, :] = total.astype(jnp.bfloat16)
-
-    result = jnp.dot(picked[...], w_ref[0], preferred_element_type=jnp.float32)
-    scaled = (result.astype(jnp.bfloat16).astype(jnp.float32) * scale_ref[...]).astype(jnp.bfloat16)
+    chunks, _, chunk = w_all.shape
     half = slots * rows // 2
-    own_ref[...] = scaled[:half]
-    other_ref[...] = scaled[half:]
+
+    def text_copy(j):
+        at = (first_slot + j) * rows
+        return pltpu.make_async_copy(
+            hidden_ref.at[at : at + text_rows],
+            picked.at[j * rows : j * rows + text_rows],
+            text_sems.at[j],
+        )
+
+    def image_copy(j, z):
+        source = sources_ref[(first_slot + j) * seq_count + z]
+        start = pl.multiple_of(source * rows + text_rows, 16)
+        return pltpu.make_async_copy(
+            hidden_ref.at[pl.ds(start, image_rows)],
+            column.at[j, z * image_rows : (z + 1) * image_rows],
+            image_sems.at[j, z],
+        )
+
+    def weight_copy(i):
+        part = pl.ds(pl.multiple_of(i * chunk, chunk), chunk)
+        return pltpu.make_async_copy(w_ref.at[0, :, part], w_all.at[i], w_sems.at[i])
+
+    def out_copies(i):
+        part = pl.ds(pl.multiple_of(i * chunk, chunk), chunk)
+        return (
+            pltpu.make_async_copy(y_all.at[i, :half], own_ref.at[:, part], y_sems.at[0, i]),
+            pltpu.make_async_copy(y_all.at[i, half:], other_ref.at[:, part], y_sems.at[1, i]),
+        )
+
+    for j in range(slots):
+        text_copy(j).start()
+        for z in range(seq_count):
+            image_copy(j, z).start()
+    for i in range(chunks):
+        weight_copy(i).start()
+    wanted = lax.broadcasted_iota(jnp.int32, (image_rows, seq_count * image_rows), 0)
+    for j in range(slots):
+        text_copy(j).wait()
+        for z in range(seq_count):
+            image_copy(j, z).wait()
+        match = jnp.where(order_ref[j] == wanted, 1.0, 0.0).astype(jnp.bfloat16)
+        rows_here = jnp.dot(match, column[j], preferred_element_type=jnp.float32)
+        picked[j * rows + text_rows : (j + 1) * rows, :] = rows_here.astype(jnp.bfloat16)
+
+    @pl.loop(0, chunks)
+    def _(i):
+        weight_copy(i).wait()
+        result = jnp.dot(picked[...], w_all[i], preferred_element_type=jnp.float32)
+        scaled = result.astype(jnp.bfloat16).astype(jnp.float32) * scale_ref[...]
+        y_all[i] = scaled.astype(jnp.bfloat16)
+        for copy in out_copies(i):
+            copy.start()
+
+    for i in range(chunks):
+        for copy in out_copies(i):
+            copy.wait()
 
 
 def down_call(hidden, order, scale, sources, down_weight, first_slot, slots, rows, text_rows):
     _, ff, wide = down_weight.shape
     chunk = 512
+    chunks = wide // chunk
     half = slots * rows // 2
+    source_rows = order.shape[2]
+    seq_count = source_rows // (rows - text_rows)
     grid_spec = pltpu.PrefetchScalarGridSpec(
         num_scalar_prefetch=1,
-        grid=(wide // chunk,),
+        grid=(1,),
         in_specs=[
-            pl.BlockSpec(hidden.shape, lambda i, s: (0, 0), pipeline_mode=pl.Buffered(1)),
-            pl.BlockSpec((slots, 1, order.shape[2]), lambda i, s: (first_slot // slots, 0, 0)),
+            pl.BlockSpec(memory_space=pl.ANY),
+            pl.BlockSpec((slots, 1, source_rows), lambda i, s: (first_slot // slots, 0, 0)),
             pl.BlockSpec((slots * rows, 1), lambda i, s: (first_slot // slots, 0)),
-            pl.BlockSpec((1, ff, chunk), lambda i, s: (0, 0, i)),
+            pl.BlockSpec(memory_space=pl.ANY),
         ],
-        out_specs=[pl.BlockSpec((half, chunk), lambda i, s: (0, i))] * 2,
-        scratch_shapes=[pltpu.VMEM((slots * rows, ff), jnp.bfloat16)],
+        out_specs=[pl.BlockSpec(memory_space=pl.ANY)] * 2,
+        scratch_shapes=[
+            pltpu.VMEM((slots, source_rows, ff), jnp.bfloat16),
+            pltpu.VMEM((slots * rows, ff), jnp.bfloat16),
+            pltpu.VMEM((chunks, ff, chunk), jnp.bfloat16),
+            pltpu.VMEM((chunks, slots * rows, chunk), jnp.bfloat16),
+            pltpu.SemaphoreType.DMA((slots,)),
+            pltpu.SemaphoreType.DMA((slots, seq_count)),
+            pltpu.SemaphoreType.DMA((chunks,)),
+            pltpu.SemaphoreType.DMA((2, chunks)),
+        ],
     )
     return pl.pallas_call(
-        functools.partial(down_kernel, slots, first_slot, rows, text_rows),
+        functools.partial(down_kernel, slots, first_slot, rows, text_rows, seq_count),
         grid_spec=grid_spec,
         out_shape=[jax.ShapeDtypeStruct((half, wide), jnp.bfloat16)] * 2,
-        compiler_params=pltpu.CompilerParams(vmem_limit_bytes=40 * 1024 * 1024),
+        compiler_params=pltpu.CompilerParams(vmem_limit_bytes=32 * 1024 * 1024),
         cost_estimate=pl.CostEstimate(
             flops=2 * slots * rows * wide * ff,
-            bytes_accessed=2 * ff * wide + 2 * hidden.size + 2 * slots * rows * wide,
+            bytes_accessed=2 * ff * wide + 2 * slots * rows * wide,
             transcendentals=0,
         ),
     )(sources, hidden, order, scale, down_weight)
@@ -308,34 +391,42 @@
     experts = jnp.arange(ring.devices, dtype=jnp.int32)[:, None, None]
     routed = jnp.where(expert_ids[None] == experts, gate_weights[None], 0.0).sum(axis=-1)
     targets = jnp.broadcast_to(panel_target.astype(jnp.float32), (ring.devices, pan_count))
-    tables = lax.all_to_all(
-        jnp.concatenate([routed, targets], axis=1), AXES, split_axis=0, concat_axis=0, tiled=True
-    )
-    weights = tables[:, :tok_count]
-    target = tables[:, tok_count:].astype(jnp.int32)
-    target_seq = target // pan_count // expert_count
-    first_row = target_seq * image_rows + target % pan_count * panel_rows
-    target_row = first_row[:, :, None] + jnp.arange(panel_rows, dtype=jnp.int32)
-    by_column = target_row.reshape(seq_count, expert_count, image_rows).transpose(1, 0, 2)
-    by_column = by_column.reshape(expert_count, seq_count * image_rows)
-    owners = jnp.asarray(ring.owner_of)[me]
-    sources = jnp.asarray(ring.sources_of.reshape(ring.devices, -1))[me]
-    order = by_column[owners % expert_count] - (owners // expert_count * image_rows)[:, None]
-    order = order[:, None, :]
-    scale = weights[owners].reshape(slot_count * tok_count, 1)
-
-    hidden = hidden_call([own, other], gate_up_weight, None, 0, slot_count)
+    outgoing = jnp.concatenate([routed, targets], axis=1)
+    tables = (lax.all_to_all(outgoing, AXES, split_axis=0, concat_axis=0, tiled=True),)
+
+    def read_tables(tables):
+        weights = tables[:, :tok_count]
+        target = tables[:, tok_count:].astype(jnp.int32)
+        target_seq = target // pan_count // expert_count
+        first_row = target_seq * image_rows + target % pan_count * panel_rows
+        target_row = first_row[:, :, None] + jnp.arange(panel_rows, dtype=jnp.int32)
+        by_column = target_row.reshape(seq_count, expert_count, image_rows).transpose(1, 0, 2)
+        by_column = by_column.reshape(expert_count, seq_count * image_rows)
+        owners = jnp.asarray(ring.owner_of)[me]
+        sources = jnp.asarray(ring.sources_of.reshape(ring.devices, -1))[me]
+        order = by_column[owners % expert_count] - (owners // expert_count * image_rows)[:, None]
+        order = order[:, None, :]
+        scale = weights[owners].reshape(slot_count * tok_count, 1)
+        return order, scale, sources
+
+    all_rows = slot_count * tok_count
+    hidden = hidden_call([own, other], gate_up_weight, None, 0, all_rows)
+    hidden, before, after = lax.optimization_barrier((hidden, before, after))
+    cut = tok_count // 2
     for s in range(1, ring.half):
         here = [after, before]
         there = [across(after), across(before)]
-        if s + 1 < ring.half:
-            before, after = onward(before), back(after)
-        else:
-            cut = tok_count // 2
-            far_before, far_after = onward(before[:cut]), back(after[cut:])
-        hidden = hidden_call(here + there, gate_up_weight, hidden, 4 * s, slot_count)
-    far = jnp.concatenate([far_before, far_after], axis=0)
-    hidden = hidden_call([far, across(far)], gate_up_weight, hidden, 2, slot_count)
+        if s + 1 == ring.half:
+            before, after = before[:cut], after[cut:]
+        before, after = onward(before), back(after)
+        first_row = 4 * s * tok_count
+        hidden = hidden_call(here + there, gate_up_weight, hidden, first_row, all_rows)
+        hidden, before, after, *tables = lax.optimization_barrier((hidden, before, after, *tables))
+        if s == 1:
+            tables = read_tables(*tables)
+    order, scale, sources = tables
+    far = [before, after, across(before), across(after)]
+    hidden = hidden_call(far, gate_up_weight, hidden, 2 * tok_count, all_rows)
 
     def outputs(first_slot, slots):
         mine, others = down_call(
@@ -343,7 +434,6 @@
         )
         return mine, across(others)
 
-    cut = tok_count // 2
     mine, swapped = outputs(2, 2)
     leaving = add_up(mine[:cut], swapped[:cut]), add_up(mine[cut:], swapped[cut:])
     for s in range(ring.half - 1, -1, -1):

time: 209 us -> 218 us (1.043)
  local copies, waits for them, and re-layouts: 4.11 us -> 24.2 us
  waiting for transfers between devices: 63.2 us -> 51.9 us
    unnamed x8 -> x21, local copies, waits for them, and re-layouts: 0.04 us -> 20.8 us
    ppermute x8, waiting for transfers between devices: 46.3 us -> 26 us  [onward(): return lax.ppermute(array, AXES, ring.step(1))]
    ppermute x8, waiting for transfers between devices: 2.72 us -> 18.6 us  [back(): return lax.ppermute(array, AXES, ring.step(-1))]
    all_to_all x1, waiting for transfers between devices: 14.2 us -> 5.08 us  [ring_shards(): lax.all_to_all(outgoing, AXES, split_axis=0, concat_axis=0, tiled=True)]
    pallas_call x5, Pallas kernels: 45.5 us -> 49.9 us  [down_call(): pl.pallas_call(functools.partial(down_kernel, slots, first_slot, rows, te...]
    pallas_call x5, Pallas kernels: 62.4 us -> 59.4 us  [hidden_call(): pl.pallas_call(functools.partial(hidden_kernel, count, rows, first_row, c...]
    ppermute x8, starting transfers between devices: 8.21 us -> 5.96 us  [onward(): return lax.ppermute(array, AXES, ring.step(1))]
    ppermute x13 -> x14, waiting for transfers between devices: 0.03 us -> 2.25 us  [across(): return lax.ppermute(array, AXES, ring.swap())]
  transfers between devices with their start and end apart: 30 -> 31, of which waited for: 10 -> 12; matrix products, arithmetic and copies ran while one was open for 4% -> 3% of each run, Pallas kernels for 44% -> 43%
where the time goes in v3:
time: 218 us; the launch traced here: 217 us
  Pallas kernels  109 us (50%)
  waiting for transfers between devices  51.9 us (24%)
  starting transfers between devices  25.5 us (12%)
  local copies, waits for them, and re-layouts  24.2 us (11%)
  other arithmetic  5.94 us (3%)
    pallas_call x5, Pallas kernels, hidden_call(): pl.pallas_call(functools.partial(hidden_kernel, count, rows, first_row, c...  59.4 us
    pallas_call x5, Pallas kernels, down_call(): pl.pallas_call(functools.partial(down_kernel, slots, first_slot, rows, te...  49.9 us
    ppermute x8, waiting for transfers between devices, onward(): return lax.ppermute(array, AXES, ring.step(1))  26 us
    unnamed x21, local copies, waits for them, and re-layouts  20.8 us
    ppermute x8, waiting for transfers between devices, back(): return lax.ppermute(array, AXES, ring.step(-1))  18.6 us
    ppermute x8, starting transfers between devices, back(): return lax.ppermute(array, AXES, ring.step(-1))  11.2 us
    ppermute x8, starting transfers between devices, onward(): return lax.ppermute(array, AXES, ring.step(1))  5.96 us
    all_to_all x1, waiting for transfers between devices, ring_shards(): lax.all_to_all(outgoing, AXES, split_axis=0, concat_axis=0, tiled=True)  5.08 us
  transfers between devices with their start and end apart: 31, of which 12 were waited for; matrix products, arithmetic and copies ran while one was open for 3% of the time, Pallas kernels for 43%

profile of v3, /device:TPU:0, one launch (start us, length us, event | category | flops | bytes accessed | tf_op | source)
XLA Modules:
  0.0 217.2 jit_solution(11871006916936205772)
XLA Ops:
  1.7 2.6 %collective-permute-start.1 = (bf16[160,2560]{1,0:T(8,128)(2,1)S(1)}, bf16[160,2560]{1,0:T(8,128)(2,1)S(1)}, u32[]{:S(2)}, u32[]{:S(2)}) collective-permute-start(bf16[160,2560]{1,0:T(8,128)(2,1)S(1)} %pad_maximum_fusion.refs_0_), channel_id=1, source_target_pairs={{0,4},{1,5},{2,0},{3,1},{4,8},{5,9},{6,2},{7,3},{8,12},{9,13},{10,... | collective-permute-start | bytes 2457608 | tf_op jit(solution)/shard_map/ppermute | solution.py:379
  4.4 8.1 %shard_map.91.refs_5_ = bf16[2560,1408]{1,0:T(8,128)(2,1)S(1)} custom-call(bf16[160,2560]{1,0:T(8,128)(2,1)S(1)} %pad_maximum_fusion.refs_0_, bf16[160,2560]{1,0:T(8,128)(2,1)S(1)} %collective-permute-done.refs_1_, bf16[1,2,1408,2560]{3,2,1,0:T(8,128)(2,1)} %refs_4_.7), custom_call_target="tpu_custom_call" | custom-call | flops 4613734400 | bytes 16957440 | tf_op jit(solution)/shard_map/pallas_call | solution.py:230
  12.5 2.9 %copy-done = bf16[2560,1408]{1,0:T(8,128)(2,1)} copy-done((bf16[2560,1408]{1,0:T(8,128)(2,1)}, bf16[2560,1408]{1,0:T(8,128)(2,1)S(1)}, u32[]{:S(2)}) %copy-start) | copy-done | bytes 7208984
  15.4 7.7 %collective-permute-done.1.refs_1_ = bf16[160,2560]{1,0:T(8,128)(2,1)S(1)} collective-permute-done((bf16[160,2560]{1,0:T(8,128)(2,1)S(1)}, bf16[160,2560]{1,0:T(8,128)(2,1)S(1)}, u32[]{:S(2)}, u32[]{:S(2)}) %collective-permute-start.1) | collective-permute-done | bytes 819232 | tf_op jit(solution)/shard_map/ppermute | solution.py:379
  23.1 1.5 collective-permute-done.2.refs_0_
  25.9 4.9 %all-to-all-start = ((f32[16,1,176]{2,1,0:T(1,128)}), f32[16,1,176]{2,1,0:T(1,128)S(1)}, u32[]{:S(2)}, u32[]{:S(2)}) async-start(f32[16,1,176]{2,1,0:T(1,128)} %copy.30), calls=%async_computation | async-start | bytes 32768 | tf_op jit(solution)/shard_map/all_to_all | solution.py:395
  32.3 5.1 %all-to-all-done = f32[16,1,176]{2,1,0:T(1,128)S(1)} async-done(((f32[16,1,176]{2,1,0:T(1,128)}), f32[16,1,176]{2,1,0:T(1,128)S(1)}, u32[]{:S(2)}, u32[]{:S(2)}) %all-to-all-start) | async-done | bytes 11296 | tf_op jit(solution)/shard_map/all_to_all | solution.py:395
  37.8 1.6 collective-permute-start.6
  39.4 3.0 %copy-done.1 = bf16[2560,1408]{1,0:T(8,128)(2,1)S(1)} copy-done((bf16[2560,1408]{1,0:T(8,128)(2,1)S(1)}, bf16[2560,1408]{1,0:T(8,128)(2,1)}, u32[]{:S(2)}) %copy-start.1) | copy-done | bytes 7208984
  42.4 13.1 %shard_map.92.refs_5_ = bf16[2560,1408]{1,0:T(8,128)(2,1)S(1)} custom-call(bf16[160,2560]{1,0:T(8,128)(2,1)S(1)} %collective-permute-done.2.refs_0_, bf16[160,2560]{1,0:T(8,128)(2,1)S(1)} %collective-permute-done.1.refs_1_, bf16[160,2560]{1,0:T(8,128)(2,1)S(1)} %collective-permute-done.3.refs_2_, ...), custom_call_target="tpu_custom_call", output_to_operand_aliasing={{}: (5, {})} | custom-call | flops 9227468800 | bytes 19496960 | tf_op jit(solution)/shard_map/pallas_call | solution.py:230
  55.5 2.9 %copy-done.2 = bf16[2560,1408]{1,0:T(8,128)(2,1)} copy-done((bf16[2560,1408]{1,0:T(8,128)(2,1)}, bf16[2560,1408]{1,0:T(8,128)(2,1)S(1)}, u32[]{:S(2)}) %copy-start.2) | copy-done | bytes 7208984
  60.2 1.6 collective-permute-start.10
  63.5 3.0 %copy-done.3 = bf16[2560,1408]{1,0:T(8,128)(2,1)S(1)} copy-done((bf16[2560,1408]{1,0:T(8,128)(2,1)S(1)}, bf16[2560,1408]{1,0:T(8,128)(2,1)}, u32[]{:S(2)}) %copy-start.3) | copy-done | bytes 7208984
  66.5 16.4 %shard_map.93.refs_5_ = bf16[2560,1408]{1,0:T(8,128)(2,1)S(1)} custom-call(bf16[160,2560]{1,0:T(8,128)(2,1)} %collective-permute-done.6.refs_0_, bf16[160,2560]{1,0:T(8,128)(2,1)} %collective-permute-done.5.refs_1_, bf16[160,2560]{1,0:T(8,128)(2,1)S(1)} %collective-permute-done.7.refs_2_, ...), custom_call_target="tpu_custom_call", output_to_operand_aliasing={{}: (5, {})} | custom-call | flops 9227468800 | bytes 19496960 | tf_op jit(solution)/shard_map/pallas_call | solution.py:230
  84.1 1.6 collective-permute-start.14
  86.5 13.1 %shard_map.94.refs_5_ = bf16[2560,1408]{1,0:T(8,128)(2,1)S(1)} custom-call(bf16[160,2560]{1,0:T(8,128)(2,1)S(1)} %collective-permute-done.10.refs_0_, bf16[160,2560]{1,0:T(8,128)(2,1)S(1)} %collective-permute-done.9.refs_1_, bf16[160,2560]{1,0:T(8,128)(2,1)S(1)} %collective-permute-done.11.refs_2_, ...), custom_call_target="tpu_custom_call", output_to_operand_aliasing={{}: (5, {})} | custom-call | flops 9227468800 | bytes 19496960 | tf_op jit(solution)/shard_map/pallas_call | solution.py:230
  99.6 2.9 %copy-done.4 = bf16[2560,1408]{1,0:T(8,128)(2,1)} copy-done((bf16[2560,1408]{1,0:T(8,128)(2,1)}, bf16[2560,1408]{1,0:T(8,128)(2,1)S(1)}, u32[]{:S(2)}) %copy-start.4) | copy-done | bytes 7208984
  104.8 3.0 %copy-done.5 = bf16[2560,1408]{1,0:T(8,128)(2,1)S(1)} copy-done((bf16[2560,1408]{1,0:T(8,128)(2,1)S(1)}, bf16[2560,1408]{1,0:T(8,128)(2,1)}, u32[]{:S(2)}) %copy-start.5) | copy-done | bytes 7208984
  107.8 8.8 %shard_map.95.hidden_ref = bf16[2560,1408]{1,0:T(8,128)(2,1)S(1)} custom-call(bf16[80,2560]{1,0:T(8,128)(2,1)S(1)} %collective-permute-done.13.refs_0_, bf16[80,2560]{1,0:T(8,128)(2,1)S(1)} %collective-permute-done.14.refs_1_, bf16[80,2560]{1,0:T(8,128)(2,1)S(1)} %collective-permute-done.15.refs_2_, ...), custom_call_target="tpu_custom_call", output_to_operand_aliasing={{}: (5, {})} | custom-call | flops 4613734400 | bytes 16957440 | tf_op jit(solution)/shard_map/pallas_call | solution.py:230
  116.6 3.0 %copy-done.6 = bf16[1,1408,2560]{2,1,0:T(8,128)(2,1)S(1)} copy-done((bf16[1,1408,2560]{2,1,0:T(8,128)(2,1)S(1)}, bf16[1,1408,2560]{2,1,0:T(8,128)(2,1)}, u32[]{:S(2)}) %copy-start.6) | copy-done | bytes 7208984
  119.6 7.0 %shard_map.97 = (bf16[160,2560]{1,0:T(8,128)(2,1)S(1)}, bf16[160,2560]{1,0:T(8,128)(2,1)S(1)}) custom-call(s32[64]{0:T(128)S(1)} %dynamic-slice_bitcast_fusion.sources_ref, bf16[2560,1408]{1,0:T(8,128)(2,1)S(1)} %shard_map.95.hidden_ref, s32[16,1,512]{2,1,0:T(1,128)S(1)} %reshape_subtract_fusion.order_ref, f32[2560,1]{1,0:T(8,128)S(1)} %copy.31.scale_ref, ...), custom_call_target="tpu_custom_call" | custom-call | flops 2306867200 | bytes 8847360 | tf_op jit(solution)/shard_map/pallas_call | solution.py:346
  126.9 12.0 %shard_map.98 = (bf16[320,2560]{1,0:T(8,128)(2,1)S(1)}, bf16[320,2560]{1,0:T(8,128)(2,1)S(1)}) custom-call(s32[64]{0:T(128)S(1)} %dynamic-slice_bitcast_fusion.sources_ref, bf16[2560,1408]{1,0:T(8,128)(2,1)S(1)} %shard_map.95.hidden_ref, s32[16,1,512]{2,1,0:T(1,128)S(1)} %reshape_subtract_fusion.order_ref, f32[2560,1]{1,0:T(8,128)S(1)} %copy.31.scale_ref, ...), custom_call_target="tpu_custom_call" | custom-call | flops 4613734400 | bytes 10485760 | tf_op jit(solution)/shard_map/pallas_call | solution.py:346
  140.0 1.6 collective-permute-start.26
  141.5 12.0 %shard_map.99 = (bf16[320,2560]{1,0:T(8,128)(2,1)S(1)}, bf16[320,2560]{1,0:T(8,128)(2,1)S(1)}) custom-call(s32[64]{0:T(128)S(1)} %dynamic-slice_bitcast_fusion.sources_ref, bf16[2560,1408]{1,0:T(8,128)(2,1)S(1)} %shard_map.95.hidden_ref, s32[16,1,512]{2,1,0:T(1,128)S(1)} %reshape_subtract_fusion.order_ref, f32[2560,1]{1,0:T(8,128)S(1)} %copy.31.scale_ref, ...), custom_call_target="tpu_custom_call" | custom-call | flops 4613734400 | bytes 10485760 | tf_op jit(solution)/shard_map/pallas_call | solution.py:346
  154.6 1.6 collective-permute-start.27
  156.2 12.0 %shard_map.100 = (bf16[320,2560]{1,0:T(8,128)(2,1)S(1)}, bf16[320,2560]{1,0:T(8,128)(2,1)S(1)}) custom-call(s32[64]{0:T(128)S(1)} %dynamic-slice_bitcast_fusion.sources_ref, bf16[2560,1408]{1,0:T(8,128)(2,1)S(1)} %shard_map.95.hidden_ref, s32[16,1,512]{2,1,0:T(1,128)S(1)} %reshape_subtract_fusion.order_ref, f32[2560,1]{1,0:T(8,128)S(1)} %copy.31.scale_ref, ...), custom_call_target="tpu_custom_call" | custom-call | flops 4613734400 | bytes 10485760 | tf_op jit(solution)/shard_map/pallas_call | solution.py:346
  168.2 6.5 %collective-permute-done.21 = bf16[160,2560]{1,0:T(8,128)(2,1)S(1)} collective-permute-done((bf16[160,2560]{1,0:T(8,128)(2,1)S(1)}, bf16[160,2560]{1,0:T(8,128)(2,1)S(1)}, u32[]{:S(2)}, u32[]{:S(2)}) %collective-permute-start.21) | collective-permute-done | bytes 819232 | tf_op jit(solution)/shard_map/ppermute | solution.py:379
  176.2 1.6 collective-permute-start.28
  177.7 7.0 %shard_map.96 = (bf16[160,2560]{1,0:T(8,128)(2,1)S(1)}, bf16[160,2560]{1,0:T(8,128)(2,1)S(1)}) custom-call(s32[64]{0:T(128)S(1)} %dynamic-slice_bitcast_fusion.sources_ref, bf16[2560,1408]{1,0:T(8,128)(2,1)S(1)} %shard_map.95.hidden_ref, s32[16,1,512]{2,1,0:T(1,128)S(1)} %reshape_subtract_fusion.order_ref, f32[2560,1]{1,0:T(8,128)S(1)} %copy.31.scale_ref, ...), custom_call_target="tpu_custom_call" | custom-call | flops 2306867200 | bytes 8847360 | tf_op jit(solution)/shard_map/pallas_call | solution.py:346
  184.9 10.5 %collective-permute-done.23 = bf16[160,2560]{1,0:T(8,128)(2,1)S(1)} collective-permute-done((bf16[160,2560]{1,0:T(8,128)(2,1)S(1)}, bf16[160,2560]{1,0:T(8,128)(2,1)S(1)}, u32[]{:S(2)}, u32[]{:S(2)}) %collective-permute-start.23) | collective-permute-done | bytes 819232 | tf_op jit(solution)/shard_map/ppermute | solution.py:379
  196.0 1.7 collective-permute-start.29
  198.1 16.6 %collective-permute-done.29 = bf16[160,2560]{1,0:T(8,128)(2,1)S(1)} collective-permute-done((bf16[160,2560]{1,0:T(8,128)(2,1)S(1)}, bf16[160,2560]{1,0:T(8,128)(2,1)S(1)}, u32[]{:S(2)}, u32[]{:S(2)}) %collective-permute-start.29) | collective-permute-done | bytes 819232 | tf_op jit(solution)/shard_map/ppermute | solution.py:382
  (89 shorter events, 20.0 us)
Async XLA Ops:
  1.2 24.1 %copy-start.7 = (f32[160,6]{0,1:T(8,128)S(1)}, f32[160,6]{0,1:T(8,128)}, u32[]{:S(2)}) copy-start(f32[160,6]{0,1:T(8,128)} %param.13) | copy-start | bytes 11524
  1.2 3.2 %collective-permute-start = (bf16[160,2560]{1,0:T(8,128)(2,1)S(1)}, bf16[160,2560]{1,0:T(8,128)(2,1)S(1)}, u32[]{:S(2)}, u32[]{:S(2)}) collective-permute-start(bf16[160,2560]{1,0:T(8,128)(2,1)S(1)} %pad_maximum_fusion.refs_0_), channel_id=1, source_target_pairs={{0,1},{1,0},{2,3},{3,2},{4,5},{5,4},{6,7},{7,6},{8,9},{9,8},{10,11... | collective-permute-start | bytes 2457608 | tf_op jit(solution)/shard_map/ppermute | solution.py:385
  1.7 21.4 %collective-permute-start.1 = (bf16[160,2560]{1,0:T(8,128)(2,1)S(1)}, bf16[160,2560]{1,0:T(8,128)(2,1)S(1)}, u32[]{:S(2)}, u32[]{:S(2)}) collective-permute-start(bf16[160,2560]{1,0:T(8,128)(2,1)S(1)} %pad_maximum_fusion.refs_0_), channel_id=1, source_target_pairs={{0,4},{1,5},{2,0},{3,1},{4,8},{5,9},{6,2},{7,3},{8,12},{9,13},{10,... | collective-permute-start | bytes 2457608 | tf_op jit(solution)/shard_map/ppermute | solution.py:379
  4.4 20.3 %collective-permute-start.2 = (bf16[160,2560]{1,0:T(8,128)(2,1)S(1)}, bf16[160,2560]{1,0:T(8,128)(2,1)S(1)}, u32[]{:S(2)}, u32[]{:S(2)}) collective-permute-start(bf16[160,2560]{1,0:T(8,128)(2,1)S(1)} %pad_maximum_fusion.refs_0_), channel_id=1, source_target_pairs={{0,2},{1,3},{2,6},{3,7},{4,0},{5,1},{6,10},{7,11},{8,4},{9,5},{10,... | collective-permute-start | bytes 2457608 | tf_op jit(solution)/shard_map/ppermute | solution.py:382
  24.7 14.7 %collective-permute-start.3 = (bf16[160,2560]{1,0:T(8,128)(2,1)S(1)}, bf16[160,2560]{1,0:T(8,128)(2,1)S(1)}, u32[]{:S(2)}, u32[]{:S(2)}) collective-permute-start(bf16[160,2560]{1,0:T(8,128)(2,1)S(1)} %collective-permute-done.2.refs_0_), channel_id=1, source_target_pairs={{0,1},{1,0},{2,3},{3,2},{4,5},{5,4},{6,7},{7,6},{8,9},{9,8},{10,11... | collective-permute-start | bytes 2457608 | tf_op jit(solution)/shard_map/ppermute | solution.py:385
  24.7 14.7 %collective-permute-start.4 = (bf16[160,2560]{1,0:T(8,128)(2,1)S(1)}, bf16[160,2560]{1,0:T(8,128)(2,1)S(1)}, u32[]{:S(2)}, u32[]{:S(2)}) collective-permute-start(bf16[160,2560]{1,0:T(8,128)(2,1)S(1)} %collective-permute-done.1.refs_1_), channel_id=1, source_target_pairs={{0,1},{1,0},{2,3},{3,2},{4,5},{5,4},{6,7},{7,6},{8,9},{9,8},{10,11... | collective-permute-start | bytes 2457608 | tf_op jit(solution)/shard_map/ppermute | solution.py:385
  25.9 11.4 %all-to-all-start = ((f32[16,1,176]{2,1,0:T(1,128)}), f32[16,1,176]{2,1,0:T(1,128)S(1)}, u32[]{:S(2)}, u32[]{:S(2)}) async-start(f32[16,1,176]{2,1,0:T(1,128)} %copy.30), calls=%async_computation | async-start | bytes 32768 | tf_op jit(solution)/shard_map/all_to_all | solution.py:395
  37.3 21.0 %collective-permute-start.5 = (bf16[160,2560]{1,0:T(8,128)(2,1)S(1)}, bf16[160,2560]{1,0:T(8,128)(2,1)}, u32[]{:S(2)}, u32[]{:S(2)}) collective-permute-start(bf16[160,2560]{1,0:T(8,128)(2,1)S(1)} %collective-permute-done.1.refs_1_), channel_id=1, source_target_pairs={{0,4},{1,5},{2,0},{3,1},{4,8},{5,9},{6,2},{7,3},{8,12},{9,13},{10,... | collective-permute-start | bytes 2457608 | tf_op jit(solution)/shard_map/ppermute | solution.py:379
  37.8 20.6 %collective-permute-start.6 = (bf16[160,2560]{1,0:T(8,128)(2,1)S(1)}, bf16[160,2560]{1,0:T(8,128)(2,1)}, u32[]{:S(2)}, u32[]{:S(2)}) collective-permute-start(bf16[160,2560]{1,0:T(8,128)(2,1)S(1)} %collective-permute-done.2.refs_0_), channel_id=1, source_target_pairs={{0,2},{1,3},{2,6},{3,7},{4,0},{5,1},{6,10},{7,11},{8,4},{9,5},{10,... | collective-permute-start | bytes 2457608 | tf_op jit(solution)/shard_map/ppermute | solution.py:382
  58.4 5.1 %collective-permute-start.7 = (bf16[160,2560]{1,0:T(8,128)(2,1)}, bf16[160,2560]{1,0:T(8,128)(2,1)S(1)}, u32[]{:S(2)}, u32[]{:S(2)}) collective-permute-start(bf16[160,2560]{1,0:T(8,128)(2,1)} %collective-permute-done.6.refs_0_), channel_id=1, source_target_pairs={{0,1},{1,0},{2,3},{3,2},{4,5},{5,4},{6,7},{7,6},{8,9},{9,8},{10,11... | collective-permute-start | bytes 2457608 | tf_op jit(solution)/shard_map/ppermute | solution.py:385
  58.4 5.1 %collective-permute-start.8 = (bf16[160,2560]{1,0:T(8,128)(2,1)}, bf16[160,2560]{1,0:T(8,128)(2,1)}, u32[]{:S(2)}, u32[]{:S(2)}) collective-permute-start(bf16[160,2560]{1,0:T(8,128)(2,1)} %collective-permute-done.5.refs_1_), channel_id=1, source_target_pairs={{0,1},{1,0},{2,3},{3,2},{4,5},{5,4},{6,7},{7,6},{8,9},{9,8},{10,11... | collective-permute-start | bytes 2457608 | tf_op jit(solution)/shard_map/ppermute | solution.py:385
  59.7 23.2 %collective-permute-start.9 = (bf16[160,2560]{1,0:T(8,128)(2,1)}, bf16[160,2560]{1,0:T(8,128)(2,1)S(1)}, u32[]{:S(2)}, u32[]{:S(2)}) collective-permute-start(bf16[160,2560]{1,0:T(8,128)(2,1)} %collective-permute-done.5.refs_1_), channel_id=1, source_target_pairs={{0,4},{1,5},{2,0},{3,1},{4,8},{5,9},{6,2},{7,3},{8,12},{9,13},{10,... | collective-permute-start | bytes 2457608 | tf_op jit(solution)/shard_map/ppermute | solution.py:379
  60.2 22.7 %collective-permute-start.10 = (bf16[160,2560]{1,0:T(8,128)(2,1)}, bf16[160,2560]{1,0:T(8,128)(2,1)S(1)}, u32[]{:S(2)}, u32[]{:S(2)}) collective-permute-start(bf16[160,2560]{1,0:T(8,128)(2,1)} %collective-permute-done.6.refs_0_), channel_id=1, source_target_pairs={{0,2},{1,3},{2,6},{3,7},{4,0},{5,1},{6,10},{7,11},{8,4},{9,5},{10,... | collective-permute-start | bytes 2457608 | tf_op jit(solution)/shard_map/ppermute | solution.py:382
  82.9 2.7 %collective-permute-start.11 = (bf16[160,2560]{1,0:T(8,128)(2,1)S(1)}, bf16[160,2560]{1,0:T(8,128)(2,1)S(1)}, u32[]{:S(2)}, u32[]{:S(2)}) collective-permute-start(bf16[160,2560]{1,0:T(8,128)(2,1)S(1)} %collective-permute-done.10.refs_0_), channel_id=1, source_target_pairs={{0,1},{1,0},{2,3},{3,2},{4,5},{5,4},{6,7},{7,6},{8,9},{9,8},{10,11... | collective-permute-start | bytes 2457608 | tf_op jit(solution)/shard_map/ppermute | solution.py:385
  83.0 3.5 %collective-permute-start.12 = (bf16[160,2560]{1,0:T(8,128)(2,1)S(1)}, bf16[160,2560]{1,0:T(8,128)(2,1)S(1)}, u32[]{:S(2)}, u32[]{:S(2)}) collective-permute-start(bf16[160,2560]{1,0:T(8,128)(2,1)S(1)} %collective-permute-done.9.refs_1_), channel_id=1, source_target_pairs={{0,1},{1,0},{2,3},{3,2},{4,5},{5,4},{6,7},{7,6},{8,9},{9,8},{10,11... | collective-permute-start | bytes 2457608 | tf_op jit(solution)/shard_map/ppermute | solution.py:385
  83.6 18.9 %collective-permute-start.13 = (bf16[80,2560]{1,0:T(8,128)(2,1)S(1)}, bf16[80,2560]{1,0:T(8,128)(2,1)S(1)}, u32[]{:S(2)}, u32[]{:S(2)}) collective-permute-start(bf16[80,2560]{1,0:T(8,128)(2,1)S(1)} %slice.62), channel_id=1, source_target_pairs={{0,4},{1,5},{2,0},{3,1},{4,8},{5,9},{6,2},{7,3},{8,12},{9,13},{10,... | collective-permute-start | bytes 1228808 | tf_op jit(solution)/shard_map/ppermute | solution.py:379
  84.1 18.4 %collective-permute-start.14 = (bf16[80,2560]{1,0:T(8,128)(2,1)S(1)}, bf16[80,2560]{1,0:T(8,128)(2,1)S(1)}, u32[]{:S(2)}, u32[]{:S(2)}) collective-permute-start(bf16[80,2560]{1,0:T(8,128)(2,1)S(1)} %slice.63), channel_id=1, source_target_pairs={{0,2},{1,3},{2,6},{3,7},{4,0},{5,1},{6,10},{7,11},{8,4},{9,5},{10,... | collective-permute-start | bytes 1228808 | tf_op jit(solution)/shard_map/ppermute | solution.py:382
  102.4 1.7 collective-permute-start.15
  102.6 2.2 %collective-permute-start.16 = (bf16[80,2560]{1,0:T(8,128)(2,1)S(1)}, bf16[80,2560]{1,0:T(8,128)(2,1)S(1)}, u32[]{:S(2)}, u32[]{:S(2)}) collective-permute-start(bf16[80,2560]{1,0:T(8,128)(2,1)S(1)} %collective-permute-done.14.refs_1_), channel_id=1, source_target_pairs={{0,1},{1,0},{2,3},{3,2},{4,5},{5,4},{6,7},{7,6},{8,9},{9,8},{10,11... | collective-permute-start | bytes 1228808 | tf_op jit(solution)/shard_map/ppermute | solution.py:385
  126.7 12.6 %collective-permute-start.18 = (bf16[160,2560]{1,0:T(8,128)(2,1)S(1)}, bf16[160,2560]{1,0:T(8,128)(2,1)S(1)}, u32[]{:S(2)}, u32[]{:S(2)}) collective-permute-start(bf16[160,2560]{1,0:T(8,128)(2,1)S(1)} %get-tuple-element.56), channel_id=1, source_target_pairs={{0,1},{1,0},{2,3},{3,2},{4,5},{5,4},{6,7},{7,6},{8,9},{9,8},{10,11... | collective-permute-start | bytes 2457608 | tf_op jit(solution)/shard_map/ppermute | solution.py:385
  138.9 14.7 %collective-permute-start.20 = (bf16[320,2560]{1,0:T(8,128)(2,1)S(1)}, bf16[320,2560]{1,0:T(8,128)(2,1)S(1)}, u32[]{:S(2)}, u32[]{:S(2)}) collective-permute-start(bf16[320,2560]{1,0:T(8,128)(2,1)S(1)} %get-tuple-element.58), channel_id=1, source_target_pairs={{0,1},{1,0},{2,3},{3,2},{4,5},{5,4},{6,7},{7,6},{8,9},{9,8},{10,11... | collective-permute-start | bytes 4915208 | tf_op jit(solution)/shard_map/ppermute | solution.py:385
  139.5 14.1 %collective-permute-start.19 = (bf16[80,2560]{1,0:T(8,128)(2,1)S(1)}, bf16[80,2560]{1,0:T(8,128)(2,1)S(1)}, u32[]{:S(2)}, u32[]{:S(2)}) collective-permute-start(bf16[80,2560]{1,0:T(8,128)(2,1)S(1)} %get-tuple-element.69), channel_id=1, source_target_pairs={{0,4},{1,5},{2,0},{3,1},{4,8},{5,9},{6,2},{7,3},{8,12},{9,13},{10,... | collective-permute-start | bytes 1228808 | tf_op jit(solution)/shard_map/ppermute | solution.py:379
  140.0 13.6 %collective-permute-start.26 = (bf16[80,2560]{1,0:T(8,128)(2,1)S(1)}, bf16[80,2560]{1,0:T(8,128)(2,1)S(1)}, u32[]{:S(2)}, u32[]{:S(2)}) collective-permute-start(bf16[80,2560]{1,0:T(8,128)(2,1)S(1)} %get-tuple-element.70), channel_id=1, source_target_pairs={{0,2},{1,3},{2,6},{3,7},{4,0},{5,1},{6,10},{7,11},{8,4},{9,5},{10,... | collective-permute-start | bytes 1228808 | tf_op jit(solution)/shard_map/ppermute | solution.py:382
  153.5 14.7 %collective-permute-start.22 = (bf16[320,2560]{1,0:T(8,128)(2,1)S(1)}, bf16[320,2560]{1,0:T(8,128)(2,1)S(1)}, u32[]{:S(2)}, u32[]{:S(2)}) collective-permute-start(bf16[320,2560]{1,0:T(8,128)(2,1)S(1)} %get-tuple-element.60), channel_id=1, source_target_pairs={{0,1},{1,0},{2,3},{3,2},{4,5},{5,4},{6,7},{7,6},{8,9},{9,8},{10,11... | collective-permute-start | bytes 4915208 | tf_op jit(solution)/shard_map/ppermute | solution.py:385
  154.1 20.7 %collective-permute-start.21 = (bf16[160,2560]{1,0:T(8,128)(2,1)S(1)}, bf16[160,2560]{1,0:T(8,128)(2,1)S(1)}, u32[]{:S(2)}, u32[]{:S(2)}) collective-permute-start(bf16[160,2560]{1,0:T(8,128)(2,1)S(1)} %get-tuple-element.67), channel_id=1, source_target_pairs={{0,4},{1,5},{2,0},{3,1},{4,8},{5,9},{6,2},{7,3},{8,12},{9,13},{10,... | collective-permute-start | bytes 2457608 | tf_op jit(solution)/shard_map/ppermute | solution.py:379
  154.6 20.5 %collective-permute-start.27 = (bf16[160,2560]{1,0:T(8,128)(2,1)S(1)}, bf16[160,2560]{1,0:T(8,128)(2,1)S(1)}, u32[]{:S(2)}, u32[]{:S(2)}) collective-permute-start(bf16[160,2560]{1,0:T(8,128)(2,1)S(1)} %get-tuple-element.68), channel_id=1, source_target_pairs={{0,2},{1,3},{2,6},{3,7},{4,0},{5,1},{6,10},{7,11},{8,4},{9,5},{10,... | collective-permute-start | bytes 2457608 | tf_op jit(solution)/shard_map/ppermute | solution.py:382
  168.2 16.7 %collective-permute-start.24 = (bf16[320,2560]{1,0:T(8,128)(2,1)S(1)}, bf16[320,2560]{1,0:T(8,128)(2,1)S(1)}, u32[]{:S(2)}, u32[]{:S(2)}) collective-permute-start(bf16[320,2560]{1,0:T(8,128)(2,1)S(1)} %get-tuple-element.62), channel_id=1, source_target_pairs={{0,1},{1,0},{2,3},{3,2},{4,5},{5,4},{6,7},{7,6},{8,9},{9,8},{10,11... | collective-permute-start | bytes 4915208 | tf_op jit(solution)/shard_map/ppermute | solution.py:385
  175.7 19.7 %collective-permute-start.23 = (bf16[160,2560]{1,0:T(8,128)(2,1)S(1)}, bf16[160,2560]{1,0:T(8,128)(2,1)S(1)}, u32[]{:S(2)}, u32[]{:S(2)}) collective-permute-start(bf16[160,2560]{1,0:T(8,128)(2,1)S(1)} %get-tuple-element.65), channel_id=1, source_target_pairs={{0,4},{1,5},{2,0},{3,1},{4,8},{5,9},{6,2},{7,3},{8,12},{9,13},{10,... | collective-permute-start | bytes 2457608 | tf_op jit(solution)/shard_map/ppermute | solution.py:379
  176.2 19.3 %collective-permute-start.28 = (bf16[160,2560]{1,0:T(8,128)(2,1)S(1)}, bf16[160,2560]{1,0:T(8,128)(2,1)S(1)}, u32[]{:S(2)}, u32[]{:S(2)}) collective-permute-start(bf16[160,2560]{1,0:T(8,128)(2,1)S(1)} %get-tuple-element.66), channel_id=1, source_target_pairs={{0,2},{1,3},{2,6},{3,7},{4,0},{5,1},{6,10},{7,11},{8,4},{9,5},{10,... | collective-permute-start | bytes 2457608 | tf_op jit(solution)/shard_map/ppermute | solution.py:382
  184.8 13.3 %collective-permute-start.17 = (bf16[160,2560]{1,0:T(8,128)(2,1)S(1)}, bf16[160,2560]{1,0:T(8,128)(2,1)S(1)}, u32[]{:S(2)}, u32[]{:S(2)}) collective-permute-start(bf16[160,2560]{1,0:T(8,128)(2,1)S(1)} %get-tuple-element.54), channel_id=1, source_target_pairs={{0,1},{1,0},{2,3},{3,2},{4,5},{5,4},{6,7},{7,6},{8,9},{9,8},{10,11... | collective-permute-start | bytes 2457608 | tf_op jit(solution)/shard_map/ppermute | solution.py:385
  196.0 18.7 %collective-permute-start.29 = (bf16[160,2560]{1,0:T(8,128)(2,1)S(1)}, bf16[160,2560]{1,0:T(8,128)(2,1)S(1)}, u32[]{:S(2)}, u32[]{:S(2)}) collective-permute-start(bf16[160,2560]{1,0:T(8,128)(2,1)S(1)} %get-tuple-element.64), channel_id=1, source_target_pairs={{0,2},{1,3},{2,6},{3,7},{4,0},{5,1},{6,10},{7,11},{8,4},{9,5},{10,... | collective-permute-start | bytes 2457608 | tf_op jit(solution)/shard_map/ppermute | solution.py:382
  197.8 18.2 %collective-permute-start.25 = (bf16[160,2560]{1,0:T(8,128)(2,1)S(1)}, bf16[160,2560]{1,0:T(8,128)(2,1)S(1)}, u32[]{:S(2)}, u32[]{:S(2)}) collective-permute-start(bf16[160,2560]{1,0:T(8,128)(2,1)S(1)} %get-tuple-element.63), channel_id=1, source_target_pairs={{0,4},{1,5},{2,0},{3,1},{4,8},{5,9},{6,2},{7,3},{8,12},{9,13},{10,... | collective-permute-start | bytes 2457608 | tf_op jit(solution)/shard_map/ppermute | solution.py:379
  (9 other events, 68.9 us)

commit v4 on v2

--- a/solution.py
+++ b/solution.py
@@ -162,48 +162,96 @@
         return [(d, d ^ 1) for d in range(self.devices)]
 
 
-def hidden_kernel(count, rows, *refs):
-    x_refs = refs[:count]
-    w_ref = refs[count]
-    out_ref, x_all = refs[-2:]
-
-    @pl.when(pl.program_id(0) == 0)
-    def _():
-        for i in range(count):
-            x_all[i * rows : (i + 1) * rows, :] = x_refs[i][...]
-
-    width = w_ref.shape[2]
-    weight = w_ref[0].reshape(2 * width, w_ref.shape[3])
-    both = lax.dot_general(
-        x_all[...], weight, (((1,), (1,)), ((), ())), preferred_element_type=jnp.float32
-    )
-    gate, up = both[:, :width], both[:, width:]
-    out_ref[...] = (gate / (1.0 + jnp.exp(-gate)) * up).astype(out_ref.dtype)
-
-
-def hidden_call(blocks, gate_up_weight, hidden, first_slot, slot_count):
+def hidden_kernel(count, rows, first_row, chunk, fetch, *refs):
+    x_refs, refs = refs[:count], refs[count:]
+    if fetch == "gate_up":
+        far_ref, out_ref, w_ref, x_all, sems = refs
+    elif fetch == "down":
+        w_ref, _, far_ref, out_ref, _, down_ref, x_all, sems = refs
+    else:
+        w_ref, _, out_ref, x_all = refs[0], refs[1], refs[2], refs[-1]
+    ff, wide = w_ref.shape[2:]
+    whole, rest = divmod(ff, chunk)
+    total = count * rows
+
+    def fetched(i, width):
+        part = pl.ds(pl.multiple_of(i * chunk, chunk), width)
+        return pltpu.make_async_copy(far_ref.at[0, :, part], w_ref.at[0, :, part], sems.at[i])
+
+    if fetch == "gate_up":
+        for i in range(whole):
+            fetched(i, chunk).start()
+        if rest:
+            fetched(whole, rest).start()
+    if fetch == "down":
+        pltpu.make_async_copy(far_ref, down_ref, sems.at[0]).start()
+    for i in range(count):
+        x_all[i * rows : (i + 1) * rows, :] = x_refs[i][...]
+
+    def step(i, width):
+        if fetch == "gate_up":
+            fetched(i, width).wait()
+        part = pl.ds(pl.multiple_of(i * chunk, chunk), width)
+        weight = w_ref[0, :, part, :].reshape(2 * width, wide)
+        both = lax.dot_general(
+            x_all[...], weight, (((1,), (1,)), ((), ())), preferred_element_type=jnp.float32
+        )
+        gate, up = both[:, :width], both[:, width:]
+        hidden = (gate / (1.0 + jnp.exp(-gate)) * up).astype(out_ref.dtype)
+        out_ref[first_row : first_row + total, part] = hidden
+
+    @pl.loop(0, whole)
+    def _(i):
+        step(i, chunk)
+
+    if rest:
+        step(whole, rest)
+    if fetch == "down":
+        pltpu.make_async_copy(far_ref, down_ref, sems.at[0]).wait()
+
+
+def kept(array):
+    return pltpu.with_memory_space_constraint(array, pltpu.VMEM)
+
+
+def distant(array):
+    return pltpu.with_memory_space_constraint(array, pltpu.HBM)
+
+
+def hidden_call(blocks, gate_up_weight, hidden, first_row, all_rows, down_weight=None, last=False):
     rows, wide = blocks[0].shape
-    _, _, ff, _ = gate_up_weight.shape
+    ff = gate_up_weight.shape[2]
     count = len(blocks)
     chunk = 256
-    place = first_slot // count
-    whole = pl.BlockSpec((rows, wide), lambda i: (0, 0))
-    in_specs = [whole] * count + [pl.BlockSpec((1, 2, chunk, wide), lambda i: (0, 0, i, 0))]
-    args = list(blocks) + [gate_up_weight]
-    aliases = {}
-    if hidden is not None:
-        in_specs.append(pl.BlockSpec(memory_space=pl.ANY))
-        args.append(hidden)
-        aliases = {len(args) - 1: 0}
+    here, far = pl.BlockSpec(memory_space=pltpu.VMEM), pl.BlockSpec(memory_space=pltpu.HBM)
+    args, in_specs = [kept(block) for block in blocks], [here] * count
+    out_shape, aliases = [pltpu.VMEM((all_rows, ff), jnp.bfloat16)], {}
+    scratch = [pltpu.VMEM((count * rows, wide), jnp.bfloat16)]
+    fetch = None
+    if hidden is None:
+        fetch = "gate_up"
+        args, in_specs = args + [distant(gate_up_weight)], in_specs + [far]
+        out_shape.append(pltpu.VMEM(gate_up_weight.shape, gate_up_weight.dtype))
+        scratch.append(pltpu.SemaphoreType.DMA((pl.cdiv(ff, chunk),)))
+    else:
+        args, in_specs = args + [kept(gate_up_weight), kept(hidden)], in_specs + [here, here]
+        aliases = {count + 1: 0}
+        if not last:
+            out_shape.append(pltpu.VMEM(gate_up_weight.shape, gate_up_weight.dtype))
+            aliases[count] = 1
+        if down_weight is not None:
+            fetch = "down"
+            args, in_specs = args + [distant(down_weight)], in_specs + [far]
+            out_shape.append(pltpu.VMEM(down_weight.shape, down_weight.dtype))
+            scratch.append(pltpu.SemaphoreType.DMA((1,)))
     return pl.pallas_call(
-        functools.partial(hidden_kernel, count, rows),
-        grid=(pl.cdiv(ff, chunk),),
+        functools.partial(hidden_kernel, count, rows, first_row, chunk, fetch),
         in_specs=in_specs,
-        out_specs=pl.BlockSpec((count * rows, chunk), lambda i: (place, i)),
-        out_shape=jax.ShapeDtypeStruct((slot_count * rows, ff), jnp.bfloat16),
-        scratch_shapes=[pltpu.VMEM((count * rows, wide), jnp.bfloat16)],
+        out_specs=[here] * len(out_shape),
+        out_shape=out_shape,
+        scratch_shapes=scratch,
         input_output_aliases=aliases,
-        compiler_params=pltpu.CompilerParams(vmem_limit_bytes=32 * 1024 * 1024),
+        compiler_params=pltpu.CompilerParams(vmem_limit_bytes=14 * 1024 * 1024),
         cost_estimate=pl.CostEstimate(
             flops=4 * count * rows * wide * ff,
             bytes_accessed=4 * ff * wide + 2 * count * rows * (wide + ff),
@@ -213,64 +261,76 @@
 
 
 def down_kernel(
-    slots, first_slot, rows, text_rows, sources_ref, hidden_ref, order_ref, scale_ref, w_ref,
-    own_ref, other_ref, picked,
+    slots, first_slot, rows, text_rows, seq_count, expert_count, chunk, places_ref, hidden_ref,
+    tables_ref, w_ref, own_ref, other_ref, column, picked, scale,
 ):
     image_rows = rows - text_rows
-    seq_count = order_ref.shape[2] // image_rows
-
-    @pl.when(pl.program_id(0) == 0)
-    def _():
-        for j in range(slots):
-            at = (first_slot + j) * rows
-            picked[j * rows : j * rows + text_rows, :] = hidden_ref[at : at + text_rows, :]
-            wanted = lax.broadcasted_iota(jnp.int32, (image_rows, order_ref.shape[2]), 0)
-            match = jnp.where(order_ref[j] == wanted, 1.0, 0.0).astype(jnp.bfloat16)
-            total = jnp.zeros((image_rows, hidden_ref.shape[1]), jnp.float32)
-            for z in range(seq_count):
-                source = sources_ref[(first_slot + j) * seq_count + z]
-                start = pl.multiple_of(source * rows + text_rows, 16)
-                total += jnp.dot(
-                    match[:, z * image_rows : (z + 1) * image_rows],
-                    hidden_ref[pl.ds(start, image_rows), :],
-                    preferred_element_type=jnp.float32,
-                )
-            picked[j * rows + text_rows : (j + 1) * rows, :] = total.astype(jnp.bfloat16)
-
-    result = jnp.dot(picked[...], w_ref[0], preferred_element_type=jnp.float32)
-    scaled = (result.astype(jnp.bfloat16).astype(jnp.float32) * scale_ref[...]).astype(jnp.bfloat16)
     half = slots * rows // 2
-    own_ref[...] = scaled[:half]
-    other_ref[...] = scaled[half:]
-
-
-def down_call(hidden, order, scale, sources, down_weight, first_slot, slots, rows, text_rows):
+    slot_total = hidden_ref.shape[0] // rows
+    targets_at = tables_ref.shape[2] - image_rows
+    wanted = lax.broadcasted_iota(jnp.int32, (image_rows, image_rows), 0).astype(jnp.float32)
+    diagonal = lax.broadcasted_iota(jnp.int32, (rows, rows), 0) == lax.broadcasted_iota(
+        jnp.int32, (rows, rows), 1
+    )
+    for j in range(slots):
+        at = (first_slot + j) * rows
+        picked[j * rows : j * rows + text_rows, :] = hidden_ref[at : at + text_rows, :]
+        owner = places_ref[first_slot + j]
+        first_wanted = wanted + (owner // expert_count * image_rows).astype(jnp.float32)
+        matches = []
+        for z in range(seq_count):
+            source = places_ref[slot_total + (first_slot + j) * seq_count + z]
+            start = pl.multiple_of(source * rows + text_rows, 16)
+            column[z * image_rows : (z + 1) * image_rows, :] = hidden_ref[
+                pl.ds(start, image_rows), :
+            ]
+            targets = tables_ref[places_ref[source], :, targets_at:]
+            matches.append(jnp.where(targets == first_wanted, 1.0, 0.0).astype(jnp.bfloat16))
+        match = jnp.concatenate(matches, axis=1)
+        rows_here = jnp.dot(match, column[...], preferred_element_type=jnp.float32)
+        picked[j * rows + text_rows : (j + 1) * rows, :] = rows_here.astype(jnp.bfloat16)
+        weights = jnp.where(diagonal, tables_ref[owner, :, :rows], 0.0)
+        scale[j * rows : (j + 1) * rows, :] = jnp.sum(weights, axis=1, keepdims=True)
+
+    @pl.loop(0, w_ref.shape[2] // chunk)
+    def _(i):
+        part = pl.ds(pl.multiple_of(i * chunk, chunk), chunk)
+        result = jnp.dot(picked[...], w_ref[0, :, part], preferred_element_type=jnp.float32)
+        scaled = result.astype(jnp.bfloat16).astype(jnp.float32) * scale[...]
+        scaled = scaled.astype(jnp.bfloat16)
+        own_ref[:, part] = scaled[:half]
+        other_ref[:, part] = scaled[half:]
+
+
+def down_call(
+    hidden, tables, places, down_weight, first_slot, slots, rows, text_rows, seq_count, expert_count
+):
     _, ff, wide = down_weight.shape
-    chunk = 512
     half = slots * rows // 2
-    grid_spec = pltpu.PrefetchScalarGridSpec(
-        num_scalar_prefetch=1,
-        grid=(wide // chunk,),
-        in_specs=[
-            pl.BlockSpec(hidden.shape, lambda i, s: (0, 0), pipeline_mode=pl.Buffered(1)),
-            pl.BlockSpec((slots, 1, order.shape[2]), lambda i, s: (first_slot // slots, 0, 0)),
-            pl.BlockSpec((slots * rows, 1), lambda i, s: (first_slot // slots, 0)),
-            pl.BlockSpec((1, ff, chunk), lambda i, s: (0, 0, i)),
-        ],
-        out_specs=[pl.BlockSpec((half, chunk), lambda i, s: (0, i))] * 2,
-        scratch_shapes=[pltpu.VMEM((slots * rows, ff), jnp.bfloat16)],
-    )
+    here = pl.BlockSpec(memory_space=pltpu.VMEM)
     return pl.pallas_call(
-        functools.partial(down_kernel, slots, first_slot, rows, text_rows),
-        grid_spec=grid_spec,
-        out_shape=[jax.ShapeDtypeStruct((half, wide), jnp.bfloat16)] * 2,
-        compiler_params=pltpu.CompilerParams(vmem_limit_bytes=40 * 1024 * 1024),
+        functools.partial(
+            down_kernel, slots, first_slot, rows, text_rows, seq_count, expert_count, 512
+        ),
+        grid_spec=pltpu.PrefetchScalarGridSpec(
+            num_scalar_prefetch=1,
+            grid=(1,),
+            in_specs=[here] * 3,
+            out_specs=[here] * 2,
+            scratch_shapes=[
+                pltpu.VMEM((seq_count * (rows - text_rows), ff), jnp.bfloat16),
+                pltpu.VMEM((slots * rows, ff), jnp.bfloat16),
+                pltpu.VMEM((slots * rows, 1), jnp.float32),
+            ],
+        ),
+        out_shape=[pltpu.VMEM((half, wide), jnp.bfloat16)] * 2,
+        compiler_params=pltpu.CompilerParams(vmem_limit_bytes=14 * 1024 * 1024),
         cost_estimate=pl.CostEstimate(
             flops=2 * slots * rows * wide * ff,
-            bytes_accessed=2 * ff * wide + 2 * hidden.size + 2 * slots * rows * wide,
+            bytes_accessed=2 * ff * wide + 2 * slots * rows * wide,
             transcendentals=0,
         ),
-    )(sources, hidden, order, scale, down_weight)
+    )(places, kept(hidden), tables, kept(down_weight))
 
 
 def add_up(*parts):
@@ -307,43 +367,44 @@
 
     experts = jnp.arange(ring.devices, dtype=jnp.int32)[:, None, None]
     routed = jnp.where(expert_ids[None] == experts, gate_weights[None], 0.0).sum(axis=-1)
-    targets = jnp.broadcast_to(panel_target.astype(jnp.float32), (ring.devices, pan_count))
-    tables = lax.all_to_all(
-        jnp.concatenate([routed, targets], axis=1), AXES, split_axis=0, concat_axis=0, tiled=True
-    )
-    weights = tables[:, :tok_count]
-    target = tables[:, tok_count:].astype(jnp.int32)
-    target_seq = target // pan_count // expert_count
-    first_row = target_seq * image_rows + target % pan_count * panel_rows
-    target_row = first_row[:, :, None] + jnp.arange(panel_rows, dtype=jnp.int32)
-    by_column = target_row.reshape(seq_count, expert_count, image_rows).transpose(1, 0, 2)
-    by_column = by_column.reshape(expert_count, seq_count * image_rows)
-    owners = jnp.asarray(ring.owner_of)[me]
-    sources = jnp.asarray(ring.sources_of.reshape(ring.devices, -1))[me]
-    order = by_column[owners % expert_count] - (owners // expert_count * image_rows)[:, None]
-    order = order[:, None, :]
-    scale = weights[owners].reshape(slot_count * tok_count, 1)
-
-    hidden = hidden_call([own, other], gate_up_weight, None, 0, slot_count)
+    target_seq = panel_target // pan_count // expert_count
+    targets = target_seq * image_rows + panel_target % pan_count * panel_rows
+    targets = (targets[:, None] + jnp.arange(panel_rows, dtype=jnp.int32)).reshape(image_rows)
+    targets = jnp.broadcast_to(targets.astype(jnp.float32), (ring.devices, image_rows))
+    routed = jnp.pad(routed, ((0, 0), (0, -tok_count % 128)))
+    outgoing = jnp.concatenate([routed, targets], axis=1)[:, None, :]
+    tables = lax.all_to_all(outgoing, AXES, split_axis=0, concat_axis=0, tiled=True)
+    places = np.concatenate([ring.owner_of, ring.sources_of.reshape(ring.devices, -1)], axis=1)
+    places = jnp.asarray(places)[me]
+
+    all_rows = slot_count * tok_count
+    hidden, gate_up = hidden_call([own, other], gate_up_weight, None, 0, all_rows)
+    hidden, before, after, tables = lax.optimization_barrier((hidden, before, after, tables))
+    cut = tok_count // 2
     for s in range(1, ring.half):
         here = [after, before]
         there = [across(after), across(before)]
-        if s + 1 < ring.half:
-            before, after = onward(before), back(after)
-        else:
-            cut = tok_count // 2
-            far_before, far_after = onward(before[:cut]), back(after[cut:])
-        hidden = hidden_call(here + there, gate_up_weight, hidden, 4 * s, slot_count)
-    far = jnp.concatenate([far_before, far_after], axis=0)
-    hidden = hidden_call([far, across(far)], gate_up_weight, hidden, 2, slot_count)
+        if s + 1 == ring.half:
+            before, after = before[:cut], after[cut:]
+        before, after = onward(before), back(after)
+        first_row = 4 * s * tok_count
+        extra = down_weight if s == 1 else None
+        hidden, gate_up, *down = hidden_call(
+            here + there, gate_up, hidden, first_row, all_rows, extra
+        )
+        if down:
+            (down_here,) = down
+        hidden, before, after = lax.optimization_barrier((hidden, before, after))
+    far = [before, after, across(before), across(after)]
+    (hidden,) = hidden_call(far, gate_up, hidden, 2 * tok_count, all_rows, last=True)
 
     def outputs(first_slot, slots):
         mine, others = down_call(
-            hidden, order, scale, sources, down_weight, first_slot, slots, tok_count, text_rows
+            hidden, tables, places, down_here, first_slot, slots, tok_count, text_rows,
+            seq_count, expert_count,
         )
         return mine, across(others)
 
-    cut = tok_count // 2
     mine, swapped = outputs(2, 2)
     leaving = add_up(mine[:cut], swapped[:cut]), add_up(mine[cut:], swapped[cut:])
     for s in range(ring.half - 1, -1, -1):

time: 209 us -> 208 us (level)
  local copies, waits for them, and re-layouts: 4.11 us -> 42.5 us
  Pallas kernels: 108 us -> 78.7 us
  waiting for transfers between devices: 63.2 us -> 54.4 us
    unnamed x8 -> x36, local copies, waits for them, and re-layouts: 0.04 us -> 41 us
    pallas_call x5, Pallas kernels: 62.4 us -> 46.1 us  [hidden_call(): pl.pallas_call(functools.partial(hidden_kernel, count, rows, first_row, c...]
    all_to_all x1, waiting for transfers between devices: 14.2 us -> 0.01 us  [ring_shards(): lax.all_to_all(outgoing, AXES, split_axis=0, concat_axis=0, tiled=True)]
    pallas_call x5, Pallas kernels: 45.5 us -> 32.6 us  [down_call(): pl.pallas_call(functools.partial(down_kernel, slots, first_slot, rows, te...]
    ppermute x8, waiting for transfers between devices: 2.72 us -> 9.12 us  [back(): return lax.ppermute(array, AXES, ring.step(-1))]
    ppermute x8, waiting for transfers between devices: 46.3 us -> 41.4 us  [onward(): return lax.ppermute(array, AXES, ring.step(1))]
    ppermute x13 -> x14, waiting for transfers between devices: 0.03 us -> 3.94 us  [across(): return lax.ppermute(array, AXES, ring.swap())]
  transfers between devices with their start and end apart: 30 -> 31, of which waited for: 10 -> 13; matrix products, arithmetic and copies ran while one was open for 4% -> 2% of each run, Pallas kernels for 44% -> 33%
where the time goes in v4:
time: 208 us; the launch traced here: 207 us
  Pallas kernels  78.7 us (38%)
  waiting for transfers between devices  54.4 us (26%)
  local copies, waits for them, and re-layouts  42.5 us (20%)
  starting transfers between devices  27 us (13%)
  other arithmetic  4.47 us (2%)
    pallas_call x5, Pallas kernels, hidden_call(): pl.pallas_call(functools.partial(hidden_kernel, count, rows, first_row, c...  46.1 us
    ppermute x8, waiting for transfers between devices, onward(): return lax.ppermute(array, AXES, ring.step(1))  41.4 us
    unnamed x36, local copies, waits for them, and re-layouts  41 us
    pallas_call x5, Pallas kernels, down_call(): pl.pallas_call(functools.partial(down_kernel, slots, first_slot, rows, te...  32.6 us
    ppermute x8, waiting for transfers between devices, back(): return lax.ppermute(array, AXES, ring.step(-1))  9.12 us
    ppermute x8, starting transfers between devices, onward(): return lax.ppermute(array, AXES, ring.step(1))  9.11 us
    ppermute x8, starting transfers between devices, back(): return lax.ppermute(array, AXES, ring.step(-1))  7.99 us
    all_to_all x1, starting transfers between devices, ring_shards(): lax.all_to_all(outgoing, AXES, split_axis=0, concat_axis=0, tiled=True)  6.36 us
  transfers between devices with their start and end apart: 31, of which 13 were waited for; matrix products, arithmetic and copies ran while one was open for 2% of the time, Pallas kernels for 33%

profile of v4, /device:TPU:0, one launch (start us, length us, event | category | flops | bytes accessed | tf_op | source)
XLA Modules:
  0.0 207.5 jit_solution(14729131549448948830)
XLA Ops:
  1.7 2.6 %collective-permute-start.1 = (bf16[160,2560]{1,0:T(8,128)(2,1)S(1)}, bf16[160,2560]{1,0:T(8,128)(2,1)S(1)}, u32[]{:S(2)}, u32[]{:S(2)}) collective-permute-start(bf16[160,2560]{1,0:T(8,128)(2,1)S(1)} %pad_maximum_fusion.refs_0_), channel_id=1, source_target_pairs={{0,4},{1,5},{2,0},{3,1},{4,8},{5,9},{6,2},{7,3},{8,12},{9,13},{10,... | collective-permute-start | bytes 2457608 | tf_op jit(solution)/shard_map/ppermute | solution.py:356
  5.3 6.4 %all-to-all-start = ((f32[16,1,384]{2,1,0:T(1,128)}), f32[16,1,384]{2,1,0:T(1,128)S(1)}, u32[]{:S(2)}, u32[]{:S(2)}) async-start(f32[16,1,384]{2,1,0:T(1,128)} %broadcast_in_dim.26), calls=%async_computation | async-start | bytes 49152 | tf_op jit(solution)/shard_map/all_to_all | solution.py:376
  11.6 7.7 %shard_map.82 = (bf16[2560,1408]{1,0:T(8,128)(2,1)S(1)}, bf16[1,2,1408,2560]{3,2,1,0:T(8,128)(2,1)S(1)}) custom-call(bf16[160,2560]{1,0:T(8,128)(2,1)S(1)} %pad_maximum_fusion.refs_0_, bf16[160,2560]{1,0:T(8,128)(2,1)S(1)} %collective-permute-done.refs_1_, bf16[1,2,1408,2560]{3,2,1,0:T(8,128)(2,1)} %refs_2_.1), custom_call_target="tpu_custom_call" | custom-call | flops 4613734400 | bytes 16957440 | tf_op jit(solution)/shard_map/pallas_call | solution.py:247
  19.4 2.9 %copy-done = bf16[2560,1408]{1,0:T(8,128)(2,1)} copy-done((bf16[2560,1408]{1,0:T(8,128)(2,1)}, bf16[2560,1408]{1,0:T(8,128)(2,1)S(1)}, u32[]{:S(2)}) %copy-start) | copy-done | bytes 7208984
  22.3 5.1 %copy-done.9 = bf16[1,2,1408,2560]{3,2,1,0:T(8,128)(2,1)} copy-done((bf16[1,2,1408,2560]{3,2,1,0:T(8,128)(2,1)}, bf16[1,2,1408,2560]{3,2,1,0:T(8,128)(2,1)S(1)}, u32[]{:S(2)}) %copy-start.9) | copy-done | bytes 14417944
  28.0 1.9 collective-permute-start.5
  31.0 3.0 %copy-done.1 = bf16[2560,1408]{1,0:T(8,128)(2,1)S(1)} copy-done((bf16[2560,1408]{1,0:T(8,128)(2,1)S(1)}, bf16[2560,1408]{1,0:T(8,128)(2,1)}, u32[]{:S(2)}) %copy-start.1) | copy-done | bytes 7208984
  34.1 5.1 %copy-done.10 = bf16[1,2,1408,2560]{3,2,1,0:T(8,128)(2,1)S(1)} copy-done((bf16[1,2,1408,2560]{3,2,1,0:T(8,128)(2,1)S(1)}, bf16[1,2,1408,2560]{3,2,1,0:T(8,128)(2,1)}, u32[]{:S(2)}) %copy-start.10) | copy-done | bytes 14417944
  39.2 10.8 %shard_map.83 = (bf16[2560,1408]{1,0:T(8,128)(2,1)S(1)}, bf16[1,2,1408,2560]{3,2,1,0:T(8,128)(2,1)S(1)}, bf16[1,1408,2560]{2,1,0:T(8,128)(2,1)S(1)}) custom-call(bf16[160,2560]{1,0:T(8,128)(2,1)S(1)} %collective-permute-done.2.refs_0_, bf16[160,2560]{1,0:T(8,128)(2,1)S(1)} %collective-permute-done.1.refs_1_, ...), custom_call_target="tpu_custom_call", output_to_operand_aliasing={{0}: (5, {}), {1}: (4, {})} | custom-call | flops 9227468800 | bytes 19496960 | tf_op jit(solution)/shard_map/pallas_call | solution.py:247
  50.6 1.9 collective-permute-start.10
  53.6 10.8 %shard_map.84 = (bf16[2560,1408]{1,0:T(8,128)(2,1)S(1)}, bf16[1,2,1408,2560]{3,2,1,0:T(8,128)(2,1)S(1)}) custom-call(bf16[160,2560]{1,0:T(8,128)(2,1)S(1)} %collective-permute-done.6.refs_0_, bf16[160,2560]{1,0:T(8,128)(2,1)S(1)} %collective-permute-done.5.refs_1_, ...), custom_call_target="tpu_custom_call", output_to_operand_aliasing={{0}: (5, {}), {1}: (4, {})} | custom-call | flops 9227468800 | bytes 19496960 | tf_op jit(solution)/shard_map/pallas_call | solution.py:247
  64.4 6.7 %collective-permute-done.10.refs_0_ = bf16[160,2560]{1,0:T(8,128)(2,1)S(1)} collective-permute-done((bf16[160,2560]{1,0:T(8,128)(2,1)S(1)}, bf16[160,2560]{1,0:T(8,128)(2,1)S(1)}, u32[]{:S(2)}, u32[]{:S(2)}) %collective-permute-start.10) | collective-permute-done | bytes 819232 | tf_op jit(solution)/shard_map/ppermute | solution.py:359
  73.5 1.7 collective-permute-start.14
  76.0 10.8 %shard_map.85 = (bf16[2560,1408]{1,0:T(8,128)(2,1)S(1)}, bf16[1,2,1408,2560]{3,2,1,0:T(8,128)(2,1)S(1)}) custom-call(bf16[160,2560]{1,0:T(8,128)(2,1)S(1)} %collective-permute-done.10.refs_0_, bf16[160,2560]{1,0:T(8,128)(2,1)S(1)} %collective-permute-done.9.refs_1_, ...), custom_call_target="tpu_custom_call", output_to_operand_aliasing={{0}: (5, {}), {1}: (4, {})} | custom-call | flops 9227468800 | bytes 19496960 | tf_op jit(solution)/shard_map/pallas_call | solution.py:247
  86.8 2.9 %copy-done.2 = bf16[2560,1408]{1,0:T(8,128)(2,1)} copy-done((bf16[2560,1408]{1,0:T(8,128)(2,1)}, bf16[2560,1408]{1,0:T(8,128)(2,1)S(1)}, u32[]{:S(2)}) %copy-start.2) | copy-done | bytes 7208984
  89.7 5.1 %copy-done.11 = bf16[1,2,1408,2560]{3,2,1,0:T(8,128)(2,1)} copy-done((bf16[1,2,1408,2560]{3,2,1,0:T(8,128)(2,1)}, bf16[1,2,1408,2560]{3,2,1,0:T(8,128)(2,1)S(1)}, u32[]{:S(2)}) %copy-start.11) | copy-done | bytes 14417944
  97.1 3.0 %copy-done.3 = bf16[2560,1408]{1,0:T(8,128)(2,1)S(1)} copy-done((bf16[2560,1408]{1,0:T(8,128)(2,1)S(1)}, bf16[2560,1408]{1,0:T(8,128)(2,1)}, u32[]{:S(2)}) %copy-start.3) | copy-done | bytes 7208984
  100.2 5.1 %copy-done.12 = bf16[1,2,1408,2560]{3,2,1,0:T(8,128)(2,1)S(1)} copy-done((bf16[1,2,1408,2560]{3,2,1,0:T(8,128)(2,1)S(1)}, bf16[1,2,1408,2560]{3,2,1,0:T(8,128)(2,1)}, u32[]{:S(2)}) %copy-start.12) | copy-done | bytes 14417944
  105.3 6.0 %shard_map.86.hidden_ref = bf16[2560,1408]{1,0:T(8,128)(2,1)S(1)} custom-call(bf16[80,2560]{1,0:T(8,128)(2,1)S(1)} %collective-permute-done.13.refs_0_, bf16[80,2560]{1,0:T(8,128)(2,1)S(1)} %collective-permute-done.14.refs_1_, bf16[80,2560]{1,0:T(8,128)(2,1)S(1)} %collective-permute-done.15.refs_2_, ...), custom_call_target="tpu_custom_call", output_to_operand_aliasing={{}: (5, {})} | custom-call | flops 4613734400 | bytes 16957440 | tf_op jit(solution)/shard_map/pallas_call | solution.py:247
  111.3 5.6 %copy-done.8 = bf16[1,1408,2560]{2,1,0:T(8,128)(2,1)S(1)} copy-done((bf16[1,1408,2560]{2,1,0:T(8,128)(2,1)S(1)}, bf16[1,1408,2560]{2,1,0:T(8,128)(2,1)}, u32[]{:S(2)}) %copy-start.8) | copy-done | bytes 7208984
  117.0 4.6 %shard_map.88 = (bf16[160,2560]{1,0:T(8,128)(2,1)S(1)}, bf16[160,2560]{1,0:T(8,128)(2,1)S(1)}) custom-call(s32[80]{0:T(128)S(1)} %dynamic-slice_bitcast_fusion.places_ref, bf16[2560,1408]{1,0:T(8,128)(2,1)S(1)} %shard_map.86.hidden_ref, f32[16,1,384]{2,1,0:T(1,128)S(1)} %all-to-all-done.tables_ref, bf16[1,1408,2560]{2,1,0:T(8,128)(2,1)S(1)} %copy-done.8), custom_call_target="tpu_custom_call" | custom-call | flops 2306867200 | bytes 8847360 | tf_op jit(solution)/shard_map/pallas_call | solution.py:311
  121.8 7.8 %shard_map.89 = (bf16[320,2560]{1,0:T(8,128)(2,1)S(1)}, bf16[320,2560]{1,0:T(8,128)(2,1)S(1)}) custom-call(s32[80]{0:T(128)S(1)} %dynamic-slice_bitcast_fusion.places_ref, bf16[2560,1408]{1,0:T(8,128)(2,1)S(1)} %shard_map.86.hidden_ref, f32[16,1,384]{2,1,0:T(1,128)S(1)} %all-to-all-done.tables_ref, bf16[1,1408,2560]{2,1,0:T(8,128)(2,1)S(1)} %copy-done.8), custom_call_target="tpu_custom_call" | custom-call | flops 4613734400 | bytes 10485760 | tf_op jit(solution)/shard_map/pallas_call | solution.py:311
  130.6 1.7 collective-permute-start.26
  132.3 3.0 %copy-done.5 = bf16[2560,1408]{1,0:T(8,128)(2,1)S(1)} copy-done((bf16[2560,1408]{1,0:T(8,128)(2,1)S(1)}, bf16[2560,1408]{1,0:T(8,128)(2,1)}, u32[]{:S(2)}) %copy-start.5) | copy-done | bytes 7208984
  135.3 7.8 %shard_map.90 = (bf16[320,2560]{1,0:T(8,128)(2,1)S(1)}, bf16[320,2560]{1,0:T(8,128)(2,1)S(1)}) custom-call(s32[80]{0:T(128)S(1)} %dynamic-slice_bitcast_fusion.places_ref, bf16[2560,1408]{1,0:T(8,128)(2,1)S(1)} %copy-done.5, f32[16,1,384]{2,1,0:T(1,128)S(1)} %all-to-all-done.tables_ref, bf16[1,1408,2560]{2,1,0:T(8,128)(2,1)S(1)} %copy-done.8), custom_call_target="tpu_custom_call" | custom-call | flops 4613734400 | bytes 10485760 | tf_op jit(solution)/shard_map/pallas_call | solution.py:311
  144.1 1.7 collective-permute-start.27
  145.8 7.9 %shard_map.91 = (bf16[320,2560]{1,0:T(8,128)(2,1)S(1)}, bf16[320,2560]{1,0:T(8,128)(2,1)S(1)}) custom-call(s32[80]{0:T(128)S(1)} %dynamic-slice_bitcast_fusion.places_ref, bf16[2560,1408]{1,0:T(8,128)(2,1)S(1)} %copy-done.6, f32[16,1,384]{2,1,0:T(1,128)S(1)} %all-to-all-done.tables_ref, bf16[1,1408,2560]{2,1,0:T(8,128)(2,1)S(1)} %bitcast.4), custom_call_target="tpu_custom_call" | custom-call | flops 4613734400 | bytes 10485760 | tf_op jit(solution)/shard_map/pallas_call | solution.py:311
  153.8 10.6 %collective-permute-done.21 = bf16[160,2560]{1,0:T(8,128)(2,1)S(1)} collective-permute-done((bf16[160,2560]{1,0:T(8,128)(2,1)S(1)}, bf16[160,2560]{1,0:T(8,128)(2,1)S(1)}, u32[]{:S(2)}, u32[]{:S(2)}) %collective-permute-start.21) | collective-permute-done | bytes 819232 | tf_op jit(solution)/shard_map/ppermute | solution.py:356
  165.0 1.7 collective-permute-start.23
  167.1 4.6 %shard_map.87 = (bf16[160,2560]{1,0:T(8,128)(2,1)S(1)}, bf16[160,2560]{1,0:T(8,128)(2,1)S(1)}) custom-call(s32[80]{0:T(128)S(1)} %dynamic-slice_bitcast_fusion.places_ref, bf16[2560,1408]{1,0:T(8,128)(2,1)S(1)} %copy-done.6, f32[16,1,384]{2,1,0:T(1,128)S(1)} %all-to-all-done.tables_ref, bf16[1,1408,2560]{2,1,0:T(8,128)(2,1)S(1)} %bitcast.4), custom_call_target="tpu_custom_call" | custom-call | flops 2306867200 | bytes 8847360 | tf_op jit(solution)/shard_map/pallas_call | solution.py:311
  171.8 13.1 %collective-permute-done.23 = bf16[160,2560]{1,0:T(8,128)(2,1)S(1)} collective-permute-done((bf16[160,2560]{1,0:T(8,128)(2,1)S(1)}, bf16[160,2560]{1,0:T(8,128)(2,1)S(1)}, u32[]{:S(2)}, u32[]{:S(2)}) %collective-permute-start.23) | collective-permute-done | bytes 819232 | tf_op jit(solution)/shard_map/ppermute | solution.py:356
  188.7 16.3 %collective-permute-done.25 = bf16[160,2560]{1,0:T(8,128)(2,1)S(1)} collective-permute-done((bf16[160,2560]{1,0:T(8,128)(2,1)S(1)}, bf16[160,2560]{1,0:T(8,128)(2,1)S(1)}, u32[]{:S(2)}, u32[]{:S(2)}) %collective-permute-start.25) | collective-permute-done | bytes 819232 | tf_op jit(solution)/shard_map/ppermute | solution.py:356
  (93 shorter events, 21.1 us)
Async XLA Ops:
  1.2 10.4 %collective-permute-start = (bf16[160,2560]{1,0:T(8,128)(2,1)S(1)}, bf16[160,2560]{1,0:T(8,128)(2,1)S(1)}, u32[]{:S(2)}, u32[]{:S(2)}) collective-permute-start(bf16[160,2560]{1,0:T(8,128)(2,1)S(1)} %pad_maximum_fusion.refs_0_), channel_id=1, source_target_pairs={{0,1},{1,0},{2,3},{3,2},{4,5},{5,4},{6,7},{7,6},{8,9},{9,8},{10,11... | collective-permute-start | bytes 2457608 | tf_op jit(solution)/shard_map/ppermute | solution.py:362
  1.7 25.7 %collective-permute-start.1 = (bf16[160,2560]{1,0:T(8,128)(2,1)S(1)}, bf16[160,2560]{1,0:T(8,128)(2,1)S(1)}, u32[]{:S(2)}, u32[]{:S(2)}) collective-permute-start(bf16[160,2560]{1,0:T(8,128)(2,1)S(1)} %pad_maximum_fusion.refs_0_), channel_id=1, source_target_pairs={{0,4},{1,5},{2,0},{3,1},{4,8},{5,9},{6,2},{7,3},{8,12},{9,13},{10,... | collective-permute-start | bytes 2457608 | tf_op jit(solution)/shard_map/ppermute | solution.py:356
  4.4 23.0 %collective-permute-start.2 = (bf16[160,2560]{1,0:T(8,128)(2,1)S(1)}, bf16[160,2560]{1,0:T(8,128)(2,1)S(1)}, u32[]{:S(2)}, u32[]{:S(2)}) collective-permute-start(bf16[160,2560]{1,0:T(8,128)(2,1)S(1)} %pad_maximum_fusion.refs_0_), channel_id=1, source_target_pairs={{0,2},{1,3},{2,6},{3,7},{4,0},{5,1},{6,10},{7,11},{8,4},{9,5},{10,... | collective-permute-start | bytes 2457608 | tf_op jit(solution)/shard_map/ppermute | solution.py:359
  5.3 22.1 %all-to-all-start = ((f32[16,1,384]{2,1,0:T(1,128)}), f32[16,1,384]{2,1,0:T(1,128)S(1)}, u32[]{:S(2)}, u32[]{:S(2)}) async-start(f32[16,1,384]{2,1,0:T(1,128)} %broadcast_in_dim.26), calls=%async_computation | async-start | bytes 49152 | tf_op jit(solution)/shard_map/all_to_all | solution.py:376
  27.4 2.6 %collective-permute-start.3 = (bf16[160,2560]{1,0:T(8,128)(2,1)S(1)}, bf16[160,2560]{1,0:T(8,128)(2,1)S(1)}, u32[]{:S(2)}, u32[]{:S(2)}) collective-permute-start(bf16[160,2560]{1,0:T(8,128)(2,1)S(1)} %collective-permute-done.2.refs_0_), channel_id=1, source_target_pairs={{0,1},{1,0},{2,3},{3,2},{4,5},{5,4},{6,7},{7,6},{8,9},{9,8},{10,11... | collective-permute-start | bytes 2457608 | tf_op jit(solution)/shard_map/ppermute | solution.py:362
  27.9 3.1 %collective-permute-start.4 = (bf16[160,2560]{1,0:T(8,128)(2,1)S(1)}, bf16[160,2560]{1,0:T(8,128)(2,1)S(1)}, u32[]{:S(2)}, u32[]{:S(2)}) collective-permute-start(bf16[160,2560]{1,0:T(8,128)(2,1)S(1)} %collective-permute-done.1.refs_1_), channel_id=1, source_target_pairs={{0,1},{1,0},{2,3},{3,2},{4,5},{5,4},{6,7},{7,6},{8,9},{9,8},{10,11... | collective-permute-start | bytes 2457608 | tf_op jit(solution)/shard_map/ppermute | solution.py:362
  28.0 22.0 %collective-permute-start.5 = (bf16[160,2560]{1,0:T(8,128)(2,1)S(1)}, bf16[160,2560]{1,0:T(8,128)(2,1)S(1)}, u32[]{:S(2)}, u32[]{:S(2)}) collective-permute-start(bf16[160,2560]{1,0:T(8,128)(2,1)S(1)} %collective-permute-done.1.refs_1_), channel_id=1, source_target_pairs={{0,4},{1,5},{2,0},{3,1},{4,8},{5,9},{6,2},{7,3},{8,12},{9,13},{10,... | collective-permute-start | bytes 2457608 | tf_op jit(solution)/shard_map/ppermute | solution.py:356
  29.9 20.1 %collective-permute-start.6 = (bf16[160,2560]{1,0:T(8,128)(2,1)S(1)}, bf16[160,2560]{1,0:T(8,128)(2,1)S(1)}, u32[]{:S(2)}, u32[]{:S(2)}) collective-permute-start(bf16[160,2560]{1,0:T(8,128)(2,1)S(1)} %collective-permute-done.2.refs_0_), channel_id=1, source_target_pairs={{0,2},{1,3},{2,6},{3,7},{4,0},{5,1},{6,10},{7,11},{8,4},{9,5},{10,... | collective-permute-start | bytes 2457608 | tf_op jit(solution)/shard_map/ppermute | solution.py:359
  50.0 2.6 %collective-permute-start.7 = (bf16[160,2560]{1,0:T(8,128)(2,1)S(1)}, bf16[160,2560]{1,0:T(8,128)(2,1)S(1)}, u32[]{:S(2)}, u32[]{:S(2)}) collective-permute-start(bf16[160,2560]{1,0:T(8,128)(2,1)S(1)} %collective-permute-done.6.refs_0_), channel_id=1, source_target_pairs={{0,1},{1,0},{2,3},{3,2},{4,5},{5,4},{6,7},{7,6},{8,9},{9,8},{10,11... | collective-permute-start | bytes 2457608 | tf_op jit(solution)/shard_map/ppermute | solution.py:362
  50.4 3.1 %collective-permute-start.8 = (bf16[160,2560]{1,0:T(8,128)(2,1)S(1)}, bf16[160,2560]{1,0:T(8,128)(2,1)S(1)}, u32[]{:S(2)}, u32[]{:S(2)}) collective-permute-start(bf16[160,2560]{1,0:T(8,128)(2,1)S(1)} %collective-permute-done.5.refs_1_), channel_id=1, source_target_pairs={{0,1},{1,0},{2,3},{3,2},{4,5},{5,4},{6,7},{7,6},{8,9},{9,8},{10,11... | collective-permute-start | bytes 2457608 | tf_op jit(solution)/shard_map/ppermute | solution.py:362
  50.6 20.5 %collective-permute-start.10 = (bf16[160,2560]{1,0:T(8,128)(2,1)S(1)}, bf16[160,2560]{1,0:T(8,128)(2,1)S(1)}, u32[]{:S(2)}, u32[]{:S(2)}) collective-permute-start(bf16[160,2560]{1,0:T(8,128)(2,1)S(1)} %collective-permute-done.6.refs_0_), channel_id=1, source_target_pairs={{0,2},{1,3},{2,6},{3,7},{4,0},{5,1},{6,10},{7,11},{8,4},{9,5},{10,... | collective-permute-start | bytes 2457608 | tf_op jit(solution)/shard_map/ppermute | solution.py:359
  52.5 20.0 %collective-permute-start.9 = (bf16[160,2560]{1,0:T(8,128)(2,1)S(1)}, bf16[160,2560]{1,0:T(8,128)(2,1)S(1)}, u32[]{:S(2)}, u32[]{:S(2)}) collective-permute-start(bf16[160,2560]{1,0:T(8,128)(2,1)S(1)} %collective-permute-done.5.refs_1_), channel_id=1, source_target_pairs={{0,4},{1,5},{2,0},{3,1},{4,8},{5,9},{6,2},{7,3},{8,12},{9,13},{10,... | collective-permute-start | bytes 2457608 | tf_op jit(solution)/shard_map/ppermute | solution.py:356
  72.5 2.7 %collective-permute-start.11 = (bf16[160,2560]{1,0:T(8,128)(2,1)S(1)}, bf16[160,2560]{1,0:T(8,128)(2,1)S(1)}, u32[]{:S(2)}, u32[]{:S(2)}) collective-permute-start(bf16[160,2560]{1,0:T(8,128)(2,1)S(1)} %collective-permute-done.10.refs_0_), channel_id=1, source_target_pairs={{0,1},{1,0},{2,3},{3,2},{4,5},{5,4},{6,7},{7,6},{8,9},{9,8},{10,11... | collective-permute-start | bytes 2457608 | tf_op jit(solution)/shard_map/ppermute | solution.py:362
  72.5 3.5 %collective-permute-start.12 = (bf16[160,2560]{1,0:T(8,128)(2,1)S(1)}, bf16[160,2560]{1,0:T(8,128)(2,1)S(1)}, u32[]{:S(2)}, u32[]{:S(2)}) collective-permute-start(bf16[160,2560]{1,0:T(8,128)(2,1)S(1)} %collective-permute-done.9.refs_1_), channel_id=1, source_target_pairs={{0,1},{1,0},{2,3},{3,2},{4,5},{5,4},{6,7},{7,6},{8,9},{9,8},{10,11... | collective-permute-start | bytes 2457608 | tf_op jit(solution)/shard_map/ppermute | solution.py:362
  73.1 21.7 %collective-permute-start.13 = (bf16[80,2560]{1,0:T(8,128)(2,1)S(1)}, bf16[80,2560]{1,0:T(8,128)(2,1)S(1)}, u32[]{:S(2)}, u32[]{:S(2)}) collective-permute-start(bf16[80,2560]{1,0:T(8,128)(2,1)S(1)} %slice.54), channel_id=1, source_target_pairs={{0,4},{1,5},{2,0},{3,1},{4,8},{5,9},{6,2},{7,3},{8,12},{9,13},{10,... | collective-permute-start | bytes 1228808 | tf_op jit(solution)/shard_map/ppermute | solution.py:356
  73.5 21.3 %collective-permute-start.14 = (bf16[80,2560]{1,0:T(8,128)(2,1)S(1)}, bf16[80,2560]{1,0:T(8,128)(2,1)S(1)}, u32[]{:S(2)}, u32[]{:S(2)}) collective-permute-start(bf16[80,2560]{1,0:T(8,128)(2,1)S(1)} %slice.55), channel_id=1, source_target_pairs={{0,2},{1,3},{2,6},{3,7},{4,0},{5,1},{6,10},{7,11},{8,4},{9,5},{10,... | collective-permute-start | bytes 1228808 | tf_op jit(solution)/shard_map/ppermute | solution.py:359
  94.8 1.7 collective-permute-start.15
  94.9 2.2 %collective-permute-start.16 = (bf16[80,2560]{1,0:T(8,128)(2,1)S(1)}, bf16[80,2560]{1,0:T(8,128)(2,1)S(1)}, u32[]{:S(2)}, u32[]{:S(2)}) collective-permute-start(bf16[80,2560]{1,0:T(8,128)(2,1)S(1)} %collective-permute-done.14.refs_1_), channel_id=1, source_target_pairs={{0,1},{1,0},{2,3},{3,2},{4,5},{5,4},{6,7},{7,6},{8,9},{9,8},{10,11... | collective-permute-start | bytes 1228808 | tf_op jit(solution)/shard_map/ppermute | solution.py:362
  117.0 28.8 %slice-start = ((s8[7208960]{0:T(1024)(128)(4,1)}), s8[4194304]{0:T(1024)(128)(4,1)S(1)}, s32[]{:S(2)}) async-start(s8[7208960]{0:T(1024)(128)(4,1)} %bitcast.3), calls=%async_computation.1 | async-start | bytes 8388608
  121.6 8.4 %collective-permute-start.18 = (bf16[160,2560]{1,0:T(8,128)(2,1)S(1)}, bf16[160,2560]{1,0:T(8,128)(2,1)S(1)}, u32[]{:S(2)}, u32[]{:S(2)}) collective-permute-start(bf16[160,2560]{1,0:T(8,128)(2,1)S(1)} %get-tuple-element.62), channel_id=1, source_target_pairs={{0,1},{1,0},{2,3},{3,2},{4,5},{5,4},{6,7},{7,6},{8,9},{9,8},{10,11... | collective-permute-start | bytes 2457608 | tf_op jit(solution)/shard_map/ppermute | solution.py:362
  129.6 13.6 %collective-permute-start.20 = (bf16[320,2560]{1,0:T(8,128)(2,1)S(1)}, bf16[320,2560]{1,0:T(8,128)(2,1)S(1)}, u32[]{:S(2)}, u32[]{:S(2)}) collective-permute-start(bf16[320,2560]{1,0:T(8,128)(2,1)S(1)} %get-tuple-element.64), channel_id=1, source_target_pairs={{0,1},{1,0},{2,3},{3,2},{4,5},{5,4},{6,7},{7,6},{8,9},{9,8},{10,11... | collective-permute-start | bytes 4915208 | tf_op jit(solution)/shard_map/ppermute | solution.py:362
  130.2 13.0 %collective-permute-start.19 = (bf16[80,2560]{1,0:T(8,128)(2,1)S(1)}, bf16[80,2560]{1,0:T(8,128)(2,1)S(1)}, u32[]{:S(2)}, u32[]{:S(2)}) collective-permute-start(bf16[80,2560]{1,0:T(8,128)(2,1)S(1)} %get-tuple-element.75), channel_id=1, source_target_pairs={{0,4},{1,5},{2,0},{3,1},{4,8},{5,9},{6,2},{7,3},{8,12},{9,13},{10,... | collective-permute-start | bytes 1228808 | tf_op jit(solution)/shard_map/ppermute | solution.py:356
  130.6 12.6 %collective-permute-start.26 = (bf16[80,2560]{1,0:T(8,128)(2,1)S(1)}, bf16[80,2560]{1,0:T(8,128)(2,1)S(1)}, u32[]{:S(2)}, u32[]{:S(2)}) collective-permute-start(bf16[80,2560]{1,0:T(8,128)(2,1)S(1)} %get-tuple-element.76), channel_id=1, source_target_pairs={{0,2},{1,3},{2,6},{3,7},{4,0},{5,1},{6,10},{7,11},{8,4},{9,5},{10,... | collective-permute-start | bytes 1228808 | tf_op jit(solution)/shard_map/ppermute | solution.py:359
  143.1 10.7 %collective-permute-start.22 = (bf16[320,2560]{1,0:T(8,128)(2,1)S(1)}, bf16[320,2560]{1,0:T(8,128)(2,1)S(1)}, u32[]{:S(2)}, u32[]{:S(2)}) collective-permute-start(bf16[320,2560]{1,0:T(8,128)(2,1)S(1)} %get-tuple-element.66), channel_id=1, source_target_pairs={{0,1},{1,0},{2,3},{3,2},{4,5},{5,4},{6,7},{7,6},{8,9},{9,8},{10,11... | collective-permute-start | bytes 4915208 | tf_op jit(solution)/shard_map/ppermute | solution.py:362
  143.7 20.7 %collective-permute-start.21 = (bf16[160,2560]{1,0:T(8,128)(2,1)S(1)}, bf16[160,2560]{1,0:T(8,128)(2,1)S(1)}, u32[]{:S(2)}, u32[]{:S(2)}) collective-permute-start(bf16[160,2560]{1,0:T(8,128)(2,1)S(1)} %get-tuple-element.73), channel_id=1, source_target_pairs={{0,4},{1,5},{2,0},{3,1},{4,8},{5,9},{6,2},{7,3},{8,12},{9,13},{10,... | collective-permute-start | bytes 2457608 | tf_op jit(solution)/shard_map/ppermute | solution.py:356
  144.1 20.4 %collective-permute-start.27 = (bf16[160,2560]{1,0:T(8,128)(2,1)S(1)}, bf16[160,2560]{1,0:T(8,128)(2,1)S(1)}, u32[]{:S(2)}, u32[]{:S(2)}) collective-permute-start(bf16[160,2560]{1,0:T(8,128)(2,1)S(1)} %get-tuple-element.74), channel_id=1, source_target_pairs={{0,2},{1,3},{2,6},{3,7},{4,0},{5,1},{6,10},{7,11},{8,4},{9,5},{10,... | collective-permute-start | bytes 2457608 | tf_op jit(solution)/shard_map/ppermute | solution.py:359
  153.7 18.1 %collective-permute-start.24 = (bf16[320,2560]{1,0:T(8,128)(2,1)S(1)}, bf16[320,2560]{1,0:T(8,128)(2,1)S(1)}, u32[]{:S(2)}, u32[]{:S(2)}) collective-permute-start(bf16[320,2560]{1,0:T(8,128)(2,1)S(1)} %get-tuple-element.68), channel_id=1, source_target_pairs={{0,1},{1,0},{2,3},{3,2},{4,5},{5,4},{6,7},{7,6},{8,9},{9,8},{10,11... | collective-permute-start | bytes 4915208 | tf_op jit(solution)/shard_map/ppermute | solution.py:362
  165.0 19.8 %collective-permute-start.23 = (bf16[160,2560]{1,0:T(8,128)(2,1)S(1)}, bf16[160,2560]{1,0:T(8,128)(2,1)S(1)}, u32[]{:S(2)}, u32[]{:S(2)}) collective-permute-start(bf16[160,2560]{1,0:T(8,128)(2,1)S(1)} %get-tuple-element.71), channel_id=1, source_target_pairs={{0,4},{1,5},{2,0},{3,1},{4,8},{5,9},{6,2},{7,3},{8,12},{9,13},{10,... | collective-permute-start | bytes 2457608 | tf_op jit(solution)/shard_map/ppermute | solution.py:356
  166.8 19.2 %collective-permute-start.28 = (bf16[160,2560]{1,0:T(8,128)(2,1)S(1)}, bf16[160,2560]{1,0:T(8,128)(2,1)S(1)}, u32[]{:S(2)}, u32[]{:S(2)}) collective-permute-start(bf16[160,2560]{1,0:T(8,128)(2,1)S(1)} %get-tuple-element.72), channel_id=1, source_target_pairs={{0,2},{1,3},{2,6},{3,7},{4,0},{5,1},{6,10},{7,11},{8,4},{9,5},{10,... | collective-permute-start | bytes 2457608 | tf_op jit(solution)/shard_map/ppermute | solution.py:359
  171.7 17.0 %collective-permute-start.17 = (bf16[160,2560]{1,0:T(8,128)(2,1)S(1)}, bf16[160,2560]{1,0:T(8,128)(2,1)S(1)}, u32[]{:S(2)}, u32[]{:S(2)}) collective-permute-start(bf16[160,2560]{1,0:T(8,128)(2,1)S(1)} %get-tuple-element.60), channel_id=1, source_target_pairs={{0,1},{1,0},{2,3},{3,2},{4,5},{5,4},{6,7},{7,6},{8,9},{9,8},{10,11... | collective-permute-start | bytes 2457608 | tf_op jit(solution)/shard_map/ppermute | solution.py:362
  186.6 18.4 %collective-permute-start.25 = (bf16[160,2560]{1,0:T(8,128)(2,1)S(1)}, bf16[160,2560]{1,0:T(8,128)(2,1)S(1)}, u32[]{:S(2)}, u32[]{:S(2)}) collective-permute-start(bf16[160,2560]{1,0:T(8,128)(2,1)S(1)} %get-tuple-element.69), channel_id=1, source_target_pairs={{0,4},{1,5},{2,0},{3,1},{4,8},{5,9},{6,2},{7,3},{8,12},{9,13},{10,... | collective-permute-start | bytes 2457608 | tf_op jit(solution)/shard_map/ppermute | solution.py:356
  188.1 18.0 %collective-permute-start.29 = (bf16[160,2560]{1,0:T(8,128)(2,1)S(1)}, bf16[160,2560]{1,0:T(8,128)(2,1)S(1)}, u32[]{:S(2)}, u32[]{:S(2)}) collective-permute-start(bf16[160,2560]{1,0:T(8,128)(2,1)S(1)} %get-tuple-element.70), channel_id=1, source_target_pairs={{0,2},{1,3},{2,6},{3,7},{4,0},{5,1},{6,10},{7,11},{8,4},{9,5},{10,... | collective-permute-start | bytes 2457608 | tf_op jit(solution)/shard_map/ppermute | solution.py:359
  (17 other events, 114.1 us)

commit v5 on v4

--- a/solution.py
+++ b/solution.py
@@ -162,6 +162,56 @@
         return [(d, d ^ 1) for d in range(self.devices)]
 
 
+def pack_kernel(experts, expert_count, text_ref, panels_ref, target_ref, ids_ref, gates_ref, out_ref):
+    text_rows, wide = text_ref.shape
+    rows, width = out_ref.shape[0], out_ref.shape[1] - wide
+    image_rows = rows - text_rows
+    pan_count = target_ref.shape[1]
+    panel_rows = image_rows // pan_count
+    out_ref[:text_rows, :wide] = text_ref[...]
+    out_ref[text_rows:, :wide] = panels_ref[...]
+    lane = lax.broadcasted_iota(jnp.int32, (rows, width), 1)
+    term = sum((lane >= i * experts).astype(jnp.int32) for i in range(1, 4))
+    expert = lane - term * experts
+    gate = jnp.zeros((rows, width), jnp.float32)
+    for k in range(ids_ref.shape[1]):
+        gate += jnp.where(ids_ref[:, k : k + 1] == expert, gates_ref[:, k : k + 1], 0.0)
+    high = gate.astype(jnp.bfloat16).astype(jnp.float32)
+    middle = (gate - high).astype(jnp.bfloat16).astype(jnp.float32)
+    low = gate - high - middle
+    panel = lax.broadcasted_iota(jnp.int32, (rows, pan_count), 1)
+    row = lax.broadcasted_iota(jnp.int32, (rows, pan_count), 0) - text_rows
+    past = row - panel * panel_rows
+    mine = (past >= 0) & (past < panel_rows)
+    target = jnp.sum(
+        jnp.where(mine, target_ref[...].astype(jnp.float32), 0.0), axis=1, keepdims=True
+    )
+    within = jnp.sum(jnp.where(mine, past.astype(jnp.float32), 0.0), axis=1, keepdims=True)
+    owner, seq = jnp.zeros_like(target), jnp.zeros_like(target)
+    for i in range(1, experts):
+        passed = jnp.where(target >= i * pan_count, 1.0, 0.0)
+        owner += passed
+        if i % expert_count == 0:
+            seq += passed
+    place = (target - owner * pan_count) * panel_rows + within
+    tags = jnp.where(term == 0, high, jnp.where(term == 1, middle, jnp.where(term == 2, low, 0.0)))
+    tags = jnp.where(lane == 3 * experts, seq, jnp.where(lane == 3 * experts + 1, place, tags))
+    out_ref[:, wide:] = tags.astype(jnp.bfloat16)
+
+
+def pack_call(text_tokens, panels, panel_target, expert_ids, gate_weights, experts, expert_count):
+    rows, wide = expert_ids.shape[0], text_tokens.shape[1]
+    width = (3 * experts + 2 + 127) // 128 * 128
+    here = pl.BlockSpec(memory_space=pltpu.VMEM)
+    return pl.pallas_call(
+        functools.partial(pack_kernel, experts, expert_count),
+        in_specs=[here] * 5,
+        out_specs=here,
+        out_shape=pltpu.VMEM((rows, wide + width), jnp.bfloat16),
+        compiler_params=pltpu.CompilerParams(vmem_limit_bytes=14 * 1024 * 1024),
+    )(text_tokens, panels.reshape(-1, wide), panel_target[None, :], expert_ids, gate_weights)
+
+
 def hidden_kernel(count, rows, first_row, chunk, fetch, *refs):
     x_refs, refs = refs[:count], refs[count:]
     if fetch == "gate_up":
@@ -186,7 +236,9 @@
     if fetch == "down":
         pltpu.make_async_copy(far_ref, down_ref, sems.at[0]).start()
     for i in range(count):
-        x_all[i * rows : (i + 1) * rows, :] = x_refs[i][...]
+        x_all[i * rows : (i + 1) * rows, :] = x_refs[i][:, :wide]
+        at = first_row + i * rows
+        out_ref[at : at + rows, ff:] = x_refs[i][:, wide:]
 
     def step(i, width):
         if fetch == "gate_up":
@@ -219,13 +271,13 @@
 
 
 def hidden_call(blocks, gate_up_weight, hidden, first_row, all_rows, down_weight=None, last=False):
-    rows, wide = blocks[0].shape
-    ff = gate_up_weight.shape[2]
+    rows, width = blocks[0].shape
+    ff, wide = gate_up_weight.shape[2:]
     count = len(blocks)
     chunk = 256
     here, far = pl.BlockSpec(memory_space=pltpu.VMEM), pl.BlockSpec(memory_space=pltpu.HBM)
     args, in_specs = [kept(block) for block in blocks], [here] * count
-    out_shape, aliases = [pltpu.VMEM((all_rows, ff), jnp.bfloat16)], {}
+    out_shape, aliases = [pltpu.VMEM((all_rows, ff + width - wide), jnp.bfloat16)], {}
     scratch = [pltpu.VMEM((count * rows, wide), jnp.bfloat16)]
     fetch = None
     if hidden is None:
@@ -261,36 +313,42 @@
 
 
 def down_kernel(
-    slots, first_slot, rows, text_rows, seq_count, expert_count, chunk, places_ref, hidden_ref,
-    tables_ref, w_ref, own_ref, other_ref, column, picked, scale,
+    slots, first_slot, rows, text_rows, seq_count, experts, chunk, places_ref, hidden_ref, w_ref,
+    own_ref, other_ref, column, picked, scale,
 ):
     image_rows = rows - text_rows
     half = slots * rows // 2
     slot_total = hidden_ref.shape[0] // rows
-    targets_at = tables_ref.shape[2] - image_rows
-    wanted = lax.broadcasted_iota(jnp.int32, (image_rows, image_rows), 0).astype(jnp.float32)
-    diagonal = lax.broadcasted_iota(jnp.int32, (rows, rows), 0) == lax.broadcasted_iota(
-        jnp.int32, (rows, rows), 1
-    )
+    ff = w_ref.shape[1]
+    width = hidden_ref.shape[1] - ff
+    expert = places_ref[0]
+    lane = lax.broadcasted_iota(jnp.int32, (1, width), 1)
+    is_gate = (lane == expert) | (lane == expert + experts) | (lane == expert + 2 * experts)
+    place_of = jnp.where(lane == 3 * experts, float(image_rows), 0.0)
+    place_of = jnp.where(lane == 3 * experts + 1, 1.0, place_of)
+    wanted = lax.broadcasted_iota(jnp.int32, (1, image_rows), 1)
     for j in range(slots):
         at = (first_slot + j) * rows
-        picked[j * rows : j * rows + text_rows, :] = hidden_ref[at : at + text_rows, :]
-        owner = places_ref[first_slot + j]
-        first_wanted = wanted + (owner // expert_count * image_rows).astype(jnp.float32)
-        matches = []
+        picked[j * rows : j * rows + text_rows, :] = hidden_ref[at : at + text_rows, :ff]
         for z in range(seq_count):
-            source = places_ref[slot_total + (first_slot + j) * seq_count + z]
+            source = places_ref[1 + slot_total + (first_slot + j) * seq_count + z]
             start = pl.multiple_of(source * rows + text_rows, 16)
             column[z * image_rows : (z + 1) * image_rows, :] = hidden_ref[
                 pl.ds(start, image_rows), :
             ]
-            targets = tables_ref[places_ref[source], :, targets_at:]
-            matches.append(jnp.where(targets == first_wanted, 1.0, 0.0).astype(jnp.bfloat16))
-        match = jnp.concatenate(matches, axis=1)
-        rows_here = jnp.dot(match, column[...], preferred_element_type=jnp.float32)
+        place = column[:, ff:].astype(jnp.float32) * place_of
+        place = jnp.sum(place, axis=1, keepdims=True)
+        first = places_ref[1 + first_slot + j] * image_rows
+        match = jnp.where(place == (wanted + first).astype(jnp.float32), 1.0, 0.0)
+        rows_here = lax.dot_general(
+            match.astype(jnp.bfloat16),
+            column[:, :ff],
+            (((0,), (0,)), ((), ())),
+            preferred_element_type=jnp.float32,
+        )
         picked[j * rows + text_rows : (j + 1) * rows, :] = rows_here.astype(jnp.bfloat16)
-        weights = jnp.where(diagonal, tables_ref[owner, :, :rows], 0.0)
-        scale[j * rows : (j + 1) * rows, :] = jnp.sum(weights, axis=1, keepdims=True)
+        gates = jnp.where(is_gate, hidden_ref[at : at + rows, ff:].astype(jnp.float32), 0.0)
+        scale[j * rows : (j + 1) * rows, :] = jnp.sum(gates, axis=1, keepdims=True)
 
     @pl.loop(0, w_ref.shape[2] // chunk)
     def _(i):
@@ -303,22 +361,22 @@
 
 
 def down_call(
-    hidden, tables, places, down_weight, first_slot, slots, rows, text_rows, seq_count, expert_count
+    hidden, places, down_weight, first_slot, slots, rows, text_rows, seq_count, experts
 ):
     _, ff, wide = down_weight.shape
     half = slots * rows // 2
     here = pl.BlockSpec(memory_space=pltpu.VMEM)
     return pl.pallas_call(
         functools.partial(
-            down_kernel, slots, first_slot, rows, text_rows, seq_count, expert_count, 512
+            down_kernel, slots, first_slot, rows, text_rows, seq_count, experts, 512
         ),
         grid_spec=pltpu.PrefetchScalarGridSpec(
             num_scalar_prefetch=1,
             grid=(1,),
-            in_specs=[here] * 3,
+            in_specs=[here] * 2,
             out_specs=[here] * 2,
             scratch_shapes=[
-                pltpu.VMEM((seq_count * (rows - text_rows), ff), jnp.bfloat16),
+                pltpu.VMEM((seq_count * (rows - text_rows), hidden.shape[1]), jnp.bfloat16),
                 pltpu.VMEM((slots * rows, ff), jnp.bfloat16),
                 pltpu.VMEM((slots * rows, 1), jnp.float32),
             ],
@@ -330,7 +388,7 @@
             bytes_accessed=2 * ff * wide + 2 * slots * rows * wide,
             transcendentals=0,
         ),
-    )(places, kept(hidden), tables, kept(down_weight))
+    )(places, kept(hidden), kept(down_weight))
 
 
 def add_up(*parts):
@@ -361,25 +419,21 @@
     def across(array):
         return lax.ppermute(array, AXES, ring.swap())
 
-    own = jnp.concatenate([text_tokens, panels.reshape(image_rows, wide)], axis=0)
+    own = pack_call(
+        text_tokens, panels, panel_target, expert_ids, gate_weights, ring.devices, expert_count
+    )
+    seq_of = ring.owner_of // expert_count
+    numbers = np.arange(ring.devices, dtype=np.int32)[:, None]
+    places = np.concatenate([numbers, seq_of, ring.sources_of.reshape(ring.devices, -1)], axis=1)
+    places = jnp.asarray(places)[me]
+
     before, after = onward(own), back(own)
     other = across(own)
-
-    experts = jnp.arange(ring.devices, dtype=jnp.int32)[:, None, None]
-    routed = jnp.where(expert_ids[None] == experts, gate_weights[None], 0.0).sum(axis=-1)
-    target_seq = panel_target // pan_count // expert_count
-    targets = target_seq * image_rows + panel_target % pan_count * panel_rows
-    targets = (targets[:, None] + jnp.arange(panel_rows, dtype=jnp.int32)).reshape(image_rows)
-    targets = jnp.broadcast_to(targets.astype(jnp.float32), (ring.devices, image_rows))
-    routed = jnp.pad(routed, ((0, 0), (0, -tok_count % 128)))
-    outgoing = jnp.concatenate([routed, targets], axis=1)[:, None, :]
-    tables = lax.all_to_all(outgoing, AXES, split_axis=0, concat_axis=0, tiled=True)
-    places = np.concatenate([ring.owner_of, ring.sources_of.reshape(ring.devices, -1)], axis=1)
-    places = jnp.asarray(places)[me]
+    own, places = lax.optimization_barrier((own, places))
 
     all_rows = slot_count * tok_count
     hidden, gate_up = hidden_call([own, other], gate_up_weight, None, 0, all_rows)
-    hidden, before, after, tables = lax.optimization_barrier((hidden, before, after, tables))
+    hidden, before, after = lax.optimization_barrier((hidden, before, after))
     cut = tok_count // 2
     for s in range(1, ring.half):
         here = [after, before]
@@ -400,8 +454,8 @@
 
     def outputs(first_slot, slots):
         mine, others = down_call(
-            hidden, tables, places, down_here, first_slot, slots, tok_count, text_rows,
-            seq_count, expert_count,
+            hidden, places, down_here, first_slot, slots, tok_count, text_rows, seq_count,
+            ring.devices,
         )
         return mine, across(others)
 

time: 208 us -> 183 us (0.88)
  local copies, waits for them, and re-layouts: 42.5 us -> 5.01 us
  waiting for transfers between devices: 54.4 us -> 74.4 us
  starting transfers between devices: 27 us -> 20.6 us
    unnamed x36 -> x8, local copies, waits for them, and re-layouts: 41 us -> 4.26 us
    ppermute x8, waiting for transfers between devices: 9.12 us -> 21.1 us  [back(): return lax.ppermute(array, AXES, ring.step(-1))]
    ppermute x8, waiting for transfers between devices: 41.4 us -> 48.3 us  [onward(): return lax.ppermute(array, AXES, ring.step(1))]
    all_to_all x1 -> x0, starting transfers between devices: 6.36 us -> none  [ring_shards(): lax.all_to_all(outgoing, AXES, split_axis=0, concat_axis=0, tiled=True)]
  transfers between devices with their start and end apart: 31 -> 30, of which waited for: 13 -> 19; matrix products, arithmetic and copies ran while one was open for 2% -> 1% of each run, Pallas kernels for 33% -> 37%
where the time goes in v5:
time: 183 us
  Pallas kernels  79.7 us (44%)
  waiting for transfers between devices  74.4 us (41%)
  starting transfers between devices  20.6 us (11%)
  local copies, waits for them, and re-layouts  5.01 us (3%)
  other arithmetic  3.15 us (2%)
    ppermute x8, waiting for transfers between devices, onward(): return lax.ppermute(array, AXES, ring.step(1))  48.3 us
    pallas_call x5, Pallas kernels, hidden_call(): pl.pallas_call(functools.partial(hidden_kernel, count, rows, first_row, c...  46.2 us
    pallas_call x5, Pallas kernels, down_call(): pl.pallas_call(functools.partial(down_kernel, slots, first_slot, rows, te...  32.9 us
    ppermute x8, waiting for transfers between devices, back(): return lax.ppermute(array, AXES, ring.step(-1))  21.1 us
    ppermute x8, starting transfers between devices, onward(): return lax.ppermute(array, AXES, ring.step(1))  10.7 us
    ppermute x8, starting transfers between devices, back(): return lax.ppermute(array, AXES, ring.step(-1))  6.4 us
    ppermute x14, waiting for transfers between devices, across(): return lax.ppermute(array, AXES, ring.swap())  5.02 us
    unnamed x8, local copies, waits for them, and re-layouts  4.26 us
  transfers between devices with their start and end apart: 30, of which 19 were waited for; matrix products, arithmetic and copies ran while one was open for 1% of the time, Pallas kernels for 37%

profile of v5, /device:TPU:0, one launch (start us, length us, event | category | flops | bytes accessed | tf_op | source)
XLA Modules:
  0.0 183.0 jit_solution(12535396885482579580)
XLA Ops:
  1.6 1.1 copy-done
  5.3 2.6 %collective-permute-start.1 = (bf16[160,2688]{1,0:T(8,128)(2,1)S(1)}, bf16[160,2688]{1,0:T(8,128)(2,1)S(1)}, u32[]{:S(2)}, u32[]{:S(2)}) collective-permute-start(bf16[160,2688]{1,0:T(8,128)(2,1)S(1)} %shard_map.82.refs_0_), channel_id=1, source_target_pairs={{0,4},{1,5},{2,0},{3,1},{4,8},{5,9},{6,2},{7,3},{8,12},{9,13},{10,... | collective-permute-start | bytes 2580488 | tf_op jit(solution)/shard_map/ppermute | solution.py:414
  8.6 7.7 %shard_map.83 = (bf16[2560,1536]{1,0:T(8,128)(2,1)S(1)}, bf16[1,2,1408,2560]{3,2,1,0:T(8,128)(2,1)S(1)}) custom-call(bf16[160,2688]{1,0:T(8,128)(2,1)S(1)} %shard_map.82.refs_0_, bf16[160,2688]{1,0:T(8,128)(2,1)S(1)} %collective-permute-done.refs_1_, bf16[1,2,1408,2560]{3,2,1,0:T(8,128)(2,1)} %refs_2_.1), custom_call_target="tpu_custom_call" | custom-call | flops 4613734400 | bytes 16957440 | tf_op jit(solution)/shard_map/pallas_call | solution.py:299
  16.4 11.2 %collective-permute-done.1.refs_1_ = bf16[160,2688]{1,0:T(8,128)(2,1)S(1)} collective-permute-done((bf16[160,2688]{1,0:T(8,128)(2,1)S(1)}, bf16[160,2688]{1,0:T(8,128)(2,1)S(1)}, u32[]{:S(2)}, u32[]{:S(2)}) %collective-permute-start.1) | collective-permute-done | bytes 860192 | tf_op jit(solution)/shard_map/ppermute | solution.py:414
  27.6 1.5 collective-permute-done.2.refs_0_
  29.6 1.6 collective-permute-start.5
  32.8 10.8 %shard_map.84 = (bf16[2560,1536]{1,0:T(8,128)(2,1)S(1)}, bf16[1,2,1408,2560]{3,2,1,0:T(8,128)(2,1)S(1)}, bf16[1,1408,2560]{2,1,0:T(8,128)(2,1)S(1)}) custom-call(bf16[160,2688]{1,0:T(8,128)(2,1)S(1)} %collective-permute-done.2.refs_0_, bf16[160,2688]{1,0:T(8,128)(2,1)S(1)} %collective-permute-done.1.refs_1_, ...), custom_call_target="tpu_custom_call", output_to_operand_aliasing={{0}: (5, {}), {1}: (4, {})} | custom-call | flops 9227468800 | bytes 19496960 | tf_op jit(solution)/shard_map/pallas_call | solution.py:299
  43.6 7.1 %collective-permute-done.5.refs_1_ = bf16[160,2688]{1,0:T(8,128)(2,1)S(1)} collective-permute-done((bf16[160,2688]{1,0:T(8,128)(2,1)S(1)}, bf16[160,2688]{1,0:T(8,128)(2,1)S(1)}, u32[]{:S(2)}, u32[]{:S(2)}) %collective-permute-start.5) | collective-permute-done | bytes 860192 | tf_op jit(solution)/shard_map/ppermute | solution.py:414
  50.7 1.3 collective-permute-done.6.refs_0_
  52.5 1.6 collective-permute-start.9
  55.6 10.8 %shard_map.85 = (bf16[2560,1536]{1,0:T(8,128)(2,1)S(1)}, bf16[1,2,1408,2560]{3,2,1,0:T(8,128)(2,1)S(1)}) custom-call(bf16[160,2688]{1,0:T(8,128)(2,1)S(1)} %collective-permute-done.6.refs_0_, bf16[160,2688]{1,0:T(8,128)(2,1)S(1)} %collective-permute-done.5.refs_1_, ...), custom_call_target="tpu_custom_call", output_to_operand_aliasing={{0}: (5, {}), {1}: (4, {})} | custom-call | flops 9227468800 | bytes 19496960 | tf_op jit(solution)/shard_map/pallas_call | solution.py:299
  66.4 7.1 %collective-permute-done.9.refs_1_ = bf16[160,2688]{1,0:T(8,128)(2,1)S(1)} collective-permute-done((bf16[160,2688]{1,0:T(8,128)(2,1)S(1)}, bf16[160,2688]{1,0:T(8,128)(2,1)S(1)}, u32[]{:S(2)}, u32[]{:S(2)}) %collective-permute-start.9) | collective-permute-done | bytes 860192 | tf_op jit(solution)/shard_map/ppermute | solution.py:414
  73.5 1.3 collective-permute-done.10.refs_0_
  75.4 1.5 collective-permute-start.13
  78.4 10.8 %shard_map.86 = (bf16[2560,1536]{1,0:T(8,128)(2,1)S(1)}, bf16[1,2,1408,2560]{3,2,1,0:T(8,128)(2,1)S(1)}) custom-call(bf16[160,2688]{1,0:T(8,128)(2,1)S(1)} %collective-permute-done.10.refs_0_, bf16[160,2688]{1,0:T(8,128)(2,1)S(1)} %collective-permute-done.9.refs_1_, ...), custom_call_target="tpu_custom_call", output_to_operand_aliasing={{0}: (5, {}), {1}: (4, {})} | custom-call | flops 9227468800 | bytes 19496960 | tf_op jit(solution)/shard_map/pallas_call | solution.py:299
  89.8 1.3 collective-permute-done.15.refs_2_
  91.7 6.1 %shard_map.87.hidden_ref = bf16[2560,1536]{1,0:T(8,128)(2,1)S(1)} custom-call(bf16[80,2688]{1,0:T(8,128)(2,1)S(1)} %collective-permute-done.13.refs_0_, bf16[80,2688]{1,0:T(8,128)(2,1)S(1)} %collective-permute-done.14.refs_1_, bf16[80,2688]{1,0:T(8,128)(2,1)S(1)} %collective-permute-done.15.refs_2_, ...), custom_call_target="tpu_custom_call", output_to_operand_aliasing={{}: (5, {})} | custom-call | flops 4613734400 | bytes 16957440 | tf_op jit(solution)/shard_map/pallas_call | solution.py:299
  97.8 4.7 %shard_map.89 = (bf16[160,2560]{1,0:T(8,128)(2,1)S(1)}, bf16[160,2560]{1,0:T(8,128)(2,1)S(1)}) custom-call(s32[81]{0:T(128)S(1)} %dynamic-slice_bitcast_fusion.places_ref, bf16[2560,1536]{1,0:T(8,128)(2,1)S(1)} %shard_map.87.hidden_ref, bf16[1,1408,2560]{2,1,0:T(8,128)(2,1)S(1)} %get-tuple-element.60.w_ref), custom_call_target="tpu_custom_call" | custom-call | flops 2306867200 | bytes 8847360 | tf_op jit(solution)/shard_map/pallas_call | solution.py:369
  102.7 7.9 %shard_map.90 = (bf16[320,2560]{1,0:T(8,128)(2,1)S(1)}, bf16[320,2560]{1,0:T(8,128)(2,1)S(1)}) custom-call(s32[81]{0:T(128)S(1)} %dynamic-slice_bitcast_fusion.places_ref, bf16[2560,1536]{1,0:T(8,128)(2,1)S(1)} %shard_map.87.hidden_ref, bf16[1,1408,2560]{2,1,0:T(8,128)(2,1)S(1)} %get-tuple-element.60.w_ref), custom_call_target="tpu_custom_call" | custom-call | flops 4613734400 | bytes 10485760 | tf_op jit(solution)/shard_map/pallas_call | solution.py:369
  111.2 1.5 collective-permute-start.19
  113.3 7.9 %shard_map.91 = (bf16[320,2560]{1,0:T(8,128)(2,1)S(1)}, bf16[320,2560]{1,0:T(8,128)(2,1)S(1)}) custom-call(s32[81]{0:T(128)S(1)} %dynamic-slice_bitcast_fusion.places_ref, bf16[2560,1536]{1,0:T(8,128)(2,1)S(1)} %shard_map.87.hidden_ref, bf16[1,1408,2560]{2,1,0:T(8,128)(2,1)S(1)} %get-tuple-element.60.w_ref), custom_call_target="tpu_custom_call" | custom-call | flops 4613734400 | bytes 10485760 | tf_op jit(solution)/shard_map/pallas_call | solution.py:369
  121.2 1.5 collective-permute-done.19
  122.7 1.2 collective-permute-done.26
  124.9 1.6 collective-permute-start.27
  126.5 7.9 %shard_map.92 = (bf16[320,2560]{1,0:T(8,128)(2,1)S(1)}, bf16[320,2560]{1,0:T(8,128)(2,1)S(1)}) custom-call(s32[81]{0:T(128)S(1)} %dynamic-slice_bitcast_fusion.places_ref, bf16[2560,1536]{1,0:T(8,128)(2,1)S(1)} %shard_map.87.hidden_ref, bf16[1,1408,2560]{2,1,0:T(8,128)(2,1)S(1)} %get-tuple-element.60.w_ref), custom_call_target="tpu_custom_call" | custom-call | flops 4613734400 | bytes 10485760 | tf_op jit(solution)/shard_map/pallas_call | solution.py:369
  134.5 9.2 %collective-permute-done.21 = bf16[160,2560]{1,0:T(8,128)(2,1)S(1)} collective-permute-done((bf16[160,2560]{1,0:T(8,128)(2,1)S(1)}, bf16[160,2560]{1,0:T(8,128)(2,1)S(1)}, u32[]{:S(2)}, u32[]{:S(2)}) %collective-permute-start.21) | collective-permute-done | bytes 819232 | tf_op jit(solution)/shard_map/ppermute | solution.py:414
  145.2 1.5 collective-permute-start.28
  146.6 4.7 %shard_map.88 = (bf16[160,2560]{1,0:T(8,128)(2,1)S(1)}, bf16[160,2560]{1,0:T(8,128)(2,1)S(1)}) custom-call(s32[81]{0:T(128)S(1)} %dynamic-slice_bitcast_fusion.places_ref, bf16[2560,1536]{1,0:T(8,128)(2,1)S(1)} %shard_map.87.hidden_ref, bf16[1,1408,2560]{2,1,0:T(8,128)(2,1)S(1)} %get-tuple-element.60.w_ref), custom_call_target="tpu_custom_call" | custom-call | flops 2306867200 | bytes 8847360 | tf_op jit(solution)/shard_map/pallas_call | solution.py:369
  151.4 11.3 %collective-permute-done.23 = bf16[160,2560]{1,0:T(8,128)(2,1)S(1)} collective-permute-done((bf16[160,2560]{1,0:T(8,128)(2,1)S(1)}, bf16[160,2560]{1,0:T(8,128)(2,1)S(1)}, u32[]{:S(2)}, u32[]{:S(2)}) %collective-permute-start.23) | collective-permute-done | bytes 819232 | tf_op jit(solution)/shard_map/ppermute | solution.py:414
  163.7 1.4 collective-permute-start.29
  165.8 15.0 %collective-permute-done.29 = bf16[160,2560]{1,0:T(8,128)(2,1)S(1)} collective-permute-done((bf16[160,2560]{1,0:T(8,128)(2,1)S(1)}, bf16[160,2560]{1,0:T(8,128)(2,1)S(1)}, u32[]{:S(2)}, u32[]{:S(2)}) %collective-permute-start.29) | collective-permute-done | bytes 819232 | tf_op jit(solution)/shard_map/ppermute | solution.py:417
  181.7 1.3 add_convert_fusion
  (55 shorter events, 19.0 us)
Async XLA Ops:
  1.6 1.1 copy-start
  2.7 0.9 copy-start.1
  4.8 3.9 %collective-permute-start = (bf16[160,2688]{1,0:T(8,128)(2,1)S(1)}, bf16[160,2688]{1,0:T(8,128)(2,1)S(1)}, u32[]{:S(2)}, u32[]{:S(2)}) collective-permute-start(bf16[160,2688]{1,0:T(8,128)(2,1)S(1)} %shard_map.82.refs_0_), channel_id=1, source_target_pairs={{0,1},{1,0},{2,3},{3,2},{4,5},{5,4},{6,7},{7,6},{8,9},{9,8},{10,11... | collective-permute-start | bytes 2580488 | tf_op jit(solution)/shard_map/ppermute | solution.py:420
  5.3 22.3 %collective-permute-start.1 = (bf16[160,2688]{1,0:T(8,128)(2,1)S(1)}, bf16[160,2688]{1,0:T(8,128)(2,1)S(1)}, u32[]{:S(2)}, u32[]{:S(2)}) collective-permute-start(bf16[160,2688]{1,0:T(8,128)(2,1)S(1)} %shard_map.82.refs_0_), channel_id=1, source_target_pairs={{0,4},{1,5},{2,0},{3,1},{4,8},{5,9},{6,2},{7,3},{8,12},{9,13},{10,... | collective-permute-start | bytes 2580488 | tf_op jit(solution)/shard_map/ppermute | solution.py:414
  7.9 21.2 %collective-permute-start.2 = (bf16[160,2688]{1,0:T(8,128)(2,1)S(1)}, bf16[160,2688]{1,0:T(8,128)(2,1)S(1)}, u32[]{:S(2)}, u32[]{:S(2)}) collective-permute-start(bf16[160,2688]{1,0:T(8,128)(2,1)S(1)} %shard_map.82.refs_0_), channel_id=1, source_target_pairs={{0,2},{1,3},{2,6},{3,7},{4,0},{5,1},{6,10},{7,11},{8,4},{9,5},{10,... | collective-permute-start | bytes 2580488 | tf_op jit(solution)/shard_map/ppermute | solution.py:417
  29.1 2.5 %collective-permute-start.3 = (bf16[160,2688]{1,0:T(8,128)(2,1)S(1)}, bf16[160,2688]{1,0:T(8,128)(2,1)S(1)}, u32[]{:S(2)}, u32[]{:S(2)}) collective-permute-start(bf16[160,2688]{1,0:T(8,128)(2,1)S(1)} %collective-permute-done.2.refs_0_), channel_id=1, source_target_pairs={{0,1},{1,0},{2,3},{3,2},{4,5},{5,4},{6,7},{7,6},{8,9},{9,8},{10,11... | collective-permute-start | bytes 2580488 | tf_op jit(solution)/shard_map/ppermute | solution.py:420
  29.1 3.6 %collective-permute-start.4 = (bf16[160,2688]{1,0:T(8,128)(2,1)S(1)}, bf16[160,2688]{1,0:T(8,128)(2,1)S(1)}, u32[]{:S(2)}, u32[]{:S(2)}) collective-permute-start(bf16[160,2688]{1,0:T(8,128)(2,1)S(1)} %collective-permute-done.1.refs_1_), channel_id=1, source_target_pairs={{0,1},{1,0},{2,3},{3,2},{4,5},{5,4},{6,7},{7,6},{8,9},{9,8},{10,11... | collective-permute-start | bytes 2580488 | tf_op jit(solution)/shard_map/ppermute | solution.py:420
  29.6 21.0 %collective-permute-start.5 = (bf16[160,2688]{1,0:T(8,128)(2,1)S(1)}, bf16[160,2688]{1,0:T(8,128)(2,1)S(1)}, u32[]{:S(2)}, u32[]{:S(2)}) collective-permute-start(bf16[160,2688]{1,0:T(8,128)(2,1)S(1)} %collective-permute-done.1.refs_1_), channel_id=1, source_target_pairs={{0,4},{1,5},{2,0},{3,1},{4,8},{5,9},{6,2},{7,3},{8,12},{9,13},{10,... | collective-permute-start | bytes 2580488 | tf_op jit(solution)/shard_map/ppermute | solution.py:414
  31.2 20.7 %collective-permute-start.6 = (bf16[160,2688]{1,0:T(8,128)(2,1)S(1)}, bf16[160,2688]{1,0:T(8,128)(2,1)S(1)}, u32[]{:S(2)}, u32[]{:S(2)}) collective-permute-start(bf16[160,2688]{1,0:T(8,128)(2,1)S(1)} %collective-permute-done.2.refs_0_), channel_id=1, source_target_pairs={{0,2},{1,3},{2,6},{3,7},{4,0},{5,1},{6,10},{7,11},{8,4},{9,5},{10,... | collective-permute-start | bytes 2580488 | tf_op jit(solution)/shard_map/ppermute | solution.py:417
  52.0 2.5 %collective-permute-start.7 = (bf16[160,2688]{1,0:T(8,128)(2,1)S(1)}, bf16[160,2688]{1,0:T(8,128)(2,1)S(1)}, u32[]{:S(2)}, u32[]{:S(2)}) collective-permute-start(bf16[160,2688]{1,0:T(8,128)(2,1)S(1)} %collective-permute-done.6.refs_0_), channel_id=1, source_target_pairs={{0,1},{1,0},{2,3},{3,2},{4,5},{5,4},{6,7},{7,6},{8,9},{9,8},{10,11... | collective-permute-start | bytes 2580488 | tf_op jit(solution)/shard_map/ppermute | solution.py:420
  52.0 3.6 %collective-permute-start.8 = (bf16[160,2688]{1,0:T(8,128)(2,1)S(1)}, bf16[160,2688]{1,0:T(8,128)(2,1)S(1)}, u32[]{:S(2)}, u32[]{:S(2)}) collective-permute-start(bf16[160,2688]{1,0:T(8,128)(2,1)S(1)} %collective-permute-done.5.refs_1_), channel_id=1, source_target_pairs={{0,1},{1,0},{2,3},{3,2},{4,5},{5,4},{6,7},{7,6},{8,9},{9,8},{10,11... | collective-permute-start | bytes 2580488 | tf_op jit(solution)/shard_map/ppermute | solution.py:420
  52.5 21.0 %collective-permute-start.9 = (bf16[160,2688]{1,0:T(8,128)(2,1)S(1)}, bf16[160,2688]{1,0:T(8,128)(2,1)S(1)}, u32[]{:S(2)}, u32[]{:S(2)}) collective-permute-start(bf16[160,2688]{1,0:T(8,128)(2,1)S(1)} %collective-permute-done.5.refs_1_), channel_id=1, source_target_pairs={{0,4},{1,5},{2,0},{3,1},{4,8},{5,9},{6,2},{7,3},{8,12},{9,13},{10,... | collective-permute-start | bytes 2580488 | tf_op jit(solution)/shard_map/ppermute | solution.py:414
  54.1 20.7 %collective-permute-start.10 = (bf16[160,2688]{1,0:T(8,128)(2,1)S(1)}, bf16[160,2688]{1,0:T(8,128)(2,1)S(1)}, u32[]{:S(2)}, u32[]{:S(2)}) collective-permute-start(bf16[160,2688]{1,0:T(8,128)(2,1)S(1)} %collective-permute-done.6.refs_0_), channel_id=1, source_target_pairs={{0,2},{1,3},{2,6},{3,7},{4,0},{5,1},{6,10},{7,11},{8,4},{9,5},{10,... | collective-permute-start | bytes 2580488 | tf_op jit(solution)/shard_map/ppermute | solution.py:417
  74.8 2.7 %collective-permute-start.11 = (bf16[160,2688]{1,0:T(8,128)(2,1)S(1)}, bf16[160,2688]{1,0:T(8,128)(2,1)S(1)}, u32[]{:S(2)}, u32[]{:S(2)}) collective-permute-start(bf16[160,2688]{1,0:T(8,128)(2,1)S(1)} %collective-permute-done.10.refs_0_), channel_id=1, source_target_pairs={{0,1},{1,0},{2,3},{3,2},{4,5},{5,4},{6,7},{7,6},{8,9},{9,8},{10,11... | collective-permute-start | bytes 2580488 | tf_op jit(solution)/shard_map/ppermute | solution.py:420
  74.8 3.6 %collective-permute-start.12 = (bf16[160,2688]{1,0:T(8,128)(2,1)S(1)}, bf16[160,2688]{1,0:T(8,128)(2,1)S(1)}, u32[]{:S(2)}, u32[]{:S(2)}) collective-permute-start(bf16[160,2688]{1,0:T(8,128)(2,1)S(1)} %collective-permute-done.9.refs_1_), channel_id=1, source_target_pairs={{0,1},{1,0},{2,3},{3,2},{4,5},{5,4},{6,7},{7,6},{8,9},{9,8},{10,11... | collective-permute-start | bytes 2580488 | tf_op jit(solution)/shard_map/ppermute | solution.py:420
  75.4 13.8 %collective-permute-start.13 = (bf16[80,2688]{1,0:T(8,128)(2,1)S(1)}, bf16[80,2688]{1,0:T(8,128)(2,1)S(1)}, u32[]{:S(2)}, u32[]{:S(2)}) collective-permute-start(bf16[80,2688]{1,0:T(8,128)(2,1)S(1)} %slice.54), channel_id=1, source_target_pairs={{0,4},{1,5},{2,0},{3,1},{4,8},{5,9},{6,2},{7,3},{8,12},{9,13},{10,... | collective-permute-start | bytes 1290248 | tf_op jit(solution)/shard_map/ppermute | solution.py:414
  76.9 12.3 %collective-permute-start.14 = (bf16[80,2688]{1,0:T(8,128)(2,1)S(1)}, bf16[80,2688]{1,0:T(8,128)(2,1)S(1)}, u32[]{:S(2)}, u32[]{:S(2)}) collective-permute-start(bf16[80,2688]{1,0:T(8,128)(2,1)S(1)} %slice.55), channel_id=1, source_target_pairs={{0,2},{1,3},{2,6},{3,7},{4,0},{5,1},{6,10},{7,11},{8,4},{9,5},{10,... | collective-permute-start | bytes 1290248 | tf_op jit(solution)/shard_map/ppermute | solution.py:417
  89.3 1.8 %collective-permute-start.15 = (bf16[80,2688]{1,0:T(8,128)(2,1)S(1)}, bf16[80,2688]{1,0:T(8,128)(2,1)S(1)}, u32[]{:S(2)}, u32[]{:S(2)}) collective-permute-start(bf16[80,2688]{1,0:T(8,128)(2,1)S(1)} %collective-permute-done.13.refs_0_), channel_id=1, source_target_pairs={{0,1},{1,0},{2,3},{3,2},{4,5},{5,4},{6,7},{7,6},{8,9},{9,8},{10,11... | collective-permute-start | bytes 1290248 | tf_op jit(solution)/shard_map/ppermute | solution.py:420
  89.5 2.3 %collective-permute-start.16 = (bf16[80,2688]{1,0:T(8,128)(2,1)S(1)}, bf16[80,2688]{1,0:T(8,128)(2,1)S(1)}, u32[]{:S(2)}, u32[]{:S(2)}) collective-permute-start(bf16[80,2688]{1,0:T(8,128)(2,1)S(1)} %collective-permute-done.14.refs_1_), channel_id=1, source_target_pairs={{0,1},{1,0},{2,3},{3,2},{4,5},{5,4},{6,7},{7,6},{8,9},{9,8},{10,11... | collective-permute-start | bytes 1290248 | tf_op jit(solution)/shard_map/ppermute | solution.py:420
  102.5 8.5 %collective-permute-start.18 = (bf16[160,2560]{1,0:T(8,128)(2,1)S(1)}, bf16[160,2560]{1,0:T(8,128)(2,1)S(1)}, u32[]{:S(2)}, u32[]{:S(2)}) collective-permute-start(bf16[160,2560]{1,0:T(8,128)(2,1)S(1)} %get-tuple-element.64), channel_id=1, source_target_pairs={{0,1},{1,0},{2,3},{3,2},{4,5},{5,4},{6,7},{7,6},{8,9},{9,8},{10,11... | collective-permute-start | bytes 2457608 | tf_op jit(solution)/shard_map/ppermute | solution.py:420
  110.5 13.4 %collective-permute-start.20 = (bf16[320,2560]{1,0:T(8,128)(2,1)S(1)}, bf16[320,2560]{1,0:T(8,128)(2,1)S(1)}, u32[]{:S(2)}, u32[]{:S(2)}) collective-permute-start(bf16[320,2560]{1,0:T(8,128)(2,1)S(1)} %get-tuple-element.66), channel_id=1, source_target_pairs={{0,1},{1,0},{2,3},{3,2},{4,5},{5,4},{6,7},{7,6},{8,9},{9,8},{10,11... | collective-permute-start | bytes 4915208 | tf_op jit(solution)/shard_map/ppermute | solution.py:420
  111.2 11.6 %collective-permute-start.19 = (bf16[80,2560]{1,0:T(8,128)(2,1)S(1)}, bf16[80,2560]{1,0:T(8,128)(2,1)S(1)}, u32[]{:S(2)}, u32[]{:S(2)}) collective-permute-start(bf16[80,2560]{1,0:T(8,128)(2,1)S(1)} %get-tuple-element.77), channel_id=1, source_target_pairs={{0,4},{1,5},{2,0},{3,1},{4,8},{5,9},{6,2},{7,3},{8,12},{9,13},{10,... | collective-permute-start | bytes 1228808 | tf_op jit(solution)/shard_map/ppermute | solution.py:414
  112.7 11.2 %collective-permute-start.26 = (bf16[80,2560]{1,0:T(8,128)(2,1)S(1)}, bf16[80,2560]{1,0:T(8,128)(2,1)S(1)}, u32[]{:S(2)}, u32[]{:S(2)}) collective-permute-start(bf16[80,2560]{1,0:T(8,128)(2,1)S(1)} %get-tuple-element.78), channel_id=1, source_target_pairs={{0,2},{1,3},{2,6},{3,7},{4,0},{5,1},{6,10},{7,11},{8,4},{9,5},{10,... | collective-permute-start | bytes 1228808 | tf_op jit(solution)/shard_map/ppermute | solution.py:417
  121.1 13.3 %collective-permute-start.22 = (bf16[320,2560]{1,0:T(8,128)(2,1)S(1)}, bf16[320,2560]{1,0:T(8,128)(2,1)S(1)}, u32[]{:S(2)}, u32[]{:S(2)}) collective-permute-start(bf16[320,2560]{1,0:T(8,128)(2,1)S(1)} %get-tuple-element.68), channel_id=1, source_target_pairs={{0,1},{1,0},{2,3},{3,2},{4,5},{5,4},{6,7},{7,6},{8,9},{9,8},{10,11... | collective-permute-start | bytes 4915208 | tf_op jit(solution)/shard_map/ppermute | solution.py:420
  124.4 19.2 %collective-permute-start.21 = (bf16[160,2560]{1,0:T(8,128)(2,1)S(1)}, bf16[160,2560]{1,0:T(8,128)(2,1)S(1)}, u32[]{:S(2)}, u32[]{:S(2)}) collective-permute-start(bf16[160,2560]{1,0:T(8,128)(2,1)S(1)} %get-tuple-element.75), channel_id=1, source_target_pairs={{0,4},{1,5},{2,0},{3,1},{4,8},{5,9},{6,2},{7,3},{8,12},{9,13},{10,... | collective-permute-start | bytes 2457608 | tf_op jit(solution)/shard_map/ppermute | solution.py:414
  124.9 19.0 %collective-permute-start.27 = (bf16[160,2560]{1,0:T(8,128)(2,1)S(1)}, bf16[160,2560]{1,0:T(8,128)(2,1)S(1)}, u32[]{:S(2)}, u32[]{:S(2)}) collective-permute-start(bf16[160,2560]{1,0:T(8,128)(2,1)S(1)} %get-tuple-element.76), channel_id=1, source_target_pairs={{0,2},{1,3},{2,6},{3,7},{4,0},{5,1},{6,10},{7,11},{8,4},{9,5},{10,... | collective-permute-start | bytes 2457608 | tf_op jit(solution)/shard_map/ppermute | solution.py:417
  134.4 17.0 %collective-permute-start.24 = (bf16[320,2560]{1,0:T(8,128)(2,1)S(1)}, bf16[320,2560]{1,0:T(8,128)(2,1)S(1)}, u32[]{:S(2)}, u32[]{:S(2)}) collective-permute-start(bf16[320,2560]{1,0:T(8,128)(2,1)S(1)} %get-tuple-element.70), channel_id=1, source_target_pairs={{0,1},{1,0},{2,3},{3,2},{4,5},{5,4},{6,7},{7,6},{8,9},{9,8},{10,11... | collective-permute-start | bytes 4915208 | tf_op jit(solution)/shard_map/ppermute | solution.py:420
  144.5 18.1 %collective-permute-start.23 = (bf16[160,2560]{1,0:T(8,128)(2,1)S(1)}, bf16[160,2560]{1,0:T(8,128)(2,1)S(1)}, u32[]{:S(2)}, u32[]{:S(2)}) collective-permute-start(bf16[160,2560]{1,0:T(8,128)(2,1)S(1)} %get-tuple-element.73), channel_id=1, source_target_pairs={{0,4},{1,5},{2,0},{3,1},{4,8},{5,9},{6,2},{7,3},{8,12},{9,13},{10,... | collective-permute-start | bytes 2457608 | tf_op jit(solution)/shard_map/ppermute | solution.py:414
  145.2 17.9 %collective-permute-start.28 = (bf16[160,2560]{1,0:T(8,128)(2,1)S(1)}, bf16[160,2560]{1,0:T(8,128)(2,1)S(1)}, u32[]{:S(2)}, u32[]{:S(2)}) collective-permute-start(bf16[160,2560]{1,0:T(8,128)(2,1)S(1)} %get-tuple-element.74), channel_id=1, source_target_pairs={{0,2},{1,3},{2,6},{3,7},{4,0},{5,1},{6,10},{7,11},{8,4},{9,5},{10,... | collective-permute-start | bytes 2457608 | tf_op jit(solution)/shard_map/ppermute | solution.py:417
  151.3 14.5 %collective-permute-start.17 = (bf16[160,2560]{1,0:T(8,128)(2,1)S(1)}, bf16[160,2560]{1,0:T(8,128)(2,1)S(1)}, u32[]{:S(2)}, u32[]{:S(2)}) collective-permute-start(bf16[160,2560]{1,0:T(8,128)(2,1)S(1)} %get-tuple-element.62), channel_id=1, source_target_pairs={{0,1},{1,0},{2,3},{3,2},{4,5},{5,4},{6,7},{7,6},{8,9},{9,8},{10,11... | collective-permute-start | bytes 2457608 | tf_op jit(solution)/shard_map/ppermute | solution.py:420
  163.7 17.1 %collective-permute-start.29 = (bf16[160,2560]{1,0:T(8,128)(2,1)S(1)}, bf16[160,2560]{1,0:T(8,128)(2,1)S(1)}, u32[]{:S(2)}, u32[]{:S(2)}) collective-permute-start(bf16[160,2560]{1,0:T(8,128)(2,1)S(1)} %get-tuple-element.72), channel_id=1, source_target_pairs={{0,2},{1,3},{2,6},{3,7},{4,0},{5,1},{6,10},{7,11},{8,4},{9,5},{10,... | collective-permute-start | bytes 2457608 | tf_op jit(solution)/shard_map/ppermute | solution.py:417
  165.1 16.6 %collective-permute-start.25 = (bf16[160,2560]{1,0:T(8,128)(2,1)S(1)}, bf16[160,2560]{1,0:T(8,128)(2,1)S(1)}, u32[]{:S(2)}, u32[]{:S(2)}) collective-permute-start(bf16[160,2560]{1,0:T(8,128)(2,1)S(1)} %get-tuple-element.71), channel_id=1, source_target_pairs={{0,4},{1,5},{2,0},{3,1},{4,8},{5,9},{6,2},{7,3},{8,12},{9,13},{10,... | collective-permute-start | bytes 2457608 | tf_op jit(solution)/shard_map/ppermute | solution.py:414
  (1 other events, 0.7 us)

commit v6 on v5

--- a/solution.py
+++ b/solution.py
@@ -162,20 +162,41 @@
         return [(d, d ^ 1) for d in range(self.devices)]
 
 
-def pack_kernel(experts, expert_count, text_ref, panels_ref, target_ref, ids_ref, gates_ref, out_ref):
+def kept(array):
+    return pltpu.with_memory_space_constraint(array, pltpu.VMEM)
+
+
+def distant(array):
+    return pltpu.with_memory_space_constraint(array, pltpu.HBM)
+
+
+def pack_kernel(
+    experts, expert_count, text_ref, panels_ref, target_ref, ids_ref, gates_ref, out_ref, sems
+):
     text_rows, wide = text_ref.shape
     rows, width = out_ref.shape[0], out_ref.shape[1] - wide
-    image_rows = rows - text_rows
     pan_count = target_ref.shape[1]
-    panel_rows = image_rows // pan_count
-    out_ref[:text_rows, :wide] = text_ref[...]
-    out_ref[text_rows:, :wide] = panels_ref[...]
+    panel_rows = (rows - text_rows) // pan_count
+    copies = [
+        pltpu.make_async_copy(text_ref, out_ref.at[:text_rows, :wide], sems.at[0]),
+        pltpu.make_async_copy(panels_ref, out_ref.at[text_rows:, :wide], sems.at[1]),
+    ]
+    for copy in copies:
+        copy.start()
     lane = lax.broadcasted_iota(jnp.int32, (rows, width), 1)
     term = sum((lane >= i * experts).astype(jnp.int32) for i in range(1, 4))
-    expert = lane - term * experts
+    expert = (lane - term * experts).astype(jnp.float32)
+    diagonal = lax.broadcasted_iota(jnp.int32, (rows, rows), 0) == lax.broadcasted_iota(
+        jnp.int32, (rows, rows), 1
+    )
+
+    def upright(row):
+        return jnp.sum(jnp.where(diagonal, row, 0.0), axis=1, keepdims=True)
+
     gate = jnp.zeros((rows, width), jnp.float32)
-    for k in range(ids_ref.shape[1]):
-        gate += jnp.where(ids_ref[:, k : k + 1] == expert, gates_ref[:, k : k + 1], 0.0)
+    for k in range(ids_ref.shape[0]):
+        number = upright(ids_ref[k : k + 1, :].astype(jnp.float32))
+        gate += jnp.where(number == expert, upright(gates_ref[k : k + 1, :]), 0.0)
     high = gate.astype(jnp.bfloat16).astype(jnp.float32)
     middle = (gate - high).astype(jnp.bfloat16).astype(jnp.float32)
     low = gate - high - middle
@@ -197,22 +218,31 @@
     tags = jnp.where(term == 0, high, jnp.where(term == 1, middle, jnp.where(term == 2, low, 0.0)))
     tags = jnp.where(lane == 3 * experts, seq, jnp.where(lane == 3 * experts + 1, place, tags))
     out_ref[:, wide:] = tags.astype(jnp.bfloat16)
+    for copy in copies:
+        copy.wait()
 
 
 def pack_call(text_tokens, panels, panel_target, expert_ids, gate_weights, experts, expert_count):
     rows, wide = expert_ids.shape[0], text_tokens.shape[1]
     width = (3 * experts + 2 + 127) // 128 * 128
-    here = pl.BlockSpec(memory_space=pltpu.VMEM)
+    here, far = pl.BlockSpec(memory_space=pltpu.VMEM), pl.BlockSpec(memory_space=pltpu.HBM)
     return pl.pallas_call(
         functools.partial(pack_kernel, experts, expert_count),
-        in_specs=[here] * 5,
+        in_specs=[far, far, here, here, here],
         out_specs=here,
         out_shape=pltpu.VMEM((rows, wide + width), jnp.bfloat16),
+        scratch_shapes=[pltpu.SemaphoreType.DMA((2,))],
         compiler_params=pltpu.CompilerParams(vmem_limit_bytes=14 * 1024 * 1024),
-    )(text_tokens, panels.reshape(-1, wide), panel_target[None, :], expert_ids, gate_weights)
-
-
-def hidden_kernel(count, rows, first_row, chunk, fetch, *refs):
+    )(
+        distant(text_tokens),
+        distant(panels.reshape(-1, wide)),
+        panel_target[None, :],
+        expert_ids.T,
+        gate_weights.T,
+    )
+
+
+def hidden_kernel(count, pieces, rows, first_row, chunk, fetch, *refs):
     x_refs, refs = refs[:count], refs[count:]
     if fetch == "gate_up":
         far_ref, out_ref, w_ref, x_all, sems = refs
@@ -222,7 +252,7 @@
         w_ref, _, out_ref, x_all = refs[0], refs[1], refs[2], refs[-1]
     ff, wide = w_ref.shape[2:]
     whole, rest = divmod(ff, chunk)
-    total = count * rows
+    total = len(pieces) * rows
 
     def fetched(i, width):
         part = pl.ds(pl.multiple_of(i * chunk, chunk), width)
@@ -235,10 +265,10 @@
             fetched(whole, rest).start()
     if fetch == "down":
         pltpu.make_async_copy(far_ref, down_ref, sems.at[0]).start()
-    for i in range(count):
-        x_all[i * rows : (i + 1) * rows, :] = x_refs[i][:, :wide]
+    for i, (block, start) in enumerate(pieces):
+        x_all[i * rows : (i + 1) * rows, :] = x_refs[block][start : start + rows, :wide]
         at = first_row + i * rows
-        out_ref[at : at + rows, ff:] = x_refs[i][:, wide:]
+        out_ref[at : at + rows, ff:] = x_refs[block][start : start + rows, wide:]
 
     def step(i, width):
         if fetch == "gate_up":
@@ -262,23 +292,17 @@
         pltpu.make_async_copy(far_ref, down_ref, sems.at[0]).wait()
 
 
-def kept(array):
-    return pltpu.with_memory_space_constraint(array, pltpu.VMEM)
-
-
-def distant(array):
-    return pltpu.with_memory_space_constraint(array, pltpu.HBM)
-
-
-def hidden_call(blocks, gate_up_weight, hidden, first_row, all_rows, down_weight=None, last=False):
-    rows, width = blocks[0].shape
+def hidden_call(
+    blocks, pieces, rows, gate_up_weight, hidden, first_row, all_rows, down_weight=None, last=False
+):
+    width = blocks[0].shape[1]
     ff, wide = gate_up_weight.shape[2:]
     count = len(blocks)
     chunk = 256
     here, far = pl.BlockSpec(memory_space=pltpu.VMEM), pl.BlockSpec(memory_space=pltpu.HBM)
     args, in_specs = [kept(block) for block in blocks], [here] * count
     out_shape, aliases = [pltpu.VMEM((all_rows, ff + width - wide), jnp.bfloat16)], {}
-    scratch = [pltpu.VMEM((count * rows, wide), jnp.bfloat16)]
+    scratch = [pltpu.VMEM((len(pieces) * rows, wide), jnp.bfloat16)]
     fetch = None
     if hidden is None:
         fetch = "gate_up"
@@ -297,7 +321,7 @@
             out_shape.append(pltpu.VMEM(down_weight.shape, down_weight.dtype))
             scratch.append(pltpu.SemaphoreType.DMA((1,)))
     return pl.pallas_call(
-        functools.partial(hidden_kernel, count, rows, first_row, chunk, fetch),
+        functools.partial(hidden_kernel, count, pieces, rows, first_row, chunk, fetch),
         in_specs=in_specs,
         out_specs=[here] * len(out_shape),
         out_shape=out_shape,
@@ -305,9 +329,9 @@
         input_output_aliases=aliases,
         compiler_params=pltpu.CompilerParams(vmem_limit_bytes=14 * 1024 * 1024),
         cost_estimate=pl.CostEstimate(
-            flops=4 * count * rows * wide * ff,
-            bytes_accessed=4 * ff * wide + 2 * count * rows * (wide + ff),
-            transcendentals=count * rows * ff,
+            flops=4 * len(pieces) * rows * wide * ff,
+            bytes_accessed=4 * ff * wide + 2 * len(pieces) * rows * (wide + ff),
+            transcendentals=len(pieces) * rows * ff,
         ),
     )(*args)
 
@@ -403,11 +427,7 @@
 ):
     seq_count, expert_count = lax.axis_size("seq"), lax.axis_size("expert")
     ring = Ring(seq_count, expert_count)
-    pan_count, panel_rows, wide = panels.shape
-    text_rows = text_tokens.shape[0]
-    tok_count = expert_ids.shape[0]
-    image_rows = pan_count * panel_rows
-    slot_count = len(ring.slots)
+    text_rows, tok_count = text_tokens.shape[0], expert_ids.shape[0]
     me = lax.axis_index(AXES)
 
     def onward(array):
@@ -431,9 +451,17 @@
     other = across(own)
     own, places = lax.optimization_barrier((own, places))
 
-    all_rows = slot_count * tok_count
-    hidden, gate_up = hidden_call([own, other], gate_up_weight, None, 0, all_rows)
-    hidden, before, after = lax.optimization_barrier((hidden, before, after))
+    all_rows = len(ring.slots) * tok_count
+
+    def whole(blocks):
+        return [(i, 0) for i in range(len(blocks))]
+
+    blocks = [own, other]
+    hidden, gate_up = hidden_call(
+        blocks, whole(blocks), tok_count, gate_up_weight, None, 0, all_rows
+    )
+    hidden, before = lax.optimization_barrier((hidden, before))
+    hidden, after = lax.optimization_barrier((hidden, after))
     cut = tok_count // 2
     for s in range(1, ring.half):
         here = [after, before]
@@ -443,14 +471,19 @@
         before, after = onward(before), back(after)
         first_row = 4 * s * tok_count
         extra = down_weight if s == 1 else None
+        blocks = here + there
         hidden, gate_up, *down = hidden_call(
-            here + there, gate_up, hidden, first_row, all_rows, extra
+            blocks, whole(blocks), tok_count, gate_up, hidden, first_row, all_rows, extra
         )
         if down:
             (down_here,) = down
-        hidden, before, after = lax.optimization_barrier((hidden, before, after))
+        hidden, before = lax.optimization_barrier((hidden, before))
+        hidden, after = lax.optimization_barrier((hidden, after))
     far = [before, after, across(before), across(after)]
-    (hidden,) = hidden_call(far, gate_up, hidden, 2 * tok_count, all_rows, last=True)
+    first_row = 2 * tok_count
+    (hidden,) = hidden_call(
+        far, whole(far), cut, gate_up, hidden, first_row, all_rows, last=True
+    )
 
     def outputs(first_slot, slots):
         mine, others = down_call(
@@ -495,6 +528,7 @@
         slot_rows = experts_all * slot_capacity(tok_count, top_count, experts_all)
         dense = owners * tok_count <= 2 * slot_rows
         ring = dense and mesh.shape["tensor"] == 1 and expert_count == 4 and experts_all == owners
+        ring = ring and seq_count > 2
         body = ring_shards if ring else slot_shards
         return jax.shard_map(
             body,

time: 183 us -> 182 us (level)
  local copies, waits for them, and re-layouts: 5.01 us -> 2.8 us
    unnamed x8 -> x6, local copies, waits for them, and re-layouts: 4.26 us -> 2.05 us
  transfers between devices with their start and end apart: 30 -> 30, of which waited for: 19 -> 19; matrix products, arithmetic and copies ran while one was open for 1% -> 1% of each run, Pallas kernels for 37% -> 38%
where the time goes in v6:
time: 182 us; the launch traced here: 181 us
  Pallas kernels  80.4 us (44%)
  waiting for transfers between devices  74.4 us (41%)
  starting transfers between devices  20.6 us (11%)
  other arithmetic  3.15 us (2%)
  local copies, waits for them, and re-layouts  2.8 us (2%)
    ppermute x8, waiting for transfers between devices, onward(): return lax.ppermute(array, AXES, ring.step(1))  48.3 us
    pallas_call x5, Pallas kernels, hidden_call(): pl.pallas_call(functools.partial(hidden_kernel, count, pieces, rows, firs...  46.2 us
    pallas_call x5, Pallas kernels, down_call(): pl.pallas_call(functools.partial(down_kernel, slots, first_slot, rows, te...  32.9 us
    ppermute x8, waiting for transfers between devices, back(): return lax.ppermute(array, AXES, ring.step(-1))  21.1 us
    ppermute x8, starting transfers between devices, onward(): return lax.ppermute(array, AXES, ring.step(1))  10.7 us
    ppermute x8, starting transfers between devices, back(): return lax.ppermute(array, AXES, ring.step(-1))  6.4 us
    ppermute x14, waiting for transfers between devices, across(): return lax.ppermute(array, AXES, ring.swap())  5.02 us
  transfers between devices with their start and end apart: 30, of which 19 were waited for; matrix products, arithmetic and copies ran while one was open for 1% of the time, Pallas kernels for 38%

profile of v6, /device:TPU:0, one launch (start us, length us, event | category | flops | bytes accessed | tf_op | source)
XLA Modules:
  0.0 181.4 jit_solution(2661255663393873579)
XLA Ops:
  2.1 1.2 shard_map.82.refs_0_
  3.8 2.6 %collective-permute-start.1 = (bf16[160,2688]{1,0:T(8,128)(2,1)S(1)}, bf16[160,2688]{1,0:T(8,128)(2,1)S(1)}, u32[]{:S(2)}, u32[]{:S(2)}) collective-permute-start(bf16[160,2688]{1,0:T(8,128)(2,1)S(1)} %shard_map.82.refs_0_), channel_id=1, source_target_pairs={{0,4},{1,5},{2,0},{3,1},{4,8},{5,9},{6,2},{7,3},{8,12},{9,13},{10,... | collective-permute-start | bytes 2580488 | tf_op jit(solution)/shard_map/ppermute | solution.py:434
  7.1 7.7 %shard_map.83 = (bf16[2560,1536]{1,0:T(8,128)(2,1)S(1)}, bf16[1,2,1408,2560]{3,2,1,0:T(8,128)(2,1)S(1)}) custom-call(bf16[160,2688]{1,0:T(8,128)(2,1)S(1)} %shard_map.82.refs_0_, bf16[160,2688]{1,0:T(8,128)(2,1)S(1)} %collective-permute-done.refs_1_, bf16[1,2,1408,2560]{3,2,1,0:T(8,128)(2,1)} %refs_2_.1), custom_call_target="tpu_custom_call" | custom-call | flops 4613734400 | bytes 16957440 | tf_op jit(solution)/shard_map/pallas_call | solution.py:323
  14.8 11.2 %collective-permute-done.1.refs_1_ = bf16[160,2688]{1,0:T(8,128)(2,1)S(1)} collective-permute-done((bf16[160,2688]{1,0:T(8,128)(2,1)S(1)}, bf16[160,2688]{1,0:T(8,128)(2,1)S(1)}, u32[]{:S(2)}, u32[]{:S(2)}) %collective-permute-start.1) | collective-permute-done | bytes 860192 | tf_op jit(solution)/shard_map/ppermute | solution.py:434
  26.1 1.5 collective-permute-done.2.refs_0_
  28.1 1.6 collective-permute-start.5
  31.2 10.8 %shard_map.84 = (bf16[2560,1536]{1,0:T(8,128)(2,1)S(1)}, bf16[1,2,1408,2560]{3,2,1,0:T(8,128)(2,1)S(1)}, bf16[1,1408,2560]{2,1,0:T(8,128)(2,1)S(1)}) custom-call(bf16[160,2688]{1,0:T(8,128)(2,1)S(1)} %collective-permute-done.2.refs_0_, bf16[160,2688]{1,0:T(8,128)(2,1)S(1)} %collective-permute-done.1.refs_1_, ...), custom_call_target="tpu_custom_call", output_to_operand_aliasing={{0}: (5, {}), {1}: (4, {})} | custom-call | flops 9227468800 | bytes 19496960 | tf_op jit(solution)/shard_map/pallas_call | solution.py:323
  42.1 7.1 %collective-permute-done.5.refs_1_ = bf16[160,2688]{1,0:T(8,128)(2,1)S(1)} collective-permute-done((bf16[160,2688]{1,0:T(8,128)(2,1)S(1)}, bf16[160,2688]{1,0:T(8,128)(2,1)S(1)}, u32[]{:S(2)}, u32[]{:S(2)}) %collective-permute-start.5) | collective-permute-done | bytes 860192 | tf_op jit(solution)/shard_map/ppermute | solution.py:434
  49.1 1.3 collective-permute-done.6.refs_0_
  51.0 1.6 collective-permute-start.9
  54.1 10.8 %shard_map.85 = (bf16[2560,1536]{1,0:T(8,128)(2,1)S(1)}, bf16[1,2,1408,2560]{3,2,1,0:T(8,128)(2,1)S(1)}) custom-call(bf16[160,2688]{1,0:T(8,128)(2,1)S(1)} %collective-permute-done.6.refs_0_, bf16[160,2688]{1,0:T(8,128)(2,1)S(1)} %collective-permute-done.5.refs_1_, ...), custom_call_target="tpu_custom_call", output_to_operand_aliasing={{0}: (5, {}), {1}: (4, {})} | custom-call | flops 9227468800 | bytes 19496960 | tf_op jit(solution)/shard_map/pallas_call | solution.py:323
  64.9 7.1 %collective-permute-done.9.refs_1_ = bf16[160,2688]{1,0:T(8,128)(2,1)S(1)} collective-permute-done((bf16[160,2688]{1,0:T(8,128)(2,1)S(1)}, bf16[160,2688]{1,0:T(8,128)(2,1)S(1)}, u32[]{:S(2)}, u32[]{:S(2)}) %collective-permute-start.9) | collective-permute-done | bytes 860192 | tf_op jit(solution)/shard_map/ppermute | solution.py:434
  72.0 1.3 collective-permute-done.10.refs_0_
  73.9 1.5 collective-permute-start.13
  76.9 10.8 %shard_map.86 = (bf16[2560,1536]{1,0:T(8,128)(2,1)S(1)}, bf16[1,2,1408,2560]{3,2,1,0:T(8,128)(2,1)S(1)}) custom-call(bf16[160,2688]{1,0:T(8,128)(2,1)S(1)} %collective-permute-done.10.refs_0_, bf16[160,2688]{1,0:T(8,128)(2,1)S(1)} %collective-permute-done.9.refs_1_, ...), custom_call_target="tpu_custom_call", output_to_operand_aliasing={{0}: (5, {}), {1}: (4, {})} | custom-call | flops 9227468800 | bytes 19496960 | tf_op jit(solution)/shard_map/pallas_call | solution.py:323
  88.3 1.3 collective-permute-done.15.refs_2_
  90.2 6.1 %shard_map.87.hidden_ref = bf16[2560,1536]{1,0:T(8,128)(2,1)S(1)} custom-call(bf16[80,2688]{1,0:T(8,128)(2,1)S(1)} %collective-permute-done.13.refs_0_, bf16[80,2688]{1,0:T(8,128)(2,1)S(1)} %collective-permute-done.14.refs_1_, bf16[80,2688]{1,0:T(8,128)(2,1)S(1)} %collective-permute-done.15.refs_2_, ...), custom_call_target="tpu_custom_call", output_to_operand_aliasing={{}: (5, {})} | custom-call | flops 4613734400 | bytes 16957440 | tf_op jit(solution)/shard_map/pallas_call | solution.py:323
  96.2 4.7 %shard_map.89 = (bf16[160,2560]{1,0:T(8,128)(2,1)S(1)}, bf16[160,2560]{1,0:T(8,128)(2,1)S(1)}) custom-call(s32[81]{0:T(128)S(1)} %dynamic-slice_bitcast_fusion.places_ref, bf16[2560,1536]{1,0:T(8,128)(2,1)S(1)} %shard_map.87.hidden_ref, bf16[1,1408,2560]{2,1,0:T(8,128)(2,1)S(1)} %get-tuple-element.68.w_ref), custom_call_target="tpu_custom_call" | custom-call | flops 2306867200 | bytes 8847360 | tf_op jit(solution)/shard_map/pallas_call | solution.py:393
  101.1 7.9 %shard_map.90 = (bf16[320,2560]{1,0:T(8,128)(2,1)S(1)}, bf16[320,2560]{1,0:T(8,128)(2,1)S(1)}) custom-call(s32[81]{0:T(128)S(1)} %dynamic-slice_bitcast_fusion.places_ref, bf16[2560,1536]{1,0:T(8,128)(2,1)S(1)} %shard_map.87.hidden_ref, bf16[1,1408,2560]{2,1,0:T(8,128)(2,1)S(1)} %get-tuple-element.68.w_ref), custom_call_target="tpu_custom_call" | custom-call | flops 4613734400 | bytes 10485760 | tf_op jit(solution)/shard_map/pallas_call | solution.py:393
  109.6 1.5 collective-permute-start.19
  111.7 7.9 %shard_map.91 = (bf16[320,2560]{1,0:T(8,128)(2,1)S(1)}, bf16[320,2560]{1,0:T(8,128)(2,1)S(1)}) custom-call(s32[81]{0:T(128)S(1)} %dynamic-slice_bitcast_fusion.places_ref, bf16[2560,1536]{1,0:T(8,128)(2,1)S(1)} %shard_map.87.hidden_ref, bf16[1,1408,2560]{2,1,0:T(8,128)(2,1)S(1)} %get-tuple-element.68.w_ref), custom_call_target="tpu_custom_call" | custom-call | flops 4613734400 | bytes 10485760 | tf_op jit(solution)/shard_map/pallas_call | solution.py:393
  119.7 1.5 collective-permute-done.19
  121.2 1.2 collective-permute-done.26
  123.4 1.6 collective-permute-start.27
  125.0 7.9 %shard_map.92 = (bf16[320,2560]{1,0:T(8,128)(2,1)S(1)}, bf16[320,2560]{1,0:T(8,128)(2,1)S(1)}) custom-call(s32[81]{0:T(128)S(1)} %dynamic-slice_bitcast_fusion.places_ref, bf16[2560,1536]{1,0:T(8,128)(2,1)S(1)} %shard_map.87.hidden_ref, bf16[1,1408,2560]{2,1,0:T(8,128)(2,1)S(1)} %get-tuple-element.68.w_ref), custom_call_target="tpu_custom_call" | custom-call | flops 4613734400 | bytes 10485760 | tf_op jit(solution)/shard_map/pallas_call | solution.py:393
  132.9 9.2 %collective-permute-done.21 = bf16[160,2560]{1,0:T(8,128)(2,1)S(1)} collective-permute-done((bf16[160,2560]{1,0:T(8,128)(2,1)S(1)}, bf16[160,2560]{1,0:T(8,128)(2,1)S(1)}, u32[]{:S(2)}, u32[]{:S(2)}) %collective-permute-start.21) | collective-permute-done | bytes 819232 | tf_op jit(solution)/shard_map/ppermute | solution.py:434
  143.6 1.5 collective-permute-start.28
  145.1 4.7 %shard_map.88 = (bf16[160,2560]{1,0:T(8,128)(2,1)S(1)}, bf16[160,2560]{1,0:T(8,128)(2,1)S(1)}) custom-call(s32[81]{0:T(128)S(1)} %dynamic-slice_bitcast_fusion.places_ref, bf16[2560,1536]{1,0:T(8,128)(2,1)S(1)} %shard_map.87.hidden_ref, bf16[1,1408,2560]{2,1,0:T(8,128)(2,1)S(1)} %get-tuple-element.68.w_ref), custom_call_target="tpu_custom_call" | custom-call | flops 2306867200 | bytes 8847360 | tf_op jit(solution)/shard_map/pallas_call | solution.py:393
  149.9 11.3 %collective-permute-done.23 = bf16[160,2560]{1,0:T(8,128)(2,1)S(1)} collective-permute-done((bf16[160,2560]{1,0:T(8,128)(2,1)S(1)}, bf16[160,2560]{1,0:T(8,128)(2,1)S(1)}, u32[]{:S(2)}, u32[]{:S(2)}) %collective-permute-start.23) | collective-permute-done | bytes 819232 | tf_op jit(solution)/shard_map/ppermute | solution.py:434
  162.2 1.4 collective-permute-start.29
  164.2 15.0 %collective-permute-done.29 = bf16[160,2560]{1,0:T(8,128)(2,1)S(1)} collective-permute-done((bf16[160,2560]{1,0:T(8,128)(2,1)S(1)}, bf16[160,2560]{1,0:T(8,128)(2,1)S(1)}, u32[]{:S(2)}, u32[]{:S(2)}) %collective-permute-start.29) | collective-permute-done | bytes 819232 | tf_op jit(solution)/shard_map/ppermute | solution.py:437
  180.2 1.3 add_convert_fusion
  (53 shorter events, 17.3 us)
Async XLA Ops:
  0.0 0.7 copy-start
  0.7 0.7 copy-start.1
  3.3 3.9 %collective-permute-start = (bf16[160,2688]{1,0:T(8,128)(2,1)S(1)}, bf16[160,2688]{1,0:T(8,128)(2,1)S(1)}, u32[]{:S(2)}, u32[]{:S(2)}) collective-permute-start(bf16[160,2688]{1,0:T(8,128)(2,1)S(1)} %shard_map.82.refs_0_), channel_id=1, source_target_pairs={{0,1},{1,0},{2,3},{3,2},{4,5},{5,4},{6,7},{7,6},{8,9},{9,8},{10,11... | collective-permute-start | bytes 2580488 | tf_op jit(solution)/shard_map/ppermute | solution.py:440
  3.8 22.3 %collective-permute-start.1 = (bf16[160,2688]{1,0:T(8,128)(2,1)S(1)}, bf16[160,2688]{1,0:T(8,128)(2,1)S(1)}, u32[]{:S(2)}, u32[]{:S(2)}) collective-permute-start(bf16[160,2688]{1,0:T(8,128)(2,1)S(1)} %shard_map.82.refs_0_), channel_id=1, source_target_pairs={{0,4},{1,5},{2,0},{3,1},{4,8},{5,9},{6,2},{7,3},{8,12},{9,13},{10,... | collective-permute-start | bytes 2580488 | tf_op jit(solution)/shard_map/ppermute | solution.py:434
  6.4 21.2 %collective-permute-start.2 = (bf16[160,2688]{1,0:T(8,128)(2,1)S(1)}, bf16[160,2688]{1,0:T(8,128)(2,1)S(1)}, u32[]{:S(2)}, u32[]{:S(2)}) collective-permute-start(bf16[160,2688]{1,0:T(8,128)(2,1)S(1)} %shard_map.82.refs_0_), channel_id=1, source_target_pairs={{0,2},{1,3},{2,6},{3,7},{4,0},{5,1},{6,10},{7,11},{8,4},{9,5},{10,... | collective-permute-start | bytes 2580488 | tf_op jit(solution)/shard_map/ppermute | solution.py:437
  27.6 2.5 %collective-permute-start.3 = (bf16[160,2688]{1,0:T(8,128)(2,1)S(1)}, bf16[160,2688]{1,0:T(8,128)(2,1)S(1)}, u32[]{:S(2)}, u32[]{:S(2)}) collective-permute-start(bf16[160,2688]{1,0:T(8,128)(2,1)S(1)} %collective-permute-done.2.refs_0_), channel_id=1, source_target_pairs={{0,1},{1,0},{2,3},{3,2},{4,5},{5,4},{6,7},{7,6},{8,9},{9,8},{10,11... | collective-permute-start | bytes 2580488 | tf_op jit(solution)/shard_map/ppermute | solution.py:440
  27.6 3.6 %collective-permute-start.4 = (bf16[160,2688]{1,0:T(8,128)(2,1)S(1)}, bf16[160,2688]{1,0:T(8,128)(2,1)S(1)}, u32[]{:S(2)}, u32[]{:S(2)}) collective-permute-start(bf16[160,2688]{1,0:T(8,128)(2,1)S(1)} %collective-permute-done.1.refs_1_), channel_id=1, source_target_pairs={{0,1},{1,0},{2,3},{3,2},{4,5},{5,4},{6,7},{7,6},{8,9},{9,8},{10,11... | collective-permute-start | bytes 2580488 | tf_op jit(solution)/shard_map/ppermute | solution.py:440
  28.1 21.0 %collective-permute-start.5 = (bf16[160,2688]{1,0:T(8,128)(2,1)S(1)}, bf16[160,2688]{1,0:T(8,128)(2,1)S(1)}, u32[]{:S(2)}, u32[]{:S(2)}) collective-permute-start(bf16[160,2688]{1,0:T(8,128)(2,1)S(1)} %collective-permute-done.1.refs_1_), channel_id=1, source_target_pairs={{0,4},{1,5},{2,0},{3,1},{4,8},{5,9},{6,2},{7,3},{8,12},{9,13},{10,... | collective-permute-start | bytes 2580488 | tf_op jit(solution)/shard_map/ppermute | solution.py:434
  29.7 20.7 %collective-permute-start.6 = (bf16[160,2688]{1,0:T(8,128)(2,1)S(1)}, bf16[160,2688]{1,0:T(8,128)(2,1)S(1)}, u32[]{:S(2)}, u32[]{:S(2)}) collective-permute-start(bf16[160,2688]{1,0:T(8,128)(2,1)S(1)} %collective-permute-done.2.refs_0_), channel_id=1, source_target_pairs={{0,2},{1,3},{2,6},{3,7},{4,0},{5,1},{6,10},{7,11},{8,4},{9,5},{10,... | collective-permute-start | bytes 2580488 | tf_op jit(solution)/shard_map/ppermute | solution.py:437
  50.4 2.5 %collective-permute-start.7 = (bf16[160,2688]{1,0:T(8,128)(2,1)S(1)}, bf16[160,2688]{1,0:T(8,128)(2,1)S(1)}, u32[]{:S(2)}, u32[]{:S(2)}) collective-permute-start(bf16[160,2688]{1,0:T(8,128)(2,1)S(1)} %collective-permute-done.6.refs_0_), channel_id=1, source_target_pairs={{0,1},{1,0},{2,3},{3,2},{4,5},{5,4},{6,7},{7,6},{8,9},{9,8},{10,11... | collective-permute-start | bytes 2580488 | tf_op jit(solution)/shard_map/ppermute | solution.py:440
  50.4 3.6 %collective-permute-start.8 = (bf16[160,2688]{1,0:T(8,128)(2,1)S(1)}, bf16[160,2688]{1,0:T(8,128)(2,1)S(1)}, u32[]{:S(2)}, u32[]{:S(2)}) collective-permute-start(bf16[160,2688]{1,0:T(8,128)(2,1)S(1)} %collective-permute-done.5.refs_1_), channel_id=1, source_target_pairs={{0,1},{1,0},{2,3},{3,2},{4,5},{5,4},{6,7},{7,6},{8,9},{9,8},{10,11... | collective-permute-start | bytes 2580488 | tf_op jit(solution)/shard_map/ppermute | solution.py:440
  51.0 21.0 %collective-permute-start.9 = (bf16[160,2688]{1,0:T(8,128)(2,1)S(1)}, bf16[160,2688]{1,0:T(8,128)(2,1)S(1)}, u32[]{:S(2)}, u32[]{:S(2)}) collective-permute-start(bf16[160,2688]{1,0:T(8,128)(2,1)S(1)} %collective-permute-done.5.refs_1_), channel_id=1, source_target_pairs={{0,4},{1,5},{2,0},{3,1},{4,8},{5,9},{6,2},{7,3},{8,12},{9,13},{10,... | collective-permute-start | bytes 2580488 | tf_op jit(solution)/shard_map/ppermute | solution.py:434
  52.5 20.7 %collective-permute-start.10 = (bf16[160,2688]{1,0:T(8,128)(2,1)S(1)}, bf16[160,2688]{1,0:T(8,128)(2,1)S(1)}, u32[]{:S(2)}, u32[]{:S(2)}) collective-permute-start(bf16[160,2688]{1,0:T(8,128)(2,1)S(1)} %collective-permute-done.6.refs_0_), channel_id=1, source_target_pairs={{0,2},{1,3},{2,6},{3,7},{4,0},{5,1},{6,10},{7,11},{8,4},{9,5},{10,... | collective-permute-start | bytes 2580488 | tf_op jit(solution)/shard_map/ppermute | solution.py:437
  73.3 2.7 %collective-permute-start.11 = (bf16[160,2688]{1,0:T(8,128)(2,1)S(1)}, bf16[160,2688]{1,0:T(8,128)(2,1)S(1)}, u32[]{:S(2)}, u32[]{:S(2)}) collective-permute-start(bf16[160,2688]{1,0:T(8,128)(2,1)S(1)} %collective-permute-done.10.refs_0_), channel_id=1, source_target_pairs={{0,1},{1,0},{2,3},{3,2},{4,5},{5,4},{6,7},{7,6},{8,9},{9,8},{10,11... | collective-permute-start | bytes 2580488 | tf_op jit(solution)/shard_map/ppermute | solution.py:440
  73.3 3.6 %collective-permute-start.12 = (bf16[160,2688]{1,0:T(8,128)(2,1)S(1)}, bf16[160,2688]{1,0:T(8,128)(2,1)S(1)}, u32[]{:S(2)}, u32[]{:S(2)}) collective-permute-start(bf16[160,2688]{1,0:T(8,128)(2,1)S(1)} %collective-permute-done.9.refs_1_), channel_id=1, source_target_pairs={{0,1},{1,0},{2,3},{3,2},{4,5},{5,4},{6,7},{7,6},{8,9},{9,8},{10,11... | collective-permute-start | bytes 2580488 | tf_op jit(solution)/shard_map/ppermute | solution.py:440
  73.9 13.9 %collective-permute-start.13 = (bf16[80,2688]{1,0:T(8,128)(2,1)S(1)}, bf16[80,2688]{1,0:T(8,128)(2,1)S(1)}, u32[]{:S(2)}, u32[]{:S(2)}) collective-permute-start(bf16[80,2688]{1,0:T(8,128)(2,1)S(1)} %slice.54), channel_id=1, source_target_pairs={{0,4},{1,5},{2,0},{3,1},{4,8},{5,9},{6,2},{7,3},{8,12},{9,13},{10,... | collective-permute-start | bytes 1290248 | tf_op jit(solution)/shard_map/ppermute | solution.py:434
  75.4 12.3 %collective-permute-start.14 = (bf16[80,2688]{1,0:T(8,128)(2,1)S(1)}, bf16[80,2688]{1,0:T(8,128)(2,1)S(1)}, u32[]{:S(2)}, u32[]{:S(2)}) collective-permute-start(bf16[80,2688]{1,0:T(8,128)(2,1)S(1)} %slice.55), channel_id=1, source_target_pairs={{0,2},{1,3},{2,6},{3,7},{4,0},{5,1},{6,10},{7,11},{8,4},{9,5},{10,... | collective-permute-start | bytes 1290248 | tf_op jit(solution)/shard_map/ppermute | solution.py:437
  87.7 1.8 %collective-permute-start.15 = (bf16[80,2688]{1,0:T(8,128)(2,1)S(1)}, bf16[80,2688]{1,0:T(8,128)(2,1)S(1)}, u32[]{:S(2)}, u32[]{:S(2)}) collective-permute-start(bf16[80,2688]{1,0:T(8,128)(2,1)S(1)} %collective-permute-done.13.refs_0_), channel_id=1, source_target_pairs={{0,1},{1,0},{2,3},{3,2},{4,5},{5,4},{6,7},{7,6},{8,9},{9,8},{10,11... | collective-permute-start | bytes 1290248 | tf_op jit(solution)/shard_map/ppermute | solution.py:440
  87.9 2.3 %collective-permute-start.16 = (bf16[80,2688]{1,0:T(8,128)(2,1)S(1)}, bf16[80,2688]{1,0:T(8,128)(2,1)S(1)}, u32[]{:S(2)}, u32[]{:S(2)}) collective-permute-start(bf16[80,2688]{1,0:T(8,128)(2,1)S(1)} %collective-permute-done.14.refs_1_), channel_id=1, source_target_pairs={{0,1},{1,0},{2,3},{3,2},{4,5},{5,4},{6,7},{7,6},{8,9},{9,8},{10,11... | collective-permute-start | bytes 1290248 | tf_op jit(solution)/shard_map/ppermute | solution.py:440
  100.9 8.5 %collective-permute-start.18 = (bf16[160,2560]{1,0:T(8,128)(2,1)S(1)}, bf16[160,2560]{1,0:T(8,128)(2,1)S(1)}, u32[]{:S(2)}, u32[]{:S(2)}) collective-permute-start(bf16[160,2560]{1,0:T(8,128)(2,1)S(1)} %get-tuple-element.72), channel_id=1, source_target_pairs={{0,1},{1,0},{2,3},{3,2},{4,5},{5,4},{6,7},{7,6},{8,9},{9,8},{10,11... | collective-permute-start | bytes 2457608 | tf_op jit(solution)/shard_map/ppermute | solution.py:440
  109.0 13.4 %collective-permute-start.20 = (bf16[320,2560]{1,0:T(8,128)(2,1)S(1)}, bf16[320,2560]{1,0:T(8,128)(2,1)S(1)}, u32[]{:S(2)}, u32[]{:S(2)}) collective-permute-start(bf16[320,2560]{1,0:T(8,128)(2,1)S(1)} %get-tuple-element.74), channel_id=1, source_target_pairs={{0,1},{1,0},{2,3},{3,2},{4,5},{5,4},{6,7},{7,6},{8,9},{9,8},{10,11... | collective-permute-start | bytes 4915208 | tf_op jit(solution)/shard_map/ppermute | solution.py:440
  109.6 11.6 %collective-permute-start.19 = (bf16[80,2560]{1,0:T(8,128)(2,1)S(1)}, bf16[80,2560]{1,0:T(8,128)(2,1)S(1)}, u32[]{:S(2)}, u32[]{:S(2)}) collective-permute-start(bf16[80,2560]{1,0:T(8,128)(2,1)S(1)} %get-tuple-element.85), channel_id=1, source_target_pairs={{0,4},{1,5},{2,0},{3,1},{4,8},{5,9},{6,2},{7,3},{8,12},{9,13},{10,... | collective-permute-start | bytes 1228808 | tf_op jit(solution)/shard_map/ppermute | solution.py:434
  111.2 11.2 %collective-permute-start.26 = (bf16[80,2560]{1,0:T(8,128)(2,1)S(1)}, bf16[80,2560]{1,0:T(8,128)(2,1)S(1)}, u32[]{:S(2)}, u32[]{:S(2)}) collective-permute-start(bf16[80,2560]{1,0:T(8,128)(2,1)S(1)} %get-tuple-element.86), channel_id=1, source_target_pairs={{0,2},{1,3},{2,6},{3,7},{4,0},{5,1},{6,10},{7,11},{8,4},{9,5},{10,... | collective-permute-start | bytes 1228808 | tf_op jit(solution)/shard_map/ppermute | solution.py:437
  119.6 13.3 %collective-permute-start.22 = (bf16[320,2560]{1,0:T(8,128)(2,1)S(1)}, bf16[320,2560]{1,0:T(8,128)(2,1)S(1)}, u32[]{:S(2)}, u32[]{:S(2)}) collective-permute-start(bf16[320,2560]{1,0:T(8,128)(2,1)S(1)} %get-tuple-element.76), channel_id=1, source_target_pairs={{0,1},{1,0},{2,3},{3,2},{4,5},{5,4},{6,7},{7,6},{8,9},{9,8},{10,11... | collective-permute-start | bytes 4915208 | tf_op jit(solution)/shard_map/ppermute | solution.py:440
  122.9 19.2 %collective-permute-start.21 = (bf16[160,2560]{1,0:T(8,128)(2,1)S(1)}, bf16[160,2560]{1,0:T(8,128)(2,1)S(1)}, u32[]{:S(2)}, u32[]{:S(2)}) collective-permute-start(bf16[160,2560]{1,0:T(8,128)(2,1)S(1)} %get-tuple-element.83), channel_id=1, source_target_pairs={{0,4},{1,5},{2,0},{3,1},{4,8},{5,9},{6,2},{7,3},{8,12},{9,13},{10,... | collective-permute-start | bytes 2457608 | tf_op jit(solution)/shard_map/ppermute | solution.py:434
  123.4 19.0 %collective-permute-start.27 = (bf16[160,2560]{1,0:T(8,128)(2,1)S(1)}, bf16[160,2560]{1,0:T(8,128)(2,1)S(1)}, u32[]{:S(2)}, u32[]{:S(2)}) collective-permute-start(bf16[160,2560]{1,0:T(8,128)(2,1)S(1)} %get-tuple-element.84), channel_id=1, source_target_pairs={{0,2},{1,3},{2,6},{3,7},{4,0},{5,1},{6,10},{7,11},{8,4},{9,5},{10,... | collective-permute-start | bytes 2457608 | tf_op jit(solution)/shard_map/ppermute | solution.py:437
  132.9 17.0 %collective-permute-start.24 = (bf16[320,2560]{1,0:T(8,128)(2,1)S(1)}, bf16[320,2560]{1,0:T(8,128)(2,1)S(1)}, u32[]{:S(2)}, u32[]{:S(2)}) collective-permute-start(bf16[320,2560]{1,0:T(8,128)(2,1)S(1)} %get-tuple-element.78), channel_id=1, source_target_pairs={{0,1},{1,0},{2,3},{3,2},{4,5},{5,4},{6,7},{7,6},{8,9},{9,8},{10,11... | collective-permute-start | bytes 4915208 | tf_op jit(solution)/shard_map/ppermute | solution.py:440
  143.0 18.1 %collective-permute-start.23 = (bf16[160,2560]{1,0:T(8,128)(2,1)S(1)}, bf16[160,2560]{1,0:T(8,128)(2,1)S(1)}, u32[]{:S(2)}, u32[]{:S(2)}) collective-permute-start(bf16[160,2560]{1,0:T(8,128)(2,1)S(1)} %get-tuple-element.81), channel_id=1, source_target_pairs={{0,4},{1,5},{2,0},{3,1},{4,8},{5,9},{6,2},{7,3},{8,12},{9,13},{10,... | collective-permute-start | bytes 2457608 | tf_op jit(solution)/shard_map/ppermute | solution.py:434
  143.6 17.9 %collective-permute-start.28 = (bf16[160,2560]{1,0:T(8,128)(2,1)S(1)}, bf16[160,2560]{1,0:T(8,128)(2,1)S(1)}, u32[]{:S(2)}, u32[]{:S(2)}) collective-permute-start(bf16[160,2560]{1,0:T(8,128)(2,1)S(1)} %get-tuple-element.82), channel_id=1, source_target_pairs={{0,2},{1,3},{2,6},{3,7},{4,0},{5,1},{6,10},{7,11},{8,4},{9,5},{10,... | collective-permute-start | bytes 2457608 | tf_op jit(solution)/shard_map/ppermute | solution.py:437
  149.8 14.5 %collective-permute-start.17 = (bf16[160,2560]{1,0:T(8,128)(2,1)S(1)}, bf16[160,2560]{1,0:T(8,128)(2,1)S(1)}, u32[]{:S(2)}, u32[]{:S(2)}) collective-permute-start(bf16[160,2560]{1,0:T(8,128)(2,1)S(1)} %get-tuple-element.70), channel_id=1, source_target_pairs={{0,1},{1,0},{2,3},{3,2},{4,5},{5,4},{6,7},{7,6},{8,9},{9,8},{10,11... | collective-permute-start | bytes 2457608 | tf_op jit(solution)/shard_map/ppermute | solution.py:440
  162.2 17.1 %collective-permute-start.29 = (bf16[160,2560]{1,0:T(8,128)(2,1)S(1)}, bf16[160,2560]{1,0:T(8,128)(2,1)S(1)}, u32[]{:S(2)}, u32[]{:S(2)}) collective-permute-start(bf16[160,2560]{1,0:T(8,128)(2,1)S(1)} %get-tuple-element.80), channel_id=1, source_target_pairs={{0,2},{1,3},{2,6},{3,7},{4,0},{5,1},{6,10},{7,11},{8,4},{9,5},{10,... | collective-permute-start | bytes 2457608 | tf_op jit(solution)/shard_map/ppermute | solution.py:437
  163.5 16.6 %collective-permute-start.25 = (bf16[160,2560]{1,0:T(8,128)(2,1)S(1)}, bf16[160,2560]{1,0:T(8,128)(2,1)S(1)}, u32[]{:S(2)}, u32[]{:S(2)}) collective-permute-start(bf16[160,2560]{1,0:T(8,128)(2,1)S(1)} %get-tuple-element.79), channel_id=1, source_target_pairs={{0,4},{1,5},{2,0},{3,1},{4,8},{5,9},{6,2},{7,3},{8,12},{9,13},{10,... | collective-permute-start | bytes 2457608 | tf_op jit(solution)/shard_map/ppermute | solution.py:434
  (1 other events, 0.7 us)

commit v7 on v6

--- a/solution.py
+++ b/solution.py
@@ -337,11 +337,11 @@
 
 
 def down_kernel(
-    slots, first_slot, rows, text_rows, seq_count, experts, chunk, places_ref, hidden_ref, w_ref,
-    own_ref, other_ref, column, picked, scale,
+    groups, rows, text_rows, seq_count, experts, chunk, places_ref, hidden_ref, w_ref, *refs
 ):
+    out_refs, (column, picked, scale) = refs[:-3], refs[-3:]
+    slots = [slot for group in groups for slot in group]
     image_rows = rows - text_rows
-    half = slots * rows // 2
     slot_total = hidden_ref.shape[0] // rows
     ff = w_ref.shape[1]
     width = hidden_ref.shape[1] - ff
@@ -351,18 +351,18 @@
     place_of = jnp.where(lane == 3 * experts, float(image_rows), 0.0)
     place_of = jnp.where(lane == 3 * experts + 1, 1.0, place_of)
     wanted = lax.broadcasted_iota(jnp.int32, (1, image_rows), 1)
-    for j in range(slots):
-        at = (first_slot + j) * rows
+    for j, slot in enumerate(slots):
+        at = slot * rows
         picked[j * rows : j * rows + text_rows, :] = hidden_ref[at : at + text_rows, :ff]
         for z in range(seq_count):
-            source = places_ref[1 + slot_total + (first_slot + j) * seq_count + z]
+            source = places_ref[1 + slot_total + slot * seq_count + z]
             start = pl.multiple_of(source * rows + text_rows, 16)
             column[z * image_rows : (z + 1) * image_rows, :] = hidden_ref[
                 pl.ds(start, image_rows), :
             ]
         place = column[:, ff:].astype(jnp.float32) * place_of
         place = jnp.sum(place, axis=1, keepdims=True)
-        first = places_ref[1 + first_slot + j] * image_rows
+        first = places_ref[1 + slot] * image_rows
         match = jnp.where(place == (wanted + first).astype(jnp.float32), 1.0, 0.0)
         rows_here = lax.dot_general(
             match.astype(jnp.bfloat16),
@@ -380,36 +380,34 @@
         result = jnp.dot(picked[...], w_ref[0, :, part], preferred_element_type=jnp.float32)
         scaled = result.astype(jnp.bfloat16).astype(jnp.float32) * scale[...]
         scaled = scaled.astype(jnp.bfloat16)
-        own_ref[:, part] = scaled[:half]
-        other_ref[:, part] = scaled[half:]
-
-
-def down_call(
-    hidden, places, down_weight, first_slot, slots, rows, text_rows, seq_count, experts
-):
+        start = 0
+        for out_ref in out_refs:
+            out_ref[:, part] = scaled[start : start + out_ref.shape[0]]
+            start += out_ref.shape[0]
+
+
+def down_call(hidden, places, down_weight, groups, rows, text_rows, seq_count, experts):
     _, ff, wide = down_weight.shape
-    half = slots * rows // 2
+    total = sum(len(group) for group in groups) * rows
     here = pl.BlockSpec(memory_space=pltpu.VMEM)
     return pl.pallas_call(
-        functools.partial(
-            down_kernel, slots, first_slot, rows, text_rows, seq_count, experts, 512
-        ),
+        functools.partial(down_kernel, groups, rows, text_rows, seq_count, experts, 512),
         grid_spec=pltpu.PrefetchScalarGridSpec(
             num_scalar_prefetch=1,
             grid=(1,),
             in_specs=[here] * 2,
-            out_specs=[here] * 2,
+            out_specs=[here] * len(groups),
             scratch_shapes=[
                 pltpu.VMEM((seq_count * (rows - text_rows), hidden.shape[1]), jnp.bfloat16),
-                pltpu.VMEM((slots * rows, ff), jnp.bfloat16),
-                pltpu.VMEM((slots * rows, 1), jnp.float32),
+                pltpu.VMEM((total, ff), jnp.bfloat16),
+                pltpu.VMEM((total, 1), jnp.float32),
             ],
         ),
-        out_shape=[pltpu.VMEM((half, wide), jnp.bfloat16)] * 2,
+        out_shape=[pltpu.VMEM((len(group) * rows, wide), jnp.bfloat16) for group in groups],
         compiler_params=pltpu.CompilerParams(vmem_limit_bytes=14 * 1024 * 1024),
         cost_estimate=pl.CostEstimate(
-            flops=2 * slots * rows * wide * ff,
-            bytes_accessed=2 * ff * wide + 2 * slots * rows * wide,
+            flops=2 * total * wide * ff,
+            bytes_accessed=2 * ff * wide + 2 * total * wide,
             transcendentals=0,
         ),
     )(places, kept(hidden), kept(down_weight))
@@ -485,27 +483,30 @@
         far, whole(far), cut, gate_up, hidden, first_row, all_rows, last=True
     )
 
-    def outputs(first_slot, slots):
-        mine, others = down_call(
-            hidden, places, down_here, first_slot, slots, tok_count, text_rows, seq_count,
-            ring.devices,
+    def outputs(*groups):
+        return down_call(
+            hidden, places, down_here, groups, tok_count, text_rows, seq_count, ring.devices
         )
+
+    def summed(kind):
+        if kind == ring.half:
+            mine, others = outputs((2,), (3,))
+        else:
+            slots = range(4 * kind, 4 * kind + 4) if kind else range(2)
+            (others,) = outputs(tuple(slots[len(slots) // 2 :]))
+            (mine,) = outputs(tuple(slots[: len(slots) // 2]))
         return mine, across(others)
 
-    mine, swapped = outputs(2, 2)
-    leaving = add_up(mine[:cut], swapped[:cut]), add_up(mine[cut:], swapped[cut:])
-    for s in range(ring.half - 1, -1, -1):
-        ahead, behind = onward(leaving[0]), back(leaving[1])
-        if s == ring.half - 1:
-            ahead = jnp.pad(ahead, ((0, tok_count - cut), (0, 0)))
-            behind = jnp.pad(behind, ((cut, 0), (0, 0)))
-        if s:
-            mine, swapped = outputs(4 * s, 4)
-            leaving = (
-                add_up(ahead, mine[:tok_count], swapped[:tok_count]),
-                add_up(behind, mine[tok_count:], swapped[tok_count:]),
-            )
-    mine, swapped = outputs(0, 2)
+    mine, swapped = summed(ring.half)
+    ahead = onward(add_up(mine[:cut], swapped[:cut]))
+    behind = back(add_up(mine[cut:], swapped[cut:]))
+    ahead = jnp.pad(ahead, ((0, tok_count - cut), (0, 0)))
+    behind = jnp.pad(behind, ((cut, 0), (0, 0)))
+    for s in range(ring.half - 1, 0, -1):
+        mine, swapped = summed(s)
+        ahead = onward(add_up(ahead, mine[:tok_count], swapped[:tok_count]))
+        behind = back(add_up(behind, mine[tok_count:], swapped[tok_count:]))
+    mine, swapped = summed(0)
     return add_up(mine, swapped, ahead, behind)
 
 

time: 182 us -> 182 us (level)
  Pallas kernels: 80.4 us -> 86.6 us
  waiting for transfers between devices: 74.4 us -> 68.7 us
    pallas_call x5 -> x9, Pallas kernels: 32.9 us -> 39.2 us  [down_call(): pl.pallas_call(functools.partial(down_kernel, groups, rows, text_rows, se...]
    ppermute x8, waiting for transfers between devices: 48.3 us -> 43.7 us  [onward(): return lax.ppermute(array, AXES, ring.step(1))]
  transfers between devices with their start and end apart: 30 -> 30, of which waited for: 19 -> 18; matrix products, arithmetic and copies ran while one was open for 1% -> 1% of each run, Pallas kernels for 38% -> 41%
where the time goes in v7:
time: 182 us
  Pallas kernels  86.6 us (48%)
  waiting for transfers between devices  68.7 us (38%)
  starting transfers between devices  20.6 us (11%)
  other arithmetic  3.15 us (2%)
  local copies, waits for them, and re-layouts  2.8 us (2%)
    pallas_call x5, Pallas kernels, hidden_call(): pl.pallas_call(functools.partial(hidden_kernel, count, pieces, rows, firs...  46.2 us
    ppermute x8, waiting for transfers between devices, onward(): return lax.ppermute(array, AXES, ring.step(1))  43.7 us
    pallas_call x9, Pallas kernels, down_call(): pl.pallas_call(functools.partial(down_kernel, groups, rows, text_rows, se...  39.2 us
    ppermute x8, waiting for transfers between devices, back(): return lax.ppermute(array, AXES, ring.step(-1))  19.9 us
    ppermute x8, starting transfers between devices, onward(): return lax.ppermute(array, AXES, ring.step(1))  10.5 us
    ppermute x8, starting transfers between devices, back(): return lax.ppermute(array, AXES, ring.step(-1))  6.6 us
    ppermute x14, waiting for transfers between devices, across(): return lax.ppermute(array, AXES, ring.swap())  5.02 us
  transfers between devices with their start and end apart: 30, of which 18 were waited for; matrix products, arithmetic and copies ran while one was open for 1% of the time, Pallas kernels for 41%

profile of v7, /device:TPU:0, one launch (start us, length us, event | category | flops | bytes accessed | tf_op | source)
XLA Modules:
  0.0 182.0 jit_solution(9984122471955997612)
XLA Ops:
  3.8 2.6 %collective-permute-start.1 = (bf16[160,2688]{1,0:T(8,128)(2,1)S(1)}, bf16[160,2688]{1,0:T(8,128)(2,1)S(1)}, u32[]{:S(2)}, u32[]{:S(2)}) collective-permute-start(bf16[160,2688]{1,0:T(8,128)(2,1)S(1)} %shard_map.82.refs_0_), channel_id=1, source_target_pairs={{0,4},{1,5},{2,0},{3,1},{4,8},{5,9},{6,2},{7,3},{8,12},{9,13},{10,... | collective-permute-start | bytes 2580488 | tf_op jit(solution)/shard_map/ppermute | solution.py:432
  7.1 7.7 %shard_map.83 = (bf16[2560,1536]{1,0:T(8,128)(2,1)S(1)}, bf16[1,2,1408,2560]{3,2,1,0:T(8,128)(2,1)S(1)}) custom-call(bf16[160,2688]{1,0:T(8,128)(2,1)S(1)} %shard_map.82.refs_0_, bf16[160,2688]{1,0:T(8,128)(2,1)S(1)} %collective-permute-done.refs_1_, bf16[1,2,1408,2560]{3,2,1,0:T(8,128)(2,1)} %refs_2_.1), custom_call_target="tpu_custom_call" | custom-call | flops 4613734400 | bytes 16957440 | tf_op jit(solution)/shard_map/pallas_call | solution.py:323
  14.8 11.2 %collective-permute-done.1.refs_1_ = bf16[160,2688]{1,0:T(8,128)(2,1)S(1)} collective-permute-done((bf16[160,2688]{1,0:T(8,128)(2,1)S(1)}, bf16[160,2688]{1,0:T(8,128)(2,1)S(1)}, u32[]{:S(2)}, u32[]{:S(2)}) %collective-permute-start.1) | collective-permute-done | bytes 860192 | tf_op jit(solution)/shard_map/ppermute | solution.py:432
  26.1 1.5 collective-permute-done.2.refs_0_
  28.1 1.6 collective-permute-start.5
  31.2 10.8 %shard_map.84 = (bf16[2560,1536]{1,0:T(8,128)(2,1)S(1)}, bf16[1,2,1408,2560]{3,2,1,0:T(8,128)(2,1)S(1)}, bf16[1,1408,2560]{2,1,0:T(8,128)(2,1)S(1)}) custom-call(bf16[160,2688]{1,0:T(8,128)(2,1)S(1)} %collective-permute-done.2.refs_0_, bf16[160,2688]{1,0:T(8,128)(2,1)S(1)} %collective-permute-done.1.refs_1_, ...), custom_call_target="tpu_custom_call", output_to_operand_aliasing={{0}: (5, {}), {1}: (4, {})} | custom-call | flops 9227468800 | bytes 19496960 | tf_op jit(solution)/shard_map/pallas_call | solution.py:323
  42.1 7.1 %collective-permute-done.5.refs_1_ = bf16[160,2688]{1,0:T(8,128)(2,1)S(1)} collective-permute-done((bf16[160,2688]{1,0:T(8,128)(2,1)S(1)}, bf16[160,2688]{1,0:T(8,128)(2,1)S(1)}, u32[]{:S(2)}, u32[]{:S(2)}) %collective-permute-start.5) | collective-permute-done | bytes 860192 | tf_op jit(solution)/shard_map/ppermute | solution.py:432
  49.1 1.3 collective-permute-done.6.refs_0_
  51.0 1.6 collective-permute-start.9
  54.1 10.8 %shard_map.85 = (bf16[2560,1536]{1,0:T(8,128)(2,1)S(1)}, bf16[1,2,1408,2560]{3,2,1,0:T(8,128)(2,1)S(1)}) custom-call(bf16[160,2688]{1,0:T(8,128)(2,1)S(1)} %collective-permute-done.6.refs_0_, bf16[160,2688]{1,0:T(8,128)(2,1)S(1)} %collective-permute-done.5.refs_1_, ...), custom_call_target="tpu_custom_call", output_to_operand_aliasing={{0}: (5, {}), {1}: (4, {})} | custom-call | flops 9227468800 | bytes 19496960 | tf_op jit(solution)/shard_map/pallas_call | solution.py:323
  64.9 7.1 %collective-permute-done.9.refs_1_ = bf16[160,2688]{1,0:T(8,128)(2,1)S(1)} collective-permute-done((bf16[160,2688]{1,0:T(8,128)(2,1)S(1)}, bf16[160,2688]{1,0:T(8,128)(2,1)S(1)}, u32[]{:S(2)}, u32[]{:S(2)}) %collective-permute-start.9) | collective-permute-done | bytes 860192 | tf_op jit(solution)/shard_map/ppermute | solution.py:432
  72.0 1.3 collective-permute-done.10.refs_0_
  73.9 1.5 collective-permute-start.13
  76.9 10.8 %shard_map.86 = (bf16[2560,1536]{1,0:T(8,128)(2,1)S(1)}, bf16[1,2,1408,2560]{3,2,1,0:T(8,128)(2,1)S(1)}) custom-call(bf16[160,2688]{1,0:T(8,128)(2,1)S(1)} %collective-permute-done.10.refs_0_, bf16[160,2688]{1,0:T(8,128)(2,1)S(1)} %collective-permute-done.9.refs_1_, ...), custom_call_target="tpu_custom_call", output_to_operand_aliasing={{0}: (5, {}), {1}: (4, {})} | custom-call | flops 9227468800 | bytes 19496960 | tf_op jit(solution)/shard_map/pallas_call | solution.py:323
  90.2 6.1 %shard_map.87.hidden_ref = bf16[2560,1536]{1,0:T(8,128)(2,1)S(1)} custom-call(bf16[80,2688]{1,0:T(8,128)(2,1)S(1)} %collective-permute-done.13.refs_0_, bf16[80,2688]{1,0:T(8,128)(2,1)S(1)} %collective-permute-done.14.refs_1_, bf16[80,2688]{1,0:T(8,128)(2,1)S(1)} %collective-permute-done.15.refs_2_, ...), custom_call_target="tpu_custom_call", output_to_operand_aliasing={{}: (5, {})} | custom-call | flops 4613734400 | bytes 16957440 | tf_op jit(solution)/shard_map/pallas_call | solution.py:323
  96.2 4.7 %shard_map.90 = (bf16[160,2560]{1,0:T(8,128)(2,1)S(1)}, bf16[160,2560]{1,0:T(8,128)(2,1)S(1)}) custom-call(s32[81]{0:T(128)S(1)} %dynamic-slice_bitcast_fusion.places_ref, bf16[2560,1536]{1,0:T(8,128)(2,1)S(1)} %shard_map.87.hidden_ref, bf16[1,1408,2560]{2,1,0:T(8,128)(2,1)S(1)} %get-tuple-element.60.w_ref), custom_call_target="tpu_custom_call" | custom-call | flops 2306867200 | bytes 8847360 | tf_op jit(solution)/shard_map/pallas_call | solution.py:393
  101.1 4.7 %shard_map.92 = bf16[320,2560]{1,0:T(8,128)(2,1)S(1)} custom-call(s32[81]{0:T(128)S(1)} %dynamic-slice_bitcast_fusion.places_ref, bf16[2560,1536]{1,0:T(8,128)(2,1)S(1)} %shard_map.87.hidden_ref, bf16[1,1408,2560]{2,1,0:T(8,128)(2,1)S(1)} %get-tuple-element.60.w_ref), custom_call_target="tpu_custom_call" | custom-call | flops 2306867200 | bytes 8847360 | tf_op jit(solution)/shard_map/pallas_call | solution.py:393
  106.5 1.5 collective-permute-start.19
  108.5 4.7 %shard_map.94 = bf16[320,2560]{1,0:T(8,128)(2,1)S(1)} custom-call(s32[81]{0:T(128)S(1)} %dynamic-slice_bitcast_fusion.places_ref, bf16[2560,1536]{1,0:T(8,128)(2,1)S(1)} %shard_map.87.hidden_ref, bf16[1,1408,2560]{2,1,0:T(8,128)(2,1)S(1)} %get-tuple-element.60.w_ref), custom_call_target="tpu_custom_call" | custom-call | flops 2306867200 | bytes 8847360 | tf_op jit(solution)/shard_map/pallas_call | solution.py:393
  113.3 4.7 %shard_map.91 = bf16[320,2560]{1,0:T(8,128)(2,1)S(1)} custom-call(s32[81]{0:T(128)S(1)} %dynamic-slice_bitcast_fusion.places_ref, bf16[2560,1536]{1,0:T(8,128)(2,1)S(1)} %shard_map.87.hidden_ref, bf16[1,1408,2560]{2,1,0:T(8,128)(2,1)S(1)} %get-tuple-element.60.w_ref), custom_call_target="tpu_custom_call" | custom-call | flops 2306867200 | bytes 8847360 | tf_op jit(solution)/shard_map/pallas_call | solution.py:393
  120.2 1.6 collective-permute-start.27
  121.8 4.7 %shard_map.96 = bf16[320,2560]{1,0:T(8,128)(2,1)S(1)} custom-call(s32[81]{0:T(128)S(1)} %dynamic-slice_bitcast_fusion.places_ref, bf16[2560,1536]{1,0:T(8,128)(2,1)S(1)} %shard_map.87.hidden_ref, bf16[1,1408,2560]{2,1,0:T(8,128)(2,1)S(1)} %get-tuple-element.60.w_ref), custom_call_target="tpu_custom_call" | custom-call | flops 2306867200 | bytes 8847360 | tf_op jit(solution)/shard_map/pallas_call | solution.py:393
  126.6 4.7 %shard_map.93 = bf16[320,2560]{1,0:T(8,128)(2,1)S(1)} custom-call(s32[81]{0:T(128)S(1)} %dynamic-slice_bitcast_fusion.places_ref, bf16[2560,1536]{1,0:T(8,128)(2,1)S(1)} %shard_map.87.hidden_ref, bf16[1,1408,2560]{2,1,0:T(8,128)(2,1)S(1)} %get-tuple-element.60.w_ref), custom_call_target="tpu_custom_call" | custom-call | flops 2306867200 | bytes 8847360 | tf_op jit(solution)/shard_map/pallas_call | solution.py:393
  131.3 7.9 %collective-permute-done.21 = bf16[160,2560]{1,0:T(8,128)(2,1)S(1)} collective-permute-done((bf16[160,2560]{1,0:T(8,128)(2,1)S(1)}, bf16[160,2560]{1,0:T(8,128)(2,1)S(1)}, u32[]{:S(2)}, u32[]{:S(2)}) %collective-permute-start.21) | collective-permute-done | bytes 819232 | tf_op jit(solution)/shard_map/ppermute | solution.py:432
  141.5 1.6 collective-permute-start.28
  143.1 3.2 %shard_map.89 = bf16[160,2560]{1,0:T(8,128)(2,1)S(1)} custom-call(s32[81]{0:T(128)S(1)} %dynamic-slice_bitcast_fusion.places_ref, bf16[2560,1536]{1,0:T(8,128)(2,1)S(1)} %shard_map.87.hidden_ref, bf16[1,1408,2560]{2,1,0:T(8,128)(2,1)S(1)} %get-tuple-element.60.w_ref), custom_call_target="tpu_custom_call" | custom-call | flops 1153433600 | bytes 8028160 | tf_op jit(solution)/shard_map/pallas_call | solution.py:393
  146.4 4.7 %shard_map.95 = bf16[320,2560]{1,0:T(8,128)(2,1)S(1)} custom-call(s32[81]{0:T(128)S(1)} %dynamic-slice_bitcast_fusion.places_ref, bf16[2560,1536]{1,0:T(8,128)(2,1)S(1)} %shard_map.87.hidden_ref, bf16[1,1408,2560]{2,1,0:T(8,128)(2,1)S(1)} %get-tuple-element.60.w_ref), custom_call_target="tpu_custom_call" | custom-call | flops 2306867200 | bytes 8847360 | tf_op jit(solution)/shard_map/pallas_call | solution.py:393
  151.1 9.3 %collective-permute-done.23 = bf16[160,2560]{1,0:T(8,128)(2,1)S(1)} collective-permute-done((bf16[160,2560]{1,0:T(8,128)(2,1)S(1)}, bf16[160,2560]{1,0:T(8,128)(2,1)S(1)}, u32[]{:S(2)}, u32[]{:S(2)}) %collective-permute-start.23) | collective-permute-done | bytes 819232 | tf_op jit(solution)/shard_map/ppermute | solution.py:432
  161.4 1.5 collective-permute-start.29
  163.4 3.2 %shard_map.88 = bf16[160,2560]{1,0:T(8,128)(2,1)S(1)} custom-call(s32[81]{0:T(128)S(1)} %dynamic-slice_bitcast_fusion.places_ref, bf16[2560,1536]{1,0:T(8,128)(2,1)S(1)} %shard_map.87.hidden_ref, bf16[1,1408,2560]{2,1,0:T(8,128)(2,1)S(1)} %get-tuple-element.60.w_ref), custom_call_target="tpu_custom_call" | custom-call | flops 1153433600 | bytes 8028160 | tf_op jit(solution)/shard_map/pallas_call | solution.py:393
  166.7 13.1 %collective-permute-done.29 = bf16[160,2560]{1,0:T(8,128)(2,1)S(1)} collective-permute-done((bf16[160,2560]{1,0:T(8,128)(2,1)S(1)}, bf16[160,2560]{1,0:T(8,128)(2,1)S(1)}, u32[]{:S(2)}, u32[]{:S(2)}) %collective-permute-start.29) | collective-permute-done | bytes 819232 | tf_op jit(solution)/shard_map/ppermute | solution.py:435
  180.7 1.3 add_convert_fusion
  (57 shorter events, 21.7 us)
Async XLA Ops:
  0.0 0.7 copy-start
  0.7 0.7 copy-start.1
  3.3 3.9 %collective-permute-start = (bf16[160,2688]{1,0:T(8,128)(2,1)S(1)}, bf16[160,2688]{1,0:T(8,128)(2,1)S(1)}, u32[]{:S(2)}, u32[]{:S(2)}) collective-permute-start(bf16[160,2688]{1,0:T(8,128)(2,1)S(1)} %shard_map.82.refs_0_), channel_id=1, source_target_pairs={{0,1},{1,0},{2,3},{3,2},{4,5},{5,4},{6,7},{7,6},{8,9},{9,8},{10,11... | collective-permute-start | bytes 2580488 | tf_op jit(solution)/shard_map/ppermute | solution.py:438
  3.8 22.3 %collective-permute-start.1 = (bf16[160,2688]{1,0:T(8,128)(2,1)S(1)}, bf16[160,2688]{1,0:T(8,128)(2,1)S(1)}, u32[]{:S(2)}, u32[]{:S(2)}) collective-permute-start(bf16[160,2688]{1,0:T(8,128)(2,1)S(1)} %shard_map.82.refs_0_), channel_id=1, source_target_pairs={{0,4},{1,5},{2,0},{3,1},{4,8},{5,9},{6,2},{7,3},{8,12},{9,13},{10,... | collective-permute-start | bytes 2580488 | tf_op jit(solution)/shard_map/ppermute | solution.py:432
  6.4 21.2 %collective-permute-start.2 = (bf16[160,2688]{1,0:T(8,128)(2,1)S(1)}, bf16[160,2688]{1,0:T(8,128)(2,1)S(1)}, u32[]{:S(2)}, u32[]{:S(2)}) collective-permute-start(bf16[160,2688]{1,0:T(8,128)(2,1)S(1)} %shard_map.82.refs_0_), channel_id=1, source_target_pairs={{0,2},{1,3},{2,6},{3,7},{4,0},{5,1},{6,10},{7,11},{8,4},{9,5},{10,... | collective-permute-start | bytes 2580488 | tf_op jit(solution)/shard_map/ppermute | solution.py:435
  27.6 2.5 %collective-permute-start.3 = (bf16[160,2688]{1,0:T(8,128)(2,1)S(1)}, bf16[160,2688]{1,0:T(8,128)(2,1)S(1)}, u32[]{:S(2)}, u32[]{:S(2)}) collective-permute-start(bf16[160,2688]{1,0:T(8,128)(2,1)S(1)} %collective-permute-done.2.refs_0_), channel_id=1, source_target_pairs={{0,1},{1,0},{2,3},{3,2},{4,5},{5,4},{6,7},{7,6},{8,9},{9,8},{10,11... | collective-permute-start | bytes 2580488 | tf_op jit(solution)/shard_map/ppermute | solution.py:438
  27.6 3.6 %collective-permute-start.4 = (bf16[160,2688]{1,0:T(8,128)(2,1)S(1)}, bf16[160,2688]{1,0:T(8,128)(2,1)S(1)}, u32[]{:S(2)}, u32[]{:S(2)}) collective-permute-start(bf16[160,2688]{1,0:T(8,128)(2,1)S(1)} %collective-permute-done.1.refs_1_), channel_id=1, source_target_pairs={{0,1},{1,0},{2,3},{3,2},{4,5},{5,4},{6,7},{7,6},{8,9},{9,8},{10,11... | collective-permute-start | bytes 2580488 | tf_op jit(solution)/shard_map/ppermute | solution.py:438
  28.1 21.0 %collective-permute-start.5 = (bf16[160,2688]{1,0:T(8,128)(2,1)S(1)}, bf16[160,2688]{1,0:T(8,128)(2,1)S(1)}, u32[]{:S(2)}, u32[]{:S(2)}) collective-permute-start(bf16[160,2688]{1,0:T(8,128)(2,1)S(1)} %collective-permute-done.1.refs_1_), channel_id=1, source_target_pairs={{0,4},{1,5},{2,0},{3,1},{4,8},{5,9},{6,2},{7,3},{8,12},{9,13},{10,... | collective-permute-start | bytes 2580488 | tf_op jit(solution)/shard_map/ppermute | solution.py:432
  29.7 20.7 %collective-permute-start.6 = (bf16[160,2688]{1,0:T(8,128)(2,1)S(1)}, bf16[160,2688]{1,0:T(8,128)(2,1)S(1)}, u32[]{:S(2)}, u32[]{:S(2)}) collective-permute-start(bf16[160,2688]{1,0:T(8,128)(2,1)S(1)} %collective-permute-done.2.refs_0_), channel_id=1, source_target_pairs={{0,2},{1,3},{2,6},{3,7},{4,0},{5,1},{6,10},{7,11},{8,4},{9,5},{10,... | collective-permute-start | bytes 2580488 | tf_op jit(solution)/shard_map/ppermute | solution.py:435
  50.4 2.5 %collective-permute-start.7 = (bf16[160,2688]{1,0:T(8,128)(2,1)S(1)}, bf16[160,2688]{1,0:T(8,128)(2,1)S(1)}, u32[]{:S(2)}, u32[]{:S(2)}) collective-permute-start(bf16[160,2688]{1,0:T(8,128)(2,1)S(1)} %collective-permute-done.6.refs_0_), channel_id=1, source_target_pairs={{0,1},{1,0},{2,3},{3,2},{4,5},{5,4},{6,7},{7,6},{8,9},{9,8},{10,11... | collective-permute-start | bytes 2580488 | tf_op jit(solution)/shard_map/ppermute | solution.py:438
  50.4 3.6 %collective-permute-start.8 = (bf16[160,2688]{1,0:T(8,128)(2,1)S(1)}, bf16[160,2688]{1,0:T(8,128)(2,1)S(1)}, u32[]{:S(2)}, u32[]{:S(2)}) collective-permute-start(bf16[160,2688]{1,0:T(8,128)(2,1)S(1)} %collective-permute-done.5.refs_1_), channel_id=1, source_target_pairs={{0,1},{1,0},{2,3},{3,2},{4,5},{5,4},{6,7},{7,6},{8,9},{9,8},{10,11... | collective-permute-start | bytes 2580488 | tf_op jit(solution)/shard_map/ppermute | solution.py:438
  51.0 21.0 %collective-permute-start.9 = (bf16[160,2688]{1,0:T(8,128)(2,1)S(1)}, bf16[160,2688]{1,0:T(8,128)(2,1)S(1)}, u32[]{:S(2)}, u32[]{:S(2)}) collective-permute-start(bf16[160,2688]{1,0:T(8,128)(2,1)S(1)} %collective-permute-done.5.refs_1_), channel_id=1, source_target_pairs={{0,4},{1,5},{2,0},{3,1},{4,8},{5,9},{6,2},{7,3},{8,12},{9,13},{10,... | collective-permute-start | bytes 2580488 | tf_op jit(solution)/shard_map/ppermute | solution.py:432
  52.5 20.7 %collective-permute-start.10 = (bf16[160,2688]{1,0:T(8,128)(2,1)S(1)}, bf16[160,2688]{1,0:T(8,128)(2,1)S(1)}, u32[]{:S(2)}, u32[]{:S(2)}) collective-permute-start(bf16[160,2688]{1,0:T(8,128)(2,1)S(1)} %collective-permute-done.6.refs_0_), channel_id=1, source_target_pairs={{0,2},{1,3},{2,6},{3,7},{4,0},{5,1},{6,10},{7,11},{8,4},{9,5},{10,... | collective-permute-start | bytes 2580488 | tf_op jit(solution)/shard_map/ppermute | solution.py:435
  73.3 2.7 %collective-permute-start.11 = (bf16[160,2688]{1,0:T(8,128)(2,1)S(1)}, bf16[160,2688]{1,0:T(8,128)(2,1)S(1)}, u32[]{:S(2)}, u32[]{:S(2)}) collective-permute-start(bf16[160,2688]{1,0:T(8,128)(2,1)S(1)} %collective-permute-done.10.refs_0_), channel_id=1, source_target_pairs={{0,1},{1,0},{2,3},{3,2},{4,5},{5,4},{6,7},{7,6},{8,9},{9,8},{10,11... | collective-permute-start | bytes 2580488 | tf_op jit(solution)/shard_map/ppermute | solution.py:438
  73.3 3.6 %collective-permute-start.12 = (bf16[160,2688]{1,0:T(8,128)(2,1)S(1)}, bf16[160,2688]{1,0:T(8,128)(2,1)S(1)}, u32[]{:S(2)}, u32[]{:S(2)}) collective-permute-start(bf16[160,2688]{1,0:T(8,128)(2,1)S(1)} %collective-permute-done.9.refs_1_), channel_id=1, source_target_pairs={{0,1},{1,0},{2,3},{3,2},{4,5},{5,4},{6,7},{7,6},{8,9},{9,8},{10,11... | collective-permute-start | bytes 2580488 | tf_op jit(solution)/shard_map/ppermute | solution.py:438
  73.9 13.9 %collective-permute-start.13 = (bf16[80,2688]{1,0:T(8,128)(2,1)S(1)}, bf16[80,2688]{1,0:T(8,128)(2,1)S(1)}, u32[]{:S(2)}, u32[]{:S(2)}) collective-permute-start(bf16[80,2688]{1,0:T(8,128)(2,1)S(1)} %slice.54), channel_id=1, source_target_pairs={{0,4},{1,5},{2,0},{3,1},{4,8},{5,9},{6,2},{7,3},{8,12},{9,13},{10,... | collective-permute-start | bytes 1290248 | tf_op jit(solution)/shard_map/ppermute | solution.py:432
  75.4 12.3 %collective-permute-start.14 = (bf16[80,2688]{1,0:T(8,128)(2,1)S(1)}, bf16[80,2688]{1,0:T(8,128)(2,1)S(1)}, u32[]{:S(2)}, u32[]{:S(2)}) collective-permute-start(bf16[80,2688]{1,0:T(8,128)(2,1)S(1)} %slice.55), channel_id=1, source_target_pairs={{0,2},{1,3},{2,6},{3,7},{4,0},{5,1},{6,10},{7,11},{8,4},{9,5},{10,... | collective-permute-start | bytes 1290248 | tf_op jit(solution)/shard_map/ppermute | solution.py:435
  87.7 1.8 %collective-permute-start.15 = (bf16[80,2688]{1,0:T(8,128)(2,1)S(1)}, bf16[80,2688]{1,0:T(8,128)(2,1)S(1)}, u32[]{:S(2)}, u32[]{:S(2)}) collective-permute-start(bf16[80,2688]{1,0:T(8,128)(2,1)S(1)} %collective-permute-done.13.refs_0_), channel_id=1, source_target_pairs={{0,1},{1,0},{2,3},{3,2},{4,5},{5,4},{6,7},{7,6},{8,9},{9,8},{10,11... | collective-permute-start | bytes 1290248 | tf_op jit(solution)/shard_map/ppermute | solution.py:438
  87.9 2.3 %collective-permute-start.16 = (bf16[80,2688]{1,0:T(8,128)(2,1)S(1)}, bf16[80,2688]{1,0:T(8,128)(2,1)S(1)}, u32[]{:S(2)}, u32[]{:S(2)}) collective-permute-start(bf16[80,2688]{1,0:T(8,128)(2,1)S(1)} %collective-permute-done.14.refs_1_), channel_id=1, source_target_pairs={{0,1},{1,0},{2,3},{3,2},{4,5},{5,4},{6,7},{7,6},{8,9},{9,8},{10,11... | collective-permute-start | bytes 1290248 | tf_op jit(solution)/shard_map/ppermute | solution.py:438
  100.9 5.3 %collective-permute-start.18 = (bf16[160,2560]{1,0:T(8,128)(2,1)S(1)}, bf16[160,2560]{1,0:T(8,128)(2,1)S(1)}, u32[]{:S(2)}, u32[]{:S(2)}) collective-permute-start(bf16[160,2560]{1,0:T(8,128)(2,1)S(1)} %get-tuple-element.62), channel_id=1, source_target_pairs={{0,1},{1,0},{2,3},{3,2},{4,5},{5,4},{6,7},{7,6},{8,9},{9,8},{10,11... | collective-permute-start | bytes 2457608 | tf_op jit(solution)/shard_map/ppermute | solution.py:438
  105.8 13.4 %collective-permute-start.20 = (bf16[320,2560]{1,0:T(8,128)(2,1)S(1)}, bf16[320,2560]{1,0:T(8,128)(2,1)S(1)}, u32[]{:S(2)}, u32[]{:S(2)}) collective-permute-start(bf16[320,2560]{1,0:T(8,128)(2,1)S(1)} %shard_map.92), channel_id=1, source_target_pairs={{0,1},{1,0},{2,3},{3,2},{4,5},{5,4},{6,7},{7,6},{8,9},{9,8},{10,11... | collective-permute-start | bytes 4915208 | tf_op jit(solution)/shard_map/ppermute | solution.py:438
  106.5 11.6 %collective-permute-start.19 = (bf16[80,2560]{1,0:T(8,128)(2,1)S(1)}, bf16[80,2560]{1,0:T(8,128)(2,1)S(1)}, u32[]{:S(2)}, u32[]{:S(2)}) collective-permute-start(bf16[80,2560]{1,0:T(8,128)(2,1)S(1)} %get-tuple-element.69), channel_id=1, source_target_pairs={{0,4},{1,5},{2,0},{3,1},{4,8},{5,9},{6,2},{7,3},{8,12},{9,13},{10,... | collective-permute-start | bytes 1228808 | tf_op jit(solution)/shard_map/ppermute | solution.py:432
  108.0 11.2 %collective-permute-start.26 = (bf16[80,2560]{1,0:T(8,128)(2,1)S(1)}, bf16[80,2560]{1,0:T(8,128)(2,1)S(1)}, u32[]{:S(2)}, u32[]{:S(2)}) collective-permute-start(bf16[80,2560]{1,0:T(8,128)(2,1)S(1)} %get-tuple-element.70), channel_id=1, source_target_pairs={{0,2},{1,3},{2,6},{3,7},{4,0},{5,1},{6,10},{7,11},{8,4},{9,5},{10,... | collective-permute-start | bytes 1228808 | tf_op jit(solution)/shard_map/ppermute | solution.py:435
  113.2 18.0 %collective-permute-start.22 = (bf16[320,2560]{1,0:T(8,128)(2,1)S(1)}, bf16[320,2560]{1,0:T(8,128)(2,1)S(1)}, u32[]{:S(2)}, u32[]{:S(2)}) collective-permute-start(bf16[320,2560]{1,0:T(8,128)(2,1)S(1)} %shard_map.94), channel_id=1, source_target_pairs={{0,1},{1,0},{2,3},{3,2},{4,5},{5,4},{6,7},{7,6},{8,9},{9,8},{10,11... | collective-permute-start | bytes 4915208 | tf_op jit(solution)/shard_map/ppermute | solution.py:438
  119.7 19.5 %collective-permute-start.21 = (bf16[160,2560]{1,0:T(8,128)(2,1)S(1)}, bf16[160,2560]{1,0:T(8,128)(2,1)S(1)}, u32[]{:S(2)}, u32[]{:S(2)}) collective-permute-start(bf16[160,2560]{1,0:T(8,128)(2,1)S(1)} %get-tuple-element.67), channel_id=1, source_target_pairs={{0,4},{1,5},{2,0},{3,1},{4,8},{5,9},{6,2},{7,3},{8,12},{9,13},{10,... | collective-permute-start | bytes 2457608 | tf_op jit(solution)/shard_map/ppermute | solution.py:432
  120.2 20.2 %collective-permute-start.27 = (bf16[160,2560]{1,0:T(8,128)(2,1)S(1)}, bf16[160,2560]{1,0:T(8,128)(2,1)S(1)}, u32[]{:S(2)}, u32[]{:S(2)}) collective-permute-start(bf16[160,2560]{1,0:T(8,128)(2,1)S(1)} %get-tuple-element.68), channel_id=1, source_target_pairs={{0,2},{1,3},{2,6},{3,7},{4,0},{5,1},{6,10},{7,11},{8,4},{9,5},{10,... | collective-permute-start | bytes 2457608 | tf_op jit(solution)/shard_map/ppermute | solution.py:435
  126.5 24.6 %collective-permute-start.24 = (bf16[320,2560]{1,0:T(8,128)(2,1)S(1)}, bf16[320,2560]{1,0:T(8,128)(2,1)S(1)}, u32[]{:S(2)}, u32[]{:S(2)}) collective-permute-start(bf16[320,2560]{1,0:T(8,128)(2,1)S(1)} %shard_map.96), channel_id=1, source_target_pairs={{0,1},{1,0},{2,3},{3,2},{4,5},{5,4},{6,7},{7,6},{8,9},{9,8},{10,11... | collective-permute-start | bytes 4915208 | tf_op jit(solution)/shard_map/ppermute | solution.py:438
  141.0 19.4 %collective-permute-start.23 = (bf16[160,2560]{1,0:T(8,128)(2,1)S(1)}, bf16[160,2560]{1,0:T(8,128)(2,1)S(1)}, u32[]{:S(2)}, u32[]{:S(2)}) collective-permute-start(bf16[160,2560]{1,0:T(8,128)(2,1)S(1)} %get-tuple-element.65), channel_id=1, source_target_pairs={{0,4},{1,5},{2,0},{3,1},{4,8},{5,9},{6,2},{7,3},{8,12},{9,13},{10,... | collective-permute-start | bytes 2457608 | tf_op jit(solution)/shard_map/ppermute | solution.py:432
  141.5 19.2 %collective-permute-start.28 = (bf16[160,2560]{1,0:T(8,128)(2,1)S(1)}, bf16[160,2560]{1,0:T(8,128)(2,1)S(1)}, u32[]{:S(2)}, u32[]{:S(2)}) collective-permute-start(bf16[160,2560]{1,0:T(8,128)(2,1)S(1)} %get-tuple-element.66), channel_id=1, source_target_pairs={{0,2},{1,3},{2,6},{3,7},{4,0},{5,1},{6,10},{7,11},{8,4},{9,5},{10,... | collective-permute-start | bytes 2457608 | tf_op jit(solution)/shard_map/ppermute | solution.py:435
  146.3 20.3 %collective-permute-start.17 = (bf16[160,2560]{1,0:T(8,128)(2,1)S(1)}, bf16[160,2560]{1,0:T(8,128)(2,1)S(1)}, u32[]{:S(2)}, u32[]{:S(2)}) collective-permute-start(bf16[160,2560]{1,0:T(8,128)(2,1)S(1)} %shard_map.89), channel_id=1, source_target_pairs={{0,1},{1,0},{2,3},{3,2},{4,5},{5,4},{6,7},{7,6},{8,9},{9,8},{10,11... | collective-permute-start | bytes 2457608 | tf_op jit(solution)/shard_map/ppermute | solution.py:438
  161.4 18.4 %collective-permute-start.29 = (bf16[160,2560]{1,0:T(8,128)(2,1)S(1)}, bf16[160,2560]{1,0:T(8,128)(2,1)S(1)}, u32[]{:S(2)}, u32[]{:S(2)}) collective-permute-start(bf16[160,2560]{1,0:T(8,128)(2,1)S(1)} %get-tuple-element.64), channel_id=1, source_target_pairs={{0,2},{1,3},{2,6},{3,7},{4,0},{5,1},{6,10},{7,11},{8,4},{9,5},{10,... | collective-permute-start | bytes 2457608 | tf_op jit(solution)/shard_map/ppermute | solution.py:435
  162.8 17.9 %collective-permute-start.25 = (bf16[160,2560]{1,0:T(8,128)(2,1)S(1)}, bf16[160,2560]{1,0:T(8,128)(2,1)S(1)}, u32[]{:S(2)}, u32[]{:S(2)}) collective-permute-start(bf16[160,2560]{1,0:T(8,128)(2,1)S(1)} %get-tuple-element.63), channel_id=1, source_target_pairs={{0,4},{1,5},{2,0},{3,1},{4,8},{5,9},{6,2},{7,3},{8,12},{9,13},{10,... | collective-permute-start | bytes 2457608 | tf_op jit(solution)/shard_map/ppermute | solution.py:432
  (1 other events, 0.7 us)

commit v8 on v7

--- a/solution.py
+++ b/solution.py
@@ -242,8 +242,8 @@
     )
 
 
-def hidden_kernel(count, pieces, rows, first_row, chunk, fetch, *refs):
-    x_refs, refs = refs[:count], refs[count:]
+def hidden_kernel(places, rows, chunk, fetch, *refs):
+    x_refs, refs = refs[: len(places)], refs[len(places) :]
     if fetch == "gate_up":
         far_ref, out_ref, w_ref, x_all, sems = refs
     elif fetch == "down":
@@ -252,7 +252,6 @@
         w_ref, _, out_ref, x_all = refs[0], refs[1], refs[2], refs[-1]
     ff, wide = w_ref.shape[2:]
     whole, rest = divmod(ff, chunk)
-    total = len(pieces) * rows
 
     def fetched(i, width):
         part = pl.ds(pl.multiple_of(i * chunk, chunk), width)
@@ -265,10 +264,9 @@
             fetched(whole, rest).start()
     if fetch == "down":
         pltpu.make_async_copy(far_ref, down_ref, sems.at[0]).start()
-    for i, (block, start) in enumerate(pieces):
-        x_all[i * rows : (i + 1) * rows, :] = x_refs[block][start : start + rows, :wide]
-        at = first_row + i * rows
-        out_ref[at : at + rows, ff:] = x_refs[block][start : start + rows, wide:]
+    for i, at in enumerate(places):
+        x_all[i * rows : (i + 1) * rows, :] = x_refs[i][:, :wide]
+        out_ref[at : at + rows, ff:] = x_refs[i][:, wide:]
 
     def step(i, width):
         if fetch == "gate_up":
@@ -280,7 +278,8 @@
         )
         gate, up = both[:, :width], both[:, width:]
         hidden = (gate / (1.0 + jnp.exp(-gate)) * up).astype(out_ref.dtype)
-        out_ref[first_row : first_row + total, part] = hidden
+        for i, at in enumerate(places):
+            out_ref[at : at + rows, part] = hidden[i * rows : (i + 1) * rows]
 
     @pl.loop(0, whole)
     def _(i):
@@ -292,17 +291,15 @@
         pltpu.make_async_copy(far_ref, down_ref, sems.at[0]).wait()
 
 
-def hidden_call(
-    blocks, pieces, rows, gate_up_weight, hidden, first_row, all_rows, down_weight=None, last=False
-):
-    width = blocks[0].shape[1]
+def hidden_call(blocks, places, gate_up_weight, hidden, all_rows, down_weight=None, last=False):
+    rows, width = blocks[0].shape
     ff, wide = gate_up_weight.shape[2:]
     count = len(blocks)
     chunk = 256
     here, far = pl.BlockSpec(memory_space=pltpu.VMEM), pl.BlockSpec(memory_space=pltpu.HBM)
     args, in_specs = [kept(block) for block in blocks], [here] * count
     out_shape, aliases = [pltpu.VMEM((all_rows, ff + width - wide), jnp.bfloat16)], {}
-    scratch = [pltpu.VMEM((len(pieces) * rows, wide), jnp.bfloat16)]
+    scratch = [pltpu.VMEM((count * rows, wide), jnp.bfloat16)]
     fetch = None
     if hidden is None:
         fetch = "gate_up"
@@ -321,7 +318,7 @@
             out_shape.append(pltpu.VMEM(down_weight.shape, down_weight.dtype))
             scratch.append(pltpu.SemaphoreType.DMA((1,)))
     return pl.pallas_call(
-        functools.partial(hidden_kernel, count, pieces, rows, first_row, chunk, fetch),
+        functools.partial(hidden_kernel, tuple(places), rows, chunk, fetch),
         in_specs=in_specs,
         out_specs=[here] * len(out_shape),
         out_shape=out_shape,
@@ -329,9 +326,9 @@
         input_output_aliases=aliases,
         compiler_params=pltpu.CompilerParams(vmem_limit_bytes=14 * 1024 * 1024),
         cost_estimate=pl.CostEstimate(
-            flops=4 * len(pieces) * rows * wide * ff,
-            bytes_accessed=4 * ff * wide + 2 * len(pieces) * rows * (wide + ff),
-            transcendentals=len(pieces) * rows * ff,
+            flops=4 * count * rows * wide * ff,
+            bytes_accessed=4 * ff * wide + 2 * count * rows * (wide + ff),
+            transcendentals=count * rows * ff,
         ),
     )(*args)
 
@@ -451,37 +448,32 @@
 
     all_rows = len(ring.slots) * tok_count
 
-    def whole(blocks):
-        return [(i, 0) for i in range(len(blocks))]
-
-    blocks = [own, other]
-    hidden, gate_up = hidden_call(
-        blocks, whole(blocks), tok_count, gate_up_weight, None, 0, all_rows
-    )
+    def rows_of(*slots):
+        return [slot * tok_count for slot in slots]
+
+    hidden, gate_up = hidden_call([own, other], rows_of(0, 1), gate_up_weight, None, all_rows)
     hidden, before = lax.optimization_barrier((hidden, before))
     hidden, after = lax.optimization_barrier((hidden, after))
     cut = tok_count // 2
+    swapped, swapped_rows = [], []
     for s in range(1, ring.half):
-        here = [after, before]
-        there = [across(after), across(before)]
+        blocks, places_here = [after, before, *swapped], rows_of(4 * s, 4 * s + 1) + swapped_rows
+        swapped, swapped_rows = [across(after), across(before)], rows_of(4 * s + 2, 4 * s + 3)
         if s + 1 == ring.half:
             before, after = before[:cut], after[cut:]
         before, after = onward(before), back(after)
-        first_row = 4 * s * tok_count
         extra = down_weight if s == 1 else None
-        blocks = here + there
         hidden, gate_up, *down = hidden_call(
-            blocks, whole(blocks), tok_count, gate_up, hidden, first_row, all_rows, extra
+            blocks, places_here, gate_up, hidden, all_rows, extra
         )
         if down:
             (down_here,) = down
-        hidden, before = lax.optimization_barrier((hidden, before))
+        hidden, before, swapped = lax.optimization_barrier((hidden, before, swapped))
         hidden, after = lax.optimization_barrier((hidden, after))
     far = [before, after, across(before), across(after)]
-    first_row = 2 * tok_count
-    (hidden,) = hidden_call(
-        far, whole(far), cut, gate_up, hidden, first_row, all_rows, last=True
-    )
+    hidden, gate_up = hidden_call(swapped, swapped_rows, gate_up, hidden, all_rows)
+    far_rows = [2 * tok_count + i * cut for i in range(4)]
+    (hidden,) = hidden_call(far, far_rows, gate_up, hidden, all_rows, last=True)
 
     def outputs(*groups):
         return down_call(

time: 182 us -> 184 us (1.011)
    ppermute x14, waiting for transfers between devices: 5.02 us -> 0.04 us  [across(): return lax.ppermute(array, AXES, ring.swap())]
    ppermute x8, waiting for transfers between devices: 19.9 us -> 24.6 us  [back(): return lax.ppermute(array, AXES, ring.step(-1))]
    ppermute x8, starting transfers between devices: 10.5 us -> 12.3 us  [onward(): return lax.ppermute(array, AXES, ring.step(1))]
    ppermute x8, starting transfers between devices: 6.6 us -> 4.74 us  [back(): return lax.ppermute(array, AXES, ring.step(-1))]
    pallas_call x5 -> x6, Pallas kernels: 46.2 us -> 47.5 us  [hidden_call(): pl.pallas_call(functools.partial(hidden_kernel, tuple(places), rows, chun...]
  transfers between devices with their start and end apart: 30 -> 30, of which waited for: 18 -> 14; matrix products, arithmetic and copies ran while one was open for 1% -> 1% of each run, Pallas kernels for 41% -> 41%
where the time goes in v8:
time: 184 us
  Pallas kernels  87.9 us (48%)
  waiting for transfers between devices  70 us (38%)
  starting transfers between devices  19.5 us (11%)
  other arithmetic  3.17 us (2%)
  local copies, waits for them, and re-layouts  2.8 us (2%)
    pallas_call x6, Pallas kernels, hidden_call(): pl.pallas_call(functools.partial(hidden_kernel, tuple(places), rows, chun...  47.5 us
    ppermute x8, waiting for transfers between devices, onward(): return lax.ppermute(array, AXES, ring.step(1))  45.4 us
    pallas_call x9, Pallas kernels, down_call(): pl.pallas_call(functools.partial(down_kernel, groups, rows, text_rows, se...  39.2 us
    ppermute x8, waiting for transfers between devices, back(): return lax.ppermute(array, AXES, ring.step(-1))  24.6 us
    ppermute x8, starting transfers between devices, onward(): return lax.ppermute(array, AXES, ring.step(1))  12.3 us
    ppermute x8, starting transfers between devices, back(): return lax.ppermute(array, AXES, ring.step(-1))  4.74 us
  transfers between devices with their start and end apart: 30, of which 14 were waited for; matrix products, arithmetic and copies ran while one was open for 1% of the time, Pallas kernels for 41%

profile of v8, /device:TPU:0, one launch (start us, length us, event | category | flops | bytes accessed | tf_op | source)
XLA Modules:
  0.0 183.7 jit_solution(15603572847825010674)
XLA Ops:
  2.1 1.2 shard_map.82.refs_0_
  3.8 2.6 %collective-permute-start.1 = (bf16[160,2688]{1,0:T(8,128)(2,1)S(1)}, bf16[160,2688]{1,0:T(8,128)(2,1)S(1)}, u32[]{:S(2)}, u32[]{:S(2)}) collective-permute-start(bf16[160,2688]{1,0:T(8,128)(2,1)S(1)} %shard_map.82.refs_0_), channel_id=1, source_target_pairs={{0,4},{1,5},{2,0},{3,1},{4,8},{5,9},{6,2},{7,3},{8,12},{9,13},{10,... | collective-permute-start | bytes 2580488 | tf_op jit(solution)/shard_map/ppermute | solution.py:429
  7.1 7.7 %shard_map.83 = (bf16[2560,1536]{1,0:T(8,128)(2,1)S(1)}, bf16[1,2,1408,2560]{3,2,1,0:T(8,128)(2,1)S(1)}) custom-call(bf16[160,2688]{1,0:T(8,128)(2,1)S(1)} %shard_map.82.refs_0_, bf16[160,2688]{1,0:T(8,128)(2,1)S(1)} %collective-permute-done.refs_1_, bf16[1,2,1408,2560]{3,2,1,0:T(8,128)(2,1)} %refs_2_.1), custom_call_target="tpu_custom_call" | custom-call | flops 4613734400 | bytes 16957440 | tf_op jit(solution)/shard_map/pallas_call | solution.py:320
  14.8 11.2 %collective-permute-done.1.refs_1_ = bf16[160,2688]{1,0:T(8,128)(2,1)S(1)} collective-permute-done((bf16[160,2688]{1,0:T(8,128)(2,1)S(1)}, bf16[160,2688]{1,0:T(8,128)(2,1)S(1)}, u32[]{:S(2)}, u32[]{:S(2)}) %collective-permute-start.1) | collective-permute-done | bytes 860192 | tf_op jit(solution)/shard_map/ppermute | solution.py:429
  26.1 1.5 collective-permute-done.2.refs_0_
  27.6 1.6 collective-permute-start.3
  30.1 6.1 %shard_map.84 = (bf16[2560,1536]{1,0:T(8,128)(2,1)S(1)}, bf16[1,2,1408,2560]{3,2,1,0:T(8,128)(2,1)S(1)}, bf16[1,1408,2560]{2,1,0:T(8,128)(2,1)S(1)}) custom-call(bf16[160,2688]{1,0:T(8,128)(2,1)S(1)} %collective-permute-done.2.refs_0_, bf16[160,2688]{1,0:T(8,128)(2,1)S(1)} %collective-permute-done.1.refs_1_, ...), custom_call_target="tpu_custom_call", output_to_operand_aliasing={{0}: (3, {}), {1}: (2, {})} | custom-call | flops 4613734400 | bytes 16957440 | tf_op jit(solution)/shard_map/pallas_call | solution.py:320
  36.2 11.7 %collective-permute-done.3.refs_1_ = bf16[160,2688]{1,0:T(8,128)(2,1)S(1)} collective-permute-done((bf16[160,2688]{1,0:T(8,128)(2,1)S(1)}, bf16[160,2688]{1,0:T(8,128)(2,1)S(1)}, u32[]{:S(2)}, u32[]{:S(2)}) %collective-permute-start.3) | collective-permute-done | bytes 860192 | tf_op jit(solution)/shard_map/ppermute | solution.py:429
  48.0 1.6 collective-permute-start.7
  51.2 10.8 %shard_map.85 = (bf16[2560,1536]{1,0:T(8,128)(2,1)S(1)}, bf16[1,2,1408,2560]{3,2,1,0:T(8,128)(2,1)S(1)}) custom-call(bf16[160,2688]{1,0:T(8,128)(2,1)S(1)} %collective-permute-done.6.refs_0_, bf16[160,2688]{1,0:T(8,128)(2,1)S(1)} %collective-permute-done.3.refs_1_, ...), custom_call_target="tpu_custom_call", output_to_operand_aliasing={{0}: (5, {}), {1}: (4, {})} | custom-call | flops 9227468800 | bytes 19496960 | tf_op jit(solution)/shard_map/pallas_call | solution.py:320
  62.0 5.4 %collective-permute-done.7.refs_1_ = bf16[160,2688]{1,0:T(8,128)(2,1)S(1)} collective-permute-done((bf16[160,2688]{1,0:T(8,128)(2,1)S(1)}, bf16[160,2688]{1,0:T(8,128)(2,1)S(1)}, u32[]{:S(2)}, u32[]{:S(2)}) %collective-permute-start.7) | collective-permute-done | bytes 860192 | tf_op jit(solution)/shard_map/ppermute | solution.py:429
  67.5 4.7 %collective-permute-done.10.refs_0_ = bf16[160,2688]{1,0:T(8,128)(2,1)S(1)} collective-permute-done((bf16[160,2688]{1,0:T(8,128)(2,1)S(1)}, bf16[160,2688]{1,0:T(8,128)(2,1)S(1)}, u32[]{:S(2)}, u32[]{:S(2)}) %collective-permute-start.10) | collective-permute-done | bytes 860192 | tf_op jit(solution)/shard_map/ppermute | solution.py:432
  72.3 1.6 collective-permute-start.11
  74.4 10.8 %shard_map.86 = (bf16[2560,1536]{1,0:T(8,128)(2,1)S(1)}, bf16[1,2,1408,2560]{3,2,1,0:T(8,128)(2,1)S(1)}) custom-call(bf16[160,2688]{1,0:T(8,128)(2,1)S(1)} %collective-permute-done.10.refs_0_, bf16[160,2688]{1,0:T(8,128)(2,1)S(1)} %collective-permute-done.7.refs_1_, ...), custom_call_target="tpu_custom_call", output_to_operand_aliasing={{0}: (5, {}), {1}: (4, {})} | custom-call | flops 9227468800 | bytes 19496960 | tf_op jit(solution)/shard_map/pallas_call | solution.py:320
  86.5 6.0 %shard_map.87 = (bf16[2560,1536]{1,0:T(8,128)(2,1)S(1)}, bf16[1,2,1408,2560]{3,2,1,0:T(8,128)(2,1)S(1)}) custom-call(bf16[160,2688]{1,0:T(8,128)(2,1)S(1)} %collective-permute-done.12.refs_0_, bf16[160,2688]{1,0:T(8,128)(2,1)S(1)} %collective-permute-done.13.refs_1_, ...), custom_call_target="tpu_custom_call", output_to_operand_aliasing={{0}: (3, {}), {1}: (2, {})} | custom-call | flops 4613734400 | bytes 16957440 | tf_op jit(solution)/shard_map/pallas_call | solution.py:320
  92.5 6.1 %shard_map.88.hidden_ref = bf16[2560,1536]{1,0:T(8,128)(2,1)S(1)} custom-call(bf16[80,2688]{1,0:T(8,128)(2,1)S(1)} %collective-permute-done.11.refs_0_, bf16[80,2688]{1,0:T(8,128)(2,1)S(1)} %collective-permute-done.14.refs_1_, bf16[80,2688]{1,0:T(8,128)(2,1)S(1)} %collective-permute-done.15.refs_2_, ...), custom_call_target="tpu_custom_call", output_to_operand_aliasing={{}: (5, {})} | custom-call | flops 4613734400 | bytes 16957440 | tf_op jit(solution)/shard_map/pallas_call | solution.py:320
  98.6 4.7 %shard_map.91 = (bf16[160,2560]{1,0:T(8,128)(2,1)S(1)}, bf16[160,2560]{1,0:T(8,128)(2,1)S(1)}) custom-call(s32[81]{0:T(128)S(1)} %dynamic-slice_bitcast_fusion.places_ref, bf16[2560,1536]{1,0:T(8,128)(2,1)S(1)} %shard_map.88.hidden_ref, bf16[1,1408,2560]{2,1,0:T(8,128)(2,1)S(1)} %get-tuple-element.76.w_ref), custom_call_target="tpu_custom_call" | custom-call | flops 2306867200 | bytes 8847360 | tf_op jit(solution)/shard_map/pallas_call | solution.py:390
  103.4 4.7 %shard_map.93 = bf16[320,2560]{1,0:T(8,128)(2,1)S(1)} custom-call(s32[81]{0:T(128)S(1)} %dynamic-slice_bitcast_fusion.places_ref, bf16[2560,1536]{1,0:T(8,128)(2,1)S(1)} %shard_map.88.hidden_ref, bf16[1,1408,2560]{2,1,0:T(8,128)(2,1)S(1)} %get-tuple-element.76.w_ref), custom_call_target="tpu_custom_call" | custom-call | flops 2306867200 | bytes 8847360 | tf_op jit(solution)/shard_map/pallas_call | solution.py:390
  108.8 1.6 collective-permute-start.19
  110.9 4.7 %shard_map.95 = bf16[320,2560]{1,0:T(8,128)(2,1)S(1)} custom-call(s32[81]{0:T(128)S(1)} %dynamic-slice_bitcast_fusion.places_ref, bf16[2560,1536]{1,0:T(8,128)(2,1)S(1)} %shard_map.88.hidden_ref, bf16[1,1408,2560]{2,1,0:T(8,128)(2,1)S(1)} %get-tuple-element.76.w_ref), custom_call_target="tpu_custom_call" | custom-call | flops 2306867200 | bytes 8847360 | tf_op jit(solution)/shard_map/pallas_call | solution.py:390
  115.7 4.7 %shard_map.92 = bf16[320,2560]{1,0:T(8,128)(2,1)S(1)} custom-call(s32[81]{0:T(128)S(1)} %dynamic-slice_bitcast_fusion.places_ref, bf16[2560,1536]{1,0:T(8,128)(2,1)S(1)} %shard_map.88.hidden_ref, bf16[1,1408,2560]{2,1,0:T(8,128)(2,1)S(1)} %get-tuple-element.76.w_ref), custom_call_target="tpu_custom_call" | custom-call | flops 2306867200 | bytes 8847360 | tf_op jit(solution)/shard_map/pallas_call | solution.py:390
  124.1 4.7 %shard_map.97 = bf16[320,2560]{1,0:T(8,128)(2,1)S(1)} custom-call(s32[81]{0:T(128)S(1)} %dynamic-slice_bitcast_fusion.places_ref, bf16[2560,1536]{1,0:T(8,128)(2,1)S(1)} %shard_map.88.hidden_ref, bf16[1,1408,2560]{2,1,0:T(8,128)(2,1)S(1)} %get-tuple-element.76.w_ref), custom_call_target="tpu_custom_call" | custom-call | flops 2306867200 | bytes 8847360 | tf_op jit(solution)/shard_map/pallas_call | solution.py:390
  128.8 4.7 %shard_map.94 = bf16[320,2560]{1,0:T(8,128)(2,1)S(1)} custom-call(s32[81]{0:T(128)S(1)} %dynamic-slice_bitcast_fusion.places_ref, bf16[2560,1536]{1,0:T(8,128)(2,1)S(1)} %shard_map.88.hidden_ref, bf16[1,1408,2560]{2,1,0:T(8,128)(2,1)S(1)} %get-tuple-element.76.w_ref), custom_call_target="tpu_custom_call" | custom-call | flops 2306867200 | bytes 8847360 | tf_op jit(solution)/shard_map/pallas_call | solution.py:390
  133.5 8.0 %collective-permute-done.21 = bf16[160,2560]{1,0:T(8,128)(2,1)S(1)} collective-permute-done((bf16[160,2560]{1,0:T(8,128)(2,1)S(1)}, bf16[160,2560]{1,0:T(8,128)(2,1)S(1)}, u32[]{:S(2)}, u32[]{:S(2)}) %collective-permute-start.21) | collective-permute-done | bytes 819232 | tf_op jit(solution)/shard_map/ppermute | solution.py:429
  141.6 1.2 collective-permute-done.27
  145.5 3.2 %shard_map.90 = bf16[160,2560]{1,0:T(8,128)(2,1)S(1)} custom-call(s32[81]{0:T(128)S(1)} %dynamic-slice_bitcast_fusion.places_ref, bf16[2560,1536]{1,0:T(8,128)(2,1)S(1)} %shard_map.88.hidden_ref, bf16[1,1408,2560]{2,1,0:T(8,128)(2,1)S(1)} %get-tuple-element.76.w_ref), custom_call_target="tpu_custom_call" | custom-call | flops 1153433600 | bytes 8028160 | tf_op jit(solution)/shard_map/pallas_call | solution.py:390
  148.8 4.7 %shard_map.96 = bf16[320,2560]{1,0:T(8,128)(2,1)S(1)} custom-call(s32[81]{0:T(128)S(1)} %dynamic-slice_bitcast_fusion.places_ref, bf16[2560,1536]{1,0:T(8,128)(2,1)S(1)} %shard_map.88.hidden_ref, bf16[1,1408,2560]{2,1,0:T(8,128)(2,1)S(1)} %get-tuple-element.76.w_ref), custom_call_target="tpu_custom_call" | custom-call | flops 2306867200 | bytes 8847360 | tf_op jit(solution)/shard_map/pallas_call | solution.py:390
  153.5 8.9 %collective-permute-done.23 = bf16[160,2560]{1,0:T(8,128)(2,1)S(1)} collective-permute-done((bf16[160,2560]{1,0:T(8,128)(2,1)S(1)}, bf16[160,2560]{1,0:T(8,128)(2,1)S(1)}, u32[]{:S(2)}, u32[]{:S(2)}) %collective-permute-start.23) | collective-permute-done | bytes 819232 | tf_op jit(solution)/shard_map/ppermute | solution.py:429
  164.7 1.4 collective-permute-start.25
  166.1 3.2 %shard_map.89 = bf16[160,2560]{1,0:T(8,128)(2,1)S(1)} custom-call(s32[81]{0:T(128)S(1)} %dynamic-slice_bitcast_fusion.places_ref, bf16[2560,1536]{1,0:T(8,128)(2,1)S(1)} %shard_map.88.hidden_ref, bf16[1,1408,2560]{2,1,0:T(8,128)(2,1)S(1)} %get-tuple-element.76.w_ref), custom_call_target="tpu_custom_call" | custom-call | flops 1153433600 | bytes 8028160 | tf_op jit(solution)/shard_map/pallas_call | solution.py:390
  169.4 12.9 %collective-permute-done.29 = bf16[160,2560]{1,0:T(8,128)(2,1)S(1)} collective-permute-done((bf16[160,2560]{1,0:T(8,128)(2,1)S(1)}, bf16[160,2560]{1,0:T(8,128)(2,1)S(1)}, u32[]{:S(2)}, u32[]{:S(2)}) %collective-permute-start.29) | collective-permute-done | bytes 819232 | tf_op jit(solution)/shard_map/ppermute | solution.py:432
  182.3 1.3 add_convert_fusion
  (58 shorter events, 18.1 us)
Async XLA Ops:
  0.0 0.7 copy-start
  0.7 0.7 copy-start.1
  3.3 3.9 %collective-permute-start = (bf16[160,2688]{1,0:T(8,128)(2,1)S(1)}, bf16[160,2688]{1,0:T(8,128)(2,1)S(1)}, u32[]{:S(2)}, u32[]{:S(2)}) collective-permute-start(bf16[160,2688]{1,0:T(8,128)(2,1)S(1)} %shard_map.82.refs_0_), channel_id=1, source_target_pairs={{0,1},{1,0},{2,3},{3,2},{4,5},{5,4},{6,7},{7,6},{8,9},{9,8},{10,11... | collective-permute-start | bytes 2580488 | tf_op jit(solution)/shard_map/ppermute | solution.py:435
  3.8 22.3 %collective-permute-start.1 = (bf16[160,2688]{1,0:T(8,128)(2,1)S(1)}, bf16[160,2688]{1,0:T(8,128)(2,1)S(1)}, u32[]{:S(2)}, u32[]{:S(2)}) collective-permute-start(bf16[160,2688]{1,0:T(8,128)(2,1)S(1)} %shard_map.82.refs_0_), channel_id=1, source_target_pairs={{0,4},{1,5},{2,0},{3,1},{4,8},{5,9},{6,2},{7,3},{8,12},{9,13},{10,... | collective-permute-start | bytes 2580488 | tf_op jit(solution)/shard_map/ppermute | solution.py:429
  6.4 21.2 %collective-permute-start.2 = (bf16[160,2688]{1,0:T(8,128)(2,1)S(1)}, bf16[160,2688]{1,0:T(8,128)(2,1)S(1)}, u32[]{:S(2)}, u32[]{:S(2)}) collective-permute-start(bf16[160,2688]{1,0:T(8,128)(2,1)S(1)} %shard_map.82.refs_0_), channel_id=1, source_target_pairs={{0,2},{1,3},{2,6},{3,7},{4,0},{5,1},{6,10},{7,11},{8,4},{9,5},{10,... | collective-permute-start | bytes 2580488 | tf_op jit(solution)/shard_map/ppermute | solution.py:432
  27.6 20.4 %collective-permute-start.3 = (bf16[160,2688]{1,0:T(8,128)(2,1)S(1)}, bf16[160,2688]{1,0:T(8,128)(2,1)S(1)}, u32[]{:S(2)}, u32[]{:S(2)}) collective-permute-start(bf16[160,2688]{1,0:T(8,128)(2,1)S(1)} %collective-permute-done.1.refs_1_), channel_id=1, source_target_pairs={{0,4},{1,5},{2,0},{3,1},{4,8},{5,9},{6,2},{7,3},{8,12},{9,13},{10,... | collective-permute-start | bytes 2580488 | tf_op jit(solution)/shard_map/ppermute | solution.py:429
  29.2 18.8 %collective-permute-start.4 = (bf16[160,2688]{1,0:T(8,128)(2,1)S(1)}, bf16[160,2688]{1,0:T(8,128)(2,1)S(1)}, u32[]{:S(2)}, u32[]{:S(2)}) collective-permute-start(bf16[160,2688]{1,0:T(8,128)(2,1)S(1)} %collective-permute-done.2.refs_0_), channel_id=1, source_target_pairs={{0,1},{1,0},{2,3},{3,2},{4,5},{5,4},{6,7},{7,6},{8,9},{9,8},{10,11... | collective-permute-start | bytes 2580488 | tf_op jit(solution)/shard_map/ppermute | solution.py:435
  29.2 18.8 %collective-permute-start.5 = (bf16[160,2688]{1,0:T(8,128)(2,1)S(1)}, bf16[160,2688]{1,0:T(8,128)(2,1)S(1)}, u32[]{:S(2)}, u32[]{:S(2)}) collective-permute-start(bf16[160,2688]{1,0:T(8,128)(2,1)S(1)} %collective-permute-done.1.refs_1_), channel_id=1, source_target_pairs={{0,1},{1,0},{2,3},{3,2},{4,5},{5,4},{6,7},{7,6},{8,9},{9,8},{10,11... | collective-permute-start | bytes 2580488 | tf_op jit(solution)/shard_map/ppermute | solution.py:435
  29.7 21.0 %collective-permute-start.6 = (bf16[160,2688]{1,0:T(8,128)(2,1)S(1)}, bf16[160,2688]{1,0:T(8,128)(2,1)S(1)}, u32[]{:S(2)}, u32[]{:S(2)}) collective-permute-start(bf16[160,2688]{1,0:T(8,128)(2,1)S(1)} %collective-permute-done.2.refs_0_), channel_id=1, source_target_pairs={{0,2},{1,3},{2,6},{3,7},{4,0},{5,1},{6,10},{7,11},{8,4},{9,5},{10,... | collective-permute-start | bytes 2580488 | tf_op jit(solution)/shard_map/ppermute | solution.py:432
  48.0 19.4 %collective-permute-start.7 = (bf16[160,2688]{1,0:T(8,128)(2,1)S(1)}, bf16[160,2688]{1,0:T(8,128)(2,1)S(1)}, u32[]{:S(2)}, u32[]{:S(2)}) collective-permute-start(bf16[160,2688]{1,0:T(8,128)(2,1)S(1)} %collective-permute-done.3.refs_1_), channel_id=1, source_target_pairs={{0,4},{1,5},{2,0},{3,1},{4,8},{5,9},{6,2},{7,3},{8,12},{9,13},{10,... | collective-permute-start | bytes 2580488 | tf_op jit(solution)/shard_map/ppermute | solution.py:429
  49.6 17.9 %collective-permute-start.9 = (bf16[160,2688]{1,0:T(8,128)(2,1)S(1)}, bf16[160,2688]{1,0:T(8,128)(2,1)S(1)}, u32[]{:S(2)}, u32[]{:S(2)}) collective-permute-start(bf16[160,2688]{1,0:T(8,128)(2,1)S(1)} %collective-permute-done.3.refs_1_), channel_id=1, source_target_pairs={{0,1},{1,0},{2,3},{3,2},{4,5},{5,4},{6,7},{7,6},{8,9},{9,8},{10,11... | collective-permute-start | bytes 2580488 | tf_op jit(solution)/shard_map/ppermute | solution.py:435
  50.7 16.7 %collective-permute-start.8 = (bf16[160,2688]{1,0:T(8,128)(2,1)S(1)}, bf16[160,2688]{1,0:T(8,128)(2,1)S(1)}, u32[]{:S(2)}, u32[]{:S(2)}) collective-permute-start(bf16[160,2688]{1,0:T(8,128)(2,1)S(1)} %collective-permute-done.6.refs_0_), channel_id=1, source_target_pairs={{0,1},{1,0},{2,3},{3,2},{4,5},{5,4},{6,7},{7,6},{8,9},{9,8},{10,11... | collective-permute-start | bytes 2580488 | tf_op jit(solution)/shard_map/ppermute | solution.py:435
  50.7 21.5 %collective-permute-start.10 = (bf16[160,2688]{1,0:T(8,128)(2,1)S(1)}, bf16[160,2688]{1,0:T(8,128)(2,1)S(1)}, u32[]{:S(2)}, u32[]{:S(2)}) collective-permute-start(bf16[160,2688]{1,0:T(8,128)(2,1)S(1)} %collective-permute-done.6.refs_0_), channel_id=1, source_target_pairs={{0,2},{1,3},{2,6},{3,7},{4,0},{5,1},{6,10},{7,11},{8,4},{9,5},{10,... | collective-permute-start | bytes 2580488 | tf_op jit(solution)/shard_map/ppermute | solution.py:432
  67.5 17.8 %collective-permute-start.13 = (bf16[160,2688]{1,0:T(8,128)(2,1)S(1)}, bf16[160,2688]{1,0:T(8,128)(2,1)S(1)}, u32[]{:S(2)}, u32[]{:S(2)}) collective-permute-start(bf16[160,2688]{1,0:T(8,128)(2,1)S(1)} %collective-permute-done.7.refs_1_), channel_id=1, source_target_pairs={{0,1},{1,0},{2,3},{3,2},{4,5},{5,4},{6,7},{7,6},{8,9},{9,8},{10,11... | collective-permute-start | bytes 2580488 | tf_op jit(solution)/shard_map/ppermute | solution.py:435
  72.3 12.9 %collective-permute-start.12 = (bf16[160,2688]{1,0:T(8,128)(2,1)S(1)}, bf16[160,2688]{1,0:T(8,128)(2,1)S(1)}, u32[]{:S(2)}, u32[]{:S(2)}) collective-permute-start(bf16[160,2688]{1,0:T(8,128)(2,1)S(1)} %collective-permute-done.10.refs_0_), channel_id=1, source_target_pairs={{0,1},{1,0},{2,3},{3,2},{4,5},{5,4},{6,7},{7,6},{8,9},{9,8},{10,11... | collective-permute-start | bytes 2580488 | tf_op jit(solution)/shard_map/ppermute | solution.py:435
  72.3 12.9 %collective-permute-start.11 = (bf16[80,2688]{1,0:T(8,128)(2,1)S(1)}, bf16[80,2688]{1,0:T(8,128)(2,1)S(1)}, u32[]{:S(2)}, u32[]{:S(2)}) collective-permute-start(bf16[80,2688]{1,0:T(8,128)(2,1)S(1)} %slice.54), channel_id=1, source_target_pairs={{0,4},{1,5},{2,0},{3,1},{4,8},{5,9},{6,2},{7,3},{8,12},{9,13},{10,... | collective-permute-start | bytes 1290248 | tf_op jit(solution)/shard_map/ppermute | solution.py:429
  73.9 12.0 %collective-permute-start.14 = (bf16[80,2688]{1,0:T(8,128)(2,1)S(1)}, bf16[80,2688]{1,0:T(8,128)(2,1)S(1)}, u32[]{:S(2)}, u32[]{:S(2)}) collective-permute-start(bf16[80,2688]{1,0:T(8,128)(2,1)S(1)} %slice.55), channel_id=1, source_target_pairs={{0,2},{1,3},{2,6},{3,7},{4,0},{5,1},{6,10},{7,11},{8,4},{9,5},{10,... | collective-permute-start | bytes 1290248 | tf_op jit(solution)/shard_map/ppermute | solution.py:432
  86.0 6.6 %collective-permute-start.15 = (bf16[80,2688]{1,0:T(8,128)(2,1)S(1)}, bf16[80,2688]{1,0:T(8,128)(2,1)S(1)}, u32[]{:S(2)}, u32[]{:S(2)}) collective-permute-start(bf16[80,2688]{1,0:T(8,128)(2,1)S(1)} %collective-permute-done.11.refs_0_), channel_id=1, source_target_pairs={{0,1},{1,0},{2,3},{3,2},{4,5},{5,4},{6,7},{7,6},{8,9},{9,8},{10,11... | collective-permute-start | bytes 1290248 | tf_op jit(solution)/shard_map/ppermute | solution.py:435
  86.0 6.6 %collective-permute-start.16 = (bf16[80,2688]{1,0:T(8,128)(2,1)S(1)}, bf16[80,2688]{1,0:T(8,128)(2,1)S(1)}, u32[]{:S(2)}, u32[]{:S(2)}) collective-permute-start(bf16[80,2688]{1,0:T(8,128)(2,1)S(1)} %collective-permute-done.14.refs_1_), channel_id=1, source_target_pairs={{0,1},{1,0},{2,3},{3,2},{4,5},{5,4},{6,7},{7,6},{8,9},{9,8},{10,11... | collective-permute-start | bytes 1290248 | tf_op jit(solution)/shard_map/ppermute | solution.py:435
  103.3 5.3 %collective-permute-start.18 = (bf16[160,2560]{1,0:T(8,128)(2,1)S(1)}, bf16[160,2560]{1,0:T(8,128)(2,1)S(1)}, u32[]{:S(2)}, u32[]{:S(2)}) collective-permute-start(bf16[160,2560]{1,0:T(8,128)(2,1)S(1)} %get-tuple-element.78), channel_id=1, source_target_pairs={{0,1},{1,0},{2,3},{3,2},{4,5},{5,4},{6,7},{7,6},{8,9},{9,8},{10,11... | collective-permute-start | bytes 2457608 | tf_op jit(solution)/shard_map/ppermute | solution.py:435
  108.1 13.4 %collective-permute-start.20 = (bf16[320,2560]{1,0:T(8,128)(2,1)S(1)}, bf16[320,2560]{1,0:T(8,128)(2,1)S(1)}, u32[]{:S(2)}, u32[]{:S(2)}) collective-permute-start(bf16[320,2560]{1,0:T(8,128)(2,1)S(1)} %shard_map.93), channel_id=1, source_target_pairs={{0,1},{1,0},{2,3},{3,2},{4,5},{5,4},{6,7},{7,6},{8,9},{9,8},{10,11... | collective-permute-start | bytes 4915208 | tf_op jit(solution)/shard_map/ppermute | solution.py:435
  108.8 11.5 %collective-permute-start.19 = (bf16[80,2560]{1,0:T(8,128)(2,1)S(1)}, bf16[80,2560]{1,0:T(8,128)(2,1)S(1)}, u32[]{:S(2)}, u32[]{:S(2)}) collective-permute-start(bf16[80,2560]{1,0:T(8,128)(2,1)S(1)} %get-tuple-element.85), channel_id=1, source_target_pairs={{0,4},{1,5},{2,0},{3,1},{4,8},{5,9},{6,2},{7,3},{8,12},{9,13},{10,... | collective-permute-start | bytes 1228808 | tf_op jit(solution)/shard_map/ppermute | solution.py:429
  110.4 11.1 %collective-permute-start.26 = (bf16[80,2560]{1,0:T(8,128)(2,1)S(1)}, bf16[80,2560]{1,0:T(8,128)(2,1)S(1)}, u32[]{:S(2)}, u32[]{:S(2)}) collective-permute-start(bf16[80,2560]{1,0:T(8,128)(2,1)S(1)} %get-tuple-element.86), channel_id=1, source_target_pairs={{0,2},{1,3},{2,6},{3,7},{4,0},{5,1},{6,10},{7,11},{8,4},{9,5},{10,... | collective-permute-start | bytes 1228808 | tf_op jit(solution)/shard_map/ppermute | solution.py:432
  115.6 17.9 %collective-permute-start.22 = (bf16[320,2560]{1,0:T(8,128)(2,1)S(1)}, bf16[320,2560]{1,0:T(8,128)(2,1)S(1)}, u32[]{:S(2)}, u32[]{:S(2)}) collective-permute-start(bf16[320,2560]{1,0:T(8,128)(2,1)S(1)} %shard_map.95), channel_id=1, source_target_pairs={{0,1},{1,0},{2,3},{3,2},{4,5},{5,4},{6,7},{7,6},{8,9},{9,8},{10,11... | collective-permute-start | bytes 4915208 | tf_op jit(solution)/shard_map/ppermute | solution.py:435
  122.0 19.6 %collective-permute-start.21 = (bf16[160,2560]{1,0:T(8,128)(2,1)S(1)}, bf16[160,2560]{1,0:T(8,128)(2,1)S(1)}, u32[]{:S(2)}, u32[]{:S(2)}) collective-permute-start(bf16[160,2560]{1,0:T(8,128)(2,1)S(1)} %get-tuple-element.83), channel_id=1, source_target_pairs={{0,4},{1,5},{2,0},{3,1},{4,8},{5,9},{6,2},{7,3},{8,12},{9,13},{10,... | collective-permute-start | bytes 2457608 | tf_op jit(solution)/shard_map/ppermute | solution.py:429
  123.0 19.8 %collective-permute-start.27 = (bf16[160,2560]{1,0:T(8,128)(2,1)S(1)}, bf16[160,2560]{1,0:T(8,128)(2,1)S(1)}, u32[]{:S(2)}, u32[]{:S(2)}) collective-permute-start(bf16[160,2560]{1,0:T(8,128)(2,1)S(1)} %get-tuple-element.84), channel_id=1, source_target_pairs={{0,2},{1,3},{2,6},{3,7},{4,0},{5,1},{6,10},{7,11},{8,4},{9,5},{10,... | collective-permute-start | bytes 2457608 | tf_op jit(solution)/shard_map/ppermute | solution.py:432
  128.7 24.7 %collective-permute-start.24 = (bf16[320,2560]{1,0:T(8,128)(2,1)S(1)}, bf16[320,2560]{1,0:T(8,128)(2,1)S(1)}, u32[]{:S(2)}, u32[]{:S(2)}) collective-permute-start(bf16[320,2560]{1,0:T(8,128)(2,1)S(1)} %shard_map.97), channel_id=1, source_target_pairs={{0,1},{1,0},{2,3},{3,2},{4,5},{5,4},{6,7},{7,6},{8,9},{9,8},{10,11... | collective-permute-start | bytes 4915208 | tf_op jit(solution)/shard_map/ppermute | solution.py:435
  143.4 18.9 %collective-permute-start.23 = (bf16[160,2560]{1,0:T(8,128)(2,1)S(1)}, bf16[160,2560]{1,0:T(8,128)(2,1)S(1)}, u32[]{:S(2)}, u32[]{:S(2)}) collective-permute-start(bf16[160,2560]{1,0:T(8,128)(2,1)S(1)} %get-tuple-element.81), channel_id=1, source_target_pairs={{0,4},{1,5},{2,0},{3,1},{4,8},{5,9},{6,2},{7,3},{8,12},{9,13},{10,... | collective-permute-start | bytes 2457608 | tf_op jit(solution)/shard_map/ppermute | solution.py:429
  144.3 19.1 %collective-permute-start.28 = (bf16[160,2560]{1,0:T(8,128)(2,1)S(1)}, bf16[160,2560]{1,0:T(8,128)(2,1)S(1)}, u32[]{:S(2)}, u32[]{:S(2)}) collective-permute-start(bf16[160,2560]{1,0:T(8,128)(2,1)S(1)} %get-tuple-element.82), channel_id=1, source_target_pairs={{0,2},{1,3},{2,6},{3,7},{4,0},{5,1},{6,10},{7,11},{8,4},{9,5},{10,... | collective-permute-start | bytes 2457608 | tf_op jit(solution)/shard_map/ppermute | solution.py:432
  148.7 20.7 %collective-permute-start.17 = (bf16[160,2560]{1,0:T(8,128)(2,1)S(1)}, bf16[160,2560]{1,0:T(8,128)(2,1)S(1)}, u32[]{:S(2)}, u32[]{:S(2)}) collective-permute-start(bf16[160,2560]{1,0:T(8,128)(2,1)S(1)} %shard_map.90), channel_id=1, source_target_pairs={{0,1},{1,0},{2,3},{3,2},{4,5},{5,4},{6,7},{7,6},{8,9},{9,8},{10,11... | collective-permute-start | bytes 2457608 | tf_op jit(solution)/shard_map/ppermute | solution.py:435
  164.0 18.2 %collective-permute-start.29 = (bf16[160,2560]{1,0:T(8,128)(2,1)S(1)}, bf16[160,2560]{1,0:T(8,128)(2,1)S(1)}, u32[]{:S(2)}, u32[]{:S(2)}) collective-permute-start(bf16[160,2560]{1,0:T(8,128)(2,1)S(1)} %get-tuple-element.80), channel_id=1, source_target_pairs={{0,2},{1,3},{2,6},{3,7},{4,0},{5,1},{6,10},{7,11},{8,4},{9,5},{10,... | collective-permute-start | bytes 2457608 | tf_op jit(solution)/shard_map/ppermute | solution.py:432
  164.7 17.6 %collective-permute-start.25 = (bf16[160,2560]{1,0:T(8,128)(2,1)S(1)}, bf16[160,2560]{1,0:T(8,128)(2,1)S(1)}, u32[]{:S(2)}, u32[]{:S(2)}) collective-permute-start(bf16[160,2560]{1,0:T(8,128)(2,1)S(1)} %get-tuple-element.79), channel_id=1, source_target_pairs={{0,4},{1,5},{2,0},{3,1},{4,8},{5,9},{6,2},{7,3},{8,12},{9,13},{10,... | collective-permute-start | bytes 2457608 | tf_op jit(solution)/shard_map/ppermute | solution.py:429
  (1 other events, 0.7 us)

commit v9 on v8

--- a/solution.py
+++ b/solution.py
@@ -126,15 +126,17 @@
         self.chips = 2 * seq_count
         self.half = seq_count
         self.devices = seq_count * expert_count
-        self.slots = [(0, 0), (0, 1), (self.half, 0), (self.half, 1)]
-        for s in range(1, self.half):
-            self.slots += [(s, 0), (-s, 0), (s, 1), (-s, 1)]
-        slot_of = {(r % self.chips, k): i for i, (r, k) in enumerate(self.slots)}
-        self.owner_of = np.zeros((self.devices, len(self.slots)), np.int32)
-        self.sources_of = np.zeros((self.devices, len(self.slots), seq_count), np.int32)
+        self.slot_count = 4 * self.half
+        self.owner_of = np.zeros((self.devices, self.slot_count), np.int32)
+        self.sources_of = np.zeros((self.devices, self.slot_count, seq_count), np.int32)
         for d in range(self.devices):
             p, c = self.place(d)
-            for i, (r, k) in enumerate(self.slots):
+            slots = [(0, 0), (0, 1), (self.half, 0), (self.half, 1)]
+            for s in range(1, self.half):
+                along = -s if c else s
+                slots += [(-along, 0), (-along, 1), (along, 0), (along, 1)]
+            slot_of = {(r % self.chips, k): i for i, (r, k) in enumerate(slots)}
+            for i, (r, k) in enumerate(slots):
                 q = (p + r) % self.chips
                 self.owner_of[d, i] = self.device(q, c ^ k)
                 x = q // seq_count
@@ -151,11 +153,11 @@
         x, z = (0, pos) if pos < self.seq else (1, self.chips - 1 - pos)
         return z * self.expert + x * 2 + c
 
-    def step(self, by):
+    def step(self):
         pairs = []
         for d in range(self.devices):
             p, c = self.place(d)
-            pairs.append((d, self.device((p + by) % self.chips, c)))
+            pairs.append((d, self.device((p + (-1 if c else 1)) % self.chips, c)))
         return pairs
 
     def swap(self):
@@ -425,11 +427,8 @@
     text_rows, tok_count = text_tokens.shape[0], expert_ids.shape[0]
     me = lax.axis_index(AXES)
 
-    def onward(array):
-        return lax.ppermute(array, AXES, ring.step(1))
-
-    def back(array):
-        return lax.ppermute(array, AXES, ring.step(-1))
+    def along(array):
+        return lax.ppermute(array, AXES, ring.step())
 
     def across(array):
         return lax.ppermute(array, AXES, ring.swap())
@@ -442,64 +441,70 @@
     places = np.concatenate([numbers, seq_of, ring.sources_of.reshape(ring.devices, -1)], axis=1)
     places = jnp.asarray(places)[me]
 
-    before, after = onward(own), back(own)
-    other = across(own)
-    own, places = lax.optimization_barrier((own, places))
-
-    all_rows = len(ring.slots) * tok_count
+    all_rows = ring.slot_count * tok_count
+
+    def tied(*values):
+        return lax.optimization_barrier(values)
 
     def rows_of(*slots):
         return [slot * tok_count for slot in slots]
 
+    lead = along(own)
+    other = across(own)
+    own, places = tied(own, places)
     hidden, gate_up = hidden_call([own, other], rows_of(0, 1), gate_up_weight, None, all_rows)
-    hidden, before = lax.optimization_barrier((hidden, before))
-    hidden, after = lax.optimization_barrier((hidden, after))
-    cut = tok_count // 2
+    trail = along(other)
+    hidden, lead = tied(hidden, lead)
+    hidden, trail = tied(hidden, trail)
     swapped, swapped_rows = [], []
     for s in range(1, ring.half):
-        blocks, places_here = [after, before, *swapped], rows_of(4 * s, 4 * s + 1) + swapped_rows
-        swapped, swapped_rows = [across(after), across(before)], rows_of(4 * s + 2, 4 * s + 3)
-        if s + 1 == ring.half:
-            before, after = before[:cut], after[cut:]
-        before, after = onward(before), back(after)
+        blocks, block_rows = [lead, trail, *swapped], rows_of(4 * s, 4 * s + 1) + swapped_rows
+        next_lead = along(lead)
+        next_trail = along(trail) if s + 1 < ring.half else None
+        lead_across, trail_across = across(lead), across(trail)
         extra = down_weight if s == 1 else None
-        hidden, gate_up, *down = hidden_call(
-            blocks, places_here, gate_up, hidden, all_rows, extra
-        )
+        hidden, gate_up, *down = hidden_call(blocks, block_rows, gate_up, hidden, all_rows, extra)
         if down:
             (down_here,) = down
-        hidden, before, swapped = lax.optimization_barrier((hidden, before, swapped))
-        hidden, after = lax.optimization_barrier((hidden, after))
-    far = [before, after, across(before), across(after)]
+        hidden, lead, lead_across = tied(hidden, next_lead, lead_across)
+        if s + 1 < ring.half:
+            hidden, trail, trail_across = tied(hidden, next_trail, trail_across)
+        swapped, swapped_rows = [lead_across, trail_across], rows_of(4 * s + 3, 4 * s + 2)
+    far = [lead, across(lead)]
     hidden, gate_up = hidden_call(swapped, swapped_rows, gate_up, hidden, all_rows)
-    far_rows = [2 * tok_count + i * cut for i in range(4)]
-    (hidden,) = hidden_call(far, far_rows, gate_up, hidden, all_rows, last=True)
-
-    def outputs(*groups):
+    (hidden,) = hidden_call(far, rows_of(2, 3), gate_up, hidden, all_rows, last=True)
+
+    def outputs(hidden, *groups):
         return down_call(
             hidden, places, down_here, groups, tok_count, text_rows, seq_count, ring.devices
         )
 
-    def summed(kind):
-        if kind == ring.half:
-            mine, others = outputs((2,), (3,))
+    def for_other(hidden, s):
+        first, *rest = outputs(hidden, *(((4 * s + 1,), (4 * s,)) if s else ((1,),)))
+        first, hidden = tied(first, hidden)
+        return [first, *rest], hidden
+
+    mine, others = outputs(hidden, (2,), (3,))
+    mine, hidden = tied(mine, hidden)
+    others_next, hidden = for_other(hidden, ring.half - 1)
+    near = [across(array) for array in others_next]
+    total, hidden = tied(add_up(mine, across(others)), hidden)
+    lead, trail = along(total), []
+    leading, trailing = outputs(hidden, (4 * ring.half - 2,), (4 * ring.half - 1,))
+    leading, hidden = tied(leading, hidden)
+    for s in range(ring.half - 1, 0, -1):
+        others_next, hidden = for_other(hidden, s - 1)
+        trail = [along(add_up(trailing, near[1], *trail))]
+        if s > 1:
+            next_leading, trailing = outputs(hidden, (4 * s - 2,), (4 * s - 1,))
         else:
-            slots = range(4 * kind, 4 * kind + 4) if kind else range(2)
-            (others,) = outputs(tuple(slots[len(slots) // 2 :]))
-            (mine,) = outputs(tuple(slots[: len(slots) // 2]))
-        return mine, across(others)
-
-    mine, swapped = summed(ring.half)
-    ahead = onward(add_up(mine[:cut], swapped[:cut]))
-    behind = back(add_up(mine[cut:], swapped[cut:]))
-    ahead = jnp.pad(ahead, ((0, tok_count - cut), (0, 0)))
-    behind = jnp.pad(behind, ((cut, 0), (0, 0)))
-    for s in range(ring.half - 1, 0, -1):
-        mine, swapped = summed(s)
-        ahead = onward(add_up(ahead, mine[:tok_count], swapped[:tok_count]))
-        behind = back(add_up(behind, mine[tok_count:], swapped[tok_count:]))
-    mine, swapped = summed(0)
-    return add_up(mine, swapped, ahead, behind)
+            (next_leading,) = outputs(hidden, (0,))
+        next_leading, hidden = tied(next_leading, hidden)
+        total, hidden = tied(add_up(leading, near[0], lead), hidden)
+        lead, leading = along(total), next_leading
+        if s > 1:
+            near = [across(array) for array in others_next]
+    return add_up(leading, across(add_up(*others_next, *trail)), lead)
 
 
 def solution(mesh):

time: 184 us -> 171 us (0.929)
  waiting for transfers between devices: 70 us -> 47.2 us
  starting transfers between devices: 19.5 us -> 29.7 us
    ppermute x16 -> x14, waiting for transfers between devices: 69.9 us -> 47.2 us  [along(): return lax.ppermute(array, AXES, ring.step())]
    ppermute x16 -> x14, starting transfers between devices: 17.1 us -> 27 us  [along(): return lax.ppermute(array, AXES, ring.step())]
  transfers between devices with their start and end apart: 30 -> 30, of which waited for: 14 -> 10; matrix products, arithmetic and copies ran while one was open for 1% -> 2% of each run, Pallas kernels for 41% -> 44%
where the time goes in v9:
time: 171 us
  Pallas kernels  87.9 us (51%)
  waiting for transfers between devices  47.2 us (28%)
  starting transfers between devices  29.7 us (17%)
  other arithmetic  3.29 us (2%)
  local copies, waits for them, and re-layouts  2.74 us (2%)
    pallas_call x6, Pallas kernels, hidden_call(): pl.pallas_call(functools.partial(hidden_kernel, tuple(places), rows, chun...  47.5 us
    ppermute x14, waiting for transfers between devices, along(): return lax.ppermute(array, AXES, ring.step())  47.2 us
    pallas_call x9, Pallas kernels, down_call(): pl.pallas_call(functools.partial(down_kernel, groups, rows, text_rows, se...  39.2 us
    ppermute x14, starting transfers between devices, along(): return lax.ppermute(array, AXES, ring.step())  27 us
  transfers between devices with their start and end apart: 30, of which 10 were waited for; matrix products, arithmetic and copies ran while one was open for 2% of the time, Pallas kernels for 44%

profile of v9, /device:TPU:0, one launch (start us, length us, event | category | flops | bytes accessed | tf_op | source)
XLA Modules:
  0.0 171.0 jit_solution(7709894825179613077)
XLA Ops:
  3.8 2.6 %collective-permute-start.1 = (bf16[160,2688]{1,0:T(8,128)(2,1)S(1)}, bf16[160,2688]{1,0:T(8,128)(2,1)S(1)}, u32[]{:S(2)}, u32[]{:S(2)}) collective-permute-start(bf16[160,2688]{1,0:T(8,128)(2,1)S(1)} %shard_map.82.refs_0_), channel_id=1, source_target_pairs={{0,4},{1,3},{2,0},{3,7},{4,8},{5,1},{6,2},{7,11},{8,12},{9,5},{10,... | collective-permute-start | bytes 2580488 | tf_op jit(solution)/shard_map/ppermute | solution.py:431
  6.4 2.3 %collective-permute-start.2 = (bf16[160,2688]{1,0:T(8,128)(2,1)S(1)}, bf16[160,2688]{1,0:T(8,128)(2,1)S(1)}, u32[]{:S(2)}, u32[]{:S(2)}) collective-permute-start(bf16[160,2688]{1,0:T(8,128)(2,1)S(1)} %collective-permute-done.refs_1_), channel_id=1, source_target_pairs={{0,4},{1,3},{2,0},{3,7},{4,8},{5,1},{6,2},{7,11},{8,12},{9,5},{10,... | collective-permute-start | bytes 2580488 | tf_op jit(solution)/shard_map/ppermute | solution.py:431
  9.4 7.7 %shard_map.83 = (bf16[2560,1536]{1,0:T(8,128)(2,1)S(1)}, bf16[1,2,1408,2560]{3,2,1,0:T(8,128)(2,1)S(1)}) custom-call(bf16[160,2688]{1,0:T(8,128)(2,1)S(1)} %shard_map.82.refs_0_, bf16[160,2688]{1,0:T(8,128)(2,1)S(1)} %collective-permute-done.refs_1_, bf16[1,2,1408,2560]{3,2,1,0:T(8,128)(2,1)} %refs_2_.1), custom_call_target="tpu_custom_call" | custom-call | flops 4613734400 | bytes 16957440 | tf_op jit(solution)/shard_map/pallas_call | solution.py:322
  17.2 2.0 %collective-permute-start.3 = (bf16[160,2688]{1,0:T(8,128)(2,1)S(1)}, bf16[160,2688]{1,0:T(8,128)(2,1)S(1)}, u32[]{:S(2)}, u32[]{:S(2)}) collective-permute-start(bf16[160,2688]{1,0:T(8,128)(2,1)S(1)} %collective-permute-done.1.refs_0_), channel_id=1, source_target_pairs={{0,4},{1,3},{2,0},{3,7},{4,8},{5,1},{6,2},{7,11},{8,12},{9,5},{10,... | collective-permute-start | bytes 2580488 | tf_op jit(solution)/shard_map/ppermute | solution.py:431
  19.2 7.1 %collective-permute-done.2.refs_1_ = bf16[160,2688]{1,0:T(8,128)(2,1)S(1)} collective-permute-done((bf16[160,2688]{1,0:T(8,128)(2,1)S(1)}, bf16[160,2688]{1,0:T(8,128)(2,1)S(1)}, u32[]{:S(2)}, u32[]{:S(2)}) %collective-permute-start.2) | collective-permute-done | bytes 860192 | tf_op jit(solution)/shard_map/ppermute | solution.py:431
  26.3 2.1 %collective-permute-start.5 = (bf16[160,2688]{1,0:T(8,128)(2,1)S(1)}, bf16[160,2688]{1,0:T(8,128)(2,1)S(1)}, u32[]{:S(2)}, u32[]{:S(2)}) collective-permute-start(bf16[160,2688]{1,0:T(8,128)(2,1)S(1)} %collective-permute-done.2.refs_1_), channel_id=1, source_target_pairs={{0,4},{1,3},{2,0},{3,7},{4,8},{5,1},{6,2},{7,11},{8,12},{9,5},{10,... | collective-permute-start | bytes 2580488 | tf_op jit(solution)/shard_map/ppermute | solution.py:431
  28.4 6.1 %shard_map.84 = (bf16[2560,1536]{1,0:T(8,128)(2,1)S(1)}, bf16[1,2,1408,2560]{3,2,1,0:T(8,128)(2,1)S(1)}, bf16[1,1408,2560]{2,1,0:T(8,128)(2,1)S(1)}) custom-call(bf16[160,2688]{1,0:T(8,128)(2,1)S(1)} %collective-permute-done.1.refs_0_, bf16[160,2688]{1,0:T(8,128)(2,1)S(1)} %collective-permute-done.2.refs_1_, ...), custom_call_target="tpu_custom_call", output_to_operand_aliasing={{0}: (3, {}), {1}: (2, {})} | custom-call | flops 4613734400 | bytes 16957440 | tf_op jit(solution)/shard_map/pallas_call | solution.py:322
  35.5 2.1 %collective-permute-start.7 = (bf16[160,2688]{1,0:T(8,128)(2,1)S(1)}, bf16[160,2688]{1,0:T(8,128)(2,1)S(1)}, u32[]{:S(2)}, u32[]{:S(2)}) collective-permute-start(bf16[160,2688]{1,0:T(8,128)(2,1)S(1)} %collective-permute-done.3.refs_0_), channel_id=1, source_target_pairs={{0,4},{1,3},{2,0},{3,7},{4,8},{5,1},{6,2},{7,11},{8,12},{9,5},{10,... | collective-permute-start | bytes 2580488 | tf_op jit(solution)/shard_map/ppermute | solution.py:431
  37.6 7.1 %collective-permute-done.5.refs_1_ = bf16[160,2688]{1,0:T(8,128)(2,1)S(1)} collective-permute-done((bf16[160,2688]{1,0:T(8,128)(2,1)S(1)}, bf16[160,2688]{1,0:T(8,128)(2,1)S(1)}, u32[]{:S(2)}, u32[]{:S(2)}) %collective-permute-start.5) | collective-permute-done | bytes 860192 | tf_op jit(solution)/shard_map/ppermute | solution.py:431
  44.7 2.1 %collective-permute-start.9 = (bf16[160,2688]{1,0:T(8,128)(2,1)S(1)}, bf16[160,2688]{1,0:T(8,128)(2,1)S(1)}, u32[]{:S(2)}, u32[]{:S(2)}) collective-permute-start(bf16[160,2688]{1,0:T(8,128)(2,1)S(1)} %collective-permute-done.5.refs_1_), channel_id=1, source_target_pairs={{0,4},{1,3},{2,0},{3,7},{4,8},{5,1},{6,2},{7,11},{8,12},{9,5},{10,... | collective-permute-start | bytes 2580488 | tf_op jit(solution)/shard_map/ppermute | solution.py:431
  46.8 10.8 %shard_map.85 = (bf16[2560,1536]{1,0:T(8,128)(2,1)S(1)}, bf16[1,2,1408,2560]{3,2,1,0:T(8,128)(2,1)S(1)}) custom-call(bf16[160,2688]{1,0:T(8,128)(2,1)S(1)} %collective-permute-done.3.refs_0_, bf16[160,2688]{1,0:T(8,128)(2,1)S(1)} %collective-permute-done.5.refs_1_, ...), custom_call_target="tpu_custom_call", output_to_operand_aliasing={{0}: (5, {}), {1}: (4, {})} | custom-call | flops 9227468800 | bytes 19496960 | tf_op jit(solution)/shard_map/pallas_call | solution.py:322
  57.7 1.8 %collective-permute-start.11 = (bf16[160,2688]{1,0:T(8,128)(2,1)S(1)}, bf16[160,2688]{1,0:T(8,128)(2,1)S(1)}, u32[]{:S(2)}, u32[]{:S(2)}) collective-permute-start(bf16[160,2688]{1,0:T(8,128)(2,1)S(1)} %collective-permute-done.7.refs_0_), channel_id=1, source_target_pairs={{0,4},{1,3},{2,0},{3,7},{4,8},{5,1},{6,2},{7,11},{8,12},{9,5},{10,... | collective-permute-start | bytes 2580488 | tf_op jit(solution)/shard_map/ppermute | solution.py:431
  59.5 3.7 %collective-permute-done.9.refs_1_ = bf16[160,2688]{1,0:T(8,128)(2,1)S(1)} collective-permute-done((bf16[160,2688]{1,0:T(8,128)(2,1)S(1)}, bf16[160,2688]{1,0:T(8,128)(2,1)S(1)}, u32[]{:S(2)}, u32[]{:S(2)}) %collective-permute-start.9) | collective-permute-done | bytes 860192 | tf_op jit(solution)/shard_map/ppermute | solution.py:431
  63.2 10.8 %shard_map.86 = (bf16[2560,1536]{1,0:T(8,128)(2,1)S(1)}, bf16[1,2,1408,2560]{3,2,1,0:T(8,128)(2,1)S(1)}) custom-call(bf16[160,2688]{1,0:T(8,128)(2,1)S(1)} %collective-permute-done.7.refs_0_, bf16[160,2688]{1,0:T(8,128)(2,1)S(1)} %collective-permute-done.9.refs_1_, ...), custom_call_target="tpu_custom_call", output_to_operand_aliasing={{0}: (5, {}), {1}: (4, {})} | custom-call | flops 9227468800 | bytes 19496960 | tf_op jit(solution)/shard_map/pallas_call | solution.py:322
  74.6 6.1 %shard_map.87 = (bf16[2560,1536]{1,0:T(8,128)(2,1)S(1)}, bf16[1,2,1408,2560]{3,2,1,0:T(8,128)(2,1)S(1)}) custom-call(bf16[160,2688]{1,0:T(8,128)(2,1)S(1)} %collective-permute-done.12.refs_0_, bf16[160,2688]{1,0:T(8,128)(2,1)S(1)} %collective-permute-done.14.refs_1_, ...), custom_call_target="tpu_custom_call", output_to_operand_aliasing={{0}: (3, {}), {1}: (2, {})} | custom-call | flops 4613734400 | bytes 16957440 | tf_op jit(solution)/shard_map/pallas_call | solution.py:322
  80.7 6.1 %shard_map.88.hidden_ref = bf16[2560,1536]{1,0:T(8,128)(2,1)S(1)} custom-call(bf16[160,2688]{1,0:T(8,128)(2,1)S(1)} %collective-permute-done.11.refs_0_, bf16[160,2688]{1,0:T(8,128)(2,1)S(1)} %collective-permute-done.13.refs_1_, bf16[1,2,1408,2560]{3,2,1,0:T(8,128)(2,1)S(1)} %get-tuple-element.103.refs_2_, ...), custom_call_target="tpu_custom_call", output_to_operand_aliasing={{}: (3, {})} | custom-call | flops 4613734400 | bytes 16957440 | tf_op jit(solution)/shard_map/pallas_call | solution.py:322
  86.7 4.7 %shard_map.89 = (bf16[160,2560]{1,0:T(8,128)(2,1)S(1)}, bf16[160,2560]{1,0:T(8,128)(2,1)S(1)}) custom-call(s32[81]{0:T(128)S(1)} %dynamic-slice_bitcast_fusion.places_ref, bf16[2560,1536]{1,0:T(8,128)(2,1)S(1)} %shard_map.88.hidden_ref, bf16[1,1408,2560]{2,1,0:T(8,128)(2,1)S(1)} %get-tuple-element.105.w_ref), custom_call_target="tpu_custom_call" | custom-call | flops 2306867200 | bytes 8847360 | tf_op jit(solution)/shard_map/pallas_call | solution.py:392
  91.5 4.7 %shard_map.90 = (bf16[160,2560]{1,0:T(8,128)(2,1)S(1)}, bf16[160,2560]{1,0:T(8,128)(2,1)S(1)}) custom-call(s32[81]{0:T(128)S(1)} %dynamic-slice_bitcast_fusion.places_ref, bf16[2560,1536]{1,0:T(8,128)(2,1)S(1)} %shard_map.88.hidden_ref, bf16[1,1408,2560]{2,1,0:T(8,128)(2,1)S(1)} %get-tuple-element.105.w_ref), custom_call_target="tpu_custom_call" | custom-call | flops 2306867200 | bytes 8847360 | tf_op jit(solution)/shard_map/pallas_call | solution.py:392
  97.0 2.2 %collective-permute-start.18 = (bf16[160,2560]{1,0:T(8,128)(2,1)S(1)}, bf16[160,2560]{1,0:T(8,128)(2,1)S(1)}, u32[]{:S(2)}, u32[]{:S(2)}) collective-permute-start(bf16[160,2560]{1,0:T(8,128)(2,1)S(1)} %add_convert_fusion.8), channel_id=1, source_target_pairs={{0,4},{1,3},{2,0},{3,7},{4,8},{5,1},{6,2},{7,11},{8,12},{9,5},{10,... | collective-permute-start | bytes 2457608 | tf_op jit(solution)/shard_map/ppermute | solution.py:431
  99.2 4.7 %shard_map.91 = (bf16[160,2560]{1,0:T(8,128)(2,1)S(1)}, bf16[160,2560]{1,0:T(8,128)(2,1)S(1)}) custom-call(s32[81]{0:T(128)S(1)} %dynamic-slice_bitcast_fusion.places_ref, bf16[2560,1536]{1,0:T(8,128)(2,1)S(1)} %shard_map.88.hidden_ref, bf16[1,1408,2560]{2,1,0:T(8,128)(2,1)S(1)} %get-tuple-element.105.w_ref), custom_call_target="tpu_custom_call" | custom-call | flops 2306867200 | bytes 8847360 | tf_op jit(solution)/shard_map/pallas_call | solution.py:392
  103.8 4.7 %shard_map.92 = (bf16[160,2560]{1,0:T(8,128)(2,1)S(1)}, bf16[160,2560]{1,0:T(8,128)(2,1)S(1)}) custom-call(s32[81]{0:T(128)S(1)} %dynamic-slice_bitcast_fusion.places_ref, bf16[2560,1536]{1,0:T(8,128)(2,1)S(1)} %shard_map.88.hidden_ref, bf16[1,1408,2560]{2,1,0:T(8,128)(2,1)S(1)} %get-tuple-element.105.w_ref), custom_call_target="tpu_custom_call" | custom-call | flops 2306867200 | bytes 8847360 | tf_op jit(solution)/shard_map/pallas_call | solution.py:392
  108.5 4.7 %shard_map.93 = (bf16[160,2560]{1,0:T(8,128)(2,1)S(1)}, bf16[160,2560]{1,0:T(8,128)(2,1)S(1)}) custom-call(s32[81]{0:T(128)S(1)} %dynamic-slice_bitcast_fusion.places_ref, bf16[2560,1536]{1,0:T(8,128)(2,1)S(1)} %shard_map.88.hidden_ref, bf16[1,1408,2560]{2,1,0:T(8,128)(2,1)S(1)} %get-tuple-element.105.w_ref), custom_call_target="tpu_custom_call" | custom-call | flops 2306867200 | bytes 8847360 | tf_op jit(solution)/shard_map/pallas_call | solution.py:392
  115.5 1.9 %collective-permute-start.19 = (bf16[160,2560]{1,0:T(8,128)(2,1)S(1)}, bf16[160,2560]{1,0:T(8,128)(2,1)S(1)}, u32[]{:S(2)}, u32[]{:S(2)}) collective-permute-start(bf16[160,2560]{1,0:T(8,128)(2,1)S(1)} %add_convert_fusion.7), channel_id=1, source_target_pairs={{0,4},{1,3},{2,0},{3,7},{4,8},{5,1},{6,2},{7,11},{8,12},{9,5},{10,... | collective-permute-start | bytes 2457608 | tf_op jit(solution)/shard_map/ppermute | solution.py:431
  117.3 4.7 %shard_map.94 = (bf16[160,2560]{1,0:T(8,128)(2,1)S(1)}, bf16[160,2560]{1,0:T(8,128)(2,1)S(1)}) custom-call(s32[81]{0:T(128)S(1)} %dynamic-slice_bitcast_fusion.places_ref, bf16[2560,1536]{1,0:T(8,128)(2,1)S(1)} %shard_map.88.hidden_ref, bf16[1,1408,2560]{2,1,0:T(8,128)(2,1)S(1)} %get-tuple-element.105.w_ref), custom_call_target="tpu_custom_call" | custom-call | flops 2306867200 | bytes 8847360 | tf_op jit(solution)/shard_map/pallas_call | solution.py:392
  122.0 4.0 %collective-permute-done.23 = bf16[160,2560]{1,0:T(8,128)(2,1)S(1)} collective-permute-done((bf16[160,2560]{1,0:T(8,128)(2,1)S(1)}, bf16[160,2560]{1,0:T(8,128)(2,1)S(1)}, u32[]{:S(2)}, u32[]{:S(2)}) %collective-permute-start.23) | collective-permute-done | bytes 819232 | tf_op jit(solution)/shard_map/ppermute | solution.py:431
  127.8 4.7 %shard_map.95 = (bf16[160,2560]{1,0:T(8,128)(2,1)S(1)}, bf16[160,2560]{1,0:T(8,128)(2,1)S(1)}) custom-call(s32[81]{0:T(128)S(1)} %dynamic-slice_bitcast_fusion.places_ref, bf16[2560,1536]{1,0:T(8,128)(2,1)S(1)} %shard_map.88.hidden_ref, bf16[1,1408,2560]{2,1,0:T(8,128)(2,1)S(1)} %get-tuple-element.105.w_ref), custom_call_target="tpu_custom_call" | custom-call | flops 2306867200 | bytes 8847360 | tf_op jit(solution)/shard_map/pallas_call | solution.py:392
  136.6 6.9 %collective-permute-done.24 = bf16[160,2560]{1,0:T(8,128)(2,1)S(1)} collective-permute-done((bf16[160,2560]{1,0:T(8,128)(2,1)S(1)}, bf16[160,2560]{1,0:T(8,128)(2,1)S(1)}, u32[]{:S(2)}, u32[]{:S(2)}) %collective-permute-start.24) | collective-permute-done | bytes 819232 | tf_op jit(solution)/shard_map/ppermute | solution.py:431
  145.4 3.2 %shard_map.96 = bf16[160,2560]{1,0:T(8,128)(2,1)S(1)} custom-call(s32[81]{0:T(128)S(1)} %dynamic-slice_bitcast_fusion.places_ref, bf16[2560,1536]{1,0:T(8,128)(2,1)S(1)} %shard_map.88.hidden_ref, bf16[1,1408,2560]{2,1,0:T(8,128)(2,1)S(1)} %get-tuple-element.105.w_ref), custom_call_target="tpu_custom_call" | custom-call | flops 1153433600 | bytes 8028160 | tf_op jit(solution)/shard_map/pallas_call | solution.py:392
  148.6 3.7 %collective-permute-done.28 = bf16[160,2560]{1,0:T(8,128)(2,1)S(1)} collective-permute-done((bf16[160,2560]{1,0:T(8,128)(2,1)S(1)}, bf16[160,2560]{1,0:T(8,128)(2,1)S(1)}, u32[]{:S(2)}, u32[]{:S(2)}) %collective-permute-start.28) | collective-permute-done | bytes 819232 | tf_op jit(solution)/shard_map/ppermute | solution.py:431
  154.2 6.8 %collective-permute-done.25 = bf16[160,2560]{1,0:T(8,128)(2,1)S(1)} collective-permute-done((bf16[160,2560]{1,0:T(8,128)(2,1)S(1)}, bf16[160,2560]{1,0:T(8,128)(2,1)S(1)}, u32[]{:S(2)}, u32[]{:S(2)}) %collective-permute-start.25) | collective-permute-done | bytes 819232 | tf_op jit(solution)/shard_map/ppermute | solution.py:431
  161.3 3.2 %shard_map.97 = bf16[160,2560]{1,0:T(8,128)(2,1)S(1)} custom-call(s32[81]{0:T(128)S(1)} %dynamic-slice_bitcast_fusion.places_ref, bf16[2560,1536]{1,0:T(8,128)(2,1)S(1)} %shard_map.88.hidden_ref, bf16[1,1408,2560]{2,1,0:T(8,128)(2,1)S(1)} %get-tuple-element.105.w_ref), custom_call_target="tpu_custom_call" | custom-call | flops 1153433600 | bytes 8028160 | tf_op jit(solution)/shard_map/pallas_call | solution.py:392
  164.5 5.3 %collective-permute-done.29 = bf16[160,2560]{1,0:T(8,128)(2,1)S(1)} collective-permute-done((bf16[160,2560]{1,0:T(8,128)(2,1)S(1)}, bf16[160,2560]{1,0:T(8,128)(2,1)S(1)}, u32[]{:S(2)}, u32[]{:S(2)}) %collective-permute-start.29) | collective-permute-done | bytes 819232 | tf_op jit(solution)/shard_map/ppermute | solution.py:431
  (60 shorter events, 20.5 us)
Async XLA Ops:
  0.0 0.7 copy-start
  0.7 0.7 copy-start.1
  3.3 3.2 %collective-permute-start = (bf16[160,2688]{1,0:T(8,128)(2,1)S(1)}, bf16[160,2688]{1,0:T(8,128)(2,1)S(1)}, u32[]{:S(2)}, u32[]{:S(2)}) collective-permute-start(bf16[160,2688]{1,0:T(8,128)(2,1)S(1)} %shard_map.82.refs_0_), channel_id=1, source_target_pairs={{0,1},{1,0},{2,3},{3,2},{4,5},{5,4},{6,7},{7,6},{8,9},{9,8},{10,11... | collective-permute-start | bytes 2580488 | tf_op jit(solution)/shard_map/ppermute | solution.py:434
  3.8 13.4 %collective-permute-start.1 = (bf16[160,2688]{1,0:T(8,128)(2,1)S(1)}, bf16[160,2688]{1,0:T(8,128)(2,1)S(1)}, u32[]{:S(2)}, u32[]{:S(2)}) collective-permute-start(bf16[160,2688]{1,0:T(8,128)(2,1)S(1)} %shard_map.82.refs_0_), channel_id=1, source_target_pairs={{0,4},{1,3},{2,0},{3,7},{4,8},{5,1},{6,2},{7,11},{8,12},{9,5},{10,... | collective-permute-start | bytes 2580488 | tf_op jit(solution)/shard_map/ppermute | solution.py:431
  6.4 19.9 %collective-permute-start.2 = (bf16[160,2688]{1,0:T(8,128)(2,1)S(1)}, bf16[160,2688]{1,0:T(8,128)(2,1)S(1)}, u32[]{:S(2)}, u32[]{:S(2)}) collective-permute-start(bf16[160,2688]{1,0:T(8,128)(2,1)S(1)} %collective-permute-done.refs_1_), channel_id=1, source_target_pairs={{0,4},{1,3},{2,0},{3,7},{4,8},{5,1},{6,2},{7,11},{8,12},{9,5},{10,... | collective-permute-start | bytes 2580488 | tf_op jit(solution)/shard_map/ppermute | solution.py:431
  17.2 18.3 %collective-permute-start.3 = (bf16[160,2688]{1,0:T(8,128)(2,1)S(1)}, bf16[160,2688]{1,0:T(8,128)(2,1)S(1)}, u32[]{:S(2)}, u32[]{:S(2)}) collective-permute-start(bf16[160,2688]{1,0:T(8,128)(2,1)S(1)} %collective-permute-done.1.refs_0_), channel_id=1, source_target_pairs={{0,4},{1,3},{2,0},{3,7},{4,8},{5,1},{6,2},{7,11},{8,12},{9,5},{10,... | collective-permute-start | bytes 2580488 | tf_op jit(solution)/shard_map/ppermute | solution.py:431
  19.2 16.3 %collective-permute-start.4 = (bf16[160,2688]{1,0:T(8,128)(2,1)S(1)}, bf16[160,2688]{1,0:T(8,128)(2,1)S(1)}, u32[]{:S(2)}, u32[]{:S(2)}) collective-permute-start(bf16[160,2688]{1,0:T(8,128)(2,1)S(1)} %collective-permute-done.1.refs_0_), channel_id=1, source_target_pairs={{0,1},{1,0},{2,3},{3,2},{4,5},{5,4},{6,7},{7,6},{8,9},{9,8},{10,11... | collective-permute-start | bytes 2580488 | tf_op jit(solution)/shard_map/ppermute | solution.py:434
  26.3 18.4 %collective-permute-start.5 = (bf16[160,2688]{1,0:T(8,128)(2,1)S(1)}, bf16[160,2688]{1,0:T(8,128)(2,1)S(1)}, u32[]{:S(2)}, u32[]{:S(2)}) collective-permute-start(bf16[160,2688]{1,0:T(8,128)(2,1)S(1)} %collective-permute-done.2.refs_1_), channel_id=1, source_target_pairs={{0,4},{1,3},{2,0},{3,7},{4,8},{5,1},{6,2},{7,11},{8,12},{9,5},{10,... | collective-permute-start | bytes 2580488 | tf_op jit(solution)/shard_map/ppermute | solution.py:431
  28.4 16.3 %collective-permute-start.6 = (bf16[160,2688]{1,0:T(8,128)(2,1)S(1)}, bf16[160,2688]{1,0:T(8,128)(2,1)S(1)}, u32[]{:S(2)}, u32[]{:S(2)}) collective-permute-start(bf16[160,2688]{1,0:T(8,128)(2,1)S(1)} %collective-permute-done.2.refs_1_), channel_id=1, source_target_pairs={{0,1},{1,0},{2,3},{3,2},{4,5},{5,4},{6,7},{7,6},{8,9},{9,8},{10,11... | collective-permute-start | bytes 2580488 | tf_op jit(solution)/shard_map/ppermute | solution.py:434
  35.5 22.1 %collective-permute-start.7 = (bf16[160,2688]{1,0:T(8,128)(2,1)S(1)}, bf16[160,2688]{1,0:T(8,128)(2,1)S(1)}, u32[]{:S(2)}, u32[]{:S(2)}) collective-permute-start(bf16[160,2688]{1,0:T(8,128)(2,1)S(1)} %collective-permute-done.3.refs_0_), channel_id=1, source_target_pairs={{0,4},{1,3},{2,0},{3,7},{4,8},{5,1},{6,2},{7,11},{8,12},{9,5},{10,... | collective-permute-start | bytes 2580488 | tf_op jit(solution)/shard_map/ppermute | solution.py:431
  37.6 20.0 %collective-permute-start.8 = (bf16[160,2688]{1,0:T(8,128)(2,1)S(1)}, bf16[160,2688]{1,0:T(8,128)(2,1)S(1)}, u32[]{:S(2)}, u32[]{:S(2)}) collective-permute-start(bf16[160,2688]{1,0:T(8,128)(2,1)S(1)} %collective-permute-done.3.refs_0_), channel_id=1, source_target_pairs={{0,1},{1,0},{2,3},{3,2},{4,5},{5,4},{6,7},{7,6},{8,9},{9,8},{10,11... | collective-permute-start | bytes 2580488 | tf_op jit(solution)/shard_map/ppermute | solution.py:434
  44.7 18.4 %collective-permute-start.9 = (bf16[160,2688]{1,0:T(8,128)(2,1)S(1)}, bf16[160,2688]{1,0:T(8,128)(2,1)S(1)}, u32[]{:S(2)}, u32[]{:S(2)}) collective-permute-start(bf16[160,2688]{1,0:T(8,128)(2,1)S(1)} %collective-permute-done.5.refs_1_), channel_id=1, source_target_pairs={{0,4},{1,3},{2,0},{3,7},{4,8},{5,1},{6,2},{7,11},{8,12},{9,5},{10,... | collective-permute-start | bytes 2580488 | tf_op jit(solution)/shard_map/ppermute | solution.py:431
  46.8 16.3 %collective-permute-start.10 = (bf16[160,2688]{1,0:T(8,128)(2,1)S(1)}, bf16[160,2688]{1,0:T(8,128)(2,1)S(1)}, u32[]{:S(2)}, u32[]{:S(2)}) collective-permute-start(bf16[160,2688]{1,0:T(8,128)(2,1)S(1)} %collective-permute-done.5.refs_1_), channel_id=1, source_target_pairs={{0,1},{1,0},{2,3},{3,2},{4,5},{5,4},{6,7},{7,6},{8,9},{9,8},{10,11... | collective-permute-start | bytes 2580488 | tf_op jit(solution)/shard_map/ppermute | solution.py:434
  57.7 16.3 %collective-permute-start.11 = (bf16[160,2688]{1,0:T(8,128)(2,1)S(1)}, bf16[160,2688]{1,0:T(8,128)(2,1)S(1)}, u32[]{:S(2)}, u32[]{:S(2)}) collective-permute-start(bf16[160,2688]{1,0:T(8,128)(2,1)S(1)} %collective-permute-done.7.refs_0_), channel_id=1, source_target_pairs={{0,4},{1,3},{2,0},{3,7},{4,8},{5,1},{6,2},{7,11},{8,12},{9,5},{10,... | collective-permute-start | bytes 2580488 | tf_op jit(solution)/shard_map/ppermute | solution.py:431
  59.5 14.5 %collective-permute-start.12 = (bf16[160,2688]{1,0:T(8,128)(2,1)S(1)}, bf16[160,2688]{1,0:T(8,128)(2,1)S(1)}, u32[]{:S(2)}, u32[]{:S(2)}) collective-permute-start(bf16[160,2688]{1,0:T(8,128)(2,1)S(1)} %collective-permute-done.7.refs_0_), channel_id=1, source_target_pairs={{0,1},{1,0},{2,3},{3,2},{4,5},{5,4},{6,7},{7,6},{8,9},{9,8},{10,11... | collective-permute-start | bytes 2580488 | tf_op jit(solution)/shard_map/ppermute | solution.py:434
  63.2 11.4 %collective-permute-start.14 = (bf16[160,2688]{1,0:T(8,128)(2,1)S(1)}, bf16[160,2688]{1,0:T(8,128)(2,1)S(1)}, u32[]{:S(2)}, u32[]{:S(2)}) collective-permute-start(bf16[160,2688]{1,0:T(8,128)(2,1)S(1)} %collective-permute-done.9.refs_1_), channel_id=1, source_target_pairs={{0,1},{1,0},{2,3},{3,2},{4,5},{5,4},{6,7},{7,6},{8,9},{9,8},{10,11... | collective-permute-start | bytes 2580488 | tf_op jit(solution)/shard_map/ppermute | solution.py:434
  74.0 6.6 %collective-permute-start.13 = (bf16[160,2688]{1,0:T(8,128)(2,1)S(1)}, bf16[160,2688]{1,0:T(8,128)(2,1)S(1)}, u32[]{:S(2)}, u32[]{:S(2)}) collective-permute-start(bf16[160,2688]{1,0:T(8,128)(2,1)S(1)} %collective-permute-done.11.refs_0_), channel_id=1, source_target_pairs={{0,1},{1,0},{2,3},{3,2},{4,5},{5,4},{6,7},{7,6},{8,9},{9,8},{10,11... | collective-permute-start | bytes 2580488 | tf_op jit(solution)/shard_map/ppermute | solution.py:434
  91.4 5.4 %collective-permute-start.15 = (bf16[160,2560]{1,0:T(8,128)(2,1)S(1)}, bf16[160,2560]{1,0:T(8,128)(2,1)S(1)}, u32[]{:S(2)}, u32[]{:S(2)}) collective-permute-start(bf16[160,2560]{1,0:T(8,128)(2,1)S(1)} %get-tuple-element.108), channel_id=1, source_target_pairs={{0,1},{1,0},{2,3},{3,2},{4,5},{5,4},{6,7},{7,6},{8,9},{9,8},{10,11... | collective-permute-start | bytes 2457608 | tf_op jit(solution)/shard_map/ppermute | solution.py:434
  96.2 19.0 %collective-permute-start.17 = (bf16[160,2560]{1,0:T(8,128)(2,1)S(1)}, bf16[160,2560]{1,0:T(8,128)(2,1)S(1)}, u32[]{:S(2)}, u32[]{:S(2)}) collective-permute-start(bf16[160,2560]{1,0:T(8,128)(2,1)S(1)} %get-tuple-element.121), channel_id=1, source_target_pairs={{0,1},{1,0},{2,3},{3,2},{4,5},{5,4},{6,7},{7,6},{8,9},{9,8},{10,11... | collective-permute-start | bytes 2457608 | tf_op jit(solution)/shard_map/ppermute | solution.py:434
  96.7 16.6 %collective-permute-start.22 = (bf16[160,2560]{1,0:T(8,128)(2,1)S(1)}, bf16[160,2560]{1,0:T(8,128)(2,1)S(1)}, u32[]{:S(2)}, u32[]{:S(2)}) collective-permute-start(bf16[160,2560]{1,0:T(8,128)(2,1)S(1)} %get-tuple-element.139), channel_id=1, source_target_pairs={{0,1},{1,0},{2,3},{3,2},{4,5},{5,4},{6,7},{7,6},{8,9},{9,8},{10,11... | collective-permute-start | bytes 2457608 | tf_op jit(solution)/shard_map/ppermute | solution.py:434
  97.0 18.1 %collective-permute-start.18 = (bf16[160,2560]{1,0:T(8,128)(2,1)S(1)}, bf16[160,2560]{1,0:T(8,128)(2,1)S(1)}, u32[]{:S(2)}, u32[]{:S(2)}) collective-permute-start(bf16[160,2560]{1,0:T(8,128)(2,1)S(1)} %add_convert_fusion.8), channel_id=1, source_target_pairs={{0,4},{1,3},{2,0},{3,7},{4,8},{5,1},{6,2},{7,11},{8,12},{9,5},{10,... | collective-permute-start | bytes 2457608 | tf_op jit(solution)/shard_map/ppermute | solution.py:431
  113.2 19.9 %collective-permute-start.16 = (bf16[160,2560]{1,0:T(8,128)(2,1)S(1)}, bf16[160,2560]{1,0:T(8,128)(2,1)S(1)}, u32[]{:S(2)}, u32[]{:S(2)}) collective-permute-start(bf16[160,2560]{1,0:T(8,128)(2,1)S(1)} %get-tuple-element.119), channel_id=1, source_target_pairs={{0,1},{1,0},{2,3},{3,2},{4,5},{5,4},{6,7},{7,6},{8,9},{9,8},{10,11... | collective-permute-start | bytes 2457608 | tf_op jit(solution)/shard_map/ppermute | solution.py:434
  113.6 12.4 %collective-permute-start.23 = (bf16[160,2560]{1,0:T(8,128)(2,1)S(1)}, bf16[160,2560]{1,0:T(8,128)(2,1)S(1)}, u32[]{:S(2)}, u32[]{:S(2)}) collective-permute-start(bf16[160,2560]{1,0:T(8,128)(2,1)S(1)} %add_convert_fusion.5), channel_id=1, source_target_pairs={{0,4},{1,3},{2,0},{3,7},{4,8},{5,1},{6,2},{7,11},{8,12},{9,5},{10,... | collective-permute-start | bytes 2457608 | tf_op jit(solution)/shard_map/ppermute | solution.py:431
  115.1 10.8 %collective-permute-start.21 = (bf16[160,2560]{1,0:T(8,128)(2,1)S(1)}, bf16[160,2560]{1,0:T(8,128)(2,1)S(1)}, u32[]{:S(2)}, u32[]{:S(2)}) collective-permute-start(bf16[160,2560]{1,0:T(8,128)(2,1)S(1)} %get-tuple-element.137), channel_id=1, source_target_pairs={{0,1},{1,0},{2,3},{3,2},{4,5},{5,4},{6,7},{7,6},{8,9},{9,8},{10,11... | collective-permute-start | bytes 2457608 | tf_op jit(solution)/shard_map/ppermute | solution.py:434
  115.5 19.3 %collective-permute-start.19 = (bf16[160,2560]{1,0:T(8,128)(2,1)S(1)}, bf16[160,2560]{1,0:T(8,128)(2,1)S(1)}, u32[]{:S(2)}, u32[]{:S(2)}) collective-permute-start(bf16[160,2560]{1,0:T(8,128)(2,1)S(1)} %add_convert_fusion.7), channel_id=1, source_target_pairs={{0,4},{1,3},{2,0},{3,7},{4,8},{5,1},{6,2},{7,11},{8,12},{9,5},{10,... | collective-permute-start | bytes 2457608 | tf_op jit(solution)/shard_map/ppermute | solution.py:431
  126.2 17.3 %collective-permute-start.24 = (bf16[160,2560]{1,0:T(8,128)(2,1)S(1)}, bf16[160,2560]{1,0:T(8,128)(2,1)S(1)}, u32[]{:S(2)}, u32[]{:S(2)}) collective-permute-start(bf16[160,2560]{1,0:T(8,128)(2,1)S(1)} %add_convert_fusion.4), channel_id=1, source_target_pairs={{0,4},{1,3},{2,0},{3,7},{4,8},{5,1},{6,2},{7,11},{8,12},{9,5},{10,... | collective-permute-start | bytes 2457608 | tf_op jit(solution)/shard_map/ppermute | solution.py:431
  127.8 15.7 %collective-permute-start.20 = (bf16[160,2560]{1,0:T(8,128)(2,1)S(1)}, bf16[160,2560]{1,0:T(8,128)(2,1)S(1)}, u32[]{:S(2)}, u32[]{:S(2)}) collective-permute-start(bf16[160,2560]{1,0:T(8,128)(2,1)S(1)} %get-tuple-element.135), channel_id=1, source_target_pairs={{0,1},{1,0},{2,3},{3,2},{4,5},{5,4},{6,7},{7,6},{8,9},{9,8},{10,11... | collective-permute-start | bytes 2457608 | tf_op jit(solution)/shard_map/ppermute | solution.py:434
  132.5 16.1 %collective-permute-start.27 = (bf16[160,2560]{1,0:T(8,128)(2,1)S(1)}, bf16[160,2560]{1,0:T(8,128)(2,1)S(1)}, u32[]{:S(2)}, u32[]{:S(2)}) collective-permute-start(bf16[160,2560]{1,0:T(8,128)(2,1)S(1)} %get-tuple-element.141), channel_id=1, source_target_pairs={{0,1},{1,0},{2,3},{3,2},{4,5},{5,4},{6,7},{7,6},{8,9},{9,8},{10,11... | collective-permute-start | bytes 2457608 | tf_op jit(solution)/shard_map/ppermute | solution.py:434
  135.0 17.3 %collective-permute-start.28 = (bf16[160,2560]{1,0:T(8,128)(2,1)S(1)}, bf16[160,2560]{1,0:T(8,128)(2,1)S(1)}, u32[]{:S(2)}, u32[]{:S(2)}) collective-permute-start(bf16[160,2560]{1,0:T(8,128)(2,1)S(1)} %add_convert_fusion.6), channel_id=1, source_target_pairs={{0,4},{1,3},{2,0},{3,7},{4,8},{5,1},{6,2},{7,11},{8,12},{9,5},{10,... | collective-permute-start | bytes 2457608 | tf_op jit(solution)/shard_map/ppermute | solution.py:431
  143.8 17.3 %collective-permute-start.25 = (bf16[160,2560]{1,0:T(8,128)(2,1)S(1)}, bf16[160,2560]{1,0:T(8,128)(2,1)S(1)}, u32[]{:S(2)}, u32[]{:S(2)}) collective-permute-start(bf16[160,2560]{1,0:T(8,128)(2,1)S(1)} %add_convert_fusion.3), channel_id=1, source_target_pairs={{0,4},{1,3},{2,0},{3,7},{4,8},{5,1},{6,2},{7,11},{8,12},{9,5},{10,... | collective-permute-start | bytes 2457608 | tf_op jit(solution)/shard_map/ppermute | solution.py:431
  152.6 17.2 %collective-permute-start.29 = (bf16[160,2560]{1,0:T(8,128)(2,1)S(1)}, bf16[160,2560]{1,0:T(8,128)(2,1)S(1)}, u32[]{:S(2)}, u32[]{:S(2)}) collective-permute-start(bf16[160,2560]{1,0:T(8,128)(2,1)S(1)} %add_convert_fusion.1), channel_id=1, source_target_pairs={{0,4},{1,3},{2,0},{3,7},{4,8},{5,1},{6,2},{7,11},{8,12},{9,5},{10,... | collective-permute-start | bytes 2457608 | tf_op jit(solution)/shard_map/ppermute | solution.py:431
  161.2 8.6 %collective-permute-start.26 = (bf16[160,2560]{1,0:T(8,128)(2,1)S(1)}, bf16[160,2560]{1,0:T(8,128)(2,1)S(1)}, u32[]{:S(2)}, u32[]{:S(2)}) collective-permute-start(bf16[160,2560]{1,0:T(8,128)(2,1)S(1)} %add_convert_fusion.2), channel_id=1, source_target_pairs={{0,1},{1,0},{2,3},{3,2},{4,5},{5,4},{6,7},{7,6},{8,9},{9,8},{10,11... | collective-permute-start | bytes 2457608 | tf_op jit(solution)/shard_map/ppermute | solution.py:434
  (1 other events, 0.7 us)

commit v10 on v9

--- a/solution.py
+++ b/solution.py
@@ -456,19 +456,25 @@
     trail = along(other)
     hidden, lead = tied(hidden, lead)
     hidden, trail = tied(hidden, trail)
-    swapped, swapped_rows = [], []
+    swapped = swapped_rows = None
     for s in range(1, ring.half):
-        blocks, block_rows = [lead, trail, *swapped], rows_of(4 * s, 4 * s + 1) + swapped_rows
         next_lead = along(lead)
+        lead_across = across(lead)
+        if swapped:
+            hidden, gate_up = hidden_call(swapped, swapped_rows, gate_up, hidden, all_rows)
+            hidden, trail = tied(hidden, trail)
         next_trail = along(trail) if s + 1 < ring.half else None
-        lead_across, trail_across = across(lead), across(trail)
+        trail_across = across(trail)
         extra = down_weight if s == 1 else None
-        hidden, gate_up, *down = hidden_call(blocks, block_rows, gate_up, hidden, all_rows, extra)
+        hidden, gate_up, *down = hidden_call(
+            [lead, trail], rows_of(4 * s, 4 * s + 1), gate_up, hidden, all_rows, extra
+        )
         if down:
             (down_here,) = down
-        hidden, lead, lead_across = tied(hidden, next_lead, lead_across)
-        if s + 1 < ring.half:
-            hidden, trail, trail_across = tied(hidden, next_trail, trail_across)
+        hidden, lead, lead_across, trail_across = tied(
+            hidden, next_lead, lead_across, trail_across
+        )
+        trail = next_trail
         swapped, swapped_rows = [lead_across, trail_across], rows_of(4 * s + 3, 4 * s + 2)
     far = [lead, across(lead)]
     hidden, gate_up = hidden_call(swapped, swapped_rows, gate_up, hidden, all_rows)
@@ -484,27 +490,32 @@
         first, hidden = tied(first, hidden)
         return [first, *rest], hidden
 
+    def for_own(hidden, s):
+        first, *rest = outputs(hidden, *(((4 * s + 2,), (4 * s + 3,)) if s else ((0,),)))
+        first, hidden = tied(first, hidden)
+        return [first, *rest], hidden
+
+    def sent(hidden, *parts):
+        total, hidden = tied(add_up(*parts), hidden)
+        return along(total), hidden
+
     mine, others = outputs(hidden, (2,), (3,))
     mine, hidden = tied(mine, hidden)
-    others_next, hidden = for_other(hidden, ring.half - 1)
-    near = [across(array) for array in others_next]
-    total, hidden = tied(add_up(mine, across(others)), hidden)
-    lead, trail = along(total), []
-    leading, trailing = outputs(hidden, (4 * ring.half - 2,), (4 * ring.half - 1,))
-    leading, hidden = tied(leading, hidden)
+    swapped, hidden = for_other(hidden, ring.half - 1)
+    swapped = [across(array) for array in swapped]
+    lead, hidden = sent(hidden, mine, across(others))
+    mine, hidden = for_own(hidden, ring.half - 1)
+    trail, hidden = sent(hidden, mine[1], swapped[1])
     for s in range(ring.half - 1, 0, -1):
-        others_next, hidden = for_other(hidden, s - 1)
-        trail = [along(add_up(trailing, near[1], *trail))]
+        next_swapped, hidden = for_other(hidden, s - 1)
         if s > 1:
-            next_leading, trailing = outputs(hidden, (4 * s - 2,), (4 * s - 1,))
-        else:
-            (next_leading,) = outputs(hidden, (0,))
-        next_leading, hidden = tied(next_leading, hidden)
-        total, hidden = tied(add_up(leading, near[0], lead), hidden)
-        lead, leading = along(total), next_leading
+            next_swapped = [across(array) for array in next_swapped]
+        lead, hidden = sent(hidden, mine[0], swapped[0], lead)
+        mine, hidden = for_own(hidden, s - 1)
+        swapped = next_swapped
         if s > 1:
-            near = [across(array) for array in others_next]
-    return add_up(leading, across(add_up(*others_next, *trail)), lead)
+            trail, hidden = sent(hidden, mine[1], swapped[1], trail)
+    return add_up(mine[0], across(add_up(swapped[0], trail)), lead)
 
 
 def solution(mesh):

time: 171 us -> 165 us (0.965)
  waiting for transfers between devices: 47.2 us -> 38 us
  Pallas kernels: 87.9 us -> 90.5 us
    ppermute x14, waiting for transfers between devices: 47.2 us -> 38 us  [along(): return lax.ppermute(array, AXES, ring.step())]
    pallas_call x6 -> x8, Pallas kernels: 47.5 us -> 50.1 us  [hidden_call(): pl.pallas_call(functools.partial(hidden_kernel, tuple(places), rows, chun...]
  transfers between devices with their start and end apart: 30 -> 30, of which waited for: 10 -> 12; matrix products, arithmetic and copies ran while one was open for 2% -> 2% of each run, Pallas kernels for 44% -> 48%
where the time goes in v10:
time: 165 us
  Pallas kernels  90.5 us (55%)
  waiting for transfers between devices  38 us (23%)
  starting transfers between devices  29.5 us (18%)
  other arithmetic  3.62 us (2%)
  local copies, waits for them, and re-layouts  2.74 us (2%)
    pallas_call x8, Pallas kernels, hidden_call(): pl.pallas_call(functools.partial(hidden_kernel, tuple(places), rows, chun...  50.1 us
    pallas_call x9, Pallas kernels, down_call(): pl.pallas_call(functools.partial(down_kernel, groups, rows, text_rows, se...  39.2 us
    ppermute x14, waiting for transfers between devices, along(): return lax.ppermute(array, AXES, ring.step())  38 us
    ppermute x14, starting transfers between devices, along(): return lax.ppermute(array, AXES, ring.step())  27.6 us
    convert_element_type x9, other arithmetic, add_up(): return total.astype(jnp.bfloat16)  3.62 us
  transfers between devices with their start and end apart: 30, of which 12 were waited for; matrix products, arithmetic and copies ran while one was open for 2% of the time, Pallas kernels for 48%

profile of v10, /device:TPU:0, one launch (start us, length us, event | category | flops | bytes accessed | tf_op | source)
XLA Modules:
  0.0 164.6 jit_solution(7405123068607272252)
XLA Ops:
  3.8 2.6 %collective-permute-start.1 = (bf16[160,2688]{1,0:T(8,128)(2,1)S(1)}, bf16[160,2688]{1,0:T(8,128)(2,1)S(1)}, u32[]{:S(2)}, u32[]{:S(2)}) collective-permute-start(bf16[160,2688]{1,0:T(8,128)(2,1)S(1)} %shard_map.82.refs_0_), channel_id=1, source_target_pairs={{0,4},{1,3},{2,0},{3,7},{4,8},{5,1},{6,2},{7,11},{8,12},{9,5},{10,... | collective-permute-start | bytes 2580488 | tf_op jit(solution)/shard_map/ppermute | solution.py:431
  6.4 2.3 %collective-permute-start.2 = (bf16[160,2688]{1,0:T(8,128)(2,1)S(1)}, bf16[160,2688]{1,0:T(8,128)(2,1)S(1)}, u32[]{:S(2)}, u32[]{:S(2)}) collective-permute-start(bf16[160,2688]{1,0:T(8,128)(2,1)S(1)} %collective-permute-done.refs_1_), channel_id=1, source_target_pairs={{0,4},{1,3},{2,0},{3,7},{4,8},{5,1},{6,2},{7,11},{8,12},{9,5},{10,... | collective-permute-start | bytes 2580488 | tf_op jit(solution)/shard_map/ppermute | solution.py:431
  9.4 7.7 %shard_map.83 = (bf16[2560,1536]{1,0:T(8,128)(2,1)S(1)}, bf16[1,2,1408,2560]{3,2,1,0:T(8,128)(2,1)S(1)}) custom-call(bf16[160,2688]{1,0:T(8,128)(2,1)S(1)} %shard_map.82.refs_0_, bf16[160,2688]{1,0:T(8,128)(2,1)S(1)} %collective-permute-done.refs_1_, bf16[1,2,1408,2560]{3,2,1,0:T(8,128)(2,1)} %refs_2_.1), custom_call_target="tpu_custom_call" | custom-call | flops 4613734400 | bytes 16957440 | tf_op jit(solution)/shard_map/pallas_call | solution.py:322
  19.2 7.1 %collective-permute-done.2.refs_1_ = bf16[160,2688]{1,0:T(8,128)(2,1)S(1)} collective-permute-done((bf16[160,2688]{1,0:T(8,128)(2,1)S(1)}, bf16[160,2688]{1,0:T(8,128)(2,1)S(1)}, u32[]{:S(2)}, u32[]{:S(2)}) %collective-permute-start.2) | collective-permute-done | bytes 860192 | tf_op jit(solution)/shard_map/ppermute | solution.py:431
  26.3 2.1 %collective-permute-start.6 = (bf16[160,2688]{1,0:T(8,128)(2,1)S(1)}, bf16[160,2688]{1,0:T(8,128)(2,1)S(1)}, u32[]{:S(2)}, u32[]{:S(2)}) collective-permute-start(bf16[160,2688]{1,0:T(8,128)(2,1)S(1)} %collective-permute-done.2.refs_1_), channel_id=1, source_target_pairs={{0,4},{1,3},{2,0},{3,7},{4,8},{5,1},{6,2},{7,11},{8,12},{9,5},{10,... | collective-permute-start | bytes 2580488 | tf_op jit(solution)/shard_map/ppermute | solution.py:431
  28.4 6.1 %shard_map.84 = (bf16[2560,1536]{1,0:T(8,128)(2,1)S(1)}, bf16[1,2,1408,2560]{3,2,1,0:T(8,128)(2,1)S(1)}, bf16[1,1408,2560]{2,1,0:T(8,128)(2,1)S(1)}) custom-call(bf16[160,2688]{1,0:T(8,128)(2,1)S(1)} %collective-permute-done.1.refs_0_, bf16[160,2688]{1,0:T(8,128)(2,1)S(1)} %collective-permute-done.2.refs_1_, ...), custom_call_target="tpu_custom_call", output_to_operand_aliasing={{0}: (3, {}), {1}: (2, {})} | custom-call | flops 4613734400 | bytes 16957440 | tf_op jit(solution)/shard_map/pallas_call | solution.py:322
  35.5 2.1 %collective-permute-start.7 = (bf16[160,2688]{1,0:T(8,128)(2,1)S(1)}, bf16[160,2688]{1,0:T(8,128)(2,1)S(1)}, u32[]{:S(2)}, u32[]{:S(2)}) collective-permute-start(bf16[160,2688]{1,0:T(8,128)(2,1)S(1)} %collective-permute-done.3.refs_0_), channel_id=1, source_target_pairs={{0,4},{1,3},{2,0},{3,7},{4,8},{5,1},{6,2},{7,11},{8,12},{9,5},{10,... | collective-permute-start | bytes 2580488 | tf_op jit(solution)/shard_map/ppermute | solution.py:431
  37.6 6.1 %shard_map.85 = (bf16[2560,1536]{1,0:T(8,128)(2,1)S(1)}, bf16[1,2,1408,2560]{3,2,1,0:T(8,128)(2,1)S(1)}) custom-call(bf16[160,2688]{1,0:T(8,128)(2,1)S(1)} %collective-permute-done.4.refs_0_, bf16[160,2688]{1,0:T(8,128)(2,1)S(1)} %collective-permute-done.5.refs_1_, ...), custom_call_target="tpu_custom_call", output_to_operand_aliasing={{0}: (3, {}), {1}: (2, {})} | custom-call | flops 4613734400 | bytes 16957440 | tf_op jit(solution)/shard_map/pallas_call | solution.py:322
  44.7 2.1 %collective-permute-start.10 = (bf16[160,2688]{1,0:T(8,128)(2,1)S(1)}, bf16[160,2688]{1,0:T(8,128)(2,1)S(1)}, u32[]{:S(2)}, u32[]{:S(2)}) collective-permute-start(bf16[160,2688]{1,0:T(8,128)(2,1)S(1)} %collective-permute-done.6.refs_1_), channel_id=1, source_target_pairs={{0,4},{1,3},{2,0},{3,7},{4,8},{5,1},{6,2},{7,11},{8,12},{9,5},{10,... | collective-permute-start | bytes 2580488 | tf_op jit(solution)/shard_map/ppermute | solution.py:431
  46.8 6.1 %shard_map.86 = (bf16[2560,1536]{1,0:T(8,128)(2,1)S(1)}, bf16[1,2,1408,2560]{3,2,1,0:T(8,128)(2,1)S(1)}) custom-call(bf16[160,2688]{1,0:T(8,128)(2,1)S(1)} %collective-permute-done.3.refs_0_, bf16[160,2688]{1,0:T(8,128)(2,1)S(1)} %collective-permute-done.6.refs_1_, ...), custom_call_target="tpu_custom_call", output_to_operand_aliasing={{0}: (3, {}), {1}: (2, {})} | custom-call | flops 4613734400 | bytes 16957440 | tf_op jit(solution)/shard_map/pallas_call | solution.py:322
  54.0 2.1 %collective-permute-start.11 = (bf16[160,2688]{1,0:T(8,128)(2,1)S(1)}, bf16[160,2688]{1,0:T(8,128)(2,1)S(1)}, u32[]{:S(2)}, u32[]{:S(2)}) collective-permute-start(bf16[160,2688]{1,0:T(8,128)(2,1)S(1)} %collective-permute-done.7.refs_0_), channel_id=1, source_target_pairs={{0,4},{1,3},{2,0},{3,7},{4,8},{5,1},{6,2},{7,11},{8,12},{9,5},{10,... | collective-permute-start | bytes 2580488 | tf_op jit(solution)/shard_map/ppermute | solution.py:431
  56.1 6.1 %shard_map.87 = (bf16[2560,1536]{1,0:T(8,128)(2,1)S(1)}, bf16[1,2,1408,2560]{3,2,1,0:T(8,128)(2,1)S(1)}) custom-call(bf16[160,2688]{1,0:T(8,128)(2,1)S(1)} %collective-permute-done.8.refs_0_, bf16[160,2688]{1,0:T(8,128)(2,1)S(1)} %collective-permute-done.9.refs_1_, ...), custom_call_target="tpu_custom_call", output_to_operand_aliasing={{0}: (3, {}), {1}: (2, {})} | custom-call | flops 4613734400 | bytes 16957440 | tf_op jit(solution)/shard_map/pallas_call | solution.py:322
  63.2 6.1 %shard_map.88 = (bf16[2560,1536]{1,0:T(8,128)(2,1)S(1)}, bf16[1,2,1408,2560]{3,2,1,0:T(8,128)(2,1)S(1)}) custom-call(bf16[160,2688]{1,0:T(8,128)(2,1)S(1)} %collective-permute-done.7.refs_0_, bf16[160,2688]{1,0:T(8,128)(2,1)S(1)} %collective-permute-done.10.refs_1_, ...), custom_call_target="tpu_custom_call", output_to_operand_aliasing={{0}: (3, {}), {1}: (2, {})} | custom-call | flops 4613734400 | bytes 16957440 | tf_op jit(solution)/shard_map/pallas_call | solution.py:322
  69.2 3.2 %collective-permute-done.11.refs_0_ = bf16[160,2688]{1,0:T(8,128)(2,1)S(1)} collective-permute-done((bf16[160,2688]{1,0:T(8,128)(2,1)S(1)}, bf16[160,2688]{1,0:T(8,128)(2,1)S(1)}, u32[]{:S(2)}, u32[]{:S(2)}) %collective-permute-start.11) | collective-permute-done | bytes 860192 | tf_op jit(solution)/shard_map/ppermute | solution.py:431
  72.4 6.1 %shard_map.89 = (bf16[2560,1536]{1,0:T(8,128)(2,1)S(1)}, bf16[1,2,1408,2560]{3,2,1,0:T(8,128)(2,1)S(1)}) custom-call(bf16[160,2688]{1,0:T(8,128)(2,1)S(1)} %collective-permute-done.12.refs_0_, bf16[160,2688]{1,0:T(8,128)(2,1)S(1)} %collective-permute-done.13.refs_1_, ...), custom_call_target="tpu_custom_call", output_to_operand_aliasing={{0}: (3, {}), {1}: (2, {})} | custom-call | flops 4613734400 | bytes 16957440 | tf_op jit(solution)/shard_map/pallas_call | solution.py:322
  78.5 6.1 %shard_map.90.hidden_ref = bf16[2560,1536]{1,0:T(8,128)(2,1)S(1)} custom-call(bf16[160,2688]{1,0:T(8,128)(2,1)S(1)} %collective-permute-done.11.refs_0_, bf16[160,2688]{1,0:T(8,128)(2,1)S(1)} %collective-permute-done.14.refs_1_, bf16[1,2,1408,2560]{3,2,1,0:T(8,128)(2,1)S(1)} %get-tuple-element.121.refs_2_, ...), custom_call_target="tpu_custom_call", output_to_operand_aliasing={{}: (3, {})} | custom-call | flops 4613734400 | bytes 16957440 | tf_op jit(solution)/shard_map/pallas_call | solution.py:322
  84.5 4.7 %shard_map.91 = (bf16[160,2560]{1,0:T(8,128)(2,1)S(1)}, bf16[160,2560]{1,0:T(8,128)(2,1)S(1)}) custom-call(s32[81]{0:T(128)S(1)} %dynamic-slice_bitcast_fusion.places_ref, bf16[2560,1536]{1,0:T(8,128)(2,1)S(1)} %shard_map.90.hidden_ref, bf16[1,1408,2560]{2,1,0:T(8,128)(2,1)S(1)} %get-tuple-element.123.w_ref), custom_call_target="tpu_custom_call" | custom-call | flops 2306867200 | bytes 8847360 | tf_op jit(solution)/shard_map/pallas_call | solution.py:392
  89.8 4.7 %shard_map.92 = (bf16[160,2560]{1,0:T(8,128)(2,1)S(1)}, bf16[160,2560]{1,0:T(8,128)(2,1)S(1)}) custom-call(s32[81]{0:T(128)S(1)} %dynamic-slice_bitcast_fusion.places_ref, bf16[2560,1536]{1,0:T(8,128)(2,1)S(1)} %shard_map.90.hidden_ref, bf16[1,1408,2560]{2,1,0:T(8,128)(2,1)S(1)} %get-tuple-element.123.w_ref), custom_call_target="tpu_custom_call" | custom-call | flops 2306867200 | bytes 8847360 | tf_op jit(solution)/shard_map/pallas_call | solution.py:392
  95.3 2.2 %collective-permute-start.17 = (bf16[160,2560]{1,0:T(8,128)(2,1)S(1)}, bf16[160,2560]{1,0:T(8,128)(2,1)S(1)}, u32[]{:S(2)}, u32[]{:S(2)}) collective-permute-start(bf16[160,2560]{1,0:T(8,128)(2,1)S(1)} %add_convert_fusion.8), channel_id=1, source_target_pairs={{0,4},{1,3},{2,0},{3,7},{4,8},{5,1},{6,2},{7,11},{8,12},{9,5},{10,... | collective-permute-start | bytes 2457608 | tf_op jit(solution)/shard_map/ppermute | solution.py:431
  97.4 4.7 %shard_map.93 = (bf16[160,2560]{1,0:T(8,128)(2,1)S(1)}, bf16[160,2560]{1,0:T(8,128)(2,1)S(1)}) custom-call(s32[81]{0:T(128)S(1)} %dynamic-slice_bitcast_fusion.places_ref, bf16[2560,1536]{1,0:T(8,128)(2,1)S(1)} %shard_map.90.hidden_ref, bf16[1,1408,2560]{2,1,0:T(8,128)(2,1)S(1)} %get-tuple-element.123.w_ref), custom_call_target="tpu_custom_call" | custom-call | flops 2306867200 | bytes 8847360 | tf_op jit(solution)/shard_map/pallas_call | solution.py:392
  102.3 4.7 %shard_map.94 = (bf16[160,2560]{1,0:T(8,128)(2,1)S(1)}, bf16[160,2560]{1,0:T(8,128)(2,1)S(1)}) custom-call(s32[81]{0:T(128)S(1)} %dynamic-slice_bitcast_fusion.places_ref, bf16[2560,1536]{1,0:T(8,128)(2,1)S(1)} %shard_map.90.hidden_ref, bf16[1,1408,2560]{2,1,0:T(8,128)(2,1)S(1)} %get-tuple-element.123.w_ref), custom_call_target="tpu_custom_call" | custom-call | flops 2306867200 | bytes 8847360 | tf_op jit(solution)/shard_map/pallas_call | solution.py:392
  111.0 4.7 %shard_map.95 = (bf16[160,2560]{1,0:T(8,128)(2,1)S(1)}, bf16[160,2560]{1,0:T(8,128)(2,1)S(1)}) custom-call(s32[81]{0:T(128)S(1)} %dynamic-slice_bitcast_fusion.places_ref, bf16[2560,1536]{1,0:T(8,128)(2,1)S(1)} %shard_map.90.hidden_ref, bf16[1,1408,2560]{2,1,0:T(8,128)(2,1)S(1)} %get-tuple-element.123.w_ref), custom_call_target="tpu_custom_call" | custom-call | flops 2306867200 | bytes 8847360 | tf_op jit(solution)/shard_map/pallas_call | solution.py:392
  115.6 3.9 %collective-permute-done.22 = bf16[160,2560]{1,0:T(8,128)(2,1)S(1)} collective-permute-done((bf16[160,2560]{1,0:T(8,128)(2,1)S(1)}, bf16[160,2560]{1,0:T(8,128)(2,1)S(1)}, u32[]{:S(2)}, u32[]{:S(2)}) %collective-permute-start.22) | collective-permute-done | bytes 819232 | tf_op jit(solution)/shard_map/ppermute | solution.py:431
  119.9 4.7 %shard_map.96 = (bf16[160,2560]{1,0:T(8,128)(2,1)S(1)}, bf16[160,2560]{1,0:T(8,128)(2,1)S(1)}) custom-call(s32[81]{0:T(128)S(1)} %dynamic-slice_bitcast_fusion.places_ref, bf16[2560,1536]{1,0:T(8,128)(2,1)S(1)} %shard_map.90.hidden_ref, bf16[1,1408,2560]{2,1,0:T(8,128)(2,1)S(1)} %get-tuple-element.123.w_ref), custom_call_target="tpu_custom_call" | custom-call | flops 2306867200 | bytes 8847360 | tf_op jit(solution)/shard_map/pallas_call | solution.py:392
  126.3 2.0 %collective-permute-done.20 = bf16[160,2560]{1,0:T(8,128)(2,1)S(1)} collective-permute-done((bf16[160,2560]{1,0:T(8,128)(2,1)S(1)}, bf16[160,2560]{1,0:T(8,128)(2,1)S(1)}, u32[]{:S(2)}, u32[]{:S(2)}) %collective-permute-start.20) | collective-permute-done | bytes 819232 | tf_op jit(solution)/shard_map/ppermute | solution.py:431
  130.3 4.7 %shard_map.97 = (bf16[160,2560]{1,0:T(8,128)(2,1)S(1)}, bf16[160,2560]{1,0:T(8,128)(2,1)S(1)}) custom-call(s32[81]{0:T(128)S(1)} %dynamic-slice_bitcast_fusion.places_ref, bf16[2560,1536]{1,0:T(8,128)(2,1)S(1)} %shard_map.90.hidden_ref, bf16[1,1408,2560]{2,1,0:T(8,128)(2,1)S(1)} %get-tuple-element.123.w_ref), custom_call_target="tpu_custom_call" | custom-call | flops 2306867200 | bytes 8847360 | tf_op jit(solution)/shard_map/pallas_call | solution.py:392
  134.9 2.1 %collective-permute-done.26 = bf16[160,2560]{1,0:T(8,128)(2,1)S(1)} collective-permute-done((bf16[160,2560]{1,0:T(8,128)(2,1)S(1)}, bf16[160,2560]{1,0:T(8,128)(2,1)S(1)}, u32[]{:S(2)}, u32[]{:S(2)}) %collective-permute-start.26) | collective-permute-done | bytes 819232 | tf_op jit(solution)/shard_map/ppermute | solution.py:431
  139.0 3.2 %shard_map.98 = bf16[160,2560]{1,0:T(8,128)(2,1)S(1)} custom-call(s32[81]{0:T(128)S(1)} %dynamic-slice_bitcast_fusion.places_ref, bf16[2560,1536]{1,0:T(8,128)(2,1)S(1)} %shard_map.90.hidden_ref, bf16[1,1408,2560]{2,1,0:T(8,128)(2,1)S(1)} %get-tuple-element.123.w_ref), custom_call_target="tpu_custom_call" | custom-call | flops 1153433600 | bytes 8028160 | tf_op jit(solution)/shard_map/pallas_call | solution.py:392
  142.3 3.6 %collective-permute-done.24 = bf16[160,2560]{1,0:T(8,128)(2,1)S(1)} collective-permute-done((bf16[160,2560]{1,0:T(8,128)(2,1)S(1)}, bf16[160,2560]{1,0:T(8,128)(2,1)S(1)}, u32[]{:S(2)}, u32[]{:S(2)}) %collective-permute-start.24) | collective-permute-done | bytes 819232 | tf_op jit(solution)/shard_map/ppermute | solution.py:431
  147.8 6.8 %collective-permute-done.27 = bf16[160,2560]{1,0:T(8,128)(2,1)S(1)} collective-permute-done((bf16[160,2560]{1,0:T(8,128)(2,1)S(1)}, bf16[160,2560]{1,0:T(8,128)(2,1)S(1)}, u32[]{:S(2)}, u32[]{:S(2)}) %collective-permute-start.27) | collective-permute-done | bytes 819232 | tf_op jit(solution)/shard_map/ppermute | solution.py:431
  154.9 3.2 %shard_map.99 = bf16[160,2560]{1,0:T(8,128)(2,1)S(1)} custom-call(s32[81]{0:T(128)S(1)} %dynamic-slice_bitcast_fusion.places_ref, bf16[2560,1536]{1,0:T(8,128)(2,1)S(1)} %shard_map.90.hidden_ref, bf16[1,1408,2560]{2,1,0:T(8,128)(2,1)S(1)} %get-tuple-element.123.w_ref), custom_call_target="tpu_custom_call" | custom-call | flops 1153433600 | bytes 8028160 | tf_op jit(solution)/shard_map/pallas_call | solution.py:392
  158.2 5.2 %collective-permute-done.29 = bf16[160,2560]{1,0:T(8,128)(2,1)S(1)} collective-permute-done((bf16[160,2560]{1,0:T(8,128)(2,1)S(1)}, bf16[160,2560]{1,0:T(8,128)(2,1)S(1)}, u32[]{:S(2)}, u32[]{:S(2)}) %collective-permute-start.29) | collective-permute-done | bytes 819232 | tf_op jit(solution)/shard_map/ppermute | solution.py:431
  (62 shorter events, 25.7 us)
Async XLA Ops:
  0.0 0.7 copy-start
  0.7 0.7 copy-start.1
  3.3 3.2 %collective-permute-start = (bf16[160,2688]{1,0:T(8,128)(2,1)S(1)}, bf16[160,2688]{1,0:T(8,128)(2,1)S(1)}, u32[]{:S(2)}, u32[]{:S(2)}) collective-permute-start(bf16[160,2688]{1,0:T(8,128)(2,1)S(1)} %shard_map.82.refs_0_), channel_id=1, source_target_pairs={{0,1},{1,0},{2,3},{3,2},{4,5},{5,4},{6,7},{7,6},{8,9},{9,8},{10,11... | collective-permute-start | bytes 2580488 | tf_op jit(solution)/shard_map/ppermute | solution.py:434
  3.8 13.4 %collective-permute-start.1 = (bf16[160,2688]{1,0:T(8,128)(2,1)S(1)}, bf16[160,2688]{1,0:T(8,128)(2,1)S(1)}, u32[]{:S(2)}, u32[]{:S(2)}) collective-permute-start(bf16[160,2688]{1,0:T(8,128)(2,1)S(1)} %shard_map.82.refs_0_), channel_id=1, source_target_pairs={{0,4},{1,3},{2,0},{3,7},{4,8},{5,1},{6,2},{7,11},{8,12},{9,5},{10,... | collective-permute-start | bytes 2580488 | tf_op jit(solution)/shard_map/ppermute | solution.py:431
  6.4 19.9 %collective-permute-start.2 = (bf16[160,2688]{1,0:T(8,128)(2,1)S(1)}, bf16[160,2688]{1,0:T(8,128)(2,1)S(1)}, u32[]{:S(2)}, u32[]{:S(2)}) collective-permute-start(bf16[160,2688]{1,0:T(8,128)(2,1)S(1)} %collective-permute-done.refs_1_), channel_id=1, source_target_pairs={{0,4},{1,3},{2,0},{3,7},{4,8},{5,1},{6,2},{7,11},{8,12},{9,5},{10,... | collective-permute-start | bytes 2580488 | tf_op jit(solution)/shard_map/ppermute | solution.py:431
  17.2 18.3 %collective-permute-start.3 = (bf16[160,2688]{1,0:T(8,128)(2,1)S(1)}, bf16[160,2688]{1,0:T(8,128)(2,1)S(1)}, u32[]{:S(2)}, u32[]{:S(2)}) collective-permute-start(bf16[160,2688]{1,0:T(8,128)(2,1)S(1)} %collective-permute-done.1.refs_0_), channel_id=1, source_target_pairs={{0,4},{1,3},{2,0},{3,7},{4,8},{5,1},{6,2},{7,11},{8,12},{9,5},{10,... | collective-permute-start | bytes 2580488 | tf_op jit(solution)/shard_map/ppermute | solution.py:431
  19.2 16.3 %collective-permute-start.4 = (bf16[160,2688]{1,0:T(8,128)(2,1)S(1)}, bf16[160,2688]{1,0:T(8,128)(2,1)S(1)}, u32[]{:S(2)}, u32[]{:S(2)}) collective-permute-start(bf16[160,2688]{1,0:T(8,128)(2,1)S(1)} %collective-permute-done.1.refs_0_), channel_id=1, source_target_pairs={{0,1},{1,0},{2,3},{3,2},{4,5},{5,4},{6,7},{7,6},{8,9},{9,8},{10,11... | collective-permute-start | bytes 2580488 | tf_op jit(solution)/shard_map/ppermute | solution.py:434
  26.3 9.2 %collective-permute-start.5 = (bf16[160,2688]{1,0:T(8,128)(2,1)S(1)}, bf16[160,2688]{1,0:T(8,128)(2,1)S(1)}, u32[]{:S(2)}, u32[]{:S(2)}) collective-permute-start(bf16[160,2688]{1,0:T(8,128)(2,1)S(1)} %collective-permute-done.2.refs_1_), channel_id=1, source_target_pairs={{0,1},{1,0},{2,3},{3,2},{4,5},{5,4},{6,7},{7,6},{8,9},{9,8},{10,11... | collective-permute-start | bytes 2580488 | tf_op jit(solution)/shard_map/ppermute | solution.py:434
  26.3 18.4 %collective-permute-start.6 = (bf16[160,2688]{1,0:T(8,128)(2,1)S(1)}, bf16[160,2688]{1,0:T(8,128)(2,1)S(1)}, u32[]{:S(2)}, u32[]{:S(2)}) collective-permute-start(bf16[160,2688]{1,0:T(8,128)(2,1)S(1)} %collective-permute-done.2.refs_1_), channel_id=1, source_target_pairs={{0,4},{1,3},{2,0},{3,7},{4,8},{5,1},{6,2},{7,11},{8,12},{9,5},{10,... | collective-permute-start | bytes 2580488 | tf_op jit(solution)/shard_map/ppermute | solution.py:431
  35.5 18.4 %collective-permute-start.7 = (bf16[160,2688]{1,0:T(8,128)(2,1)S(1)}, bf16[160,2688]{1,0:T(8,128)(2,1)S(1)}, u32[]{:S(2)}, u32[]{:S(2)}) collective-permute-start(bf16[160,2688]{1,0:T(8,128)(2,1)S(1)} %collective-permute-done.3.refs_0_), channel_id=1, source_target_pairs={{0,4},{1,3},{2,0},{3,7},{4,8},{5,1},{6,2},{7,11},{8,12},{9,5},{10,... | collective-permute-start | bytes 2580488 | tf_op jit(solution)/shard_map/ppermute | solution.py:431
  37.6 16.3 %collective-permute-start.8 = (bf16[160,2688]{1,0:T(8,128)(2,1)S(1)}, bf16[160,2688]{1,0:T(8,128)(2,1)S(1)}, u32[]{:S(2)}, u32[]{:S(2)}) collective-permute-start(bf16[160,2688]{1,0:T(8,128)(2,1)S(1)} %collective-permute-done.3.refs_0_), channel_id=1, source_target_pairs={{0,1},{1,0},{2,3},{3,2},{4,5},{5,4},{6,7},{7,6},{8,9},{9,8},{10,11... | collective-permute-start | bytes 2580488 | tf_op jit(solution)/shard_map/ppermute | solution.py:434
  44.7 9.2 %collective-permute-start.9 = (bf16[160,2688]{1,0:T(8,128)(2,1)S(1)}, bf16[160,2688]{1,0:T(8,128)(2,1)S(1)}, u32[]{:S(2)}, u32[]{:S(2)}) collective-permute-start(bf16[160,2688]{1,0:T(8,128)(2,1)S(1)} %collective-permute-done.6.refs_1_), channel_id=1, source_target_pairs={{0,1},{1,0},{2,3},{3,2},{4,5},{5,4},{6,7},{7,6},{8,9},{9,8},{10,11... | collective-permute-start | bytes 2580488 | tf_op jit(solution)/shard_map/ppermute | solution.py:434
  44.7 18.4 %collective-permute-start.10 = (bf16[160,2688]{1,0:T(8,128)(2,1)S(1)}, bf16[160,2688]{1,0:T(8,128)(2,1)S(1)}, u32[]{:S(2)}, u32[]{:S(2)}) collective-permute-start(bf16[160,2688]{1,0:T(8,128)(2,1)S(1)} %collective-permute-done.6.refs_1_), channel_id=1, source_target_pairs={{0,4},{1,3},{2,0},{3,7},{4,8},{5,1},{6,2},{7,11},{8,12},{9,5},{10,... | collective-permute-start | bytes 2580488 | tf_op jit(solution)/shard_map/ppermute | solution.py:431
  54.0 18.4 %collective-permute-start.11 = (bf16[160,2688]{1,0:T(8,128)(2,1)S(1)}, bf16[160,2688]{1,0:T(8,128)(2,1)S(1)}, u32[]{:S(2)}, u32[]{:S(2)}) collective-permute-start(bf16[160,2688]{1,0:T(8,128)(2,1)S(1)} %collective-permute-done.7.refs_0_), channel_id=1, source_target_pairs={{0,4},{1,3},{2,0},{3,7},{4,8},{5,1},{6,2},{7,11},{8,12},{9,5},{10,... | collective-permute-start | bytes 2580488 | tf_op jit(solution)/shard_map/ppermute | solution.py:431
  56.1 16.3 %collective-permute-start.12 = (bf16[160,2688]{1,0:T(8,128)(2,1)S(1)}, bf16[160,2688]{1,0:T(8,128)(2,1)S(1)}, u32[]{:S(2)}, u32[]{:S(2)}) collective-permute-start(bf16[160,2688]{1,0:T(8,128)(2,1)S(1)} %collective-permute-done.7.refs_0_), channel_id=1, source_target_pairs={{0,1},{1,0},{2,3},{3,2},{4,5},{5,4},{6,7},{7,6},{8,9},{9,8},{10,11... | collective-permute-start | bytes 2580488 | tf_op jit(solution)/shard_map/ppermute | solution.py:434
  63.2 9.2 %collective-permute-start.13 = (bf16[160,2688]{1,0:T(8,128)(2,1)S(1)}, bf16[160,2688]{1,0:T(8,128)(2,1)S(1)}, u32[]{:S(2)}, u32[]{:S(2)}) collective-permute-start(bf16[160,2688]{1,0:T(8,128)(2,1)S(1)} %collective-permute-done.10.refs_1_), channel_id=1, source_target_pairs={{0,1},{1,0},{2,3},{3,2},{4,5},{5,4},{6,7},{7,6},{8,9},{9,8},{10,11... | collective-permute-start | bytes 2580488 | tf_op jit(solution)/shard_map/ppermute | solution.py:434
  72.4 6.1 %collective-permute-start.14 = (bf16[160,2688]{1,0:T(8,128)(2,1)S(1)}, bf16[160,2688]{1,0:T(8,128)(2,1)S(1)}, u32[]{:S(2)}, u32[]{:S(2)}) collective-permute-start(bf16[160,2688]{1,0:T(8,128)(2,1)S(1)} %collective-permute-done.11.refs_0_), channel_id=1, source_target_pairs={{0,1},{1,0},{2,3},{3,2},{4,5},{5,4},{6,7},{7,6},{8,9},{9,8},{10,11... | collective-permute-start | bytes 2580488 | tf_op jit(solution)/shard_map/ppermute | solution.py:434
  89.2 5.8 %collective-permute-start.15 = (bf16[160,2560]{1,0:T(8,128)(2,1)S(1)}, bf16[160,2560]{1,0:T(8,128)(2,1)S(1)}, u32[]{:S(2)}, u32[]{:S(2)}) collective-permute-start(bf16[160,2560]{1,0:T(8,128)(2,1)S(1)} %get-tuple-element.126), channel_id=1, source_target_pairs={{0,1},{1,0},{2,3},{3,2},{4,5},{5,4},{6,7},{7,6},{8,9},{9,8},{10,11... | collective-permute-start | bytes 2457608 | tf_op jit(solution)/shard_map/ppermute | solution.py:434
  94.5 14.3 %collective-permute-start.16 = (bf16[160,2560]{1,0:T(8,128)(2,1)S(1)}, bf16[160,2560]{1,0:T(8,128)(2,1)S(1)}, u32[]{:S(2)}, u32[]{:S(2)}) collective-permute-start(bf16[160,2560]{1,0:T(8,128)(2,1)S(1)} %get-tuple-element.133), channel_id=1, source_target_pairs={{0,1},{1,0},{2,3},{3,2},{4,5},{5,4},{6,7},{7,6},{8,9},{9,8},{10,11... | collective-permute-start | bytes 2457608 | tf_op jit(solution)/shard_map/ppermute | solution.py:434
  94.6 7.6 %collective-permute-start.18 = (bf16[160,2560]{1,0:T(8,128)(2,1)S(1)}, bf16[160,2560]{1,0:T(8,128)(2,1)S(1)}, u32[]{:S(2)}, u32[]{:S(2)}) collective-permute-start(bf16[160,2560]{1,0:T(8,128)(2,1)S(1)} %get-tuple-element.136), channel_id=1, source_target_pairs={{0,1},{1,0},{2,3},{3,2},{4,5},{5,4},{6,7},{7,6},{8,9},{9,8},{10,11... | collective-permute-start | bytes 2457608 | tf_op jit(solution)/shard_map/ppermute | solution.py:434
  95.3 13.5 %collective-permute-start.17 = (bf16[160,2560]{1,0:T(8,128)(2,1)S(1)}, bf16[160,2560]{1,0:T(8,128)(2,1)S(1)}, u32[]{:S(2)}, u32[]{:S(2)}) collective-permute-start(bf16[160,2560]{1,0:T(8,128)(2,1)S(1)} %add_convert_fusion.8), channel_id=1, source_target_pairs={{0,4},{1,3},{2,0},{3,7},{4,8},{5,1},{6,2},{7,11},{8,12},{9,5},{10,... | collective-permute-start | bytes 2457608 | tf_op jit(solution)/shard_map/ppermute | solution.py:431
  107.0 19.2 %collective-permute-start.19 = (bf16[160,2560]{1,0:T(8,128)(2,1)S(1)}, bf16[160,2560]{1,0:T(8,128)(2,1)S(1)}, u32[]{:S(2)}, u32[]{:S(2)}) collective-permute-start(bf16[160,2560]{1,0:T(8,128)(2,1)S(1)} %get-tuple-element.144), channel_id=1, source_target_pairs={{0,1},{1,0},{2,3},{3,2},{4,5},{5,4},{6,7},{7,6},{8,9},{9,8},{10,11... | collective-permute-start | bytes 2457608 | tf_op jit(solution)/shard_map/ppermute | solution.py:434
  107.1 12.4 %collective-permute-start.22 = (bf16[160,2560]{1,0:T(8,128)(2,1)S(1)}, bf16[160,2560]{1,0:T(8,128)(2,1)S(1)}, u32[]{:S(2)}, u32[]{:S(2)}) collective-permute-start(bf16[160,2560]{1,0:T(8,128)(2,1)S(1)} %add_convert_fusion.6), channel_id=1, source_target_pairs={{0,4},{1,3},{2,0},{3,7},{4,8},{5,1},{6,2},{7,11},{8,12},{9,5},{10,... | collective-permute-start | bytes 2457608 | tf_op jit(solution)/shard_map/ppermute | solution.py:431
  108.7 10.8 %collective-permute-start.21 = (bf16[160,2560]{1,0:T(8,128)(2,1)S(1)}, bf16[160,2560]{1,0:T(8,128)(2,1)S(1)}, u32[]{:S(2)}, u32[]{:S(2)}) collective-permute-start(bf16[160,2560]{1,0:T(8,128)(2,1)S(1)} %get-tuple-element.147), channel_id=1, source_target_pairs={{0,1},{1,0},{2,3},{3,2},{4,5},{5,4},{6,7},{7,6},{8,9},{9,8},{10,11... | collective-permute-start | bytes 2457608 | tf_op jit(solution)/shard_map/ppermute | solution.py:434
  109.1 19.2 %collective-permute-start.20 = (bf16[160,2560]{1,0:T(8,128)(2,1)S(1)}, bf16[160,2560]{1,0:T(8,128)(2,1)S(1)}, u32[]{:S(2)}, u32[]{:S(2)}) collective-permute-start(bf16[160,2560]{1,0:T(8,128)(2,1)S(1)} %add_convert_fusion.7), channel_id=1, source_target_pairs={{0,4},{1,3},{2,0},{3,7},{4,8},{5,1},{6,2},{7,11},{8,12},{9,5},{10,... | collective-permute-start | bytes 2457608 | tf_op jit(solution)/shard_map/ppermute | solution.py:431
  124.5 17.7 %collective-permute-start.23 = (bf16[160,2560]{1,0:T(8,128)(2,1)S(1)}, bf16[160,2560]{1,0:T(8,128)(2,1)S(1)}, u32[]{:S(2)}, u32[]{:S(2)}) collective-permute-start(bf16[160,2560]{1,0:T(8,128)(2,1)S(1)} %get-tuple-element.156), channel_id=1, source_target_pairs={{0,1},{1,0},{2,3},{3,2},{4,5},{5,4},{6,7},{7,6},{8,9},{9,8},{10,11... | collective-permute-start | bytes 2457608 | tf_op jit(solution)/shard_map/ppermute | solution.py:434
  124.6 12.4 %collective-permute-start.26 = (bf16[160,2560]{1,0:T(8,128)(2,1)S(1)}, bf16[160,2560]{1,0:T(8,128)(2,1)S(1)}, u32[]{:S(2)}, u32[]{:S(2)}) collective-permute-start(bf16[160,2560]{1,0:T(8,128)(2,1)S(1)} %add_convert_fusion.4), channel_id=1, source_target_pairs={{0,4},{1,3},{2,0},{3,7},{4,8},{5,1},{6,2},{7,11},{8,12},{9,5},{10,... | collective-permute-start | bytes 2457608 | tf_op jit(solution)/shard_map/ppermute | solution.py:431
  126.3 10.8 %collective-permute-start.25 = (bf16[160,2560]{1,0:T(8,128)(2,1)S(1)}, bf16[160,2560]{1,0:T(8,128)(2,1)S(1)}, u32[]{:S(2)}, u32[]{:S(2)}) collective-permute-start(bf16[160,2560]{1,0:T(8,128)(2,1)S(1)} %get-tuple-element.159), channel_id=1, source_target_pairs={{0,1},{1,0},{2,3},{3,2},{4,5},{5,4},{6,7},{7,6},{8,9},{9,8},{10,11... | collective-permute-start | bytes 2457608 | tf_op jit(solution)/shard_map/ppermute | solution.py:434
  128.6 17.2 %collective-permute-start.24 = (bf16[160,2560]{1,0:T(8,128)(2,1)S(1)}, bf16[160,2560]{1,0:T(8,128)(2,1)S(1)}, u32[]{:S(2)}, u32[]{:S(2)}) collective-permute-start(bf16[160,2560]{1,0:T(8,128)(2,1)S(1)} %add_convert_fusion.5), channel_id=1, source_target_pairs={{0,4},{1,3},{2,0},{3,7},{4,8},{5,1},{6,2},{7,11},{8,12},{9,5},{10,... | collective-permute-start | bytes 2457608 | tf_op jit(solution)/shard_map/ppermute | solution.py:431
  137.4 17.2 %collective-permute-start.27 = (bf16[160,2560]{1,0:T(8,128)(2,1)S(1)}, bf16[160,2560]{1,0:T(8,128)(2,1)S(1)}, u32[]{:S(2)}, u32[]{:S(2)}) collective-permute-start(bf16[160,2560]{1,0:T(8,128)(2,1)S(1)} %add_convert_fusion.2), channel_id=1, source_target_pairs={{0,4},{1,3},{2,0},{3,7},{4,8},{5,1},{6,2},{7,11},{8,12},{9,5},{10,... | collective-permute-start | bytes 2457608 | tf_op jit(solution)/shard_map/ppermute | solution.py:431
  146.2 17.2 %collective-permute-start.29 = (bf16[160,2560]{1,0:T(8,128)(2,1)S(1)}, bf16[160,2560]{1,0:T(8,128)(2,1)S(1)}, u32[]{:S(2)}, u32[]{:S(2)}) collective-permute-start(bf16[160,2560]{1,0:T(8,128)(2,1)S(1)} %add_convert_fusion.3), channel_id=1, source_target_pairs={{0,4},{1,3},{2,0},{3,7},{4,8},{5,1},{6,2},{7,11},{8,12},{9,5},{10,... | collective-permute-start | bytes 2457608 | tf_op jit(solution)/shard_map/ppermute | solution.py:431
  154.8 8.5 %collective-permute-start.28 = (bf16[160,2560]{1,0:T(8,128)(2,1)S(1)}, bf16[160,2560]{1,0:T(8,128)(2,1)S(1)}, u32[]{:S(2)}, u32[]{:S(2)}) collective-permute-start(bf16[160,2560]{1,0:T(8,128)(2,1)S(1)} %add_convert_fusion.1), channel_id=1, source_target_pairs={{0,1},{1,0},{2,3},{3,2},{4,5},{5,4},{6,7},{7,6},{8,9},{9,8},{10,11... | collective-permute-start | bytes 2457608 | tf_op jit(solution)/shard_map/ppermute | solution.py:434
  (1 other events, 0.7 us)
